TPU v7x, 128 devices: a whole 4x4x4 slice. The times are simulated.
128 devices in a mesh: enc: 32 (over z, x, core), dec: 4 (over y).
Axes of the slice: x: 4, y: 4, z: 4, core: 2. Of those that a mesh axis runs over, the one named last changes fastest.
Arguments:
- enc_rows: bfloat16 [16384, 4096], P('enc'), may hold values from -6 to 6
- key_weight: bfloat16 [4096, 4096], P('enc', 'dec'), may hold values from -0.09375 to 0.09375
- value_weight: bfloat16 [4096, 4096], P('enc', 'dec'), may hold values from -0.09375 to 0.09375
- queries: bfloat16 [32, 16, 4096], P('enc', None, 'dec'), may hold values from -8 to 8
- ctx_grad: bfloat16 [32, 16, 4096], P('enc', None, 'dec'), may hold values from -6 to 6
- passage_len: int32 [32, 4], P('enc'), may hold values from 1 to 256, 512 in all within a row
- passage_question: int32 [128, 1], P('enc'), may hold values from 0 to 31
Outputs:
- ctx: float32 [32, 16, 4096], P('enc', None, 'dec')
- enc_grad: float32 [16384, 4096], P('enc', 'dec')
Inputs may be any that keep to these rules, and one draw needn't show every extreme that they name: Each row of passage_len sums to 512 and its largest entry is 256. `passage_question`: every question has at least one passage.
All inputs are finite; a program needn't handle non-finite values.
Results may differ from a plain program's by a relative error of at most 0.02.
Values may be sent and summed in bfloat16 or wider, within the bound.
No kernel may reach another device: no remote copies, remote signals or barrier semaphores. Data moves between devices by JAX's collectives and lax.ppermute only.
A program may use at most 128 MiB of HBM per device.

v0:
```python
import jax
import jax.numpy as jnp
from jax import lax
from jax.sharding import PartitionSpec as P

HEAD_DIM = 64


def body(enc_rows, key_weight, value_weight, queries, ctx_grad, passage_len, passage_question):
    local_width = key_weight.shape[1]
    head_count = local_width // HEAD_DIM
    token_count = enc_rows.shape[0]
    passage_count = passage_len.shape[1]
    passage_ends = jnp.cumsum(passage_len[0])
    positions = jnp.arange(token_count, dtype=jnp.int32)
    segment = jnp.sum((positions[:, None] >= passage_ends[None, :]).astype(jnp.int32), axis=1)
    member = segment[None, :] == jnp.arange(passage_count, dtype=jnp.int32)[:, None]
    assigned = passage_question[:, 0]
    pieces = (
        lax.all_gather(key_weight, "enc", axis=0, tiled=True),
        lax.all_gather(value_weight, "enc", axis=0, tiled=True),
    )
    key_proj = jnp.dot(enc_rows, pieces[0], preferred_element_type=jnp.float32)
    value_proj = jnp.dot(enc_rows, pieces[1], preferred_element_type=jnp.float32)
    key_heads = key_proj.astype(jnp.bfloat16).reshape(token_count, head_count, HEAD_DIM)
    value_heads = value_proj.astype(jnp.bfloat16).reshape(token_count, head_count, HEAD_DIM)
    all_queries, all_grads = (
        lax.all_gather(queries, "enc", axis=0, tiled=True),
        lax.all_gather(ctx_grad, "enc", axis=0, tiled=True),
    )
    question_count = all_queries.shape[0]
    dec_len = all_queries.shape[1]
    pass_queries = all_queries[assigned].reshape(passage_count, dec_len, head_count, HEAD_DIM)
    pass_grads = all_grads[assigned].reshape(passage_count, dec_len, head_count, HEAD_DIM)
    scores = jnp.einsum(
        "ptha,sha->phts", pass_queries, key_heads, preferred_element_type=jnp.float32
    )
    inside = member[:, None, None, :]
    part_max = jnp.max(jnp.where(inside, scores, -1e30), axis=3)
    owned = assigned[:, None] == jnp.arange(question_count, dtype=jnp.int32)[None, :]
    local_max = jnp.max(jnp.where(owned[:, :, None, None], part_max[:, None], -1e30), axis=0)
    global_max = lax.pmax(local_max, "enc")
    score_top = global_max[assigned]
    unnorm = jnp.where(inside, jnp.exp(scores - score_top[..., None]), 0.0)
    part_total = jnp.sum(unnorm, axis=3)
    part_numer = jnp.einsum(
        "phts,sha->ptha",
        unnorm.astype(jnp.bfloat16),
        value_heads,
        preferred_element_type=jnp.float32,
    )
    owned_float = owned.astype(jnp.float32)
    numer = jnp.einsum("pq,ptha->qtha", owned_float, part_numer, precision=lax.Precision.HIGHEST)
    denom = jnp.einsum("pq,pht->qht", owned_float, part_total, precision=lax.Precision.HIGHEST)
    own_count = queries.shape[0]
    numer_all, denom_all = lax.psum((numer, denom), "enc")
    context = numer_all / jnp.transpose(denom_all, (0, 2, 1))[..., None]
    first_row = lax.axis_index("enc") * own_count
    own_context = lax.dynamic_slice_in_dim(context, first_row, own_count, 0)
    ctx = own_context.reshape(own_count, dec_len, local_width)
    pass_context = context[assigned]
    delta = jnp.transpose(jnp.sum(pass_grads.astype(jnp.float32) * pass_context, axis=3), (0, 2, 1))
    probs = unnorm / denom_all[assigned][..., None]
    value_grad = jnp.einsum(
        "phts,ptha->sha", probs.astype(jnp.bfloat16), pass_grads, preferred_element_type=jnp.float32
    )
    dprob = jnp.einsum(
        "ptha,sha->phts", pass_grads, value_heads, preferred_element_type=jnp.float32
    )
    ds_b = (probs * (dprob - delta[..., None])).astype(jnp.bfloat16)
    key_grad = jnp.einsum("phts,ptha->sha", ds_b, pass_queries, preferred_element_type=jnp.float32)
    key_grad_b = key_grad.astype(jnp.bfloat16).reshape(token_count, local_width)
    value_grad_b = value_grad.astype(jnp.bfloat16).reshape(token_count, local_width)
    pieces = lax.all_gather((key_weight, value_weight), "enc", axis=0, tiled=True)
    result = jnp.einsum("sc,rc->sr", key_grad_b, pieces[0], preferred_element_type=jnp.float32)
    partial_grad = result + jnp.einsum(
        "sc,rc->sr", value_grad_b, pieces[1], preferred_element_type=jnp.float32
    )
    enc_grad = lax.psum_scatter(partial_grad, "dec", scatter_dimension=1, tiled=True)
    return (ctx, enc_grad)


def solution(mesh):
    return jax.shard_map(
        body,
        mesh=mesh,
        in_specs=(
            P("enc", None),
            P("enc", "dec"),
            P("enc", "dec"),
            P("enc", None, "dec"),
            P("enc", None, "dec"),
            P("enc", None),
            P("enc", None),
        ),
        out_specs=(P("enc", None, "dec"), P("enc", "dec")),
        check_vma=False,
    )
```

profile of v0, /device:TPU:1, one launch (start us, length us, event | category | flops | bytes accessed | tf_op | source)
XLA Modules:
  0.0 611.4 jit_solution(11186365072556673198)
XLA Ops:
  7.2 0.7 all-gather.9.cloned.1.call-update
  7.9 0.7 all-gather.11.cloned.1.call-update
  8.7 0.7 all-gather.5.cloned.1.call-update
  9.4 0.5 all-gather.7.cloned.1.call-update
  10.0 0.8 reduce-window.8
  10.8 0.7 fusion.16
  11.6 0.7 iota_compare_fusion.2
  12.3 44.5 %all-gather.9.cloned.1.call-done = bf16[32,16,1024]{2,1,0:T(8,128)(2,1)} async-done(((bf16[1,16,1024]{2,1,0:T(8,128)(2,1)}), bf16[32,16,1024]{2,1,0:T(8,128)(2,1)}) %all-gather.9.cloned.1.call-update) | async-done | bytes 1048592 | tf_op jit(solution)/shard_map/all_gather | solution.py:28
  56.8 1.8 gather_fusion
  58.6 0.2 reshape.97
  58.8 0.8 copy.41
  59.6 41.6 %all-gather.11.cloned.1.call-done = bf16[32,16,1024]{2,1,0:T(8,128)(2,1)} async-done(((bf16[1,16,1024]{2,1,0:T(8,128)(2,1)}), bf16[32,16,1024]{2,1,0:T(8,128)(2,1)}) %all-gather.11.cloned.1.call-update) | async-done | bytes 1048592 | tf_op jit(solution)/shard_map/all_gather | solution.py:29
  101.2 1.8 gather_fusion.3
  103.0 0.2 reshape.99
  103.2 0.8 copy.49
  104.0 51.8 %all-gather.5.cloned.1.call-done = bf16[4096,1024]{1,0:T(8,128)(2,1)} async-done(((bf16[128,1024]{1,0:T(8,128)(2,1)}), bf16[4096,1024]{1,0:T(8,128)(2,1)}) %all-gather.5.cloned.1.call-update) | async-done | bytes 8388624 | tf_op jit(solution)/shard_map/all_gather | solution.py:21
  155.8 9.1 %convolution_convert_fusion.1 = bf16[512,1024]{1,0:T(8,128)(2,1)S(1)} fusion(bf16[512,4096]{1,0:T(8,128)(2,1)} %param.7, bf16[4096,1024]{1,0:T(8,128)(2,1)} %all-gather.5.cloned.1.call-done), kind=kOutput, calls=%fused_computation.13 | convolution fusion | flops 4295491584 | bytes 13631488 | tf_op jit(solution)/shard_map/dot_general | solution.py:24
  164.9 0.5 copy.39
  165.5 45.0 %all-gather.7.cloned.1.call-done = bf16[4096,1024]{1,0:T(8,128)(2,1)} async-done(((bf16[128,1024]{1,0:T(8,128)(2,1)}), bf16[4096,1024]{1,0:T(8,128)(2,1)}) %all-gather.7.cloned.1.call-update) | async-done | bytes 8388624 | tf_op jit(solution)/shard_map/all_gather | solution.py:20
  210.4 9.1 %convolution_convert_fusion = bf16[512,1024]{1,0:T(8,128)(2,1)S(1)} fusion(bf16[512,4096]{1,0:T(8,128)(2,1)} %param.7, bf16[4096,1024]{1,0:T(8,128)(2,1)} %all-gather.7.cloned.1.call-done), kind=kOutput, calls=%fused_computation.12 | convolution fusion | flops 4295491584 | bytes 13631488 | tf_op jit(solution)/shard_map/dot_general | solution.py:23
  219.6 1.3 copy.40
  220.9 1.7 fusion.23
  222.6 0.3 select_reduce_fusion
  222.9 0.2 select_reduce_fusion.1
  223.1 0.8 copy.43
  224.0 123.7 %pmax.7 = f32[32,16,16]{2,1,0:T(8,128)} all-reduce(f32[32,16,16]{2,1,0:T(8,128)} %copy.43), channel_id=1, replica_groups=mesh['enc'=32,'dec'=4] {'enc'}, use_global_device_ids=true, to_apply=%region_4.5 | all-reduce | flops 8192 | bytes 65536 | tf_op jit(solution)/shard_map/pmax | solution.py:42
  347.6 1.5 gather_fusion.1
  349.2 0.5 convolution_bitcast_fusion
  349.7 3.6 fusion.9
  353.4 0.7 fusion.1
  354.1 1.0 fusion.14
  355.1 125.4 %psum.15 = f32[32,16,16]{0,2,1:T(8,128)S(1)} all-reduce(f32[32,16,16]{0,2,1:T(8,128)} %fusion.14), channel_id=1, replica_groups=mesh['enc'=32,'dec'=4] {'enc'}, use_global_device_ids=true, to_apply=%region_7.8 | all-reduce | flops 8192 | bytes 65536 | tf_op jit(solution)/shard_map/psum | solution.py:56
  480.5 0.8 copy.47
  481.3 0.7 copy.46
  482.0 1.5 gather_fusion.2
  483.5 2.7 fusion.24
  486.2 1.9 bitcast_convert_fusion
  488.1 2.9 broadcast_divide_fusion
  490.9 2.0 copy-done
  492.9 4.4 copy.50
  497.3 2.8 gather_fusion.4
  500.0 0.2 multiply_reduce_fusion
  500.4 2.8 bitcast_convert_fusion.1
  503.1 10.4 %fusion.22 = f32[512,4096]{1,0:T(8,128)} fusion(bf16[512,1024]{0,1:T(8,128)(2,1)S(1)} %bitcast.82, bf16[4096,1024]{1,0:T(8,128)(2,1)} %all-gather.7.cloned.1.call-done), kind=kOutput, calls=%fused_computation.43 | convolution fusion | flops 4294967296 | bytes 17825792 | tf_op jit(solution)/shard_map/sc,rc->sr/dot_general | solution.py:75
  513.6 9.0 %convolution_add_fusion = f32[512,4096]{1,0:T(8,128)} fusion(f32[512,4096]{1,0:T(8,128)} %fusion.22, bf16[512,1024]{0,1:T(8,128)(2,1)S(1)} %bitcast.81, bf16[4096,1024]{1,0:T(8,128)(2,1)S(1)} %bitcast.79), kind=kOutput, calls=%fused_computation.5 | convolution fusion | flops 4297064448 | bytes 26214400 | tf_op jit(solution)/shard_map/sc,rc->sr/dot_general | solution.py:76
  522.6 1.6 dynamic-slice_reduce_fusion
  524.2 0.7 reshape.98
  525.0 79.6 %reduce-scatter.2.cloned.1.call-done = f32[512,1024]{1,0:T(8,128)} async-done(((f32[512,4096]{1,0:T(8,128)}), f32[512,1024]{1,0:T(8,128)}) %reduce-scatter.2.cloned.1.call-update) | async-done | bytes 2097168 | tf_op jit(solution)/shard_map/reduce_scatter | solution.py:79
  (36 shorter events, 0.5 us)
Async XLA Ops:
  7.2 49.7 %all-gather.9.cloned.1.call-start = ((), (), s32[]{:S(2)}) async-start(), calls=%async_computation.3 | async-start | bytes 1081344 | tf_op jit(solution)/shard_map/all_gather | solution.py:28
  7.9 93.3 %all-gather.11.cloned.1.call-start = ((), (), s32[]{:S(2)}) async-start(), calls=%async_computation.5 | async-start | bytes 1081344 | tf_op jit(solution)/shard_map/all_gather | solution.py:29
  8.6 147.1 %all-gather.5.cloned.1.call-start = ((), (), s32[]{:S(2)}) async-start(), calls=%async_computation.1 | async-start | bytes 8650752 | tf_op jit(solution)/shard_map/all_gather | solution.py:21
  9.4 201.1 %all-gather.7.cloned.1.call-start = ((), (), s32[]{:S(2)}) async-start(), calls=%async_computation.2 | async-start | bytes 8650752 | tf_op jit(solution)/shard_map/all_gather | solution.py:20
  10.0 478.1 %all-reduce.2.cloned.1.call-start = ((), (), s32[]{:S(2)}) async-start(), calls=%async_computation.4 | async-start | bytes 8388608 | tf_op jit(solution)/shard_map/psum | solution.py:56
  58.8 45.2 %copy-start.1 = (bf16[4,16,16,64]{3,2,1,0:T(8,128)(2,1)}, bf16[4,16,16,64]{3,2,1,0:T(8,128)(2,1)S(1)}, u32[]{:S(2)}) copy-start(bf16[4,16,16,64]{3,2,1,0:T(8,128)(2,1)S(1)} %reshape.97) | copy-start | bytes 393220
  347.6 2.1 copy-start.6
  349.2 4.2 copy-start.4
  353.3 251.3 %reduce-scatter.2.cloned.1.call-start = ((), (), s32[]{:S(2)}) async-start(), calls=%async_computation.6 | async-start | bytes 10485760 | tf_op jit(solution)/shard_map/reduce_scatter | solution.py:79
  482.0 4.2 copy-start.5
  486.2 1.9 copy-start.3
  490.9 2.0 copy-start
  492.9 7.4 %copy-start.2 = (bf16[4,16,16,64]{3,2,1,0:T(8,128)(2,1)S(1)}, bf16[4,16,16,64]{3,2,1,0:T(8,128)(2,1)}, u32[]{:S(2)}) copy-start(bf16[4,16,16,64]{3,2,1,0:T(8,128)(2,1)} %copy-done.1) | copy-start | bytes 393220
  500.3 13.2 %slice-start = ((s8[8388608]{0:T(1024)(128)(4,1)}), s8[4194304]{0:T(1024)(128)(4,1)S(1)}, s32[]{:S(2)}) async-start(s8[8388608]{0:T(1024)(128)(4,1)} %bitcast.78), calls=%async_computation.7 | async-start | bytes 8388608
  503.1 10.5 %slice-start.1 = ((s8[8388608]{0:T(1024)(128)(4,1)}), s8[4194304]{0:T(1024)(128)(4,1)S(1)}, s32[]{:S(2)}) async-start(s8[8388608]{0:T(1024)(128)(4,1)} %bitcast.78), calls=%async_computation.8 | async-start | bytes 8388608
  503.1 10.5 %copy-start.7 = (bf16[16,64,512]{2,1,0:T(8,128)(2,1)S(1)}, bf16[16,64,512]{2,1,0:T(8,128)(2,1)}, u32[]{:S(2)}) copy-start(bf16[16,64,512]{2,1,0:T(8,128)(2,1)} %bitcast_convert_fusion) | copy-start | bytes 3145732
Sparse Core Ops, SparseCore 0:
  10.3 46.5 all-gather.8
  59.1 42.0 all-gather.10
  103.5 52.2 all-gather.4
  157.9 52.5 all-gather.6
  353.5 113.0 all-reduce.1
  522.7 81.7 reduce-scatter.1
where the time goes:
time: 612 us; the launch traced here: 611 us
  waiting for transfers between devices  265 us (43%)
  blocking collectives  249 us (41%)
  matrix products  51.9 us (8%)
  local copies, waits for them, and re-layouts  24.3 us (4%)
  between operations  14.3 us (2%)
  other arithmetic  6.52 us (1%)
    psum x1, blocking collectives, body(): numer_all, denom_all = lax.psum((numer, denom), 'enc')  125 us
    pmax x1, blocking collectives, body(): global_max = lax.pmax(local_max, 'enc')  124 us
    reduce_scatter x1, waiting for transfers between devices, body(): lax.psum_scatter(partial_grad, 'dec', scatter_dimension=1, tiled=True)  79.6 us
    all_gather x1, waiting for transfers between devices, body(): lax.all_gather(value_weight, 'enc', axis=0, tiled=True)  51.8 us
    all_gather x1, waiting for transfers between devices, body(): lax.all_gather(key_weight, 'enc', axis=0, tiled=True)  45 us
    all_gather x1, waiting for transfers between devices, body(): lax.all_gather(queries, 'enc', axis=0, tiled=True)  44.5 us
    all_gather x1, waiting for transfers between devices, body(): lax.all_gather(ctx_grad, 'enc', axis=0, tiled=True)  41.6 us
  transfers between devices with their start and end apart: 6, of which 5 were waited for; matrix products, arithmetic and copies ran while one was open for 5% of the time, Pallas kernels for 0%

commit v1 on v0

v1 whole, which is shorter than its diff:
```python
import functools

import jax
import jax.numpy as jnp
from jax import lax
from jax.experimental import pallas as pl
from jax.experimental.pallas import tpu as pltpu
from jax.sharding import Mesh, PartitionSpec as P

BF = jnp.bfloat16
F32 = jnp.float32
NZ, NX, NC, NY = 4, 4, 2, 4
ENC = ("z", "x", "core")
ROWS = 512
D = 4096
HALF = 512
CHUNK = 256
DEC = 16
NPASS = 4
PAIRS = 4
LOW = -1e30
NT = (((1,), (1,)), ((), ()))
TN = (((0,), (0,)), ((), ()))


def perm(v, axis, shift):
    n = {"z": NZ, "x": NX, "core": NC, "dec": NY}[axis]
    return lax.ppermute(v, axis, [(i, (i + shift) % n) for i in range(n)])


def gather4(v, axis):
    return [v] + [perm(v, axis, -o) for o in (1, 2, 3)]


def ring_near(v, axis):
    return perm(v, axis, -1), perm(v, axis, 1)


def ring_far(up, down, axis):
    return perm(up[0], axis, -1), perm(down[1], axis, 1)


def params(mib):
    return pltpu.CompilerParams(vmem_limit_bytes=mib * 1024 * 1024)


def proj_kernel(sizes, has_acc, offs, own_ref, oth_ref, *refs):
    weights = refs[: len(sizes[0]) + len(sizes[1])]
    rest = refs[len(weights) :]
    acc_ref = rest[0] if has_acc else None
    out_ref = rest[-1]
    step = pl.program_id(0)

    def run(enc_ref):
        at = 0
        place = 0
        for side in range(2):
            total = None
            for count in sizes[side]:
                w = weights[place][...].reshape(count * CHUNK, CHUNK)
                place += 1
                parts = []
                for k in range(count):
                    start = pl.multiple_of(offs[at + k] * CHUNK, CHUNK)
                    parts.append(enc_ref[:, pl.ds(start, CHUNK)])
                at += count
                lhs = jnp.concatenate(parts, axis=1)
                term = jnp.dot(lhs, w, preferred_element_type=F32)
                total = term if total is None else total + term
            cols = slice(side * CHUNK, (side + 1) * CHUNK)
            if has_acc:
                total = total + acc_ref[0, :, cols]
            out_ref[0, :, cols] = total.astype(out_ref.dtype)

    pl.when(step < 2)(lambda: run(own_ref))
    pl.when(step >= 2)(lambda: run(oth_ref))


def project(offs, own, other, a_blocks, b_blocks, acc, dtype):
    sizes = tuple(tuple(b.size // (CHUNK * CHUNK) for b in g) for g in (a_blocks, b_blocks))
    blocks = list(a_blocks) + list(b_blocks)
    tile = ROWS // 2

    def whole(b):
        return pl.BlockSpec(b.shape, lambda i, o: (0,) * b.ndim)

    tile_spec = pl.BlockSpec((1, tile, HALF), lambda i, o: (i // 2, i % 2, 0))
    in_specs = [
        pl.BlockSpec((tile, D), lambda i, o: (jnp.minimum(i, 1), 0)),
        pl.BlockSpec((tile, D), lambda i, o: (jnp.maximum(i - 2, 0), 0)),
    ] + [whole(b) for b in blocks]
    args = [offs, own, other] + blocks
    if acc is not None:
        in_specs.append(tile_spec)
        args.append(acc)
    depth = CHUNK * sum(sizes[0])
    return pl.pallas_call(
        functools.partial(proj_kernel, sizes, acc is not None),
        grid_spec=pltpu.PrefetchScalarGridSpec(
            num_scalar_prefetch=1, grid=(4,), in_specs=in_specs, out_specs=tile_spec
        ),
        out_shape=jax.ShapeDtypeStruct((2, ROWS, HALF), dtype),
        compiler_params=params(40),
        cost_estimate=pl.CostEstimate(
            flops=2 * 2 * ROWS * depth * HALF,
            bytes_accessed=2 * 2 * ROWS * D + 2 * depth * HALF + 4 * 2 * ROWS * HALF,
            transcendentals=0,
        ),
    )(*args)


def pair_matrix(meta, qg_ref, side, pair, which):
    low = lax.broadcasted_iota(jnp.int32, (DEC, 128), 1) < 64
    parts = []
    for p in range(NPASS):
        tile = qg_ref[meta[side * NPASS + p], which, :, pair * 128 : (pair + 1) * 128]
        zero = jnp.zeros_like(tile)
        parts += [jnp.where(low, tile, zero), jnp.where(low, zero, tile)]
    return jnp.concatenate(parts, axis=0)


def lane_value(meta, base, side):
    lane = lax.broadcasted_iota(jnp.int32, (1, 128), 1) // 32
    value = jnp.zeros((1, 128), jnp.int32)
    for p in range(NPASS):
        value = jnp.where(lane == p, meta[base + side * NPASS + p], value)
    return value


def inside_mask(meta, side):
    row = lax.broadcasted_iota(jnp.int32, (ROWS, 128), 0)
    return (row >= lane_value(meta, 8, side)) & (row < lane_value(meta, 16, side))


def dot_nt(a, b):
    return lax.dot_general(a, b, NT, preferred_element_type=F32)


def stats_kernel(meta, k_ref, qg_ref, out_ref):
    for side in range(2):
        inside = inside_mask(meta, side)
        question = lane_value(meta, 24, side).astype(F32)
        for pair in range(PAIRS):
            cols = slice(pair * 128, (pair + 1) * 128)
            scores = dot_nt(k_ref[side, :, cols], pair_matrix(meta, qg_ref, side, pair, 0))
            scores = jnp.where(inside, scores, LOW)
            top = jnp.max(scores, axis=0, keepdims=True)
            total = jnp.sum(jnp.exp(scores - top), axis=0, keepdims=True)
            at = side * PAIRS + pair
            out_ref[at : at + 1, :] = top
            out_ref[8 + at : 9 + at, :] = total
            out_ref[16 + at : 17 + at, :] = question


def over_group(own_question, parts, start, combine):
    totals = [None, None]
    for question, value in parts:
        for k in range(NPASS):
            q = pltpu.roll(question, 32 * k, 1) if k else question
            v = pltpu.roll(value, 32 * k, 1) if k else value
            for side in range(2):
                term = jnp.where(q == own_question[side], v, start)
                totals[side] = term if totals[side] is None else combine(totals[side], term)
    return [combine(t[0:PAIRS], t[PAIRS:]) for t in totals]


def forward_kernel(meta, k_ref, v_ref, qg_ref, st_ref, ml_ref, delta_ref, dense_ref):
    own_question = [st_ref[0, 16 + s * PAIRS : 17 + s * PAIRS, :] for s in range(2)]
    n = st_ref.shape[0]
    tops = over_group(
        own_question, [(st_ref[d, 16:24], st_ref[d, 0:8]) for d in range(n)], LOW, jnp.maximum
    )
    both = [jnp.concatenate([t, t], axis=0) for t in tops]
    totals = [None, None]
    for d in range(n):
        question, top, total = st_ref[d, 16:24], st_ref[d, 0:8], st_ref[d, 8:16]
        for k in range(NPASS):
            q = pltpu.roll(question, 32 * k, 1) if k else question
            m = pltpu.roll(top, 32 * k, 1) if k else top
            l = pltpu.roll(total, 32 * k, 1) if k else total
            for side in range(2):
                hit = q == own_question[side]
                scale = jnp.exp(jnp.where(hit, m - both[side], 0.0))
                term = jnp.where(hit, scale * l, 0.0)
                totals[side] = term if totals[side] is None else totals[side] + term
    dense_ref[...] = jnp.zeros_like(dense_ref)
    low = lax.broadcasted_iota(jnp.int32, (DEC, 128), 1) < 64
    for side in range(2):
        inside = inside_mask(meta, side)
        total = totals[side][0:PAIRS] + totals[side][PAIRS:]
        inverse = 1.0 / total
        ml_ref[side * PAIRS : (side + 1) * PAIRS, :] = tops[side]
        ml_ref[8 + side * PAIRS : 8 + (side + 1) * PAIRS, :] = inverse
        for pair in range(PAIRS):
            cols = slice(pair * 128, (pair + 1) * 128)
            scores = dot_nt(k_ref[side, :, cols], pair_matrix(meta, qg_ref, side, pair, 0))
            unnorm = jnp.where(inside, jnp.exp(scores - tops[side][pair : pair + 1]), 0.0)
            unnorm_b = unnorm.astype(BF)
            values = v_ref[side, :, cols]
            dprob = dot_nt(values, pair_matrix(meta, qg_ref, side, pair, 1))
            inv = inverse[pair : pair + 1]
            at = side * PAIRS + pair
            delta_ref[at : at + 1, :] = (
                jnp.sum(unnorm_b.astype(F32) * dprob, axis=0, keepdims=True) * inv
            )
            weighted = lax.dot_general(values, unnorm_b, TN, preferred_element_type=F32)
            context = (weighted * inv).T
            for p in range(NPASS):
                part = jnp.where(
                    low, context[p * 32 : p * 32 + 16], context[p * 32 + 16 : p * 32 + 32]
                )
                q = meta[side * NPASS + p]
                dense_ref[q, :, cols] += part


def backward_kernel(meta, k_ref, v_ref, qg_ref, st_ref, ml_ref, dl_ref, own_ref, oth_ref):
    own_question = [st_ref[0, 16 + s * PAIRS : 17 + s * PAIRS, :] for s in range(2)]
    n = st_ref.shape[0]
    deltas = over_group(
        own_question, [(st_ref[d, 16:24], dl_ref[d]) for d in range(n)], 0.0, jnp.add
    )
    for side in range(2):
        inside = inside_mask(meta, side)
        out_ref = own_ref if side == 0 else oth_ref
        for pair in range(PAIRS):
            cols = slice(pair * 128, (pair + 1) * 128)
            at = side * PAIRS + pair
            queries = pair_matrix(meta, qg_ref, side, pair, 0)
            grads = pair_matrix(meta, qg_ref, side, pair, 1)
            scores = dot_nt(k_ref[side, :, cols], queries)
            unnorm = jnp.where(inside, jnp.exp(scores - ml_ref[at : at + 1, :]), 0.0)
            probs = unnorm * ml_ref[8 + at : 9 + at, :]
            dprob = dot_nt(v_ref[side, :, cols], grads)
            ds = (probs * (dprob - deltas[side][pair : pair + 1])).astype(BF)
            out_ref[0, :, cols] = jnp.dot(ds, queries, preferred_element_type=F32).astype(BF)
            out_ref[1, :, cols] = jnp.dot(
                probs.astype(BF), grads, preferred_element_type=F32
            ).astype(BF)


def small_call(kernel, meta, args, out_shape, name_flops):
    def whole(a):
        return pl.BlockSpec(a.shape, lambda i, m: (0,) * len(a.shape))

    return pl.pallas_call(
        kernel,
        grid_spec=pltpu.PrefetchScalarGridSpec(
            num_scalar_prefetch=1,
            grid=(1,),
            in_specs=[whole(a) for a in args],
            out_specs=jax.tree.map(whole, out_shape),
        ),
        out_shape=out_shape,
        compiler_params=params(40),
        cost_estimate=pl.CostEstimate(
            flops=name_flops, bytes_accessed=4 * 1024 * 1024, transcendentals=512 * 1024
        ),
    )(meta, *args)


def grad_kernel(add, zi, own_ref, got_ref, *refs):
    weights, outs = refs[:8], refs[8:]
    lhs = jnp.concatenate([own_ref[0], got_ref[0], own_ref[1], got_ref[1]], axis=1)
    rhs = jnp.concatenate([w[...].reshape(CHUNK, CHUNK) for w in weights], axis=1)
    total = dot_nt(lhs, rhs)
    if len(outs) == 1:
        outs[0][...] = total.astype(outs[0].dtype)
    else:
        outs[0][...] = total[: ROWS // 2].astype(outs[0].dtype)
        outs[1][...] = total[ROWS // 2 :].astype(outs[1].dtype)


def grad_block(zi, own, got, wk, wk_got, wv, wv_got, dtypes):
    a_spec = pl.BlockSpec((1, 1, 1, CHUNK, CHUNK), lambda n, z: (0, z[0], n, 0, 0))
    b_spec = pl.BlockSpec((1, 1, 1, CHUNK, CHUNK), lambda n, z: (1, n, z[0], 0, 0))
    full = pl.BlockSpec((2, ROWS, HALF), lambda n, z: (0, 0, 0))
    rows = ROWS // len(dtypes)
    out_specs = [pl.BlockSpec((rows, CHUNK), lambda n, z: (0, n)) for _ in dtypes]
    return pl.pallas_call(
        functools.partial(grad_kernel, False),
        grid_spec=pltpu.PrefetchScalarGridSpec(
            num_scalar_prefetch=1,
            grid=(4,),
            in_specs=[full, full] + [a_spec, b_spec] * 4,
            out_specs=out_specs,
        ),
        out_shape=[jax.ShapeDtypeStruct((rows, 4 * CHUNK), t) for t in dtypes],
        compiler_params=params(40),
        cost_estimate=pl.CostEstimate(
            flops=2 * ROWS * 1024 * 2048, bytes_accessed=8 * 1024 * 1024, transcendentals=0
        ),
    )(zi, own, got, wk, wk, wk_got, wk_got, wv, wv, wv_got, wv_got)


def finish_kernel(place, base_ref, plus_top, plus_low, minus_top, minus_low, out_ref):
    half = ROWS // 2
    out_ref[:half] = base_ref[:half] + plus_top[...].astype(F32) + minus_top[...].astype(F32)
    out_ref[half:] = base_ref[half:] + plus_low[...].astype(F32) + minus_low[...].astype(F32)


def finish(place, base, parts):
    half = pl.BlockSpec((ROWS // 2, CHUNK), lambda n, p: (0, n))
    return pl.pallas_call(
        finish_kernel,
        grid_spec=pltpu.PrefetchScalarGridSpec(
            num_scalar_prefetch=1,
            grid=(4,),
            in_specs=[pl.BlockSpec((ROWS, CHUNK), lambda n, p: (0, n))] + [half] * 4,
            out_specs=pl.BlockSpec((ROWS, CHUNK), lambda n, p: (0, p[n])),
        ),
        out_shape=jax.ShapeDtypeStruct((ROWS, 4 * CHUNK), F32),
        cost_estimate=pl.CostEstimate(
            flops=ROWS * 2048, bytes_accessed=6 * 1024 * 1024, transcendentals=0
        ),
    )(place, base, *parts)


def body(enc_rows, key_weight, value_weight, queries, ctx_grad, passage_len, passage_question):
    z, x, core, y = (lax.axis_index(a) for a in ("z", "x", "core", "dec"))
    four = jnp.arange(4, dtype=jnp.int32)

    cat = jnp.concatenate([key_weight, value_weight, queries[0], ctx_grad[0]], axis=0)
    mine = lax.dynamic_slice_in_dim(cat, core * HALF, HALF, 1)
    theirs = lax.dynamic_slice_in_dim(cat, (1 - core) * HALF, HALF, 1)
    got = perm(theirs, "core", 1)
    first = jnp.where(core == 0, mine, got)
    second = jnp.where(core == 0, got, mine)
    chip = jnp.stack(
        [
            jnp.concatenate([first[:128], second[:128]], axis=0),
            jnp.concatenate([first[128:256], second[128:256]], axis=0),
        ]
    )
    qg = jnp.stack([first[256:].reshape(2, DEC, HALF), second[256:].reshape(2, DEC, HALF)])
    numbers = jnp.concatenate([passage_len[0], passage_question[:, 0]])
    other_numbers = perm(numbers, "core", 1)
    enc_other = perm(lax.optimization_barrier((enc_rows, got))[0], "core", 1)

    a_first = gather4(chip[:, :, :CHUNK], "x")
    b_first = gather4(chip[:, :, CHUNK:], "z")
    qg_x = jnp.stack(gather4(qg, "x"))
    qg_all = jnp.stack(gather4(qg_x, "z")).reshape(32, 2, DEC, HALF)
    a_key, a_value = (jnp.stack([p[t] for p in a_first]).reshape(2, 512, CHUNK) for t in (0, 1))
    b_key, b_value = (jnp.stack([p[t] for p in b_first]).reshape(2, 512, CHUNK) for t in (0, 1))
    ak_up, ak_down = ring_near(a_key, "z")
    bk_up, bk_down = ring_near(b_key, "x")
    a_value, b_value, ak_up, ak_down, bk_up, bk_down = lax.optimization_barrier(
        (a_value, b_value, ak_up, ak_down, bk_up, bk_down)
    )
    ak_far = ring_far(ak_up, ak_down, "z")
    bk_far = ring_far(bk_up, bk_down, "x")
    av_up, av_down = ring_near(a_value, "z")
    bv_up, bv_down = ring_near(b_value, "x")
    av_far = ring_far(av_up, av_down, "z")
    bv_far = ring_far(bv_up, bv_down, "x")

    zs, xs = (z + four) % 4, (x + four) % 4
    a_chips = zs[:, None] * 4 + xs[None, :]
    b_chips = zs[None, :] * 4 + xs[:, None]
    near = jnp.array([0, 1, 3])
    offs_near = jnp.concatenate([a_chips[near].reshape(-1), b_chips[near].reshape(-1)])
    offs_far = jnp.concatenate([a_chips[2], b_chips[2]])

    def project_all(a_own, a_up, a_down, a_far, b_own, b_up, b_down, b_far):
        part = project(
            offs_near, enc_rows, enc_other, [a_own, a_up, a_down], [b_own, b_up, b_down], None, F32
        )
        return project(offs_far, enc_rows, enc_other, a_far, b_far, part, BF)

    keys = project_all(a_key, ak_up, ak_down, ak_far, b_key, bk_up, bk_down, bk_far)

    all_numbers = jnp.stack([numbers, other_numbers])
    lengths, questions = all_numbers[:, :4], all_numbers[:, 4:]
    ends = jnp.cumsum(lengths, axis=1)
    qz, qx, qc = questions // 8, (questions // 2) % 4, questions % 2
    place = ((qz - z) % 4) * 8 + ((qx - x) % 4) * 2 + qc
    meta = jnp.concatenate(
        [v.reshape(-1) for v in (place, ends - lengths, ends, questions)]
    ).astype(jnp.int32)
    spread_flops = 2 * 2 * ROWS * 128 * 128 * PAIRS
    stats = small_call(
        stats_kernel, meta, (keys, qg_all), jax.ShapeDtypeStruct((24, 128), F32), spread_flops
    )
    stats_x = jnp.stack(gather4(stats, "x"))
    stats_all = jnp.concatenate(gather4(stats_x, "z"), axis=0)

    values = project_all(a_value, av_up, av_down, av_far, b_value, bv_up, bv_down, bv_far)

    def assemble(a_own, a_up, a_down, a_far, b_own, b_up, b_down, b_far):
        return jnp.concatenate(
            [a_own, a_up, a_far[0][None], a_far[1][None], a_down]
            + [b_own, b_up, b_far[0][None], b_far[1][None], b_down],
            axis=0,
        ).reshape(2, 4, 4, CHUNK, CHUNK)

    wk = assemble(a_key, ak_up, ak_down, ak_far, b_key, bk_up, bk_down, bk_far)
    wk_got = perm(wk, "core", 1)
    wv = assemble(a_value, av_up, av_down, av_far, b_value, bv_up, bv_down, bv_far)
    wv_got = perm(wv, "core", 1)

    ml, delta, dense = small_call(
        forward_kernel,
        meta,
        (keys, values, qg_all, stats_all),
        [
            jax.ShapeDtypeStruct((16, 128), F32),
            jax.ShapeDtypeStruct((8, 128), F32),
            jax.ShapeDtypeStruct((32, DEC, HALF), F32),
        ],
        3 * spread_flops,
    )
    delta_x = jnp.stack(gather4(delta, "x"))
    delta_all = jnp.concatenate(gather4(delta_x, "z"), axis=0)
    own, send = small_call(
        backward_kernel,
        meta,
        (keys, values, qg_all, stats_all, ml, delta_all),
        [jax.ShapeDtypeStruct((2, ROWS, HALF), BF)] * 2,
        4 * spread_flops,
    )
    received = perm(send, "core", 1)

    def block(target, dtypes):
        zi = ((target - z) % 4).astype(jnp.int32).reshape(1)
        return grad_block(zi, own, received, wk, wk_got, wv, wv_got, dtypes)

    far_top, far_low = block(y + 2, [BF, BF])
    from_below = perm(far_top, "dec", 1)
    from_above = perm(far_low, "dec", -1)
    up_top, up_low = block(y + 1, [F32, BF])
    low_below = perm(up_low, "dec", 1)
    down_top, down_low = block(y + 3, [BF, F32])
    top_above = perm(down_top, "dec", -1)
    top_below = perm((up_top + from_below.astype(F32)).astype(BF), "dec", 1)
    low_above = perm((down_low + from_above.astype(F32)).astype(BF), "dec", -1)
    (base,) = block(y, [F32])
    enc_grad = finish(xs.astype(jnp.int32), base, (top_below, low_below, top_above, low_above))

    dense = dense.reshape(4, 4, 2, DEC, HALF)
    by_z = dense[0] + perm(dense[1], "z", 1) + perm(dense[2], "z", 2) + perm(dense[3], "z", 3)
    by_x = by_z[0] + perm(by_z[1], "x", 1) + perm(by_z[2], "x", 2) + perm(by_z[3], "x", 3)
    keep = lax.dynamic_index_in_dim(by_x, core, 0, keepdims=False)
    give = lax.dynamic_index_in_dim(by_x, 1 - core, 0, keepdims=False)
    come = perm(give, "core", 1)
    ctx = jnp.where(
        core == 0,
        jnp.concatenate([keep, come], axis=1),
        jnp.concatenate([come, keep], axis=1),
    )[None]
    return ctx, enc_grad


def solution(mesh):
    grid = Mesh(mesh.devices.reshape(NZ, NX, NC, NY), ("z", "x", "core", "dec"))
    return jax.shard_map(
        body,
        mesh=grid,
        in_specs=(
            P(ENC, None),
            P(ENC, "dec"),
            P(ENC, "dec"),
            P(ENC, None, "dec"),
            P(ENC, None, "dec"),
            P(ENC, None),
            P(ENC, None),
        ),
        out_specs=(P(ENC, None, "dec"), P(ENC, "dec")),
        check_vma=False,
    )
```

time: 612 us -> 241 us (0.39)
  blocking collectives: 249 us -> 0 us
  waiting for transfers between devices: 265 us -> 83.7 us
  starting transfers between devices: 0.23 us -> 77.2 us
  matrix products: 51.9 us -> 0 us
  Pallas kernels: 0 us -> 46.4 us
  between operations: 14.3 us -> 1.16 us
    all_gather x4 -> x0, waiting for transfers between devices: 183 us -> none  [the longest x1 51.8 us: body(): lax.all_gather(value_weight, 'enc', axis=0, tiled=True)]
    psum x1 -> x0, blocking collectives: 125 us -> none  [body(): numer_all, denom_all = lax.psum((numer, denom), 'enc')]
    pmax x1 -> x0, blocking collectives: 124 us -> none  [body(): global_max = lax.pmax(local_max, 'enc')]
    ppermute x0 -> x59, waiting for transfers between devices: none -> 83.7 us  [perm(): return lax.ppermute(v, axis, [(i, (i + shift) % n) for i in range(n)])]
    reduce_scatter x1 -> x0, waiting for transfers between devices: 79.6 us -> none  [body(): lax.psum_scatter(partial_grad, 'dec', scatter_dimension=1, tiled=True)]
    ppermute x0 -> x59, starting transfers between devices: none -> 77.2 us  [perm(): return lax.ppermute(v, axis, [(i, (i + shift) % n) for i in range(n)])]
    dot_general x9 -> x0, matrix products: 47.5 us -> none  [the longest x1 10.4 us: body(): jnp.einsum('sc,rc->sr', key_grad_b, pieces[0], preferred_element_type=jnp...]
    pallas_call x0 -> x12, Pallas kernels: none -> 46.4 us  [the longest x4 20.4 us: grad_block(): pl.pallas_call(functools.partial(grad_kernel, False), grid_spec=pltpu.Pre...]
  transfers between devices with their start and end apart: 6 -> 59, of which waited for: 5 -> 27; matrix products, arithmetic and copies ran while one was open for 5% -> 11% of each run, Pallas kernels for 0% -> 15%
where the time goes in v1:
time: 241 us; the launch traced here: 237 us
  waiting for transfers between devices  83.7 us (35%)
  starting transfers between devices  77.2 us (32%)
  Pallas kernels  46.4 us (19%)
  local copies, waits for them, and re-layouts  20.1 us (8%)
  other arithmetic  8.34 us (3%)
    ppermute x59, waiting for transfers between devices, perm(): return lax.ppermute(v, axis, [(i, (i + shift) % n) for i in range(n)])  83.7 us
    ppermute x59, starting transfers between devices, perm(): return lax.ppermute(v, axis, [(i, (i + shift) % n) for i in range(n)])  77.2 us
    pallas_call x4, Pallas kernels, grad_block(): pl.pallas_call(functools.partial(grad_kernel, False), grid_spec=pltpu.Pre...  20.4 us
    unnamed x36, local copies, waits for them, and re-layouts  15.5 us
    pallas_call x4, Pallas kernels, project(): pl.pallas_call(functools.partial(proj_kernel, sizes, acc is not None), gr...  14.4 us
    pallas_call x3, Pallas kernels, small_call(): pl.pallas_call(kernel, grid_spec=pltpu.PrefetchScalarGridSpec(num_scalar_...  6.73 us
    pallas_call x1, Pallas kernels, finish(): pl.pallas_call(finish_kernel, grid_spec=pltpu.PrefetchScalarGridSpec(num_...  4.92 us
  transfers between devices with their start and end apart: 59, of which 27 were waited for; matrix products, arithmetic and copies ran while one was open for 11% of the time, Pallas kernels for 15%

profile of v1, /device:TPU:1, one launch (start us, length us, event | category | flops | bytes accessed | tf_op | source)
XLA Modules:
  0.0 236.9 jit_solution(3567056694701084298)
XLA Ops:
  1.4 1.4 collective-permute-start
  9.4 2.5 %collective-permute-start.4 = (bf16[2,256,256]{2,1,0:T(8,128)(2,1)S(1)}, bf16[2,256,256]{2,1,0:T(8,128)(2,1)S(1)}, u32[]{:S(2)}, u32[]{:S(2)}) collective-permute-start(bf16[2,256,256]{2,1,0:T(8,128)(2,1)S(1)} %get-tuple-element.45), channel_id=1, source_target_pairs={{0,16},{8,24},{16,0},{24,8},{1,17},{9,25},{17,1},{25,9},{2,18},{10... | collective-permute-start | bytes 786440 | tf_op jit(solution)/shard_map/ppermute | solution.py:28
  11.9 2.3 collective-permute-start.26
  14.6 7.0 %collective-permute-done.27 = bf16[2,2,16,512]{3,2,1,0:T(8,128)(2,1)S(1)} collective-permute-done((bf16[2,2,16,512]{3,2,1,0:T(8,128)(2,1)S(1)}, bf16[2,2,16,512]{3,2,1,0:T(8,128)(2,1)S(1)}, u32[]{:S(2)}, u32[]{:S(2)}) %collective-permute-start.27) | collective-permute-done | bytes 65568 | tf_op jit(solution)/shard_map/ppermute | solution.py:28
  21.6 3.2 %collective-permute-start.3 = (bf16[2,256,256]{2,1,0:T(8,128)(2,1)S(1)}, bf16[2,256,256]{2,1,0:T(8,128)(2,1)S(1)}, u32[]{:S(2)}, u32[]{:S(2)}) collective-permute-start(bf16[2,256,256]{2,1,0:T(8,128)(2,1)S(1)} %get-tuple-element.45), channel_id=1, source_target_pairs={{0,24},{8,0},{16,8},{24,16},{1,25},{9,1},{17,9},{25,17},{2,26},{10... | collective-permute-start | bytes 786440 | tf_op jit(solution)/shard_map/ppermute | solution.py:28
  25.9 1.6 collective-permute-start.8
  27.6 3.3 %collective-permute-start.7 = (bf16[2,256,256]{2,1,0:T(8,128)(2,1)S(1)}, bf16[2,256,256]{2,1,0:T(8,128)(2,1)S(1)}, u32[]{:S(2)}, u32[]{:S(2)}) collective-permute-start(bf16[2,256,256]{2,1,0:T(8,128)(2,1)S(1)} %get-tuple-element.44), channel_id=1, source_target_pairs={{0,64},{32,96},{64,0},{96,32},{1,65},{33,97},{65,1},{97,33},{2,66}... | collective-permute-start | bytes 786440 | tf_op jit(solution)/shard_map/ppermute | solution.py:28
  35.9 5.4 %collective-permute-done.7 = bf16[2,256,256]{2,1,0:T(8,128)(2,1)S(1)} collective-permute-done((bf16[2,256,256]{2,1,0:T(8,128)(2,1)S(1)}, bf16[2,256,256]{2,1,0:T(8,128)(2,1)S(1)}, u32[]{:S(2)}, u32[]{:S(2)}) %collective-permute-start.7) | collective-permute-done | bytes 262176 | tf_op jit(solution)/shard_map/ppermute | solution.py:28
  42.4 4.6 %collective-permute-done.30 = bf16[4,2,2,16,512]{4,3,2,1,0:T(8,128)(2,1)S(1)} collective-permute-done((bf16[4,2,2,16,512]{4,3,2,1,0:T(8,128)(2,1)S(1)}, bf16[4,2,2,16,512]{4,3,2,1,0:T(8,128)(2,1)S(1)}, u32[]{:S(2)}, u32[]{:S(2)}) %collective-permute-start.30) | collective-permute-done | bytes 262176 | tf_op jit(solution)/shard_map/ppermute | solution.py:28
  47.1 5.4 %collective-permute-done.29 = bf16[4,2,2,16,512]{4,3,2,1,0:T(8,128)(2,1)S(1)} collective-permute-done((bf16[4,2,2,16,512]{4,3,2,1,0:T(8,128)(2,1)S(1)}, bf16[4,2,2,16,512]{4,3,2,1,0:T(8,128)(2,1)S(1)}, u32[]{:S(2)}, u32[]{:S(2)}) %collective-permute-start.29) | collective-permute-done | bytes 262176 | tf_op jit(solution)/shard_map/ppermute | solution.py:28
  53.5 10.1 %collective-permute-done.28 = bf16[4,2,2,16,512]{4,3,2,1,0:T(8,128)(2,1)S(1)} collective-permute-done((bf16[4,2,2,16,512]{4,3,2,1,0:T(8,128)(2,1)S(1)}, bf16[4,2,2,16,512]{4,3,2,1,0:T(8,128)(2,1)S(1)}, u32[]{:S(2)}, u32[]{:S(2)}) %collective-permute-start.28) | collective-permute-done | bytes 262176 | tf_op jit(solution)/shard_map/ppermute | solution.py:28
  63.7 2.0 collective-permute-start.2
  65.9 2.4 %collective-permute-start.17 = (bf16[2,512,256]{2,1,0:T(8,128)(2,1)S(1)}, bf16[2,512,256]{2,1,0:T(8,128)(2,1)S(1)}, u32[]{:S(2)}, u32[]{:S(2)}) collective-permute-start(bf16[2,512,256]{2,1,0:T(8,128)(2,1)S(1)} %bitcast.123), channel_id=1, source_target_pairs={{0,96},{32,0},{64,32},{96,64},{1,97},{33,1},{65,33},{97,65},{2,98}... | collective-permute-start | bytes 1572872 | tf_op jit(solution)/shard_map/ppermute | solution.py:28
  68.3 2.7 %collective-permute-start.13 = (bf16[512,256]{1,0:T(8,128)(2,1)S(1)}, bf16[512,256]{1,0:T(8,128)(2,1)S(1)}, u32[]{:S(2)}, u32[]{:S(2)}) collective-permute-start(bf16[512,256]{1,0:T(8,128)(2,1)S(1)} %slice_bitcast_fusion.7), channel_id=1, source_target_pairs={{0,96},{32,0},{64,32},{96,64},{1,97},{33,1},{65,33},{97,65},{2,98}... | collective-permute-start | bytes 786440 | tf_op jit(solution)/shard_map/ppermute | solution.py:28
  72.9 12.4 %collective-permute-done.13.refs_0_ = bf16[512,256]{1,0:T(8,128)(2,1)S(1)} collective-permute-done((bf16[512,256]{1,0:T(8,128)(2,1)S(1)}, bf16[512,256]{1,0:T(8,128)(2,1)S(1)}, u32[]{:S(2)}, u32[]{:S(2)}) %collective-permute-start.13) | collective-permute-done | bytes 262176 | tf_op jit(solution)/shard_map/ppermute | solution.py:28
  86.0 2.4 collective-permute-done.14.refs_1_
  92.3 2.0 collective-permute-start.21
  97.8 2.0 collective-permute-start.51
  99.8 2.1 collective-permute-start.18
  102.0 2.1 collective-permute-done.21.refs_4_
  105.4 3.4 %collective-permute-done.23.refs_5_ = bf16[2,512,256]{2,1,0:T(8,128)(2,1)S(1)} collective-permute-done((bf16[2,512,256]{2,1,0:T(8,128)(2,1)S(1)}, bf16[2,512,256]{2,1,0:T(8,128)(2,1)S(1)}, u32[]{:S(2)}, u32[]{:S(2)}) %collective-permute-start.23) | collective-permute-done | bytes 524320 | tf_op jit(solution)/shard_map/ppermute | solution.py:28
  109.7 1.5 collective-permute-start.24
  117.7 4.1 %collective-permute-start.52 = (bf16[2,4,4,256,256]{4,3,2,1,0:T(8,128)(2,1)}, bf16[2,4,4,256,256]{4,3,2,1,0:T(8,128)(2,1)}, u32[]{:S(2)}, u32[]{:S(2)}) collective-permute-start(bf16[2,4,4,256,256]{4,3,2,1,0:T(8,128)(2,1)} %bitcast.61.refs_4_.refs_5_), channel_id=1, source_target_pairs={{0,4},{4,0},{1,5},{5,1},{2,6},{6,2},{3,7},{7,3},{8,12},{12,8},{9,1... | collective-permute-start | bytes 12582920 | tf_op jit(solution)/shard_map/ppermute | solution.py:28
  121.8 4.8 %shard_map.95.refs_4_ = f32[2,512,512]{2,1,0:T(8,128)S(1)} custom-call(s32[24]{0:T(128)S(1)} %pad_add_fusion.4.offs, bf16[512,4096]{1,0:T(8,128)(2,1)S(1)} %copy-done, bf16[512,4096]{1,0:T(8,128)(2,1)S(1)} %collective-permute-done.2.oth_ref, bf16[2,512,256]{2,1,0:T(8,128)(2,1)S(1)} %bitcast.118, bf16[2,512,256]{2,1,0:T(8,128)(2,1)S(1)} %collective-permute-done.9.refs_1_, ...), custom_call_target="tpu_custom_call" | custom-call | flops 3221225472 | bytes 13631488 | tf_op jit(solution)/shard_map/pallas_call | solution.py:97
  126.6 2.5 %shard_map.96.k_ref = bf16[2,512,512]{2,1,0:T(8,128)(2,1)S(1)} custom-call(s32[8]{0:T(128)S(1)} %pad_add_fusion.3.offs, bf16[512,4096]{1,0:T(8,128)(2,1)S(1)} %copy-done, bf16[512,4096]{1,0:T(8,128)(2,1)S(1)} %collective-permute-done.2.oth_ref, bf16[512,256]{1,0:T(8,128)(2,1)S(1)} %collective-permute-done.13.refs_0_, ...), custom_call_target="tpu_custom_call" | custom-call | flops 1073741824 | bytes 11534336 | tf_op jit(solution)/shard_map/pallas_call | solution.py:97
  130.5 1.4 collective-permute-start.31
  132.9 4.7 %shard_map.97.refs_4_ = f32[2,512,512]{2,1,0:T(8,128)S(1)} custom-call(s32[24]{0:T(128)S(1)} %pad_add_fusion.4.offs, bf16[512,4096]{1,0:T(8,128)(2,1)S(1)} %copy-done, bf16[512,4096]{1,0:T(8,128)(2,1)S(1)} %collective-permute-done.2.oth_ref, bf16[2,512,256]{2,1,0:T(8,128)(2,1)S(1)} %bitcast.126, bf16[2,512,256]{2,1,0:T(8,128)(2,1)S(1)} %collective-permute-done.17.refs_1_, ...), custom_call_target="tpu_custom_call" | custom-call | flops 3221225472 | bytes 13631488 | tf_op jit(solution)/shard_map/pallas_call | solution.py:97
  137.6 2.5 %shard_map.98.v_ref = bf16[2,512,512]{2,1,0:T(8,128)(2,1)S(1)} custom-call(s32[8]{0:T(128)S(1)} %pad_add_fusion.3.offs, bf16[512,4096]{1,0:T(8,128)(2,1)S(1)} %copy-done, bf16[512,4096]{1,0:T(8,128)(2,1)S(1)} %collective-permute-done.2.oth_ref, bf16[512,256]{1,0:T(8,128)(2,1)S(1)} %collective-permute-done.18.refs_0_, ...), custom_call_target="tpu_custom_call" | custom-call | flops 1073741824 | bytes 11534336 | tf_op jit(solution)/shard_map/pallas_call | solution.py:97
  140.1 1.8 collective-permute-start.34
  143.1 3.3 %collective-permute-done.35 = f32[4,24,128]{2,1,0:T(8,128)S(1)} collective-permute-done((f32[4,24,128]{2,1,0:T(8,128)S(1)}, f32[4,24,128]{2,1,0:T(8,128)S(1)}, u32[]{:S(2)}, u32[]{:S(2)}) %collective-permute-start.35) | collective-permute-done | bytes 49184 | tf_op jit(solution)/shard_map/ppermute | solution.py:28
  146.8 2.7 %shard_map.100 = (f32[16,128]{1,0:T(8,128)S(1)}, f32[8,128]{1,0:T(8,128)S(1)}, f32[32,16,512]{2,1,0:T(8,128)S(1)}) custom-call(s32[32]{0:T(128)S(1)} %pad_add_fusion.2.meta, bf16[2,512,512]{2,1,0:T(8,128)(2,1)S(1)} %shard_map.96.k_ref, bf16[2,512,512]{2,1,0:T(8,128)(2,1)S(1)} %shard_map.98.v_ref, bf16[32,2,16,512]{3,2,1,0:T(8,128)(2,1)S(1)} %bitcast.113, ...), custom_call_target="tpu_custom_call" | custom-call | flops 402653184 | bytes 4194304 | tf_op jit(solution)/shard_map/pallas_call | solution.py:245
  149.6 2.6 %collective-permute-start.44 = (f32[8,128]{1,0:T(8,128)S(1)}, f32[8,128]{1,0:T(8,128)S(1)}, u32[]{:S(2)}, u32[]{:S(2)}) collective-permute-start(f32[8,128]{1,0:T(8,128)S(1)} %get-tuple-element.29), channel_id=1, source_target_pairs={{0,24},{8,0},{16,8},{24,16},{1,25},{9,1},{17,9},{25,17},{2,26},{10... | collective-permute-start | bytes 12296 | tf_op jit(solution)/shard_map/ppermute | solution.py:28
  153.6 2.5 %collective-permute-done.45 = f32[8,128]{1,0:T(8,128)S(1)} collective-permute-done((f32[8,128]{1,0:T(8,128)S(1)}, f32[8,128]{1,0:T(8,128)S(1)}, u32[]{:S(2)}, u32[]{:S(2)}) %collective-permute-start.45) | collective-permute-done | bytes 4128 | tf_op jit(solution)/shard_map/ppermute | solution.py:28
  159.4 1.9 collective-permute-done.48
  161.7 2.6 %shard_map.101 = (bf16[2,512,512]{2,1,0:T(8,128)(2,1)S(1)}, bf16[2,512,512]{2,1,0:T(8,128)(2,1)S(1)}) custom-call(s32[32]{0:T(128)S(1)} %pad_add_fusion.2.meta, bf16[2,512,512]{2,1,0:T(8,128)(2,1)S(1)} %shard_map.96.k_ref, bf16[2,512,512]{2,1,0:T(8,128)(2,1)S(1)} %shard_map.98.v_ref, bf16[32,2,16,512]{3,2,1,0:T(8,128)(2,1)S(1)} %bitcast.114, ...), custom_call_target="tpu_custom_call" | custom-call | flops 536870912 | bytes 4194304 | tf_op jit(solution)/shard_map/pallas_call | solution.py:245
  164.3 5.7 %collective-permute-start.50 = (bf16[2,512,512]{2,1,0:T(8,128)(2,1)S(1)}, bf16[2,512,512]{2,1,0:T(8,128)(2,1)S(1)}, u32[]{:S(2)}, u32[]{:S(2)}) collective-permute-start(bf16[2,512,512]{2,1,0:T(8,128)(2,1)S(1)} %get-tuple-element.31), channel_id=1, source_target_pairs={{0,4},{4,0},{1,5},{5,1},{2,6},{6,2},{3,7},{7,3},{8,12},{12,8},{9,1... | collective-permute-start | bytes 3145736 | tf_op jit(solution)/shard_map/ppermute | solution.py:28
  172.6 6.3 %collective-permute-done.39 = f32[4,2,16,512]{3,2,1,0:T(8,128)} collective-permute-done((f32[4,2,16,512]{3,2,1,0:T(8,128)S(1)}, f32[4,2,16,512]{3,2,1,0:T(8,128)}, u32[]{:S(2)}, u32[]{:S(2)}) %collective-permute-start.39) | collective-permute-done | bytes 262176 | tf_op jit(solution)/shard_map/ppermute | solution.py:28
  179.0 2.5 %collective-permute-done.38 = f32[4,2,16,512]{3,2,1,0:T(8,128)} collective-permute-done((f32[4,2,16,512]{3,2,1,0:T(8,128)}, f32[4,2,16,512]{3,2,1,0:T(8,128)}, u32[]{:S(2)}, u32[]{:S(2)}) %collective-permute-start.38) | collective-permute-done | bytes 262176 | tf_op jit(solution)/shard_map/ppermute | solution.py:28
  181.4 5.7 %collective-permute-done.37 = f32[4,2,16,512]{3,2,1,0:T(8,128)} collective-permute-done((f32[4,2,16,512]{3,2,1,0:T(8,128)}, f32[4,2,16,512]{3,2,1,0:T(8,128)}, u32[]{:S(2)}, u32[]{:S(2)}) %collective-permute-start.37) | collective-permute-done | bytes 262176 | tf_op jit(solution)/shard_map/ppermute | solution.py:28
  188.3 5.1 %shard_map.104 = (bf16[256,1024]{1,0:T(8,128)(2,1)S(1)}, bf16[256,1024]{1,0:T(8,128)(2,1)S(1)}) custom-call(s32[1]{0:T(128)} %bitcast.63.zi, bf16[2,512,512]{2,1,0:T(8,128)(2,1)S(1)} %get-tuple-element.30.own_ref, bf16[2,512,512]{2,1,0:T(8,128)(2,1)S(1)} %collective-permute-done.50.got_ref, bf16[2,4,4,256,256]{4,3,2,1,0:T(8,128)(2,1)} %bitcast.56.refs_0_.refs_1_, ...), custom_call_target="tpu_custom_call" | custom-call | flops 2147483648 | bytes 8388608 | tf_op jit(solution)/shard_map/pallas_call | solution.py:279
  196.5 1.4 collective-permute-start.57
  198.0 5.1 %shard_map.103 = (f32[256,1024]{1,0:T(8,128)S(1)}, bf16[256,1024]{1,0:T(8,128)(2,1)S(1)}) custom-call(s32[1]{0:T(128)} %bitcast.62.zi, bf16[2,512,512]{2,1,0:T(8,128)(2,1)S(1)} %get-tuple-element.30.own_ref, bf16[2,512,512]{2,1,0:T(8,128)(2,1)S(1)} %collective-permute-done.50.got_ref, bf16[2,4,4,256,256]{4,3,2,1,0:T(8,128)(2,1)} %bitcast.56.refs_0_.refs_1_, ...), custom_call_target="tpu_custom_call" | custom-call | flops 2147483648 | bytes 8388608 | tf_op jit(solution)/shard_map/pallas_call | solution.py:279
  203.0 5.1 %shard_map.105 = (bf16[256,1024]{1,0:T(8,128)(2,1)S(1)}, f32[256,1024]{1,0:T(8,128)S(1)}) custom-call(s32[1]{0:T(128)} %bitcast.64.zi, bf16[2,512,512]{2,1,0:T(8,128)(2,1)S(1)} %get-tuple-element.30.own_ref, bf16[2,512,512]{2,1,0:T(8,128)(2,1)S(1)} %collective-permute-done.50.got_ref, bf16[2,4,4,256,256]{4,3,2,1,0:T(8,128)(2,1)} %bitcast.56.refs_0_.refs_1_, ...), custom_call_target="tpu_custom_call" | custom-call | flops 2147483648 | bytes 8388608 | tf_op jit(solution)/shard_map/pallas_call | solution.py:279
  209.3 2.7 %collective-permute-start.56 = (bf16[256,1024]{1,0:T(8,128)(2,1)S(1)}, bf16[256,1024]{1,0:T(8,128)(2,1)}, u32[]{:S(2)}, u32[]{:S(2)}) collective-permute-start(bf16[256,1024]{1,0:T(8,128)(2,1)S(1)} %get-tuple-element.35), channel_id=1, source_target_pairs={{0,3},{1,0},{2,1},{3,2},{4,7},{5,4},{6,5},{7,6},{8,11},{9,8},{10,9... | collective-permute-start | bytes 1572872 | tf_op jit(solution)/shard_map/ppermute | solution.py:28
  212.9 2.7 %collective-permute-start.58 = (bf16[256,1024]{1,0:T(8,128)(2,1)}, bf16[256,1024]{1,0:T(8,128)(2,1)}, u32[]{:S(2)}, u32[]{:S(2)}) collective-permute-start(bf16[256,1024]{1,0:T(8,128)(2,1)} %add_convert_fusion), channel_id=1, source_target_pairs={{0,3},{1,0},{2,1},{3,2},{4,7},{5,4},{6,5},{7,6},{8,11},{9,8},{10,9... | collective-permute-start | bytes 1572872 | tf_op jit(solution)/shard_map/ppermute | solution.py:28
  215.6 8.5 %collective-permute-start.43 = (f32[16,512]{1,0:T(8,128)S(1)}, f32[16,512]{1,0:T(8,128)S(1)}, u32[]{:S(2)}, u32[]{:S(2)}) collective-permute-start(f32[16,512]{1,0:T(8,128)S(1)} %get-tuple-element.72), channel_id=1, source_target_pairs={{0,4},{4,0},{1,5},{5,1},{2,6},{6,2},{3,7},{7,3},{8,12},{12,8},{9,1... | collective-permute-start | bytes 98312 | tf_op jit(solution)/shard_map/ppermute | solution.py:28
  225.6 5.1 %shard_map.102.base_ref = f32[512,1024]{1,0:T(8,128)S(1)} custom-call(s32[1]{0:T(128)} %bitcast.47.zi, bf16[2,512,512]{2,1,0:T(8,128)(2,1)S(1)} %get-tuple-element.30.own_ref, bf16[2,512,512]{2,1,0:T(8,128)(2,1)S(1)} %collective-permute-done.50.got_ref, bf16[2,4,4,256,256]{4,3,2,1,0:T(8,128)(2,1)} %bitcast.56.refs_0_.refs_1_, ...), custom_call_target="tpu_custom_call" | custom-call | flops 2147483648 | bytes 8388608 | tf_op jit(solution)/shard_map/pallas_call | solution.py:279
  232.0 4.9 %shard_map.106 = f32[512,1024]{1,0:T(8,128)} custom-call(s32[4]{0:T(128)} %copy-done.2, f32[512,1024]{1,0:T(8,128)} %copy-done.1, bf16[256,1024]{1,0:T(8,128)(2,1)} %collective-permute-done.54.plus_top, bf16[256,1024]{1,0:T(8,128)(2,1)} %collective-permute-done.55.plus_low, bf16[256,1024]{1,0:T(8,128)(2,1)} %collective-permute-done.56.minus_top, ...), custom_call_target="tpu_custom_call" | custom-call | flops 1048576 | bytes 6291456 | tf_op jit(solution)/shard_map/pallas_call | solution.py:303
  (185 shorter events, 56.0 us)
Async XLA Ops:
  8.0 22.9 %collective-permute-start.5 = (bf16[2,256,256]{2,1,0:T(8,128)(2,1)S(1)}, bf16[2,256,256]{2,1,0:T(8,128)(2,1)S(1)}, u32[]{:S(2)}, u32[]{:S(2)}) collective-permute-start(bf16[2,256,256]{2,1,0:T(8,128)(2,1)S(1)} %get-tuple-element.45), channel_id=1, source_target_pairs={{0,8},{8,16},{16,24},{24,0},{1,9},{9,17},{17,25},{25,1},{2,10},{10... | collective-permute-start | bytes 786440 | tf_op jit(solution)/shard_map/ppermute | solution.py:28
  9.4 22.4 %collective-permute-start.4 = (bf16[2,256,256]{2,1,0:T(8,128)(2,1)S(1)}, bf16[2,256,256]{2,1,0:T(8,128)(2,1)S(1)}, u32[]{:S(2)}, u32[]{:S(2)}) collective-permute-start(bf16[2,256,256]{2,1,0:T(8,128)(2,1)S(1)} %get-tuple-element.45), channel_id=1, source_target_pairs={{0,16},{8,24},{16,0},{24,8},{1,17},{9,25},{17,1},{25,9},{2,18},{10... | collective-permute-start | bytes 786440 | tf_op jit(solution)/shard_map/ppermute | solution.py:28
  11.8 9.8 %collective-permute-start.27 = (bf16[2,2,16,512]{3,2,1,0:T(8,128)(2,1)S(1)}, bf16[2,2,16,512]{3,2,1,0:T(8,128)(2,1)S(1)}, u32[]{:S(2)}, u32[]{:S(2)}) collective-permute-start(bf16[2,2,16,512]{3,2,1,0:T(8,128)(2,1)S(1)} %get-tuple-element.74), channel_id=1, source_target_pairs={{0,8},{8,16},{16,24},{24,0},{1,9},{9,17},{17,25},{25,1},{2,10},{10... | collective-permute-start | bytes 196616 | tf_op jit(solution)/shard_map/ppermute | solution.py:28
  11.9 14.0 %collective-permute-start.26 = (bf16[2,2,16,512]{3,2,1,0:T(8,128)(2,1)S(1)}, bf16[2,2,16,512]{3,2,1,0:T(8,128)(2,1)S(1)}, u32[]{:S(2)}, u32[]{:S(2)}) collective-permute-start(bf16[2,2,16,512]{3,2,1,0:T(8,128)(2,1)S(1)} %get-tuple-element.74), channel_id=1, source_target_pairs={{0,16},{8,24},{16,0},{24,8},{1,17},{9,25},{17,1},{25,9},{2,18},{10... | collective-permute-start | bytes 196616 | tf_op jit(solution)/shard_map/ppermute | solution.py:28
  14.3 13.3 %collective-permute-start.25 = (bf16[2,2,16,512]{3,2,1,0:T(8,128)(2,1)S(1)}, bf16[2,2,16,512]{3,2,1,0:T(8,128)(2,1)S(1)}, u32[]{:S(2)}, u32[]{:S(2)}) collective-permute-start(bf16[2,2,16,512]{3,2,1,0:T(8,128)(2,1)S(1)} %get-tuple-element.74), channel_id=1, source_target_pairs={{0,24},{8,0},{16,8},{24,16},{1,25},{9,1},{17,9},{25,17},{2,26},{10... | collective-permute-start | bytes 196616 | tf_op jit(solution)/shard_map/ppermute | solution.py:28
  21.6 11.0 %collective-permute-start.3 = (bf16[2,256,256]{2,1,0:T(8,128)(2,1)S(1)}, bf16[2,256,256]{2,1,0:T(8,128)(2,1)S(1)}, u32[]{:S(2)}, u32[]{:S(2)}) collective-permute-start(bf16[2,256,256]{2,1,0:T(8,128)(2,1)S(1)} %get-tuple-element.45), channel_id=1, source_target_pairs={{0,24},{8,0},{16,8},{24,16},{1,25},{9,1},{17,9},{25,17},{2,26},{10... | collective-permute-start | bytes 786440 | tf_op jit(solution)/shard_map/ppermute | solution.py:28
  25.9 8.7 %collective-permute-start.8 = (bf16[2,256,256]{2,1,0:T(8,128)(2,1)S(1)}, bf16[2,256,256]{2,1,0:T(8,128)(2,1)S(1)}, u32[]{:S(2)}, u32[]{:S(2)}) collective-permute-start(bf16[2,256,256]{2,1,0:T(8,128)(2,1)S(1)} %get-tuple-element.44), channel_id=1, source_target_pairs={{0,32},{32,64},{64,96},{96,0},{1,33},{33,65},{65,97},{97,1},{2,34}... | collective-permute-start | bytes 786440 | tf_op jit(solution)/shard_map/ppermute | solution.py:28
  27.6 13.7 %collective-permute-start.7 = (bf16[2,256,256]{2,1,0:T(8,128)(2,1)S(1)}, bf16[2,256,256]{2,1,0:T(8,128)(2,1)S(1)}, u32[]{:S(2)}, u32[]{:S(2)}) collective-permute-start(bf16[2,256,256]{2,1,0:T(8,128)(2,1)S(1)} %get-tuple-element.44), channel_id=1, source_target_pairs={{0,64},{32,96},{64,0},{96,32},{1,65},{33,97},{65,1},{97,33},{2,66}... | collective-permute-start | bytes 786440 | tf_op jit(solution)/shard_map/ppermute | solution.py:28
  30.9 11.3 %collective-permute-start.6 = (bf16[2,256,256]{2,1,0:T(8,128)(2,1)S(1)}, bf16[2,256,256]{2,1,0:T(8,128)(2,1)S(1)}, u32[]{:S(2)}, u32[]{:S(2)}) collective-permute-start(bf16[2,256,256]{2,1,0:T(8,128)(2,1)S(1)} %get-tuple-element.44), channel_id=1, source_target_pairs={{0,96},{32,0},{64,32},{96,64},{1,97},{33,1},{65,33},{97,65},{2,98}... | collective-permute-start | bytes 786440 | tf_op jit(solution)/shard_map/ppermute | solution.py:28
  31.8 15.3 %collective-permute-start.30 = (bf16[4,2,2,16,512]{4,3,2,1,0:T(8,128)(2,1)S(1)}, bf16[4,2,2,16,512]{4,3,2,1,0:T(8,128)(2,1)S(1)}, u32[]{:S(2)}, u32[]{:S(2)}) collective-permute-start(bf16[4,2,2,16,512]{4,3,2,1,0:T(8,128)(2,1)S(1)} %get-tuple-element.54), channel_id=1, source_target_pairs={{0,32},{32,64},{64,96},{96,0},{1,33},{33,65},{65,97},{97,1},{2,34}... | collective-permute-start | bytes 786440 | tf_op jit(solution)/shard_map/ppermute | solution.py:28
  32.6 19.9 %collective-permute-start.29 = (bf16[4,2,2,16,512]{4,3,2,1,0:T(8,128)(2,1)S(1)}, bf16[4,2,2,16,512]{4,3,2,1,0:T(8,128)(2,1)S(1)}, u32[]{:S(2)}, u32[]{:S(2)}) collective-permute-start(bf16[4,2,2,16,512]{4,3,2,1,0:T(8,128)(2,1)S(1)} %get-tuple-element.54), channel_id=1, source_target_pairs={{0,64},{32,96},{64,0},{96,32},{1,65},{33,97},{65,1},{97,33},{2,66}... | collective-permute-start | bytes 786440 | tf_op jit(solution)/shard_map/ppermute | solution.py:28
  34.7 31.2 %collective-permute-start.9 = (bf16[2,512,256]{2,1,0:T(8,128)(2,1)S(1)}, bf16[2,512,256]{2,1,0:T(8,128)(2,1)S(1)}, u32[]{:S(2)}, u32[]{:S(2)}) collective-permute-start(bf16[2,512,256]{2,1,0:T(8,128)(2,1)S(1)} %bitcast.115), channel_id=1, source_target_pairs={{0,96},{32,0},{64,32},{96,64},{1,97},{33,1},{65,33},{97,65},{2,98}... | collective-permute-start | bytes 1572872 | tf_op jit(solution)/shard_map/ppermute | solution.py:28
  41.2 24.6 %collective-permute-start.10 = (bf16[2,512,256]{2,1,0:T(8,128)(2,1)S(1)}, bf16[2,512,256]{2,1,0:T(8,128)(2,1)S(1)}, u32[]{:S(2)}, u32[]{:S(2)}) collective-permute-start(bf16[2,512,256]{2,1,0:T(8,128)(2,1)S(1)} %bitcast.116), channel_id=1, source_target_pairs={{0,32},{32,64},{64,96},{96,0},{1,33},{33,65},{65,97},{97,1},{2,34}... | collective-permute-start | bytes 1572872 | tf_op jit(solution)/shard_map/ppermute | solution.py:28
  42.4 23.5 %collective-permute-start.11 = (bf16[2,512,256]{2,1,0:T(8,128)(2,1)S(1)}, bf16[2,512,256]{2,1,0:T(8,128)(2,1)S(1)}, u32[]{:S(2)}, u32[]{:S(2)}) collective-permute-start(bf16[2,512,256]{2,1,0:T(8,128)(2,1)S(1)} %bitcast.119), channel_id=1, source_target_pairs={{0,24},{8,0},{16,8},{24,16},{1,25},{9,1},{17,9},{25,17},{2,26},{10... | collective-permute-start | bytes 1572872 | tf_op jit(solution)/shard_map/ppermute | solution.py:28
  47.1 18.8 %collective-permute-start.12 = (bf16[2,512,256]{2,1,0:T(8,128)(2,1)S(1)}, bf16[2,512,256]{2,1,0:T(8,128)(2,1)S(1)}, u32[]{:S(2)}, u32[]{:S(2)}) collective-permute-start(bf16[2,512,256]{2,1,0:T(8,128)(2,1)S(1)} %bitcast.120), channel_id=1, source_target_pairs={{0,8},{8,16},{16,24},{24,0},{1,9},{9,17},{17,25},{25,1},{2,10},{10... | collective-permute-start | bytes 1572872 | tf_op jit(solution)/shard_map/ppermute | solution.py:28
  52.5 11.1 %collective-permute-start.28 = (bf16[4,2,2,16,512]{4,3,2,1,0:T(8,128)(2,1)S(1)}, bf16[4,2,2,16,512]{4,3,2,1,0:T(8,128)(2,1)S(1)}, u32[]{:S(2)}, u32[]{:S(2)}) collective-permute-start(bf16[4,2,2,16,512]{4,3,2,1,0:T(8,128)(2,1)S(1)} %get-tuple-element.54), channel_id=1, source_target_pairs={{0,96},{32,0},{64,32},{96,64},{1,97},{33,1},{65,33},{97,65},{2,98}... | collective-permute-start | bytes 786440 | tf_op jit(solution)/shard_map/ppermute | solution.py:28
  63.7 58.2 %collective-permute-start.2 = (bf16[512,4096]{1,0:T(8,128)(2,1)S(1)}, bf16[512,4096]{1,0:T(8,128)(2,1)S(1)}, u32[]{:S(2)}, u32[]{:S(2)}) collective-permute-start(bf16[512,4096]{1,0:T(8,128)(2,1)S(1)} %copy-done), channel_id=1, source_target_pairs={{0,4},{4,0},{1,5},{5,1},{2,6},{6,2},{3,7},{7,3},{8,12},{12,8},{9,1... | collective-permute-start | bytes 12582920 | tf_op jit(solution)/shard_map/ppermute | solution.py:28
  65.9 31.9 %collective-permute-start.17 = (bf16[2,512,256]{2,1,0:T(8,128)(2,1)S(1)}, bf16[2,512,256]{2,1,0:T(8,128)(2,1)S(1)}, u32[]{:S(2)}, u32[]{:S(2)}) collective-permute-start(bf16[2,512,256]{2,1,0:T(8,128)(2,1)S(1)} %bitcast.123), channel_id=1, source_target_pairs={{0,96},{32,0},{64,32},{96,64},{1,97},{33,1},{65,33},{97,65},{2,98}... | collective-permute-start | bytes 1572872 | tf_op jit(solution)/shard_map/ppermute | solution.py:28
  68.3 31.6 %collective-permute-start.19 = (bf16[2,512,256]{2,1,0:T(8,128)(2,1)S(1)}, bf16[2,512,256]{2,1,0:T(8,128)(2,1)S(1)}, u32[]{:S(2)}, u32[]{:S(2)}) collective-permute-start(bf16[2,512,256]{2,1,0:T(8,128)(2,1)S(1)} %bitcast.124), channel_id=1, source_target_pairs={{0,32},{32,64},{64,96},{96,0},{1,33},{33,65},{65,97},{97,1},{2,34}... | collective-permute-start | bytes 1572872 | tf_op jit(solution)/shard_map/ppermute | solution.py:28
  68.3 17.0 %collective-permute-start.13 = (bf16[512,256]{1,0:T(8,128)(2,1)S(1)}, bf16[512,256]{1,0:T(8,128)(2,1)S(1)}, u32[]{:S(2)}, u32[]{:S(2)}) collective-permute-start(bf16[512,256]{1,0:T(8,128)(2,1)S(1)} %slice_bitcast_fusion.7), channel_id=1, source_target_pairs={{0,96},{32,0},{64,32},{96,64},{1,97},{33,1},{65,33},{97,65},{2,98}... | collective-permute-start | bytes 786440 | tf_op jit(solution)/shard_map/ppermute | solution.py:28
  71.0 17.3 %collective-permute-start.14 = (bf16[512,256]{1,0:T(8,128)(2,1)S(1)}, bf16[512,256]{1,0:T(8,128)(2,1)S(1)}, u32[]{:S(2)}, u32[]{:S(2)}) collective-permute-start(bf16[512,256]{1,0:T(8,128)(2,1)S(1)} %slice_bitcast_fusion.6), channel_id=1, source_target_pairs={{0,32},{32,64},{64,96},{96,0},{1,33},{33,65},{65,97},{97,1},{2,34}... | collective-permute-start | bytes 786440 | tf_op jit(solution)/shard_map/ppermute | solution.py:28
  85.2 7.1 %collective-permute-start.15 = (bf16[512,256]{1,0:T(8,128)(2,1)S(1)}, bf16[512,256]{1,0:T(8,128)(2,1)S(1)}, u32[]{:S(2)}, u32[]{:S(2)}) collective-permute-start(bf16[512,256]{1,0:T(8,128)(2,1)S(1)} %slice_bitcast_fusion.5), channel_id=1, source_target_pairs={{0,24},{8,0},{16,8},{24,16},{1,25},{9,1},{17,9},{25,17},{2,26},{10... | collective-permute-start | bytes 786440 | tf_op jit(solution)/shard_map/ppermute | solution.py:28
  88.3 7.9 %collective-permute-start.16 = (bf16[512,256]{1,0:T(8,128)(2,1)S(1)}, bf16[512,256]{1,0:T(8,128)(2,1)S(1)}, u32[]{:S(2)}, u32[]{:S(2)}) collective-permute-start(bf16[512,256]{1,0:T(8,128)(2,1)S(1)} %slice_bitcast_fusion.4), channel_id=1, source_target_pairs={{0,8},{8,16},{16,24},{24,0},{1,9},{9,17},{17,25},{25,1},{2,10},{10... | collective-permute-start | bytes 786440 | tf_op jit(solution)/shard_map/ppermute | solution.py:28
  92.3 11.8 %collective-permute-start.21 = (bf16[2,512,256]{2,1,0:T(8,128)(2,1)S(1)}, bf16[2,512,256]{2,1,0:T(8,128)(2,1)S(1)}, u32[]{:S(2)}, u32[]{:S(2)}) collective-permute-start(bf16[2,512,256]{2,1,0:T(8,128)(2,1)S(1)} %bitcast.127), channel_id=1, source_target_pairs={{0,24},{8,0},{16,8},{24,16},{1,25},{9,1},{17,9},{25,17},{2,26},{10... | collective-permute-start | bytes 1572872 | tf_op jit(solution)/shard_map/ppermute | solution.py:28
  96.2 12.6 %collective-permute-start.23 = (bf16[2,512,256]{2,1,0:T(8,128)(2,1)S(1)}, bf16[2,512,256]{2,1,0:T(8,128)(2,1)S(1)}, u32[]{:S(2)}, u32[]{:S(2)}) collective-permute-start(bf16[2,512,256]{2,1,0:T(8,128)(2,1)S(1)} %bitcast.128), channel_id=1, source_target_pairs={{0,8},{8,16},{16,24},{24,0},{1,9},{9,17},{17,25},{25,1},{2,10},{10... | collective-permute-start | bytes 1572872 | tf_op jit(solution)/shard_map/ppermute | solution.py:28
  97.8 90.5 %collective-permute-start.51 = (bf16[2,4,4,256,256]{4,3,2,1,0:T(8,128)(2,1)}, bf16[2,4,4,256,256]{4,3,2,1,0:T(8,128)(2,1)}, u32[]{:S(2)}, u32[]{:S(2)}) collective-permute-start(bf16[2,4,4,256,256]{4,3,2,1,0:T(8,128)(2,1)} %bitcast.56.refs_0_.refs_1_), channel_id=1, source_target_pairs={{0,4},{4,0},{1,5},{5,1},{2,6},{6,2},{3,7},{7,3},{8,12},{12,8},{9,1... | collective-permute-start | bytes 12582920 | tf_op jit(solution)/shard_map/ppermute | solution.py:28
  99.8 9.9 %collective-permute-start.18 = (bf16[512,256]{1,0:T(8,128)(2,1)S(1)}, bf16[512,256]{1,0:T(8,128)(2,1)S(1)}, u32[]{:S(2)}, u32[]{:S(2)}) collective-permute-start(bf16[512,256]{1,0:T(8,128)(2,1)S(1)} %slice_bitcast_fusion.3), channel_id=1, source_target_pairs={{0,96},{32,0},{64,32},{96,64},{1,97},{33,1},{65,33},{97,65},{2,98}... | collective-permute-start | bytes 786440 | tf_op jit(solution)/shard_map/ppermute | solution.py:28
  104.1 7.8 %collective-permute-start.20 = (bf16[512,256]{1,0:T(8,128)(2,1)S(1)}, bf16[512,256]{1,0:T(8,128)(2,1)S(1)}, u32[]{:S(2)}, u32[]{:S(2)}) collective-permute-start(bf16[512,256]{1,0:T(8,128)(2,1)S(1)} %slice_bitcast_fusion.2), channel_id=1, source_target_pairs={{0,32},{32,64},{64,96},{96,0},{1,33},{33,65},{65,97},{97,1},{2,34}... | collective-permute-start | bytes 786440 | tf_op jit(solution)/shard_map/ppermute | solution.py:28
  108.8 6.3 %collective-permute-start.22 = (bf16[512,256]{1,0:T(8,128)(2,1)S(1)}, bf16[512,256]{1,0:T(8,128)(2,1)S(1)}, u32[]{:S(2)}, u32[]{:S(2)}) collective-permute-start(bf16[512,256]{1,0:T(8,128)(2,1)S(1)} %slice_bitcast_fusion.1), channel_id=1, source_target_pairs={{0,24},{8,0},{16,8},{24,16},{1,25},{9,1},{17,9},{25,17},{2,26},{10... | collective-permute-start | bytes 786440 | tf_op jit(solution)/shard_map/ppermute | solution.py:28
  109.7 6.4 %collective-permute-start.24 = (bf16[512,256]{1,0:T(8,128)(2,1)S(1)}, bf16[512,256]{1,0:T(8,128)(2,1)S(1)}, u32[]{:S(2)}, u32[]{:S(2)}) collective-permute-start(bf16[512,256]{1,0:T(8,128)(2,1)S(1)} %slice_bitcast_fusion), channel_id=1, source_target_pairs={{0,8},{8,16},{16,24},{24,0},{1,9},{9,17},{17,25},{25,1},{2,10},{10... | collective-permute-start | bytes 786440 | tf_op jit(solution)/shard_map/ppermute | solution.py:28
  117.7 70.6 %collective-permute-start.52 = (bf16[2,4,4,256,256]{4,3,2,1,0:T(8,128)(2,1)}, bf16[2,4,4,256,256]{4,3,2,1,0:T(8,128)(2,1)}, u32[]{:S(2)}, u32[]{:S(2)}) collective-permute-start(bf16[2,4,4,256,256]{4,3,2,1,0:T(8,128)(2,1)} %bitcast.61.refs_4_.refs_5_), channel_id=1, source_target_pairs={{0,4},{4,0},{1,5},{5,1},{2,6},{6,2},{3,7},{7,3},{8,12},{12,8},{9,1... | collective-permute-start | bytes 12582920 | tf_op jit(solution)/shard_map/ppermute | solution.py:28
  130.5 9.6 %collective-permute-start.31 = (f32[24,128]{1,0:T(8,128)S(1)}, f32[24,128]{1,0:T(8,128)S(1)}, u32[]{:S(2)}, u32[]{:S(2)}) collective-permute-start(f32[24,128]{1,0:T(8,128)S(1)} %shard_map.99), channel_id=1, source_target_pairs={{0,24},{8,0},{16,8},{24,16},{1,25},{9,1},{17,9},{25,17},{2,26},{10... | collective-permute-start | bytes 36872 | tf_op jit(solution)/shard_map/ppermute | solution.py:28
  131.9 8.1 %collective-permute-start.32 = (f32[24,128]{1,0:T(8,128)S(1)}, f32[24,128]{1,0:T(8,128)S(1)}, u32[]{:S(2)}, u32[]{:S(2)}) collective-permute-start(f32[24,128]{1,0:T(8,128)S(1)} %shard_map.99), channel_id=1, source_target_pairs={{0,16},{8,24},{16,0},{24,8},{1,17},{9,25},{17,1},{25,9},{2,18},{10... | collective-permute-start | bytes 36872 | tf_op jit(solution)/shard_map/ppermute | solution.py:28
  132.9 7.2 %collective-permute-start.33 = (f32[24,128]{1,0:T(8,128)S(1)}, f32[24,128]{1,0:T(8,128)S(1)}, u32[]{:S(2)}, u32[]{:S(2)}) collective-permute-start(f32[24,128]{1,0:T(8,128)S(1)} %shard_map.99), channel_id=1, source_target_pairs={{0,8},{8,16},{16,24},{24,0},{1,9},{9,17},{17,25},{25,1},{2,10},{10... | collective-permute-start | bytes 36872 | tf_op jit(solution)/shard_map/ppermute | solution.py:28
  164.3 24.0 %collective-permute-start.50 = (bf16[2,512,512]{2,1,0:T(8,128)(2,1)S(1)}, bf16[2,512,512]{2,1,0:T(8,128)(2,1)S(1)}, u32[]{:S(2)}, u32[]{:S(2)}) collective-permute-start(bf16[2,512,512]{2,1,0:T(8,128)(2,1)S(1)} %get-tuple-element.31), channel_id=1, source_target_pairs={{0,4},{4,0},{1,5},{5,1},{2,6},{6,2},{3,7},{7,3},{8,12},{12,8},{9,1... | collective-permute-start | bytes 3145736 | tf_op jit(solution)/shard_map/ppermute | solution.py:28
  171.0 8.0 %collective-permute-start.39 = (f32[4,2,16,512]{3,2,1,0:T(8,128)S(1)}, f32[4,2,16,512]{3,2,1,0:T(8,128)}, u32[]{:S(2)}, u32[]{:S(2)}) collective-permute-start(f32[4,2,16,512]{3,2,1,0:T(8,128)S(1)} %bitcast.137), channel_id=1, source_target_pairs={{0,96},{32,0},{64,32},{96,64},{1,97},{33,1},{65,33},{97,65},{2,98}... | collective-permute-start | bytes 786440 | tf_op jit(solution)/shard_map/ppermute | solution.py:28
  172.0 9.4 %collective-permute-start.38 = (f32[4,2,16,512]{3,2,1,0:T(8,128)}, f32[4,2,16,512]{3,2,1,0:T(8,128)}, u32[]{:S(2)}, u32[]{:S(2)}) collective-permute-start(f32[4,2,16,512]{3,2,1,0:T(8,128)} %bitcast.39), channel_id=1, source_target_pairs={{0,64},{32,96},{64,0},{96,32},{1,65},{33,97},{65,1},{97,33},{2,66}... | collective-permute-start | bytes 786440 | tf_op jit(solution)/shard_map/ppermute | solution.py:28
  179.0 8.1 %collective-permute-start.37 = (f32[4,2,16,512]{3,2,1,0:T(8,128)}, f32[4,2,16,512]{3,2,1,0:T(8,128)}, u32[]{:S(2)}, u32[]{:S(2)}) collective-permute-start(f32[4,2,16,512]{3,2,1,0:T(8,128)} %bitcast.38), channel_id=1, source_target_pairs={{0,32},{32,64},{64,96},{96,0},{1,33},{33,65},{65,97},{97,1},{2,34}... | collective-permute-start | bytes 786440 | tf_op jit(solution)/shard_map/ppermute | solution.py:28
  193.5 14.7 %collective-permute-start.53 = (bf16[256,1024]{1,0:T(8,128)(2,1)S(1)}, bf16[256,1024]{1,0:T(8,128)(2,1)S(1)}, u32[]{:S(2)}, u32[]{:S(2)}) collective-permute-start(bf16[256,1024]{1,0:T(8,128)(2,1)S(1)} %get-tuple-element.33), channel_id=1, source_target_pairs={{0,1},{1,2},{2,3},{3,0},{4,5},{5,6},{6,7},{7,4},{8,9},{9,10},{10,1... | collective-permute-start | bytes 1572872 | tf_op jit(solution)/shard_map/ppermute | solution.py:28
  194.8 18.0 %collective-permute-start.42 = (f32[2,16,512]{2,1,0:T(8,128)S(1)}, f32[2,16,512]{2,1,0:T(8,128)S(1)}, u32[]{:S(2)}, u32[]{:S(2)}) collective-permute-start(f32[2,16,512]{2,1,0:T(8,128)S(1)} %get-tuple-element.51), channel_id=1, source_target_pairs={{0,24},{8,0},{16,8},{24,16},{1,25},{9,1},{17,9},{25,17},{2,26},{10... | collective-permute-start | bytes 196616 | tf_op jit(solution)/shard_map/ppermute | solution.py:28
  195.4 17.5 %collective-permute-start.41 = (f32[2,16,512]{2,1,0:T(8,128)S(1)}, f32[2,16,512]{2,1,0:T(8,128)S(1)}, u32[]{:S(2)}, u32[]{:S(2)}) collective-permute-start(f32[2,16,512]{2,1,0:T(8,128)S(1)} %get-tuple-element.52), channel_id=1, source_target_pairs={{0,16},{8,24},{16,0},{24,8},{1,17},{9,25},{17,1},{25,9},{2,18},{10... | collective-permute-start | bytes 196616 | tf_op jit(solution)/shard_map/ppermute | solution.py:28
  196.5 19.0 %collective-permute-start.40 = (f32[2,16,512]{2,1,0:T(8,128)S(1)}, f32[2,16,512]{2,1,0:T(8,128)S(1)}, u32[]{:S(2)}, u32[]{:S(2)}) collective-permute-start(f32[2,16,512]{2,1,0:T(8,128)S(1)} %get-tuple-element.50), channel_id=1, source_target_pairs={{0,8},{8,16},{16,24},{24,0},{1,9},{9,17},{17,25},{25,1},{2,10},{10... | collective-permute-start | bytes 196616 | tf_op jit(solution)/shard_map/ppermute | solution.py:28
  196.5 12.7 %collective-permute-start.57 = (bf16[256,1024]{1,0:T(8,128)(2,1)S(1)}, bf16[256,1024]{1,0:T(8,128)(2,1)S(1)}, u32[]{:S(2)}, u32[]{:S(2)}) collective-permute-start(bf16[256,1024]{1,0:T(8,128)(2,1)S(1)} %get-tuple-element.37), channel_id=1, source_target_pairs={{0,3},{1,0},{2,1},{3,2},{4,7},{5,4},{6,5},{7,6},{8,11},{9,8},{10,9... | collective-permute-start | bytes 1572872 | tf_op jit(solution)/shard_map/ppermute | solution.py:28
  208.2 23.8 %collective-permute-start.55 = (bf16[256,1024]{1,0:T(8,128)(2,1)S(1)}, bf16[256,1024]{1,0:T(8,128)(2,1)}, u32[]{:S(2)}, u32[]{:S(2)}) collective-permute-start(bf16[256,1024]{1,0:T(8,128)(2,1)S(1)} %get-tuple-element.34), channel_id=1, source_target_pairs={{0,1},{1,2},{2,3},{3,0},{4,5},{5,6},{6,7},{7,4},{8,9},{9,10},{10,1... | collective-permute-start | bytes 1572872 | tf_op jit(solution)/shard_map/ppermute | solution.py:28
  209.3 22.7 %collective-permute-start.56 = (bf16[256,1024]{1,0:T(8,128)(2,1)S(1)}, bf16[256,1024]{1,0:T(8,128)(2,1)}, u32[]{:S(2)}, u32[]{:S(2)}) collective-permute-start(bf16[256,1024]{1,0:T(8,128)(2,1)S(1)} %get-tuple-element.35), channel_id=1, source_target_pairs={{0,3},{1,0},{2,1},{3,2},{4,7},{5,4},{6,5},{7,6},{8,11},{9,8},{10,9... | collective-permute-start | bytes 1572872 | tf_op jit(solution)/shard_map/ppermute | solution.py:28
  212.9 19.1 %collective-permute-start.54 = (bf16[256,1024]{1,0:T(8,128)(2,1)}, bf16[256,1024]{1,0:T(8,128)(2,1)}, u32[]{:S(2)}, u32[]{:S(2)}) collective-permute-start(bf16[256,1024]{1,0:T(8,128)(2,1)} %add_convert_fusion.1), channel_id=1, source_target_pairs={{0,1},{1,2},{2,3},{3,0},{4,5},{5,6},{6,7},{7,4},{8,9},{9,10},{10,1... | collective-permute-start | bytes 1572872 | tf_op jit(solution)/shard_map/ppermute | solution.py:28
  212.9 19.1 %collective-permute-start.58 = (bf16[256,1024]{1,0:T(8,128)(2,1)}, bf16[256,1024]{1,0:T(8,128)(2,1)}, u32[]{:S(2)}, u32[]{:S(2)}) collective-permute-start(bf16[256,1024]{1,0:T(8,128)(2,1)} %add_convert_fusion), channel_id=1, source_target_pairs={{0,3},{1,0},{2,1},{3,2},{4,7},{5,4},{6,5},{7,6},{8,11},{9,8},{10,9... | collective-permute-start | bytes 1572872 | tf_op jit(solution)/shard_map/ppermute | solution.py:28
  215.6 9.4 %collective-permute-start.43 = (f32[16,512]{1,0:T(8,128)S(1)}, f32[16,512]{1,0:T(8,128)S(1)}, u32[]{:S(2)}, u32[]{:S(2)}) collective-permute-start(f32[16,512]{1,0:T(8,128)S(1)} %get-tuple-element.72), channel_id=1, source_target_pairs={{0,4},{4,0},{1,5},{5,1},{2,6},{6,2},{3,7},{7,3},{8,12},{12,8},{9,1... | collective-permute-start | bytes 98312 | tf_op jit(solution)/shard_map/ppermute | solution.py:28
  (14 other events, 105.6 us)

commit v2 on v0

v2 whole, which is shorter than its diff:
```python
import functools

import jax
import jax.numpy as jnp
from jax import lax
from jax.experimental import pallas as pl
from jax.experimental.pallas import tpu as pltpu
from jax.sharding import Mesh, PartitionSpec as P

BF = jnp.bfloat16
F32 = jnp.float32
NZ, NX, NC, NY = 4, 4, 2, 4
ENC = ("z", "x", "core")
ROWS = 512
D = 4096
HALF = 512
CHUNK = 256
PIECE = 576
DEC = 16
NPASS = 4
PAIRS = 4
LOW = -1e30
HIDDEN = pl.CostEstimate(flops=0, bytes_accessed=0, transcendentals=0)
NT = (((1,), (1,)), ((), ()))
TN = (((0,), (0,)), ((), ()))


def perm(v, axis, shift):
    n = {"z": NZ, "x": NX, "core": NC, "dec": NY}[axis]
    return lax.ppermute(v, axis, [(i, (i + shift) % n) for i in range(n)])


def gather4(v, axis):
    return [v] + [perm(v, axis, -o) for o in (1, 2, 3)]


def phase(*values):
    return lax.optimization_barrier(values)


def params(mib):
    return pltpu.CompilerParams(vmem_limit_bytes=mib * 1024 * 1024)


def first_kernel(*refs):
    outs = refs[10:]
    for side in range(2):
        own, up, top, low, down = refs[side * 5 : side * 5 + 5]
        mid = PIECE // 2
        outs[side][0, :PIECE] = own[...]
        outs[side][0, PIECE:] = up[...]
        outs[side][1, :mid] = top[...]
        outs[side][1, mid:PIECE] = low[...]
        outs[side][1, PIECE:] = down[...]


def first_blocks(pieces):
    return pl.pallas_call(
        first_kernel,
        out_shape=[jax.ShapeDtypeStruct((2, 2 * PIECE, CHUNK), BF)] * 2,
        compiler_params=params(16),
        cost_estimate=HIDDEN,
    )(*pieces)


def halves_kernel(a_ref, b_ref, c_ref, d_ref, *outs):
    for ref, out in zip((a_ref, b_ref, c_ref, d_ref), outs):
        out[...] = ref[0]


def take_halves(a_up, a_down, b_up, b_down):
    half = (1, 2 * PIECE, CHUNK)
    first = pl.BlockSpec(half, lambda i: (0, 0, 0))
    second = pl.BlockSpec(half, lambda i: (1, 0, 0))
    return pl.pallas_call(
        halves_kernel,
        grid=(1,),
        in_specs=[first, second, first, second],
        out_specs=[pl.BlockSpec(half[1:], lambda i: (0, 0))] * 4,
        out_shape=[jax.ShapeDtypeStruct(half[1:], BF)] * 4,
        compiler_params=params(16),
        cost_estimate=HIDDEN,
    )(a_up, a_down, b_up, b_down)


def near_kernel(pos, own_ref, oth_ref, *refs):
    blocks, (acc_ref, enc_ref, qa_ref, qb_ref) = refs[:6], refs[6:]
    z, x = pos[0], pos[1]
    step = pl.program_id(0)

    def columns(ref, side, outer, inners):
        parts = []
        for inner in inners:
            zo, xo = (outer, inner) if side == 0 else (inner, outer)
            chip = ((z + zo) & 3) * 4 + ((x + xo) & 3)
            parts.append(ref[:, pl.ds(pl.multiple_of(chip * CHUNK, CHUNK), CHUNK)])
        return jnp.concatenate(parts, axis=1)

    def run(ref):
        for side in range(2):
            totals = [None, None]
            for b, outer in enumerate((0, 1, 3)):
                for h in range(2):
                    lhs = columns(ref, side, outer, (h * 2, h * 2 + 1))
                    block = blocks[side * 3 + b].at[h]
                    for t in range(2):
                        rhs = jnp.concatenate(
                            [block[at + t * 256 : at + t * 256 + 256] for at in (0, PIECE)], axis=0
                        )
                        term = jnp.dot(lhs, rhs, preferred_element_type=F32)
                        totals[t] = term if totals[t] is None else totals[t] + term
            for t in range(2):
                at = t * HALF + side * CHUNK
                acc_ref[0, :, at : at + CHUNK] = totals[t]
            enc_ref[0, :, side * 1024 : (side + 1) * 1024] = columns(ref, side, 2, range(4))

    pl.when(step < 2)(lambda: run(own_ref))
    pl.when(step >= 2)(lambda: run(oth_ref))

    @pl.when(step == 0)
    def questions():
        for side, out in ((0, qa_ref), (1, qb_ref)):
            for b, outer in enumerate((0, 1, 3)):
                for inner in range(4):
                    row = (inner % 2) * PIECE + 512
                    at = (outer * 4 + inner) * 64
                    out[at : at + 64, :] = blocks[side * 3 + b][inner // 2, row : row + 64]
            out[512:768, :] = jnp.zeros((256, CHUNK), BF)


def project_near(pos, own, other, blocks):
    tile = ROWS // 2
    fixed = pl.BlockSpec((1024, CHUNK), lambda i, o: (0, 0))
    return pl.pallas_call(
        near_kernel,
        grid_spec=pltpu.PrefetchScalarGridSpec(
            num_scalar_prefetch=1,
            grid=(4,),
            in_specs=[
                pl.BlockSpec((tile, D), lambda i, o: (jnp.minimum(i, 1), 0)),
                pl.BlockSpec((tile, D), lambda i, o: (jnp.maximum(i - 2, 0), 0)),
            ]
            + [pl.BlockSpec(b.shape, lambda i, o: (0, 0, 0)) for b in blocks],
            out_specs=[
                pl.BlockSpec((1, tile, 2 * HALF), lambda i, o: (i // 2, i % 2, 0)),
                pl.BlockSpec((1, tile, 2048), lambda i, o: (i // 2, i % 2, 0)),
                fixed,
                fixed,
            ],
        ),
        out_shape=[
            jax.ShapeDtypeStruct((2, ROWS, 2 * HALF), F32),
            jax.ShapeDtypeStruct((2, ROWS, 2048), BF),
            jax.ShapeDtypeStruct((1024, CHUNK), BF),
            jax.ShapeDtypeStruct((1024, CHUNK), BF),
        ],
        compiler_params=params(26),
        cost_estimate=HIDDEN,
    )(pos, own, other, *blocks)


class Passages:
    def __init__(self, pos, own, other):
        self.z, self.x = pos[0], pos[1]
        self.numbers = (own, other)

    def question(self, side, p):
        return self.numbers[side][NPASS + p]

    def start(self, side, p):
        at = 0
        for k in range(p):
            at = at + self.numbers[side][k]
        return at

    def chip(self, side, p):
        q = self.question(side, p)
        return ((q >> 3) - self.z) & 3, ((q >> 1) - self.x) & 3, q & 1

    def row(self, half, side, p):
        zo, xo, core = self.chip(side, p)
        outer, inner = (zo, xo) if half == 0 else (xo, zo)
        return (outer * 4 + inner) * 64 + core * 16


def pair_matrix(meta, qg_refs, side, pair, which):
    low = lax.broadcasted_iota(jnp.int32, (DEC, 128), 1) < 64
    half, lane = pair // 2, pair % 2
    parts = []
    for p in range(NPASS):
        row = pl.multiple_of(meta.row(half, side, p) + which * 32, 16)
        tile = qg_refs[half][pl.ds(row, DEC), lane * 128 : (lane + 1) * 128]
        zero = jnp.zeros_like(tile)
        parts += [jnp.where(low, tile, zero), jnp.where(low, zero, tile)]
    return jnp.concatenate(parts, axis=0)


def lane_value(numbers):
    lane = lax.broadcasted_iota(jnp.int32, (1, 128), 1) // 32
    value = jnp.zeros((1, 128), jnp.int32)
    for p in range(NPASS):
        value = jnp.where(lane == p, numbers[p], value)
    return value


def inside_mask(meta, side):
    row = lax.broadcasted_iota(jnp.int32, (ROWS, 128), 0)
    starts = [meta.start(side, p) for p in range(NPASS + 1)]
    return (row >= lane_value(starts[:NPASS])) & (row < lane_value(starts[1:]))


def dot_nt(a, b):
    return lax.dot_general(a, b, NT, preferred_element_type=F32)


def forward_side(side, meta, k, v, qg, st_ref, num_ref):
    inside = inside_mask(meta, side)
    question = lane_value([meta.question(side, p) for p in range(NPASS)]).astype(F32)
    for pair in range(PAIRS):
        cols = slice(pair * 128, (pair + 1) * 128)
        scores = dot_nt(k[side, :, cols], pair_matrix(meta, qg, side, pair, 0))
        scores = jnp.where(inside, scores, LOW)
        top = jnp.max(scores, axis=0, keepdims=True)
        unnorm = jnp.exp(scores - top)
        unnorm_b = unnorm.astype(BF)
        values = v[side, :, cols]
        dprob = dot_nt(values, pair_matrix(meta, qg, side, pair, 1))
        at = side * PAIRS + pair
        st_ref[at : at + 1, :] = top
        st_ref[8 + at : 9 + at, :] = jnp.sum(unnorm, axis=0, keepdims=True)
        st_ref[16 + at : 17 + at, :] = jnp.sum(
            unnorm_b.astype(F32) * dprob, axis=0, keepdims=True
        )
        st_ref[24 + at : 25 + at, :] = question
        num_ref[side, pair] = lax.dot_general(values, unnorm_b, TN, preferred_element_type=F32)


def far_kernel(
    pos, own_numbers, other_numbers, enc_ref, acc_ref, a_top, a_low, b_top, b_low, qa_in, qb_in,
    k_ref, v_ref, qa_ref, qb_ref, st_ref, num_ref,
):
    meta = Passages(pos, own_numbers, other_numbers)
    step = pl.program_id(0)
    far = ((a_top, a_low), (b_top, b_low))

    @pl.when(step == 0)
    def questions():
        for side, source, out in ((0, qa_in, qa_ref), (1, qb_in, qb_ref)):
            out[...] = source[...]
            for inner in range(4):
                row = (inner % 2) * PIECE + 512
                at = (8 + inner) * 64
                out[at : at + 64, :] = far[side][inner // 2][row : row + 64, :]

    row0 = pl.multiple_of((step % 2) * (ROWS // 2), ROWS // 2)
    for side in range(2):
        lhs = enc_ref[0, :, side * 1024 : (side + 1) * 1024]
        for t, out in ((0, k_ref), (1, v_ref)):
            rhs = jnp.concatenate(
                [
                    far[side][inner // 2][(inner % 2) * PIECE + t * 256 : (inner % 2) * PIECE + t * 256 + 256]
                    for inner in range(4)
                ],
                axis=0,
            )
            at = t * HALF + side * CHUNK
            total = acc_ref[0, :, at : at + CHUNK] + jnp.dot(
                lhs, rhs, preferred_element_type=F32
            )
            out[step // 2, pl.ds(row0, ROWS // 2), side * CHUNK : (side + 1) * CHUNK] = total.astype(BF)
    for side in range(2):
        @pl.when(step == side * 2 + 1)
        def attend():
            forward_side(side, meta, k_ref, v_ref, (qa_ref, qb_ref), st_ref, num_ref)


def project_far(meta, enc_far, acc, blocks, qa, qb):
    tile = ROWS // 2

    def whole(shape):
        return pl.BlockSpec(shape, lambda i, *m: (0,) * len(shape))

    shapes = [
        jax.ShapeDtypeStruct((2, ROWS, HALF), BF),
        jax.ShapeDtypeStruct((2, ROWS, HALF), BF),
        jax.ShapeDtypeStruct((1024, CHUNK), BF),
        jax.ShapeDtypeStruct((1024, CHUNK), BF),
        jax.ShapeDtypeStruct((32, 128), F32),
        jax.ShapeDtypeStruct((2, PAIRS, 128, 128), F32),
    ]
    return pl.pallas_call(
        far_kernel,
        grid_spec=pltpu.PrefetchScalarGridSpec(
            num_scalar_prefetch=3,
            grid=(4,),
            in_specs=[
                pl.BlockSpec((1, tile, 2048), lambda i, *m: (i // 2, i % 2, 0)),
                pl.BlockSpec((1, tile, 2 * HALF), lambda i, *m: (i // 2, i % 2, 0)),
            ]
            + [whole(b.shape) for b in blocks]
            + [whole((1024, CHUNK))] * 2,
            out_specs=[whole(s.shape) for s in shapes],
        ),
        out_shape=shapes,
        compiler_params=params(24),
        cost_estimate=HIDDEN,
    )(*meta, enc_far, acc, *blocks, qa, qb)


def combine(st_ref):
    n = st_ref.shape[0]
    own_question = [st_ref[0, 24 + s * PAIRS : 25 + s * PAIRS, :] for s in range(2)]

    def turned(value, k):
        return pltpu.roll(value, 32 * k, 1) if k else value

    tops = [None, None]
    for d in range(n):
        for k in range(NPASS):
            q, m = turned(st_ref[d, 24:32], k), turned(st_ref[d, 0:8], k)
            for s in range(2):
                term = jnp.where(q == own_question[s], m, LOW)
                tops[s] = term if tops[s] is None else jnp.maximum(tops[s], term)
    tops = [jnp.maximum(t[0:PAIRS], t[PAIRS:]) for t in tops]
    both = [jnp.concatenate([t, t], axis=0) for t in tops]
    totals, deltas = [0.0, 0.0], [0.0, 0.0]
    for d in range(n):
        for k in range(NPASS):
            q, m = turned(st_ref[d, 24:32], k), turned(st_ref[d, 0:8], k)
            l, e = turned(st_ref[d, 8:16], k), turned(st_ref[d, 16:24], k)
            for s in range(2):
                hit = q == own_question[s]
                scale = jnp.where(hit, jnp.exp(jnp.where(hit, m - both[s], 0.0)), 0.0)
                totals[s] = totals[s] + scale * l
                deltas[s] = deltas[s] + scale * e
    inverse = [1.0 / (t[0:PAIRS] + t[PAIRS:]) for t in totals]
    deltas = [(t[0:PAIRS] + t[PAIRS:]) * i for t, i in zip(deltas, inverse)]
    return tops, inverse, deltas


def weight_copy(ref, row, w_ref, sems, side, n):
    return pltpu.make_async_copy(
        ref.at[pl.ds(row, 2 * CHUNK)], w_ref.at[side, n], sems.at[side, n]
    )


def wait_copies(sources, w_ref, sems):
    for side in range(2):
        for n in range(4):
            weight_copy(sources[2], 0, w_ref, sems, side, n).wait()


def start_copies(place, sources, w_ref, sems):
    a_own, a_up, a_top, a_low, a_down, b_own, b_up, b_top, b_low, b_down = sources

    def copy(ref, row, side, n):
        return weight_copy(ref, row, w_ref, sems, side, n)

    for outer in range(4):
        @pl.when(place == outer)
        def start_a():
            for n in range(4):
                half = {
                    0: a_own.at[n // 2],
                    1: a_up.at[n // 2],
                    2: (a_top, a_low)[n // 2],
                    3: a_down.at[n // 2],
                }[outer]
                copy(half, (n % 2) * PIECE, 0, n).start()

    upper = place // 2
    row = pl.multiple_of((place % 2) * PIECE, 64)
    for n, ref in ((0, b_own), (1, b_up), (3, b_down)):
        copy(ref.at[upper], row, 1, n).start()
    for h, ref in ((0, b_top), (1, b_low)):
        pl.when(upper == h)(copy(ref, row, 1, 2).start)


def weights_tile(w_ref):
    rows = [
        jnp.concatenate(
            [w_ref[side, n, t * CHUNK : (t + 1) * CHUNK] for t in range(2) for side in range(2)],
            axis=1,
        )
        for n in range(4)
    ]
    return jnp.concatenate(rows, axis=0)


WEIGHT_SPECS = [pl.BlockSpec(memory_space=pltpu.HBM)] * 10


def weight_scratch(count):
    return [
        pltpu.VMEM((count, 2, 4, 2 * CHUNK, CHUNK), BF),
        pltpu.SemaphoreType.DMA((count, 2, 4)),
    ]


def backward_kernel(
    pos, own_numbers, other_numbers, k_ref, v_ref, qa_ref, qb_ref, st_ref, num_ref, *refs
):
    sources, outs = refs[:10], refs[10:]
    kvg_ref, own_ref, oth_ref, c0_ref, c1_ref, c2_ref, c3_ref, ctx_ref, w_ref, sems = outs
    w_ref = w_ref.at[0]
    sems = sems.at[0]
    start_copies(pos[2], sources, w_ref, sems)
    meta = Passages(pos, own_numbers, other_numbers)
    qg = (qa_ref, qb_ref)
    tops, inverses, deltas = combine(st_ref)
    ctx_ref[...] = jnp.zeros_like(ctx_ref)
    low = lax.broadcasted_iota(jnp.int32, (DEC, 128), 1) < 64
    for side in (1, 0):
        inside = inside_mask(meta, side)
        for pair in range(PAIRS):
            cols = slice(pair * 128, (pair + 1) * 128)
            at = side * PAIRS + pair
            top, inverse = tops[side][pair : pair + 1], inverses[side][pair : pair + 1]
            queries = pair_matrix(meta, qg, side, pair, 0)
            grads = pair_matrix(meta, qg, side, pair, 1)
            scores = dot_nt(k_ref[side, :, cols], queries)
            unnorm = jnp.where(inside, jnp.exp(jnp.where(inside, scores - top, 0.0)), 0.0)
            probs = unnorm * inverse
            dprob = dot_nt(v_ref[side, :, cols], grads)
            ds = (probs * (dprob - deltas[side][pair : pair + 1])).astype(BF)
            for t, lanes, weight in ((0, queries, ds), (1, grads, probs.astype(BF))):
                turned = lax.dot_general(
                    lanes, weight, (((0,), (1,)), ((), ())), preferred_element_type=F32
                ).astype(BF)
                for n in range(2):
                    kvg_ref[
                        side * 2 + n, t * HALF + pair * 128 : t * HALF + (pair + 1) * 128, :
                    ] = turned[:, n * 256 : (n + 1) * 256]
            scale = jnp.exp(st_ref[0, at : at + 1, :] - top) * inverse
            context = (num_ref[side, pair] * scale).T
            for p in range(NPASS):
                zo, xo, core = meta.chip(side, p)
                ctx_ref[(zo * 4 + xo) * 2 + core, :, cols] += jnp.where(
                    low, context[p * 32 : p * 32 + 16], context[p * 32 + 16 : p * 32 + 32]
                )
        if side == 1:
            wait_copies(sources, w_ref, sems)
        out = (own_ref, oth_ref)[side]
        for n in range(2):
            out[n] = jnp.dot(
                weights_tile(w_ref), kvg_ref[side * 2 + n], preferred_element_type=F32
            ).astype(BF)
    for o, out in enumerate((c0_ref, c1_ref, c2_ref, c3_ref)):
        out[...] = ctx_ref[o * 8 : o * 8 + 8].astype(out.dtype)


def backward(meta, args, weights):
    def whole(shape):
        return pl.BlockSpec(shape, lambda i, *m: (0,) * len(shape))

    shapes = [
        jax.ShapeDtypeStruct((4, 2 * HALF, ROWS // 2), BF),
        jax.ShapeDtypeStruct((2, 1024, ROWS // 2), BF),
        jax.ShapeDtypeStruct((2, 1024, ROWS // 2), BF),
        jax.ShapeDtypeStruct((8, DEC, HALF), F32),
    ] + [jax.ShapeDtypeStruct((8, DEC, HALF), BF)] * 3
    return pl.pallas_call(
        backward_kernel,
        grid_spec=pltpu.PrefetchScalarGridSpec(
            num_scalar_prefetch=3,
            grid=(1,),
            in_specs=[whole(a.shape) for a in args]
            + WEIGHT_SPECS,
            out_specs=[whole(s.shape) for s in shapes],
            scratch_shapes=[pltpu.VMEM((32, DEC, HALF), F32)] + weight_scratch(1),
        ),
        out_shape=shapes,
        compiler_params=params(24),
        cost_estimate=HIDDEN,
    )(*meta, *args, *weights)


def grad_kernel(count, places, kvg_ref, *refs):
    sources, (own_ref, oth_ref, w_ref, sems) = refs[:10], refs[10:]
    step = pl.program_id(0)
    for k in range(count):
        @pl.when(step == 4 * k)
        def load():
            first = range(count) if k == 0 else ()
            for n in first:
                start_copies(places[n], sources, w_ref.at[n], sems.at[n])
            wait_copies(sources, w_ref.at[k], sems.at[k])

    total = jnp.dot(weights_tile(w_ref.at[step // 4]), kvg_ref[0], preferred_element_type=F32)

    @pl.when(step % 4 < 2)
    def other():
        oth_ref[0, 0] = total.astype(oth_ref.dtype)

    @pl.when(step % 4 >= 2)
    def own():
        own_ref[0, 0] = total.astype(own_ref.dtype)


def grad_blocks(places, kvg, weights, dtype):
    tile = ROWS // 2
    count = places.shape[0]
    return pl.pallas_call(
        functools.partial(grad_kernel, count),
        grid_spec=pltpu.PrefetchScalarGridSpec(
            num_scalar_prefetch=1,
            grid=(4 * count,),
            in_specs=[pl.BlockSpec((1, 2 * HALF, tile), lambda i, p: ((i + 2) % 4, 0, 0))]
            + WEIGHT_SPECS,
            out_specs=[
                pl.BlockSpec(
                    (1, 1, 1024, tile), lambda i, p: (i // 4, jnp.maximum(i % 4 - 2, 0), 0, 0)
                ),
                pl.BlockSpec((1, 1, 1024, tile), lambda i, p: (i // 4, jnp.minimum(i % 4, 1), 0, 0)),
            ],
            scratch_shapes=weight_scratch(count),
        ),
        out_shape=[
            jax.ShapeDtypeStruct((count, 2, 1024, tile), dtype),
            jax.ShapeDtypeStruct((count, 2, 1024, tile), BF),
        ],
        compiler_params=params(20),
        cost_estimate=HIDDEN,
    )(places, kvg, *weights)


def finish_kernel(place, base_ref, core_ref, up_top, up_low, down_top, down_low, out_ref):
    step = pl.program_id(0)
    total = base_ref[...] + core_ref[...].astype(F32)

    def write(up, down):
        whole = total + up[...].astype(F32) + down[...].astype(F32)
        for n in range(2):
            out_ref[n * 256 : (n + 1) * 256, :] = whole[n].T

    pl.when(step < 2)(lambda: write(up_top, down_top))
    pl.when(step >= 2)(lambda: write(up_low, down_low))


def finish(place, base, core_part, parts):
    shape = (2, CHUNK, ROWS // 2)
    block = pl.BlockSpec(shape, lambda n, p: (0, n, 0))
    top = pl.BlockSpec(shape, lambda n, p: (0, jnp.minimum(n, 1), 0))
    low = pl.BlockSpec(shape, lambda n, p: (0, jnp.maximum(n - 2, 0), 0))
    return pl.pallas_call(
        finish_kernel,
        grid_spec=pltpu.PrefetchScalarGridSpec(
            num_scalar_prefetch=1,
            grid=(4,),
            in_specs=[block, block, top, low, top, low],
            out_specs=pl.BlockSpec((ROWS, CHUNK), lambda n, p: (0, p[n])),
        ),
        out_shape=jax.ShapeDtypeStruct((ROWS, 4 * CHUNK), F32),
        compiler_params=params(16),
        cost_estimate=HIDDEN,
    )(place, base, core_part, *parts)


def body(enc_rows, key_weight, value_weight, queries, ctx_grad, passage_len, passage_question):
    z, x, core, y = (lax.axis_index(a) for a in ("z", "x", "core", "dec"))
    four = jnp.arange(4, dtype=jnp.int32)
    zs, xs = (z + four) % 4, (x + four) % 4
    places = ((y + four - z) % 4).astype(jnp.int32)
    near_places, base_place = places[1::2], places[0:1]
    pos = jnp.stack([z, x, places[2]]).astype(jnp.int32)

    cat = jnp.concatenate([key_weight, value_weight, queries[0], ctx_grad[0]], axis=0)
    mine = lax.dynamic_slice_in_dim(cat, core * HALF, HALF, 1)
    theirs = lax.dynamic_slice_in_dim(cat, (1 - core) * HALF, HALF, 1)
    got = perm(theirs, "core", 1)
    numbers = jnp.concatenate([passage_len[0], passage_question[:, 0]])
    other_numbers = perm(numbers, "core", 1)
    enc_other = perm(enc_rows, "core", 1)
    first = jnp.where(core == 0, mine, got)
    second = jnp.where(core == 0, got, mine)
    chip = jnp.concatenate(
        [v[a:b] for a, b in ((0, 128), (128, 256), (256, 272), (272, 288)) for v in (first, second)],
        axis=0,
    )
    a_chip, b_chip, enc_other, other_numbers, pos, near_places, base_place, xs = phase(
        chip[:, :CHUNK],
        chip[:, CHUNK:],
        enc_other,
        other_numbers,
        pos,
        near_places,
        base_place,
        xs.astype(jnp.int32),
    )

    ax_up, ax_down = perm(a_chip, "x", -1), perm(a_chip, "x", 1)
    bz_up, bz_down = perm(b_chip, "z", -1), perm(b_chip, "z", 1)
    ax_up, ax_down, bz_up, bz_down = phase(ax_up, ax_down, bz_up, bz_down)
    mid = PIECE // 2
    far = phase(
        perm(ax_up[:mid], "x", -1),
        perm(ax_down[mid:], "x", 1),
        perm(bz_up[:mid], "z", -1),
        perm(bz_down[mid:], "z", 1),
    )
    a_first = [a_chip, ax_up, far[0], far[1], ax_down]
    b_first = [b_chip, bz_up, far[2], far[3], bz_down]
    a_own, b_own = phase(*first_blocks(a_first + b_first))

    a_up, a_down = perm(a_own, "z", -1), perm(a_own, "z", 1)
    b_up, b_down = perm(b_own, "x", -1), perm(b_own, "x", 1)
    a_own, b_own, a_up, a_down, b_up, b_down = phase(a_own, b_own, a_up, a_down, b_up, b_down)
    give = phase(*take_halves(a_up, a_down, b_up, b_down))
    far = [perm(v, a, t) for v, a, t in zip(give, ("z", "z", "x", "x"), (-1, 1, -1, 1))]
    acc, enc_far, qa, qb = project_near(
        pos, enc_rows, enc_other, [a_own, a_up, a_down, b_own, b_up, b_down]
    )
    far, acc, enc_far, qa, qb = phase(far, acc, enc_far, qa, qb)
    meta = (pos, numbers, other_numbers)
    keys, values, qa, qb, stats, numer = project_far(meta, enc_far, acc, far, qa, qb)
    stats_x = jnp.stack(phase(*gather4(stats, "x")))
    stats_all = jnp.concatenate(gather4(stats_x, "z"), axis=0)
    weights = [a_own, a_up, far[0], far[1], a_down, b_own, b_up, far[2], far[3], b_down]
    kvg, far_own, far_other, *dense = backward(
        meta, (keys, values, qa, qb, stats_all, numer), weights
    )

    def add(*values):
        return sum(v.astype(F32) for v in values).astype(BF)

    kvg, far_other, dense = phase(kvg, far_other, dense)
    far_got = perm(far_other, "core", 1)
    by_z = [dense[0]] + [perm(dense[o], "z", o) for o in (1, 2, 3)]
    near_own, near_other = grad_blocks(near_places, kvg, weights, BF)
    far_got, by_z, kvg, near_own, near_other = phase(far_got, by_z, kvg, near_own, near_other)

    from_below = perm(add(far_own[:, :512], far_got[:, :512]), "dec", 1)
    from_above = perm(add(far_own[:, 512:], far_got[:, 512:]), "dec", -1)
    near_got = perm(near_other, "core", 1)
    base, base_other = grad_blocks(base_place, kvg, weights, F32)
    base, base_other = base[0], base_other[0]
    by_z = sum(v.astype(F32) for v in by_z).reshape(4, 2, DEC, HALF)
    from_below, from_above, near_got, base, base_other, by_z = phase(
        from_below, from_above, near_got, base, base_other, by_z
    )

    low_below = perm(add(near_own[0, :, 512:], near_got[0, :, 512:]), "dec", 1)
    top_above = perm(add(near_own[1, :, :512], near_got[1, :, :512]), "dec", -1)
    up_top = add(near_own[0, :, :512], near_got[0, :, :512], from_below)
    down_low = add(near_own[1, :, 512:], near_got[1, :, 512:], from_above)
    by_x = [by_z[0]] + [perm(by_z[o], "x", o) for o in (1, 2, 3)]
    base_got = perm(base_other, "core", 1)
    low_below, top_above, up_top, down_low, base_got, by_x = phase(
        low_below, top_above, up_top, down_low, base_got, by_x
    )

    top_below = perm(up_top, "dec", 1)
    low_above = perm(down_low, "dec", -1)
    by_x = sum(by_x)
    keep = lax.dynamic_index_in_dim(by_x, core, 0, keepdims=False)
    give = lax.dynamic_index_in_dim(by_x, 1 - core, 0, keepdims=False)
    come = perm(give, "core", 1)
    ctx = jnp.where(
        core == 0,
        jnp.concatenate([keep, come], axis=1),
        jnp.concatenate([come, keep], axis=1),
    )[None]
    enc_grad = finish(xs, base, base_got, (top_below, low_below, top_above, low_above))
    return ctx, enc_grad


def solution(mesh):
    grid = Mesh(mesh.devices.reshape(NZ, NX, NC, NY), ("z", "x", "core", "dec"))
    return jax.shard_map(
        body,
        mesh=grid,
        in_specs=(
            P(ENC, None),
            P(ENC, "dec"),
            P(ENC, "dec"),
            P(ENC, None, "dec"),
            P(ENC, None, "dec"),
            P(ENC, None),
            P(ENC, None),
        ),
        out_specs=(P(ENC, None, "dec"), P(ENC, "dec")),
        check_vma=False,
    )
```

time: 612 us -> 179 us (0.29)
  blocking collectives: 249 us -> 0 us
  waiting for transfers between devices: 265 us -> 72.4 us
  starting transfers between devices: 0.23 us -> 56 us
  matrix products: 51.9 us -> 0 us
  Pallas kernels: 0 us -> 39.1 us
  local copies, waits for them, and re-layouts: 24.3 us -> 4.63 us
  between operations: 14.3 us -> 0.97 us
    all_gather x4 -> x0, waiting for transfers between devices: 183 us -> none  [the longest x1 51.8 us: body(): lax.all_gather(value_weight, 'enc', axis=0, tiled=True)]
    psum x1 -> x0, blocking collectives: 125 us -> none  [body(): numer_all, denom_all = lax.psum((numer, denom), 'enc')]
    pmax x1 -> x0, blocking collectives: 124 us -> none  [body(): global_max = lax.pmax(local_max, 'enc')]
    reduce_scatter x1 -> x0, waiting for transfers between devices: 79.6 us -> none  [body(): lax.psum_scatter(partial_grad, 'dec', scatter_dimension=1, tiled=True)]
    ppermute x0 -> x41, waiting for transfers between devices: none -> 72.4 us  [perm(): return lax.ppermute(v, axis, [(i, (i + shift) % n) for i in range(n)])]
    ppermute x0 -> x41, starting transfers between devices: none -> 56 us  [perm(): return lax.ppermute(v, axis, [(i, (i + shift) % n) for i in range(n)])]
    dot_general x9 -> x0, matrix products: 47.5 us -> none  [the longest x1 10.4 us: body(): jnp.einsum('sc,rc->sr', key_grad_b, pieces[0], preferred_element_type=jnp...]
    pallas_call x0 -> x8, Pallas kernels: none -> 39.1 us  [the longest x2 11.6 us: grad_blocks(): pl.pallas_call(functools.partial(grad_kernel, count), grid_spec=pltpu.Pre...]
  transfers between devices with their start and end apart: 6 -> 41, of which waited for: 5 -> 20; matrix products, arithmetic and copies ran while one was open for 5% -> 4% of each run, Pallas kernels for 0% -> 12%
where the time goes in v2:
time: 179 us
  waiting for transfers between devices  72.4 us (40%)
  starting transfers between devices  56 us (31%)
  Pallas kernels  39.1 us (22%)
  other arithmetic  5.45 us (3%)
  local copies, waits for them, and re-layouts  4.63 us (3%)
    ppermute x41, waiting for transfers between devices, perm(): return lax.ppermute(v, axis, [(i, (i + shift) % n) for i in range(n)])  72.4 us
    ppermute x41, starting transfers between devices, perm(): return lax.ppermute(v, axis, [(i, (i + shift) % n) for i in range(n)])  56 us
    pallas_call x2, Pallas kernels, grad_blocks(): pl.pallas_call(functools.partial(grad_kernel, count), grid_spec=pltpu.Pre...  11.6 us
    pallas_call x1, Pallas kernels, project_near(): pl.pallas_call(near_kernel, grid_spec=pltpu.PrefetchScalarGridSpec(num_sc...  9.73 us
    pallas_call x1, Pallas kernels, project_far(): pl.pallas_call(far_kernel, grid_spec=pltpu.PrefetchScalarGridSpec(num_sca...  6.41 us
    pallas_call x1, Pallas kernels, backward(): pl.pallas_call(backward_kernel, grid_spec=pltpu.PrefetchScalarGridSpec(nu...  6.29 us
    pallas_call x1, Pallas kernels, finish(): pl.pallas_call(finish_kernel, grid_spec=pltpu.PrefetchScalarGridSpec(num_...  4.82 us
    unnamed x23, local copies, waits for them, and re-layouts  3.77 us
  transfers between devices with their start and end apart: 41, of which 20 were waited for; matrix products, arithmetic and copies ran while one was open for 4% of the time, Pallas kernels for 12%

profile of v2, /device:TPU:1, one launch (start us, length us, event | category | flops | bytes accessed | tf_op | source)
XLA Modules:
  0.0 178.6 jit_solution(8912967670441519812)
XLA Ops:
  0.6 1.5 collective-permute-start.1
  2.1 1.1 pad_maximum_fusion
  6.0 3.3 %collective-permute-done = bf16[288,512]{1,0:T(8,128)(2,1)S(1)} collective-permute-done((bf16[288,512]{1,0:T(8,128)(2,1)S(1)}, bf16[288,512]{1,0:T(8,128)(2,1)S(1)}, u32[]{:S(2)}, u32[]{:S(2)}) %collective-permute-start) | collective-permute-done | bytes 294944 | tf_op jit(solution)/shard_map/ppermute | solution.py:30
  9.7 2.6 %collective-permute-start.3 = (bf16[576,256]{1,0:T(8,128)(2,1)S(1)}, bf16[576,256]{1,0:T(8,128)(2,1)S(1)}, u32[]{:S(2)}, u32[]{:S(2)}) collective-permute-start(bf16[576,256]{1,0:T(8,128)(2,1)S(1)} %get-tuple-element.94.refs_0_), channel_id=1, source_target_pairs={{0,24},{8,0},{16,8},{24,16},{1,25},{9,1},{17,9},{25,17},{2,26},{10... | collective-permute-start | bytes 884744 | tf_op jit(solution)/shard_map/ppermute | solution.py:30
  12.3 3.8 %collective-permute-start.5 = (bf16[576,256]{1,0:T(8,128)(2,1)S(1)}, bf16[576,256]{1,0:T(8,128)(2,1)S(1)}, u32[]{:S(2)}, u32[]{:S(2)}) collective-permute-start(bf16[576,256]{1,0:T(8,128)(2,1)S(1)} %get-tuple-element.95.refs_5_), channel_id=1, source_target_pairs={{0,96},{32,0},{64,32},{96,64},{1,97},{33,1},{65,33},{97,65},{2,98}... | collective-permute-start | bytes 884744 | tf_op jit(solution)/shard_map/ppermute | solution.py:30
  16.1 2.3 %collective-permute-done.3.refs_1_ = bf16[576,256]{1,0:T(8,128)(2,1)S(1)} collective-permute-done((bf16[576,256]{1,0:T(8,128)(2,1)S(1)}, bf16[576,256]{1,0:T(8,128)(2,1)S(1)}, u32[]{:S(2)}, u32[]{:S(2)}) %collective-permute-start.3) | collective-permute-done | bytes 294944 | tf_op jit(solution)/shard_map/ppermute | solution.py:30
  18.3 3.1 %collective-permute-done.4.refs_4_ = bf16[576,256]{1,0:T(8,128)(2,1)S(1)} collective-permute-done((bf16[576,256]{1,0:T(8,128)(2,1)S(1)}, bf16[576,256]{1,0:T(8,128)(2,1)S(1)}, u32[]{:S(2)}, u32[]{:S(2)}) %collective-permute-start.4) | collective-permute-done | bytes 294944 | tf_op jit(solution)/shard_map/ppermute | solution.py:30
  21.8 3.1 %collective-permute-done.6.refs_9_ = bf16[576,256]{1,0:T(8,128)(2,1)S(1)} collective-permute-done((bf16[576,256]{1,0:T(8,128)(2,1)S(1)}, bf16[576,256]{1,0:T(8,128)(2,1)S(1)}, u32[]{:S(2)}, u32[]{:S(2)}) %collective-permute-start.6) | collective-permute-done | bytes 294944 | tf_op jit(solution)/shard_map/ppermute | solution.py:30
  25.0 2.5 %collective-permute-start.7 = (bf16[288,256]{1,0:T(8,128)(2,1)S(1)}, bf16[288,256]{1,0:T(8,128)(2,1)S(1)}, u32[]{:S(2)}, u32[]{:S(2)}) collective-permute-start(bf16[288,256]{1,0:T(8,128)(2,1)S(1)} %slice.112), channel_id=1, source_target_pairs={{0,24},{8,0},{16,8},{24,16},{1,25},{9,1},{17,9},{25,17},{2,26},{10... | collective-permute-start | bytes 442376 | tf_op jit(solution)/shard_map/ppermute | solution.py:30
  27.6 2.7 %collective-permute-start.9 = (bf16[288,256]{1,0:T(8,128)(2,1)S(1)}, bf16[288,256]{1,0:T(8,128)(2,1)S(1)}, u32[]{:S(2)}, u32[]{:S(2)}) collective-permute-start(bf16[288,256]{1,0:T(8,128)(2,1)S(1)} %slice.114), channel_id=1, source_target_pairs={{0,96},{32,0},{64,32},{96,64},{1,97},{33,1},{65,33},{97,65},{2,98}... | collective-permute-start | bytes 442376 | tf_op jit(solution)/shard_map/ppermute | solution.py:30
  30.3 2.5 %collective-permute-done.8.refs_3_ = bf16[288,256]{1,0:T(8,128)(2,1)S(1)} collective-permute-done((bf16[288,256]{1,0:T(8,128)(2,1)S(1)}, bf16[288,256]{1,0:T(8,128)(2,1)S(1)}, u32[]{:S(2)}, u32[]{:S(2)}) %collective-permute-start.8) | collective-permute-done | bytes 147488 | tf_op jit(solution)/shard_map/ppermute | solution.py:30
  32.9 2.8 %collective-permute-start.11 = (bf16[2,1152,256]{2,1,0:T(8,128)(2,1)S(1)}, bf16[2,1152,256]{2,1,0:T(8,128)(2,1)S(1)}, u32[]{:S(2)}, u32[]{:S(2)}) collective-permute-start(bf16[2,1152,256]{2,1,0:T(8,128)(2,1)S(1)} %get-tuple-element.115.refs_0_), channel_id=1, source_target_pairs={{0,96},{32,0},{64,32},{96,64},{1,97},{33,1},{65,33},{97,65},{2,98}... | collective-permute-start | bytes 3538952 | tf_op jit(solution)/shard_map/ppermute | solution.py:30
  35.7 3.0 %collective-permute-start.13 = (bf16[2,1152,256]{2,1,0:T(8,128)(2,1)S(1)}, bf16[2,1152,256]{2,1,0:T(8,128)(2,1)S(1)}, u32[]{:S(2)}, u32[]{:S(2)}) collective-permute-start(bf16[2,1152,256]{2,1,0:T(8,128)(2,1)S(1)} %get-tuple-element.116.refs_3_.refs_5_), channel_id=1, source_target_pairs={{0,24},{8,0},{16,8},{24,16},{1,25},{9,1},{17,9},{25,17},{2,26},{10... | collective-permute-start | bytes 3538952 | tf_op jit(solution)/shard_map/ppermute | solution.py:30
  38.7 18.5 %collective-permute-done.11.a_ref.refs_1_ = bf16[2,1152,256]{2,1,0:T(8,128)(2,1)S(1)} collective-permute-done((bf16[2,1152,256]{2,1,0:T(8,128)(2,1)S(1)}, bf16[2,1152,256]{2,1,0:T(8,128)(2,1)S(1)}, u32[]{:S(2)}, u32[]{:S(2)}) %collective-permute-start.11) | collective-permute-done | bytes 1179680 | tf_op jit(solution)/shard_map/ppermute | solution.py:30
  57.1 3.1 %collective-permute-done.12.b_ref.refs_2_.refs_4_ = bf16[2,1152,256]{2,1,0:T(8,128)(2,1)S(1)} collective-permute-done((bf16[2,1152,256]{2,1,0:T(8,128)(2,1)S(1)}, bf16[2,1152,256]{2,1,0:T(8,128)(2,1)S(1)}, u32[]{:S(2)}, u32[]{:S(2)}) %collective-permute-start.12) | collective-permute-done | bytes 1179680 | tf_op jit(solution)/shard_map/ppermute | solution.py:30
  60.3 2.7 %collective-permute-done.14.d_ref.refs_5_.refs_9_ = bf16[2,1152,256]{2,1,0:T(8,128)(2,1)S(1)} collective-permute-done((bf16[2,1152,256]{2,1,0:T(8,128)(2,1)S(1)}, bf16[2,1152,256]{2,1,0:T(8,128)(2,1)S(1)}, u32[]{:S(2)}, u32[]{:S(2)}) %collective-permute-start.14) | collective-permute-done | bytes 1179680 | tf_op jit(solution)/shard_map/ppermute | solution.py:30
  63.1 2.5 %collective-permute-start.15 = (bf16[1152,256]{1,0:T(8,128)(2,1)S(1)}, bf16[1152,256]{1,0:T(8,128)(2,1)S(1)}, u32[]{:S(2)}, u32[]{:S(2)}) collective-permute-start(bf16[1152,256]{1,0:T(8,128)(2,1)S(1)} %get-tuple-element.110), channel_id=1, source_target_pairs={{0,96},{32,0},{64,32},{96,64},{1,97},{33,1},{65,33},{97,65},{2,98}... | collective-permute-start | bytes 1769480 | tf_op jit(solution)/shard_map/ppermute | solution.py:30
  65.9 1.2 collective-permute-start.18
  67.0 9.7 %shard_map.88 = (f32[2,512,1024]{2,1,0:T(8,128)S(1)}, bf16[2,512,2048]{2,1,0:T(8,128)(2,1)S(1)}, bf16[1024,256]{1,0:T(8,128)(2,1)S(1)}, bf16[1024,256]{1,0:T(8,128)(2,1)S(1)}) custom-call(s32[3]{0:T(128)S(1)} %pad_add_fusion.1.pos, bf16[512,4096]{1,0:T(8,128)(2,1)S(1)} %copy-done, bf16[512,4096]{1,0:T(8,128)(2,1)} %collective-permute-done.1.oth_ref, ...), custom_call_target="tpu_custom_call" | custom-call | tf_op jit(solution)/shard_map/pallas_call | solution.py:134
  76.8 6.4 %shard_map.89 = (bf16[2,512,512]{2,1,0:T(8,128)(2,1)S(1)}, bf16[2,512,512]{2,1,0:T(8,128)(2,1)S(1)}, bf16[1024,256]{1,0:T(8,128)(2,1)S(1)}, bf16[1024,256]{1,0:T...) custom-call(s32[3]{0:T(128)S(1)} %pad_add_fusion.1.pos, s32[8]{0:T(128)S(1)} %pad_add_fusion.own_numbers, ...), custom_call_target="tpu_custom_call" | custom-call | tf_op jit(solution)/shard_map/pallas_call | solution.py:291
  83.2 1.6 collective-permute-start.19
  85.9 3.2 %collective-permute-done.20 = f32[32,128]{1,0:T(8,128)S(1)} collective-permute-done((f32[32,128]{1,0:T(8,128)S(1)}, f32[32,128]{1,0:T(8,128)S(1)}, u32[]{:S(2)}, u32[]{:S(2)}) %collective-permute-start.20) | collective-permute-done | bytes 16416 | tf_op jit(solution)/shard_map/ppermute | solution.py:30
  89.1 2.7 %collective-permute-start.22 = (f32[4,32,128]{2,1,0:T(8,128)S(1)}, f32[4,32,128]{2,1,0:T(8,128)S(1)}, u32[]{:S(2)}, u32[]{:S(2)}) collective-permute-start(f32[4,32,128]{2,1,0:T(8,128)S(1)} %pad_maximum_fusion.1), channel_id=1, source_target_pairs={{0,96},{32,0},{64,32},{96,64},{1,97},{33,1},{65,33},{97,65},{2,98}... | collective-permute-start | bytes 196616 | tf_op jit(solution)/shard_map/ppermute | solution.py:30
  92.5 1.2 collective-permute-done.22
  93.8 2.8 %collective-permute-done.23 = f32[4,32,128]{2,1,0:T(8,128)S(1)} collective-permute-done((f32[4,32,128]{2,1,0:T(8,128)S(1)}, f32[4,32,128]{2,1,0:T(8,128)S(1)}, u32[]{:S(2)}, u32[]{:S(2)}) %collective-permute-start.23) | collective-permute-done | bytes 65568 | tf_op jit(solution)/shard_map/ppermute | solution.py:30
  96.9 6.3 %shard_map.90 = (bf16[4,1024,256]{2,1,0:T(8,128)(2,1)S(1)}, bf16[2,1024,256]{2,1,0:T(8,128)(2,1)S(1)}, bf16[2,1024,256]{2,1,0:T(8,128)(2,1)S(1)}, f32[8,16,512]{...) custom-call(s32[3]{0:T(128)S(1)} %pad_add_fusion.1.pos, ...), custom_call_target="tpu_custom_call" | custom-call | tf_op jit(solution)/shard_map/pallas_call | solution.py:462
  103.2 9.5 %collective-permute-start.25 = (bf16[2,1024,256]{2,1,0:T(8,128)(2,1)S(1)}, bf16[2,1024,256]{2,1,0:T(8,128)(2,1)S(1)}, u32[]{:S(2)}, u32[]{:S(2)}) collective-permute-start(bf16[2,1024,256]{2,1,0:T(8,128)(2,1)S(1)} %get-tuple-element.145), channel_id=1, source_target_pairs={{0,4},{4,0},{1,5},{5,1},{2,6},{6,2},{3,7},{7,3},{8,12},{12,8},{9,1... | collective-permute-start | bytes 3145736 | tf_op jit(solution)/shard_map/ppermute | solution.py:30
  112.7 1.8 collective-permute-start.27
  114.5 1.6 collective-permute-start.28
  116.1 7.4 %shard_map.91 = (bf16[2,2,1024,256]{3,2,1,0:T(8,128)(2,1)S(1)}, bf16[2,2,1024,256]{3,2,1,0:T(8,128)(2,1)S(1)}) custom-call(s32[2]{0:T(128)S(1)} %slice.110.places, bf16[4,1024,256]{2,1,0:T(8,128)(2,1)S(1)} %get-tuple-element.159.kvg_ref, bf16[2,1152,256]{2,1,0:T(8,128)(2,1)S(1)} %get-tuple-element.115.refs_0_, ...), custom_call_target="tpu_custom_call" | custom-call | tf_op jit(solution)/shard_map/pallas_call | solution.py:503
  123.6 1.0 collective-permute-start.31
  124.9 1.4 collective-permute-start.29
  126.3 1.5 collective-permute-start.30
  127.8 4.1 %shard_map.92 = (f32[1,2,1024,256]{3,2,1,0:T(8,128)S(1)}, bf16[1,2,1024,256]{3,2,1,0:T(8,128)(2,1)S(1)}) custom-call(s32[1]{0:T(128)} %get-tuple-element.158.places, bf16[4,1024,256]{2,1,0:T(8,128)(2,1)S(1)} %get-tuple-element.159.kvg_ref, bf16[2,1152,256]{2,1,0:T(8,128)(2,1)S(1)} %get-tuple-element.115.refs_0_, ...), custom_call_target="tpu_custom_call" | custom-call | tf_op jit(solution)/shard_map/pallas_call | solution.py:503
  132.0 7.9 %collective-permute-done.29 = bf16[2,512,256]{2,1,0:T(8,128)(2,1)S(1)} collective-permute-done((bf16[2,512,256]{2,1,0:T(8,128)(2,1)S(1)}, bf16[2,512,256]{2,1,0:T(8,128)(2,1)S(1)}, u32[]{:S(2)}, u32[]{:S(2)}) %collective-permute-start.29) | collective-permute-done | bytes 524320 | tf_op jit(solution)/shard_map/ppermute | solution.py:30
  140.9 1.3 collective-permute-start.32
  142.3 1.5 collective-permute-start.33
  143.9 2.2 %collective-permute-start.36 = (f32[2,16,512]{2,1,0:T(8,128)S(1)}, f32[2,16,512]{2,1,0:T(8,128)S(1)}, u32[]{:S(2)}, u32[]{:S(2)}) collective-permute-start(f32[2,16,512]{2,1,0:T(8,128)S(1)} %get-tuple-element.193), channel_id=1, source_target_pairs={{0,16},{8,24},{16,0},{24,8},{1,17},{9,25},{17,1},{25,9},{2,18},{10... | collective-permute-start | bytes 196616 | tf_op jit(solution)/shard_map/ppermute | solution.py:30
  146.1 3.0 %collective-permute-done.35 = f32[2,16,512]{2,1,0:T(8,128)S(1)} collective-permute-done((f32[2,16,512]{2,1,0:T(8,128)S(1)}, f32[2,16,512]{2,1,0:T(8,128)S(1)}, u32[]{:S(2)}, u32[]{:S(2)}) %collective-permute-start.35) | collective-permute-done | bytes 65568 | tf_op jit(solution)/shard_map/ppermute | solution.py:30
  149.1 1.4 fusion
  150.6 2.0 %collective-permute-done.37 = f32[2,16,512]{2,1,0:T(8,128)S(1)} collective-permute-done((f32[2,16,512]{2,1,0:T(8,128)S(1)}, f32[2,16,512]{2,1,0:T(8,128)S(1)}, u32[]{:S(2)}, u32[]{:S(2)}) %collective-permute-start.37) | collective-permute-done | bytes 65568 | tf_op jit(solution)/shard_map/ppermute | solution.py:30
  152.5 3.3 %collective-permute-done.32.up_low = bf16[2,512,256]{2,1,0:T(8,128)(2,1)S(1)} collective-permute-done((bf16[2,512,256]{2,1,0:T(8,128)(2,1)S(1)}, bf16[2,512,256]{2,1,0:T(8,128)(2,1)S(1)}, u32[]{:S(2)}, u32[]{:S(2)}) %collective-permute-start.32) | collective-permute-done | bytes 524320 | tf_op jit(solution)/shard_map/ppermute | solution.py:30
  157.5 2.7 %collective-permute-start.40 = (bf16[2,512,256]{2,1,0:T(8,128)(2,1)}, bf16[2,512,256]{2,1,0:T(8,128)(2,1)}, u32[]{:S(2)}, u32[]{:S(2)}) collective-permute-start(bf16[2,512,256]{2,1,0:T(8,128)(2,1)} %get-tuple-element.181), channel_id=1, source_target_pairs={{0,3},{1,0},{2,1},{3,2},{4,7},{5,4},{6,5},{7,6},{8,11},{9,8},{10,9... | collective-permute-start | bytes 1572872 | tf_op jit(solution)/shard_map/ppermute | solution.py:30
  160.2 1.4 collective-permute-start.38
  163.1 8.7 %collective-permute-done.39.up_top = bf16[2,512,256]{2,1,0:T(8,128)(2,1)} collective-permute-done((bf16[2,512,256]{2,1,0:T(8,128)(2,1)}, bf16[2,512,256]{2,1,0:T(8,128)(2,1)}, u32[]{:S(2)}, u32[]{:S(2)}) %collective-permute-start.39) | collective-permute-done | bytes 524320 | tf_op jit(solution)/shard_map/ppermute | solution.py:30
  171.7 1.0 copy-done.2
  172.8 1.0 copy-done.4
  173.8 4.8 %shard_map.93 = f32[512,1024]{1,0:T(8,128)} custom-call(s32[4]{0:T(128)S(1)} %get-tuple-element.175.place, f32[2,1024,256]{2,1,0:T(8,128)S(1)} %bitcast.40, bf16[2,1024,256]{2,1,0:T(8,128)(2,1)S(1)} %collective-permute-done.34.core_ref, bf16[2,512,256]{2,1,0:T(8,128)(2,1)} %collective-permute-done.39.up_top, bf16[2,512,256]{2,1,0:T(8,128)(2,1)S(1)} %copy-done.2, ...), custom_call_target="tpu_custom_call" | custom-call | tf_op jit(solution)/shard_map/pallas_call | solution.py:545
  (89 shorter events, 10.9 us)
Async XLA Ops:
  0.6 9.0 %collective-permute-start.1 = (bf16[512,4096]{1,0:T(8,128)(2,1)}, bf16[512,4096]{1,0:T(8,128)(2,1)}, u32[]{:S(2)}, u32[]{:S(2)}) collective-permute-start(bf16[512,4096]{1,0:T(8,128)(2,1)} %own_ref.1), channel_id=1, source_target_pairs={{0,4},{4,0},{1,5},{5,1},{2,6},{6,2},{3,7},{7,3},{8,12},{12,8},{9,1... | collective-permute-start | bytes 12582920 | tf_op jit(solution)/shard_map/ppermute | solution.py:30
  3.3 6.1 %collective-permute-start = (bf16[288,512]{1,0:T(8,128)(2,1)S(1)}, bf16[288,512]{1,0:T(8,128)(2,1)S(1)}, u32[]{:S(2)}, u32[]{:S(2)}) collective-permute-start(bf16[288,512]{1,0:T(8,128)(2,1)S(1)} %constant_dynamic-slice_fusion.1), channel_id=1, source_target_pairs={{0,4},{4,0},{1,5},{5,1},{2,6},{6,2},{3,7},{7,3},{8,12},{12,8},{9,1... | collective-permute-start | bytes 884744 | tf_op jit(solution)/shard_map/ppermute | solution.py:30
  4.1 5.5 %collective-permute-start.2 = (s32[8]{0:T(128)S(1)}, s32[8]{0:T(128)S(1)}, u32[]{:S(2)}, u32[]{:S(2)}) collective-permute-start(s32[8]{0:T(128)S(1)} %pad_add_fusion.own_numbers), channel_id=1, source_target_pairs={{0,4},{4,0},{1,5},{5,1},{2,6},{6,2},{3,7},{7,3},{8,12},{12,8},{9,1... | collective-permute-start | bytes 104 | tf_op jit(solution)/shard_map/ppermute | solution.py:30
  9.7 8.7 %collective-permute-start.3 = (bf16[576,256]{1,0:T(8,128)(2,1)S(1)}, bf16[576,256]{1,0:T(8,128)(2,1)S(1)}, u32[]{:S(2)}, u32[]{:S(2)}) collective-permute-start(bf16[576,256]{1,0:T(8,128)(2,1)S(1)} %get-tuple-element.94.refs_0_), channel_id=1, source_target_pairs={{0,24},{8,0},{16,8},{24,16},{1,25},{9,1},{17,9},{25,17},{2,26},{10... | collective-permute-start | bytes 884744 | tf_op jit(solution)/shard_map/ppermute | solution.py:30
  12.3 9.1 %collective-permute-start.4 = (bf16[576,256]{1,0:T(8,128)(2,1)S(1)}, bf16[576,256]{1,0:T(8,128)(2,1)S(1)}, u32[]{:S(2)}, u32[]{:S(2)}) collective-permute-start(bf16[576,256]{1,0:T(8,128)(2,1)S(1)} %get-tuple-element.94.refs_0_), channel_id=1, source_target_pairs={{0,8},{8,16},{16,24},{24,0},{1,9},{9,17},{17,25},{25,1},{2,10},{10... | collective-permute-start | bytes 884744 | tf_op jit(solution)/shard_map/ppermute | solution.py:30
  12.3 9.5 %collective-permute-start.5 = (bf16[576,256]{1,0:T(8,128)(2,1)S(1)}, bf16[576,256]{1,0:T(8,128)(2,1)S(1)}, u32[]{:S(2)}, u32[]{:S(2)}) collective-permute-start(bf16[576,256]{1,0:T(8,128)(2,1)S(1)} %get-tuple-element.95.refs_5_), channel_id=1, source_target_pairs={{0,96},{32,0},{64,32},{96,64},{1,97},{33,1},{65,33},{97,65},{2,98}... | collective-permute-start | bytes 884744 | tf_op jit(solution)/shard_map/ppermute | solution.py:30
  16.1 8.8 %collective-permute-start.6 = (bf16[576,256]{1,0:T(8,128)(2,1)S(1)}, bf16[576,256]{1,0:T(8,128)(2,1)S(1)}, u32[]{:S(2)}, u32[]{:S(2)}) collective-permute-start(bf16[576,256]{1,0:T(8,128)(2,1)S(1)} %get-tuple-element.95.refs_5_), channel_id=1, source_target_pairs={{0,32},{32,64},{64,96},{96,0},{1,33},{33,65},{65,97},{97,1},{2,34}... | collective-permute-start | bytes 884744 | tf_op jit(solution)/shard_map/ppermute | solution.py:30
  24.9 5.4 %collective-permute-start.10 = (bf16[288,256]{1,0:T(8,128)(2,1)S(1)}, bf16[288,256]{1,0:T(8,128)(2,1)S(1)}, u32[]{:S(2)}, u32[]{:S(2)}) collective-permute-start(bf16[288,256]{1,0:T(8,128)(2,1)S(1)} %slice.115), channel_id=1, source_target_pairs={{0,32},{32,64},{64,96},{96,0},{1,33},{33,65},{65,97},{97,1},{2,34}... | collective-permute-start | bytes 442376 | tf_op jit(solution)/shard_map/ppermute | solution.py:30
  25.0 5.3 %collective-permute-start.7 = (bf16[288,256]{1,0:T(8,128)(2,1)S(1)}, bf16[288,256]{1,0:T(8,128)(2,1)S(1)}, u32[]{:S(2)}, u32[]{:S(2)}) collective-permute-start(bf16[288,256]{1,0:T(8,128)(2,1)S(1)} %slice.112), channel_id=1, source_target_pairs={{0,24},{8,0},{16,8},{24,16},{1,25},{9,1},{17,9},{25,17},{2,26},{10... | collective-permute-start | bytes 442376 | tf_op jit(solution)/shard_map/ppermute | solution.py:30
  27.4 5.3 %collective-permute-start.8 = (bf16[288,256]{1,0:T(8,128)(2,1)S(1)}, bf16[288,256]{1,0:T(8,128)(2,1)S(1)}, u32[]{:S(2)}, u32[]{:S(2)}) collective-permute-start(bf16[288,256]{1,0:T(8,128)(2,1)S(1)} %slice.113), channel_id=1, source_target_pairs={{0,8},{8,16},{16,24},{24,0},{1,9},{9,17},{17,25},{25,1},{2,10},{10... | collective-permute-start | bytes 442376 | tf_op jit(solution)/shard_map/ppermute | solution.py:30
  27.6 5.2 %collective-permute-start.9 = (bf16[288,256]{1,0:T(8,128)(2,1)S(1)}, bf16[288,256]{1,0:T(8,128)(2,1)S(1)}, u32[]{:S(2)}, u32[]{:S(2)}) collective-permute-start(bf16[288,256]{1,0:T(8,128)(2,1)S(1)} %slice.114), channel_id=1, source_target_pairs={{0,96},{32,0},{64,32},{96,64},{1,97},{33,1},{65,33},{97,65},{2,98}... | collective-permute-start | bytes 442376 | tf_op jit(solution)/shard_map/ppermute | solution.py:30
  32.9 24.2 %collective-permute-start.11 = (bf16[2,1152,256]{2,1,0:T(8,128)(2,1)S(1)}, bf16[2,1152,256]{2,1,0:T(8,128)(2,1)S(1)}, u32[]{:S(2)}, u32[]{:S(2)}) collective-permute-start(bf16[2,1152,256]{2,1,0:T(8,128)(2,1)S(1)} %get-tuple-element.115.refs_0_), channel_id=1, source_target_pairs={{0,96},{32,0},{64,32},{96,64},{1,97},{33,1},{65,33},{97,65},{2,98}... | collective-permute-start | bytes 3538952 | tf_op jit(solution)/shard_map/ppermute | solution.py:30
  35.7 24.5 %collective-permute-start.12 = (bf16[2,1152,256]{2,1,0:T(8,128)(2,1)S(1)}, bf16[2,1152,256]{2,1,0:T(8,128)(2,1)S(1)}, u32[]{:S(2)}, u32[]{:S(2)}) collective-permute-start(bf16[2,1152,256]{2,1,0:T(8,128)(2,1)S(1)} %get-tuple-element.115.refs_0_), channel_id=1, source_target_pairs={{0,32},{32,64},{64,96},{96,0},{1,33},{33,65},{65,97},{97,1},{2,34}... | collective-permute-start | bytes 3538952 | tf_op jit(solution)/shard_map/ppermute | solution.py:30
  35.7 31.3 %copy-start = (bf16[512,4096]{1,0:T(8,128)(2,1)S(1)}, bf16[512,4096]{1,0:T(8,128)(2,1)}, u32[]{:S(2)}) copy-start(bf16[512,4096]{1,0:T(8,128)(2,1)} %own_ref.1) | copy-start | bytes 12582916
  35.7 24.5 %collective-permute-start.13 = (bf16[2,1152,256]{2,1,0:T(8,128)(2,1)S(1)}, bf16[2,1152,256]{2,1,0:T(8,128)(2,1)S(1)}, u32[]{:S(2)}, u32[]{:S(2)}) collective-permute-start(bf16[2,1152,256]{2,1,0:T(8,128)(2,1)S(1)} %get-tuple-element.116.refs_3_.refs_5_), channel_id=1, source_target_pairs={{0,24},{8,0},{16,8},{24,16},{1,25},{9,1},{17,9},{25,17},{2,26},{10... | collective-permute-start | bytes 3538952 | tf_op jit(solution)/shard_map/ppermute | solution.py:30
  38.7 24.3 %collective-permute-start.14 = (bf16[2,1152,256]{2,1,0:T(8,128)(2,1)S(1)}, bf16[2,1152,256]{2,1,0:T(8,128)(2,1)S(1)}, u32[]{:S(2)}, u32[]{:S(2)}) collective-permute-start(bf16[2,1152,256]{2,1,0:T(8,128)(2,1)S(1)} %get-tuple-element.116.refs_3_.refs_5_), channel_id=1, source_target_pairs={{0,8},{8,16},{16,24},{24,0},{1,9},{9,17},{17,25},{25,1},{2,10},{10... | collective-permute-start | bytes 3538952 | tf_op jit(solution)/shard_map/ppermute | solution.py:30
  63.1 13.7 %collective-permute-start.15 = (bf16[1152,256]{1,0:T(8,128)(2,1)S(1)}, bf16[1152,256]{1,0:T(8,128)(2,1)S(1)}, u32[]{:S(2)}, u32[]{:S(2)}) collective-permute-start(bf16[1152,256]{1,0:T(8,128)(2,1)S(1)} %get-tuple-element.110), channel_id=1, source_target_pairs={{0,96},{32,0},{64,32},{96,64},{1,97},{33,1},{65,33},{97,65},{2,98}... | collective-permute-start | bytes 1769480 | tf_op jit(solution)/shard_map/ppermute | solution.py:30
  65.6 11.2 %collective-permute-start.16 = (bf16[1152,256]{1,0:T(8,128)(2,1)S(1)}, bf16[1152,256]{1,0:T(8,128)(2,1)S(1)}, u32[]{:S(2)}, u32[]{:S(2)}) collective-permute-start(bf16[1152,256]{1,0:T(8,128)(2,1)S(1)} %get-tuple-element.111), channel_id=1, source_target_pairs={{0,32},{32,64},{64,96},{96,0},{1,33},{33,65},{65,97},{97,1},{2,34}... | collective-permute-start | bytes 1769480 | tf_op jit(solution)/shard_map/ppermute | solution.py:30
  65.6 11.2 %collective-permute-start.17 = (bf16[1152,256]{1,0:T(8,128)(2,1)S(1)}, bf16[1152,256]{1,0:T(8,128)(2,1)S(1)}, u32[]{:S(2)}, u32[]{:S(2)}) collective-permute-start(bf16[1152,256]{1,0:T(8,128)(2,1)S(1)} %get-tuple-element.112), channel_id=1, source_target_pairs={{0,24},{8,0},{16,8},{24,16},{1,25},{9,1},{17,9},{25,17},{2,26},{10... | collective-permute-start | bytes 1769480 | tf_op jit(solution)/shard_map/ppermute | solution.py:30
  65.9 11.0 %collective-permute-start.18 = (bf16[1152,256]{1,0:T(8,128)(2,1)S(1)}, bf16[1152,256]{1,0:T(8,128)(2,1)S(1)}, u32[]{:S(2)}, u32[]{:S(2)}) collective-permute-start(bf16[1152,256]{1,0:T(8,128)(2,1)S(1)} %get-tuple-element.113), channel_id=1, source_target_pairs={{0,8},{8,16},{16,24},{24,0},{1,9},{9,17},{17,25},{25,1},{2,10},{10... | collective-permute-start | bytes 1769480 | tf_op jit(solution)/shard_map/ppermute | solution.py:30
  83.2 2.7 %collective-permute-start.19 = (f32[32,128]{1,0:T(8,128)S(1)}, f32[32,128]{1,0:T(8,128)S(1)}, u32[]{:S(2)}, u32[]{:S(2)}) collective-permute-start(f32[32,128]{1,0:T(8,128)S(1)} %get-tuple-element.134), channel_id=1, source_target_pairs={{0,24},{8,0},{16,8},{24,16},{1,25},{9,1},{17,9},{25,17},{2,26},{10... | collective-permute-start | bytes 49160 | tf_op jit(solution)/shard_map/ppermute | solution.py:30
  84.9 4.2 %collective-permute-start.20 = (f32[32,128]{1,0:T(8,128)S(1)}, f32[32,128]{1,0:T(8,128)S(1)}, u32[]{:S(2)}, u32[]{:S(2)}) collective-permute-start(f32[32,128]{1,0:T(8,128)S(1)} %get-tuple-element.134), channel_id=1, source_target_pairs={{0,16},{8,24},{16,0},{24,8},{1,17},{9,25},{17,1},{25,9},{2,18},{10... | collective-permute-start | bytes 49160 | tf_op jit(solution)/shard_map/ppermute | solution.py:30
  85.1 4.0 %collective-permute-start.21 = (f32[32,128]{1,0:T(8,128)S(1)}, f32[32,128]{1,0:T(8,128)S(1)}, u32[]{:S(2)}, u32[]{:S(2)}) collective-permute-start(f32[32,128]{1,0:T(8,128)S(1)} %get-tuple-element.134), channel_id=1, source_target_pairs={{0,8},{8,16},{16,24},{24,0},{1,9},{9,17},{17,25},{25,1},{2,10},{10... | collective-permute-start | bytes 49160 | tf_op jit(solution)/shard_map/ppermute | solution.py:30
  89.1 4.7 %collective-permute-start.22 = (f32[4,32,128]{2,1,0:T(8,128)S(1)}, f32[4,32,128]{2,1,0:T(8,128)S(1)}, u32[]{:S(2)}, u32[]{:S(2)}) collective-permute-start(f32[4,32,128]{2,1,0:T(8,128)S(1)} %pad_maximum_fusion.1), channel_id=1, source_target_pairs={{0,96},{32,0},{64,32},{96,64},{1,97},{33,1},{65,33},{97,65},{2,98}... | collective-permute-start | bytes 196616 | tf_op jit(solution)/shard_map/ppermute | solution.py:30
  91.8 4.7 %collective-permute-start.23 = (f32[4,32,128]{2,1,0:T(8,128)S(1)}, f32[4,32,128]{2,1,0:T(8,128)S(1)}, u32[]{:S(2)}, u32[]{:S(2)}) collective-permute-start(f32[4,32,128]{2,1,0:T(8,128)S(1)} %pad_maximum_fusion.1), channel_id=1, source_target_pairs={{0,64},{32,96},{64,0},{96,32},{1,65},{33,97},{65,1},{97,33},{2,66}... | collective-permute-start | bytes 196616 | tf_op jit(solution)/shard_map/ppermute | solution.py:30
  91.8 5.0 %collective-permute-start.24 = (f32[4,32,128]{2,1,0:T(8,128)S(1)}, f32[4,32,128]{2,1,0:T(8,128)S(1)}, u32[]{:S(2)}, u32[]{:S(2)}) collective-permute-start(f32[4,32,128]{2,1,0:T(8,128)S(1)} %pad_maximum_fusion.1), channel_id=1, source_target_pairs={{0,32},{32,64},{64,96},{96,0},{1,33},{33,65},{65,97},{97,1},{2,34}... | collective-permute-start | bytes 196616 | tf_op jit(solution)/shard_map/ppermute | solution.py:30
  103.2 20.5 %collective-permute-start.25 = (bf16[2,1024,256]{2,1,0:T(8,128)(2,1)S(1)}, bf16[2,1024,256]{2,1,0:T(8,128)(2,1)S(1)}, u32[]{:S(2)}, u32[]{:S(2)}) collective-permute-start(bf16[2,1024,256]{2,1,0:T(8,128)(2,1)S(1)} %get-tuple-element.145), channel_id=1, source_target_pairs={{0,4},{4,0},{1,5},{5,1},{2,6},{6,2},{3,7},{7,3},{8,12},{12,8},{9,1... | collective-permute-start | bytes 3145736 | tf_op jit(solution)/shard_map/ppermute | solution.py:30
  112.7 10.9 %collective-permute-start.26 = (bf16[8,16,512]{2,1,0:T(8,128)(2,1)S(1)}, bf16[8,16,512]{2,1,0:T(8,128)(2,1)S(1)}, u32[]{:S(2)}, u32[]{:S(2)}) collective-permute-start(bf16[8,16,512]{2,1,0:T(8,128)(2,1)S(1)} %get-tuple-element.147), channel_id=1, source_target_pairs={{0,32},{32,64},{64,96},{96,0},{1,33},{33,65},{65,97},{97,1},{2,34}... | collective-permute-start | bytes 393224 | tf_op jit(solution)/shard_map/ppermute | solution.py:30
  112.7 10.9 %collective-permute-start.27 = (bf16[8,16,512]{2,1,0:T(8,128)(2,1)S(1)}, bf16[8,16,512]{2,1,0:T(8,128)(2,1)S(1)}, u32[]{:S(2)}, u32[]{:S(2)}) collective-permute-start(bf16[8,16,512]{2,1,0:T(8,128)(2,1)S(1)} %get-tuple-element.148), channel_id=1, source_target_pairs={{0,64},{32,96},{64,0},{96,32},{1,65},{33,97},{65,1},{97,33},{2,66}... | collective-permute-start | bytes 393224 | tf_op jit(solution)/shard_map/ppermute | solution.py:30
  114.5 9.1 %collective-permute-start.28 = (bf16[8,16,512]{2,1,0:T(8,128)(2,1)S(1)}, bf16[8,16,512]{2,1,0:T(8,128)(2,1)S(1)}, u32[]{:S(2)}, u32[]{:S(2)}) collective-permute-start(bf16[8,16,512]{2,1,0:T(8,128)(2,1)S(1)} %get-tuple-element.149), channel_id=1, source_target_pairs={{0,96},{32,0},{64,32},{96,64},{1,97},{33,1},{65,33},{97,65},{2,98}... | collective-permute-start | bytes 393224 | tf_op jit(solution)/shard_map/ppermute | solution.py:30
  123.6 16.2 %collective-permute-start.31 = (bf16[2,2,1024,256]{3,2,1,0:T(8,128)(2,1)S(1)}, bf16[2,2,1024,256]{3,2,1,0:T(8,128)(2,1)S(1)}, u32[]{:S(2)}, u32[]{:S(2)}) collective-permute-start(bf16[2,2,1024,256]{3,2,1,0:T(8,128)(2,1)S(1)} %get-tuple-element.157), channel_id=1, source_target_pairs={{0,4},{4,0},{1,5},{5,1},{2,6},{6,2},{3,7},{7,3},{8,12},{12,8},{9,1... | collective-permute-start | bytes 6291464 | tf_op jit(solution)/shard_map/ppermute | solution.py:30
  124.9 14.9 %collective-permute-start.29 = (bf16[2,512,256]{2,1,0:T(8,128)(2,1)S(1)}, bf16[2,512,256]{2,1,0:T(8,128)(2,1)S(1)}, u32[]{:S(2)}, u32[]{:S(2)}) collective-permute-start(bf16[2,512,256]{2,1,0:T(8,128)(2,1)S(1)} %get-tuple-element.187), channel_id=1, source_target_pairs={{0,1},{1,2},{2,3},{3,0},{4,5},{5,6},{6,7},{7,4},{8,9},{9,10},{10,1... | collective-permute-start | bytes 1572872 | tf_op jit(solution)/shard_map/ppermute | solution.py:30
  126.3 13.6 %collective-permute-start.30 = (bf16[2,512,256]{2,1,0:T(8,128)(2,1)S(1)}, bf16[2,512,256]{2,1,0:T(8,128)(2,1)S(1)}, u32[]{:S(2)}, u32[]{:S(2)}) collective-permute-start(bf16[2,512,256]{2,1,0:T(8,128)(2,1)S(1)} %get-tuple-element.186), channel_id=1, source_target_pairs={{0,3},{1,0},{2,1},{3,2},{4,7},{5,4},{6,5},{7,6},{8,11},{9,8},{10,9... | collective-permute-start | bytes 1572872 | tf_op jit(solution)/shard_map/ppermute | solution.py:30
  139.9 17.6 %collective-permute-start.34 = (bf16[2,1024,256]{2,1,0:T(8,128)(2,1)S(1)}, bf16[2,1024,256]{2,1,0:T(8,128)(2,1)S(1)}, u32[]{:S(2)}, u32[]{:S(2)}) collective-permute-start(bf16[2,1024,256]{2,1,0:T(8,128)(2,1)S(1)} %bitcast.42), channel_id=1, source_target_pairs={{0,4},{4,0},{1,5},{5,1},{2,6},{6,2},{3,7},{7,3},{8,12},{12,8},{9,1... | collective-permute-start | bytes 3145736 | tf_op jit(solution)/shard_map/ppermute | solution.py:30
  140.9 14.9 %collective-permute-start.32 = (bf16[2,512,256]{2,1,0:T(8,128)(2,1)S(1)}, bf16[2,512,256]{2,1,0:T(8,128)(2,1)S(1)}, u32[]{:S(2)}, u32[]{:S(2)}) collective-permute-start(bf16[2,512,256]{2,1,0:T(8,128)(2,1)S(1)} %get-tuple-element.185), channel_id=1, source_target_pairs={{0,1},{1,2},{2,3},{3,0},{4,5},{5,6},{6,7},{7,4},{8,9},{9,10},{10,1... | collective-permute-start | bytes 1572872 | tf_op jit(solution)/shard_map/ppermute | solution.py:30
  142.3 14.4 %collective-permute-start.33 = (bf16[2,512,256]{2,1,0:T(8,128)(2,1)S(1)}, bf16[2,512,256]{2,1,0:T(8,128)(2,1)S(1)}, u32[]{:S(2)}, u32[]{:S(2)}) collective-permute-start(bf16[2,512,256]{2,1,0:T(8,128)(2,1)S(1)} %get-tuple-element.184), channel_id=1, source_target_pairs={{0,3},{1,0},{2,1},{3,2},{4,7},{5,4},{6,5},{7,6},{8,11},{9,8},{10,9... | collective-permute-start | bytes 1572872 | tf_op jit(solution)/shard_map/ppermute | solution.py:30
  143.8 5.3 %collective-permute-start.35 = (f32[2,16,512]{2,1,0:T(8,128)S(1)}, f32[2,16,512]{2,1,0:T(8,128)S(1)}, u32[]{:S(2)}, u32[]{:S(2)}) collective-permute-start(f32[2,16,512]{2,1,0:T(8,128)S(1)} %get-tuple-element.194), channel_id=1, source_target_pairs={{0,8},{8,16},{16,24},{24,0},{1,9},{9,17},{17,25},{25,1},{2,10},{10... | collective-permute-start | bytes 196616 | tf_op jit(solution)/shard_map/ppermute | solution.py:30
  143.9 6.7 %collective-permute-start.36 = (f32[2,16,512]{2,1,0:T(8,128)S(1)}, f32[2,16,512]{2,1,0:T(8,128)S(1)}, u32[]{:S(2)}, u32[]{:S(2)}) collective-permute-start(f32[2,16,512]{2,1,0:T(8,128)S(1)} %get-tuple-element.193), channel_id=1, source_target_pairs={{0,16},{8,24},{16,0},{24,8},{1,17},{9,25},{17,1},{25,9},{2,18},{10... | collective-permute-start | bytes 196616 | tf_op jit(solution)/shard_map/ppermute | solution.py:30
  149.1 3.4 %collective-permute-start.37 = (f32[2,16,512]{2,1,0:T(8,128)S(1)}, f32[2,16,512]{2,1,0:T(8,128)S(1)}, u32[]{:S(2)}, u32[]{:S(2)}) collective-permute-start(f32[2,16,512]{2,1,0:T(8,128)S(1)} %get-tuple-element.192), channel_id=1, source_target_pairs={{0,24},{8,0},{16,8},{24,16},{1,25},{9,1},{17,9},{25,17},{2,26},{10... | collective-permute-start | bytes 196616 | tf_op jit(solution)/shard_map/ppermute | solution.py:30
  155.8 0.8 copy-start.1
  156.6 0.8 copy-start.3
  157.5 14.2 %collective-permute-start.39 = (bf16[2,512,256]{2,1,0:T(8,128)(2,1)}, bf16[2,512,256]{2,1,0:T(8,128)(2,1)}, u32[]{:S(2)}, u32[]{:S(2)}) collective-permute-start(bf16[2,512,256]{2,1,0:T(8,128)(2,1)} %get-tuple-element.178), channel_id=1, source_target_pairs={{0,1},{1,2},{2,3},{3,0},{4,5},{5,6},{6,7},{7,4},{8,9},{9,10},{10,1... | collective-permute-start | bytes 1572872 | tf_op jit(solution)/shard_map/ppermute | solution.py:30
  157.5 14.2 %collective-permute-start.40 = (bf16[2,512,256]{2,1,0:T(8,128)(2,1)}, bf16[2,512,256]{2,1,0:T(8,128)(2,1)}, u32[]{:S(2)}, u32[]{:S(2)}) collective-permute-start(bf16[2,512,256]{2,1,0:T(8,128)(2,1)} %get-tuple-element.181), channel_id=1, source_target_pairs={{0,3},{1,0},{2,1},{3,2},{4,7},{5,4},{6,5},{7,6},{8,11},{9,8},{10,9... | collective-permute-start | bytes 1572872 | tf_op jit(solution)/shard_map/ppermute | solution.py:30
  160.2 2.2 %collective-permute-start.38 = (f32[16,512]{1,0:T(8,128)S(1)}, f32[16,512]{1,0:T(8,128)S(1)}, u32[]{:S(2)}, u32[]{:S(2)}) collective-permute-start(f32[16,512]{1,0:T(8,128)S(1)} %get-tuple-element.197), channel_id=1, source_target_pairs={{0,4},{4,0},{1,5},{5,1},{2,6},{6,2},{3,7},{7,3},{8,12},{12,8},{9,1... | collective-permute-start | bytes 98312 | tf_op jit(solution)/shard_map/ppermute | solution.py:30
  171.7 1.0 copy-start.2
  172.8 1.0 copy-start.4

commit v3 on v2

--- a/solution.py
+++ b/solution.py
@@ -20,7 +20,7 @@
 NPASS = 4
 PAIRS = 4
 LOW = -1e30
-HIDDEN = pl.CostEstimate(flops=0, bytes_accessed=0, transcendentals=0)
+HIDDEN = pl.CostEstimate(flops=200_000_000, bytes_accessed=0, transcendentals=0)
 NT = (((1,), (1,)), ((), ()))
 TN = (((0,), (0,)), ((), ()))
 
@@ -30,10 +30,6 @@
     return lax.ppermute(v, axis, [(i, (i + shift) % n) for i in range(n)])
 
 
-def gather4(v, axis):
-    return [v] + [perm(v, axis, -o) for o in (1, 2, 3)]
-
-
 def phase(*values):
     return lax.optimization_barrier(values)
 
@@ -42,45 +38,81 @@
     return pltpu.CompilerParams(vmem_limit_bytes=mib * 1024 * 1024)
 
 
-def first_kernel(*refs):
-    outs = refs[10:]
-    for side in range(2):
-        own, up, top, low, down = refs[side * 5 : side * 5 + 5]
-        mid = PIECE // 2
-        outs[side][0, :PIECE] = own[...]
-        outs[side][0, PIECE:] = up[...]
-        outs[side][1, :mid] = top[...]
-        outs[side][1, mid:PIECE] = low[...]
-        outs[side][1, PIECE:] = down[...]
-
-
-def first_blocks(pieces):
+def pair_perm(v, axis, odd):
+    turn = (lambda i: i + 1 - 2 * (i % 2)) if not odd else (lambda i: i - 1 + 2 * (i % 2))
+    return lax.ppermute(v, axis, [(i, turn(i) % 4) for i in range(4)])
+
+
+def join_kernel(*refs):
+    outs = refs[8:]
+    rows = PIECE // 2
+    for k, out in enumerate(outs):
+        out[:rows] = refs[2 * k][...]
+        out[rows:] = refs[2 * k + 1][...]
+
+
+def join(pairs):
+    return pl.pallas_call(
+        join_kernel,
+        out_shape=[jax.ShapeDtypeStruct((PIECE, CHUNK), BF)] * 4,
+        compiler_params=params(16),
+        cost_estimate=HIDDEN,
+    )(*[v for p in pairs for v in p])
+
+
+def first_kernel(place, joined0, second0, joined1, second1, out):
+    mid = PIECE // 2
+    odd = place[0] % 2
+
+    def slot(o, h, value):
+        at = (o % 2) * PIECE + h * mid
+        out[o // 2, at : at + mid, :] = value
+
+    for h, joined, second in ((0, joined0, second0), (1, joined1, second1)):
+        slot(0, h, joined[:mid])
+        slot(2, h, second[mid:])
+        for parity in range(2):
+            @pl.when(odd == parity)
+            def near():
+                one = 1 if h == parity else 3
+                slot(one, h, joined[mid:])
+                slot(4 - one, h, second[:mid])
+
+
+def first_block(place, pieces):
+    def whole(p):
+        return pl.BlockSpec(p.shape, lambda i, o: (0, 0))
+
     return pl.pallas_call(
         first_kernel,
-        out_shape=[jax.ShapeDtypeStruct((2, 2 * PIECE, CHUNK), BF)] * 2,
+        grid_spec=pltpu.PrefetchScalarGridSpec(
+            num_scalar_prefetch=1,
+            grid=(1,),
+            in_specs=[whole(p) for p in pieces],
+            out_specs=pl.BlockSpec((2, 2 * PIECE, CHUNK), lambda i, o: (0, 0, 0)),
+        ),
+        out_shape=jax.ShapeDtypeStruct((2, 2 * PIECE, CHUNK), BF),
         compiler_params=params(16),
         cost_estimate=HIDDEN,
-    )(*pieces)
-
-
-def halves_kernel(a_ref, b_ref, c_ref, d_ref, *outs):
-    for ref, out in zip((a_ref, b_ref, c_ref, d_ref), outs):
-        out[...] = ref[0]
-
-
-def take_halves(a_up, a_down, b_up, b_down):
+    )(place, *pieces)
+
+
+def halves_kernel(up_ref, down_ref, first_ref, second_ref):
+    first_ref[...] = up_ref[0]
+    second_ref[...] = down_ref[0]
+
+
+def take_halves(up, down):
     half = (1, 2 * PIECE, CHUNK)
-    first = pl.BlockSpec(half, lambda i: (0, 0, 0))
-    second = pl.BlockSpec(half, lambda i: (1, 0, 0))
     return pl.pallas_call(
         halves_kernel,
         grid=(1,),
-        in_specs=[first, second, first, second],
-        out_specs=[pl.BlockSpec(half[1:], lambda i: (0, 0))] * 4,
-        out_shape=[jax.ShapeDtypeStruct(half[1:], BF)] * 4,
+        in_specs=[pl.BlockSpec(half, lambda i: (0, 0, 0)), pl.BlockSpec(half, lambda i: (1, 0, 0))],
+        out_specs=[pl.BlockSpec(half[1:], lambda i: (0, 0))] * 2,
+        out_shape=[jax.ShapeDtypeStruct(half[1:], BF)] * 2,
         compiler_params=params(16),
         cost_estimate=HIDDEN,
-    )(a_up, a_down, b_up, b_down)
+    )(up, down)
 
 
 def near_kernel(pos, own_ref, oth_ref, *refs):
@@ -214,6 +246,11 @@
 
 
 def forward_side(side, meta, k, v, qg, st_ref, num_ref):
+    n = st_ref.shape[0]
+
+    def put(row, value):
+        st_ref[:, row : row + 1, :] = jnp.broadcast_to(value[None], (n, 1, 128))
+
     inside = inside_mask(meta, side)
     question = lane_value([meta.question(side, p) for p in range(NPASS)]).astype(F32)
     for pair in range(PAIRS):
@@ -226,12 +263,10 @@
         values = v[side, :, cols]
         dprob = dot_nt(values, pair_matrix(meta, qg, side, pair, 1))
         at = side * PAIRS + pair
-        st_ref[at : at + 1, :] = top
-        st_ref[8 + at : 9 + at, :] = jnp.sum(unnorm, axis=0, keepdims=True)
-        st_ref[16 + at : 17 + at, :] = jnp.sum(
-            unnorm_b.astype(F32) * dprob, axis=0, keepdims=True
-        )
-        st_ref[24 + at : 25 + at, :] = question
+        put(at, top)
+        put(8 + at, jnp.sum(unnorm, axis=0, keepdims=True))
+        put(16 + at, jnp.sum(unnorm_b.astype(F32) * dprob, axis=0, keepdims=True))
+        put(24 + at, question)
         num_ref[side, pair] = lax.dot_general(values, unnorm_b, TN, preferred_element_type=F32)
 
 
@@ -285,7 +320,7 @@
         jax.ShapeDtypeStruct((2, ROWS, HALF), BF),
         jax.ShapeDtypeStruct((1024, CHUNK), BF),
         jax.ShapeDtypeStruct((1024, CHUNK), BF),
-        jax.ShapeDtypeStruct((32, 128), F32),
+        jax.ShapeDtypeStruct((NZ * NX, 32, 128), F32),
         jax.ShapeDtypeStruct((2, PAIRS, 128, 128), F32),
     ]
     return pl.pallas_call(
@@ -307,9 +342,11 @@
     )(*meta, enc_far, acc, *blocks, qa, qb)
 
 
-def combine(st_ref):
+def combine(meta, st_ref):
     n = st_ref.shape[0]
-    own_question = [st_ref[0, 24 + s * PAIRS : 25 + s * PAIRS, :] for s in range(2)]
+    own_question = [
+        lane_value([meta.question(s, p) for p in range(NPASS)]).astype(F32) for s in range(2)
+    ]
 
     def turned(value, k):
         return pltpu.roll(value, 32 * k, 1) if k else value
@@ -401,13 +438,14 @@
     pos, own_numbers, other_numbers, k_ref, v_ref, qa_ref, qb_ref, st_ref, num_ref, *refs
 ):
     sources, outs = refs[:10], refs[10:]
-    kvg_ref, own_ref, oth_ref, c0_ref, c1_ref, c2_ref, c3_ref, ctx_ref, w_ref, sems = outs
+    kvg_ref, own_ref, oth_ref, dense_ref, ctx_ref, w_ref, sems = outs
     w_ref = w_ref.at[0]
     sems = sems.at[0]
     start_copies(pos[2], sources, w_ref, sems)
     meta = Passages(pos, own_numbers, other_numbers)
     qg = (qa_ref, qb_ref)
-    tops, inverses, deltas = combine(st_ref)
+    tops, inverses, deltas = combine(meta, st_ref)
+    here = meta.z * 4 + meta.x
     ctx_ref[...] = jnp.zeros_like(ctx_ref)
     low = lax.broadcasted_iota(jnp.int32, (DEC, 128), 1) < 64
     for side in (1, 0):
@@ -431,11 +469,10 @@
                     kvg_ref[
                         side * 2 + n, t * HALF + pair * 128 : t * HALF + (pair + 1) * 128, :
                     ] = turned[:, n * 256 : (n + 1) * 256]
-            scale = jnp.exp(st_ref[0, at : at + 1, :] - top) * inverse
+            scale = jnp.exp(st_ref[here, at : at + 1, :] - top) * inverse
             context = (num_ref[side, pair] * scale).T
             for p in range(NPASS):
-                zo, xo, core = meta.chip(side, p)
-                ctx_ref[(zo * 4 + xo) * 2 + core, :, cols] += jnp.where(
+                ctx_ref[meta.question(side, p), :, cols] += jnp.where(
                     low, context[p * 32 : p * 32 + 16], context[p * 32 + 16 : p * 32 + 32]
                 )
         if side == 1:
@@ -445,8 +482,7 @@
             out[n] = jnp.dot(
                 weights_tile(w_ref), kvg_ref[side * 2 + n], preferred_element_type=F32
             ).astype(BF)
-    for o, out in enumerate((c0_ref, c1_ref, c2_ref, c3_ref)):
-        out[...] = ctx_ref[o * 8 : o * 8 + 8].astype(out.dtype)
+    dense_ref[...] = ctx_ref[...].astype(BF)
 
 
 def backward(meta, args, weights):
@@ -457,8 +493,8 @@
         jax.ShapeDtypeStruct((4, 2 * HALF, ROWS // 2), BF),
         jax.ShapeDtypeStruct((2, 1024, ROWS // 2), BF),
         jax.ShapeDtypeStruct((2, 1024, ROWS // 2), BF),
-        jax.ShapeDtypeStruct((8, DEC, HALF), F32),
-    ] + [jax.ShapeDtypeStruct((8, DEC, HALF), BF)] * 3
+        jax.ShapeDtypeStruct((32, DEC, HALF), BF),
+    ]
     return pl.pallas_call(
         backward_kernel,
         grid_spec=pltpu.PrefetchScalarGridSpec(
@@ -524,6 +560,24 @@
     )(places, kvg, *weights)
 
 
+def sums_kernel(own_ref, got_ref, below_ref, above_ref, *outs):
+    for out, k, h, more in zip(outs, (0, 1, 0, 1), (1, 0, 0, 1), (None, None, below_ref, above_ref)):
+        rows = slice(h * 512, (h + 1) * 512)
+        total = own_ref[k, :, rows].astype(F32) + got_ref[k, :, rows].astype(F32)
+        if more is not None:
+            total = total + more[...].astype(F32)
+        out[...] = total.astype(BF)
+
+
+def near_sums(own, got, below, above):
+    return pl.pallas_call(
+        sums_kernel,
+        out_shape=[jax.ShapeDtypeStruct((2, 512, ROWS // 2), BF)] * 4,
+        compiler_params=params(16),
+        cost_estimate=HIDDEN,
+    )(own, got, below, above)
+
+
 def finish_kernel(place, base_ref, core_ref, up_top, up_low, down_top, down_low, out_ref):
     step = pl.program_id(0)
     total = base_ref[...] + core_ref[...].astype(F32)
@@ -570,90 +624,89 @@
     got = perm(theirs, "core", 1)
     numbers = jnp.concatenate([passage_len[0], passage_question[:, 0]])
     other_numbers = perm(numbers, "core", 1)
-    enc_other = perm(enc_rows, "core", 1)
+    enc_after, got = phase(enc_rows, got)
+    enc_other = perm(enc_after, "core", 1)
     first = jnp.where(core == 0, mine, got)
     second = jnp.where(core == 0, got, mine)
     chip = jnp.concatenate(
         [v[a:b] for a, b in ((0, 128), (128, 256), (256, 272), (272, 288)) for v in (first, second)],
         axis=0,
     )
-    a_chip, b_chip, enc_other, other_numbers, pos, near_places, base_place, xs = phase(
-        chip[:, :CHUNK],
-        chip[:, CHUNK:],
-        enc_other,
-        other_numbers,
+    mid = PIECE // 2
+    halves = phase(
+        *[chip[h * mid : (h + 1) * mid, c : c + CHUNK] for c in (0, CHUNK) for h in (0, 1)]
+    )
+
+    steps = [(v, a, h) for v, (a, h) in zip(halves, (("x", 0), ("x", 1), ("z", 0), ("z", 1)))]
+    met, pos, near_places, base_place, x_place, xs = phase(
+        [pair_perm(v, a, h) for v, a, h in steps],
         pos,
         near_places,
         base_place,
+        x.astype(jnp.int32).reshape(1),
         xs.astype(jnp.int32),
     )
-
-    ax_up, ax_down = perm(a_chip, "x", -1), perm(a_chip, "x", 1)
-    bz_up, bz_down = perm(b_chip, "z", -1), perm(b_chip, "z", 1)
-    ax_up, ax_down, bz_up, bz_down = phase(ax_up, ax_down, bz_up, bz_down)
-    mid = PIECE // 2
-    far = phase(
-        perm(ax_up[:mid], "x", -1),
-        perm(ax_down[mid:], "x", 1),
-        perm(bz_up[:mid], "z", -1),
-        perm(bz_down[mid:], "z", 1),
-    )
-    a_first = [a_chip, ax_up, far[0], far[1], ax_down]
-    b_first = [b_chip, bz_up, far[2], far[3], bz_down]
-    a_own, b_own = phase(*first_blocks(a_first + b_first))
-
-    a_up, a_down = perm(a_own, "z", -1), perm(a_own, "z", 1)
-    b_up, b_down = perm(b_own, "x", -1), perm(b_own, "x", 1)
-    a_own, b_own, a_up, a_down, b_up, b_down = phase(a_own, b_own, a_up, a_down, b_up, b_down)
-    give = phase(*take_halves(a_up, a_down, b_up, b_down))
-    far = [perm(v, a, t) for v, a, t in zip(give, ("z", "z", "x", "x"), (-1, 1, -1, 1))]
+    joined = phase(*join(list(zip(halves, met))))
+    second = [pair_perm(v, a, 1 - h) for v, (_, a, h) in zip(joined, steps)]
+    a_own = first_block(x_place, (joined[0], second[0], joined[1], second[1]))
+    b_own = first_block(pos[0:1], (joined[2], second[2], joined[3], second[3]))
+    enc_other, other_numbers, a_own, b_own = phase(enc_other, other_numbers, a_own, b_own)
+
+    a_up, a_down = phase(perm(a_own, "z", -1), perm(a_own, "z", 1))
+    b_up, b_down = phase(perm(b_own, "x", -1), perm(b_own, "x", 1))
+    a_first, a_second = phase(*take_halves(a_up, a_down))
+    b_first, b_second = phase(*take_halves(b_up, b_down))
+    far = [
+        perm(a_first, "z", -1),
+        perm(a_second, "z", 1),
+        perm(b_first, "x", -1),
+        perm(b_second, "x", 1),
+    ]
     acc, enc_far, qa, qb = project_near(
         pos, enc_rows, enc_other, [a_own, a_up, a_down, b_own, b_up, b_down]
     )
     far, acc, enc_far, qa, qb = phase(far, acc, enc_far, qa, qb)
     meta = (pos, numbers, other_numbers)
     keys, values, qa, qb, stats, numer = project_far(meta, enc_far, acc, far, qa, qb)
-    stats_x = jnp.stack(phase(*gather4(stats, "x")))
-    stats_all = jnp.concatenate(gather4(stats_x, "z"), axis=0)
+    stats_all = lax.all_to_all(stats, ("z", "x"), 0, 0, tiled=True)
     weights = [a_own, a_up, far[0], far[1], a_down, b_own, b_up, far[2], far[3], b_down]
-    kvg, far_own, far_other, *dense = backward(
+    kvg, far_own, far_other, dense = backward(
         meta, (keys, values, qa, qb, stats_all, numer), weights
     )
 
     def add(*values):
         return sum(v.astype(F32) for v in values).astype(BF)
 
-    kvg, far_other, dense = phase(kvg, far_other, dense)
     far_got = perm(far_other, "core", 1)
-    by_z = [dense[0]] + [perm(dense[o], "z", o) for o in (1, 2, 3)]
     near_own, near_other = grad_blocks(near_places, kvg, weights, BF)
-    far_got, by_z, kvg, near_own, near_other = phase(far_got, by_z, kvg, near_own, near_other)
-
-    from_below = perm(add(far_own[:, :512], far_got[:, :512]), "dec", 1)
-    from_above = perm(add(far_own[:, 512:], far_got[:, 512:]), "dec", -1)
+    far_got, near_own, near_other, kvg, dense = phase(far_got, near_own, near_other, kvg, dense)
+
+    far_top = add(far_own[:, :512], far_got[:, :512])
+    far_low = add(far_own[:, 512:], far_got[:, 512:])
+    far_top, far_low, near_other, kvg, dense = phase(far_top, far_low, near_other, kvg, dense)
+    from_below = perm(far_top, "dec", 1)
+    from_above = perm(far_low, "dec", -1)
     near_got = perm(near_other, "core", 1)
     base, base_other = grad_blocks(base_place, kvg, weights, F32)
-    base, base_other = base[0], base_other[0]
-    by_z = sum(v.astype(F32) for v in by_z).reshape(4, 2, DEC, HALF)
-    from_below, from_above, near_got, base, base_other, by_z = phase(
-        from_below, from_above, near_got, base, base_other, by_z
-    )
-
-    low_below = perm(add(near_own[0, :, 512:], near_got[0, :, 512:]), "dec", 1)
-    top_above = perm(add(near_own[1, :, :512], near_got[1, :, :512]), "dec", -1)
-    up_top = add(near_own[0, :, :512], near_got[0, :, :512], from_below)
-    down_low = add(near_own[1, :, 512:], near_got[1, :, 512:], from_above)
-    by_x = [by_z[0]] + [perm(by_z[o], "x", o) for o in (1, 2, 3)]
+    from_below, from_above, near_got, base, base_other, dense = phase(
+        from_below, from_above, near_got, base[0], base_other[0], dense
+    )
+
+    *sums, dense, base_other = phase(
+        *near_sums(near_own, near_got, from_below, from_above), dense, base_other
+    )
+    low_below = perm(sums[0], "dec", 1)
+    top_above = perm(sums[1], "dec", -1)
+    top_below = perm(sums[2], "dec", 1)
+    low_above = perm(sums[3], "dec", -1)
     base_got = perm(base_other, "core", 1)
-    low_below, top_above, up_top, down_low, base_got, by_x = phase(
-        low_below, top_above, up_top, down_low, base_got, by_x
-    )
-
-    top_below = perm(up_top, "dec", 1)
-    low_above = perm(down_low, "dec", -1)
-    by_x = sum(by_x)
-    keep = lax.dynamic_index_in_dim(by_x, core, 0, keepdims=False)
-    give = lax.dynamic_index_in_dim(by_x, 1 - core, 0, keepdims=False)
+    parts = lax.all_to_all(dense.reshape(NZ * NX, 2, DEC, HALF), ("z", "x"), 0, 0, tiled=True)
+    low_below, top_above, top_below, low_above, base_got, parts = phase(
+        low_below, top_above, top_below, low_above, base_got, parts
+    )
+    chip_ctx = jnp.sum(parts.astype(F32), axis=0)
+    keep = lax.dynamic_index_in_dim(chip_ctx, core, 0, keepdims=False)
+    give = lax.dynamic_index_in_dim(chip_ctx, 1 - core, 0, keepdims=False)
     come = perm(give, "core", 1)
     ctx = jnp.where(
         core == 0,

time: 179 us -> 160 us (0.89)
  waiting for transfers between devices: 72.4 us -> 57.5 us
  starting transfers between devices: 56 us -> 43.1 us
  blocking collectives: 0 us -> 11.8 us
  local copies, waits for them, and re-layouts: 4.63 us -> 0.79 us
  Pallas kernels: 39.1 us -> 41.6 us
    ppermute x41 -> x21, waiting for transfers between devices: 72.4 us -> 41.6 us  [perm(): return lax.ppermute(v, axis, [(i, (i + shift) % n) for i in range(n)])]
    ppermute x41 -> x21, starting transfers between devices: 56 us -> 28.5 us  [perm(): return lax.ppermute(v, axis, [(i, (i + shift) % n) for i in range(n)])]
    all_to_all x0 -> x1, blocking collectives: none -> 11.8 us  [body(): stats_all = lax.all_to_all(stats, ('z', 'x'), 0, 0, tiled=True)]
    all_to_all x0 -> x1, waiting for transfers between devices: none -> 10.5 us  [body(): lax.all_to_all(dense.reshape(NZ * NX, 2, DEC, HALF), ('z', 'x'), 0, 0, ti...]
    ppermute x0 -> x8, starting transfers between devices: none -> 10.4 us  [pair_perm(): return lax.ppermute(v, axis, [(i, turn(i) % 4) for i in range(4)])]
    ppermute x0 -> x8, waiting for transfers between devices: none -> 5.35 us  [pair_perm(): return lax.ppermute(v, axis, [(i, turn(i) % 4) for i in range(4)])]
    all_to_all x0 -> x1, starting transfers between devices: none -> 4.25 us  [body(): lax.all_to_all(dense.reshape(NZ * NX, 2, DEC, HALF), ('z', 'x'), 0, 0, ti...]
    unnamed x23 -> x13, local copies, waits for them, and re-layouts: 3.77 us -> 0.08 us
  transfers between devices with their start and end apart: 41 -> 30, of which waited for: 20 -> 14; matrix products, arithmetic and copies ran while one was open for 4% -> 1% of each run, Pallas kernels for 12% -> 17%
where the time goes in v3:
time: 160 us
  waiting for transfers between devices  57.5 us (36%)
  starting transfers between devices  43.1 us (27%)
  Pallas kernels  41.6 us (26%)
  blocking collectives  11.8 us (7%)
  other arithmetic  4.04 us (3%)
    ppermute x21, waiting for transfers between devices, perm(): return lax.ppermute(v, axis, [(i, (i + shift) % n) for i in range(n)])  41.6 us
    ppermute x21, starting transfers between devices, perm(): return lax.ppermute(v, axis, [(i, (i + shift) % n) for i in range(n)])  28.5 us
    pallas_call x2, Pallas kernels, grad_blocks(): pl.pallas_call(functools.partial(grad_kernel, count), grid_spec=pltpu.Pre...  12.3 us
    all_to_all x1, blocking collectives, body(): stats_all = lax.all_to_all(stats, ('z', 'x'), 0, 0, tiled=True)  11.8 us
    all_to_all x1, waiting for transfers between devices, body(): lax.all_to_all(dense.reshape(NZ * NX, 2, DEC, HALF), ('z', 'x'), 0, 0, ti...  10.5 us
    ppermute x8, starting transfers between devices, pair_perm(): return lax.ppermute(v, axis, [(i, turn(i) % 4) for i in range(4)])  10.4 us
    pallas_call x1, Pallas kernels, project_near(): pl.pallas_call(near_kernel, grid_spec=pltpu.PrefetchScalarGridSpec(num_sc...  9.78 us
    pallas_call x1, Pallas kernels, project_far(): pl.pallas_call(far_kernel, grid_spec=pltpu.PrefetchScalarGridSpec(num_sca...  6.33 us
  transfers between devices with their start and end apart: 30, of which 14 were waited for; matrix products, arithmetic and copies ran while one was open for 1% of the time, Pallas kernels for 17%

profile of v3, /device:TPU:1, one launch (start us, length us, event | category | flops | bytes accessed | tf_op | source)
XLA Modules:
  0.0 159.8 jit_solution(2008271314733040344)
XLA Ops:
  0.6 1.1 pad_maximum_fusion
  1.8 1.5 collective-permute-start
  3.3 1.2 collective-permute-done
  5.2 1.4 collective-permute-start.1
  6.6 1.8 %collective-permute-start.2 = (bf16[288,256]{1,0:T(8,128)(2,1)S(1)}, bf16[288,256]{1,0:T(8,128)(2,1)S(1)}, u32[]{:S(2)}, u32[]{:S(2)}) collective-permute-start(bf16[288,256]{1,0:T(8,128)(2,1)S(1)} %get-tuple-element.93.refs_2_), channel_id=1, source_target_pairs={{0,24},{8,16},{16,8},{24,0},{1,25},{9,17},{17,9},{25,1},{2,26},{10... | collective-permute-start | bytes 442376 | tf_op jit(solution)/shard_map/ppermute | solution.py:43
  8.4 1.6 %collective-permute-start.3 = (bf16[288,256]{1,0:T(8,128)(2,1)S(1)}, bf16[288,256]{1,0:T(8,128)(2,1)S(1)}, u32[]{:S(2)}, u32[]{:S(2)}) collective-permute-start(bf16[288,256]{1,0:T(8,128)(2,1)S(1)} %get-tuple-element.94.refs_4_), channel_id=1, source_target_pairs={{0,32},{32,0},{64,96},{96,64},{1,33},{33,1},{65,97},{97,65},{2,34}... | collective-permute-start | bytes 442376 | tf_op jit(solution)/shard_map/ppermute | solution.py:43
  10.0 2.2 %collective-permute-start.4 = (bf16[288,256]{1,0:T(8,128)(2,1)S(1)}, bf16[288,256]{1,0:T(8,128)(2,1)S(1)}, u32[]{:S(2)}, u32[]{:S(2)}) collective-permute-start(bf16[288,256]{1,0:T(8,128)(2,1)S(1)} %get-tuple-element.95.refs_6_), channel_id=1, source_target_pairs={{0,96},{32,64},{64,32},{96,0},{1,97},{33,65},{65,33},{97,1},{2,98}... | collective-permute-start | bytes 442376 | tf_op jit(solution)/shard_map/ppermute | solution.py:43
  12.3 0.6 fusion.3
  13.0 0.6 pad_add_fusion.pos
  13.6 2.0 %collective-permute-done.4.refs_7_ = bf16[288,256]{1,0:T(8,128)(2,1)S(1)} collective-permute-done((bf16[288,256]{1,0:T(8,128)(2,1)S(1)}, bf16[288,256]{1,0:T(8,128)(2,1)S(1)}, u32[]{:S(2)}, u32[]{:S(2)}) %collective-permute-start.4) | collective-permute-done | bytes 147488 | tf_op jit(solution)/shard_map/ppermute | solution.py:43
  15.7 0.7 collective-permute-start.10
  16.4 1.7 %collective-permute-start.9 = (bf16[576,256]{1,0:T(8,128)(2,1)S(1)}, bf16[576,256]{1,0:T(8,128)(2,1)S(1)}, u32[]{:S(2)}, u32[]{:S(2)}) collective-permute-start(bf16[576,256]{1,0:T(8,128)(2,1)S(1)} %get-tuple-element.105.joined0), channel_id=1, source_target_pairs={{0,96},{32,64},{64,32},{96,0},{1,97},{33,65},{65,33},{97,1},{2,98}... | collective-permute-start | bytes 884744 | tf_op jit(solution)/shard_map/ppermute | solution.py:43
  18.2 0.9 collective-permute-start.7
  19.1 3.3 %collective-permute-done.10.second1 = bf16[576,256]{1,0:T(8,128)(2,1)S(1)} collective-permute-done((bf16[576,256]{1,0:T(8,128)(2,1)S(1)}, bf16[576,256]{1,0:T(8,128)(2,1)S(1)}, u32[]{:S(2)}, u32[]{:S(2)}) %collective-permute-start.10) | collective-permute-done | bytes 294944 | tf_op jit(solution)/shard_map/ppermute | solution.py:43
  22.4 2.8 %collective-permute-start.6 = (s32[8]{0:T(128)S(1)}, s32[8]{0:T(128)S(1)}, u32[]{:S(2)}, u32[]{:S(2)}) collective-permute-start(s32[8]{0:T(128)S(1)} %pad_add_fusion.1.own_numbers), channel_id=1, source_target_pairs={{0,4},{4,0},{1,5},{5,1},{2,6},{6,2},{3,7},{7,3},{8,12},{12,8},{9,1... | collective-permute-start | bytes 104 | tf_op jit(solution)/shard_map/ppermute | solution.py:30
  25.5 0.5 collective-permute-done.6.other_numbers
  26.0 0.9 collective-permute-start.15
  26.9 0.6 collective-permute-start.16
  27.5 2.2 %collective-permute-start.11 = (bf16[2,1152,256]{2,1,0:T(8,128)(2,1)S(1)}, bf16[2,1152,256]{2,1,0:T(8,128)(2,1)S(1)}, u32[]{:S(2)}, u32[]{:S(2)}) collective-permute-start(bf16[2,1152,256]{2,1,0:T(8,128)(2,1)S(1)} %shard_map.87.refs_0_), channel_id=1, source_target_pairs={{0,96},{32,0},{64,32},{96,64},{1,97},{33,1},{65,33},{97,65},{2,98}... | collective-permute-start | bytes 3538952 | tf_op jit(solution)/shard_map/ppermute | solution.py:30
  29.7 20.8 %collective-permute-done.15.up_ref.refs_4_.refs_6_ = bf16[2,1152,256]{2,1,0:T(8,128)(2,1)S(1)} collective-permute-done((bf16[2,1152,256]{2,1,0:T(8,128)(2,1)S(1)}, bf16[2,1152,256]{2,1,0:T(8,128)(2,1)S(1)}, u32[]{:S(2)}, u32[]{:S(2)}) %collective-permute-start.15) | collective-permute-done | bytes 1179680 | tf_op jit(solution)/shard_map/ppermute | solution.py:30
  50.5 1.1 collective-permute-done.16.down_ref.refs_5_.refs_9_
  51.7 1.1 collective-permute-done.11.up_ref.refs_1_
  52.8 3.1 %collective-permute-done.12.down_ref.refs_2_.refs_4_ = bf16[2,1152,256]{2,1,0:T(8,128)(2,1)S(1)} collective-permute-done((bf16[2,1152,256]{2,1,0:T(8,128)(2,1)S(1)}, bf16[2,1152,256]{2,1,0:T(8,128)(2,1)S(1)}, u32[]{:S(2)}, u32[]{:S(2)}) %collective-permute-start.12) | collective-permute-done | bytes 1179680 | tf_op jit(solution)/shard_map/ppermute | solution.py:30
  56.0 1.5 collective-permute-start.17
  58.0 1.2 collective-permute-start.14
  59.2 9.8 %shard_map.91 = (f32[2,512,1024]{2,1,0:T(8,128)S(1)}, bf16[2,512,2048]{2,1,0:T(8,128)(2,1)S(1)}, bf16[1024,256]{1,0:T(8,128)(2,1)S(1)}, bf16[1024,256]{1,0:T(8,128)(2,1)S(1)}) custom-call(s32[3]{0:T(128)S(1)} %pad_add_fusion.pos, bf16[512,4096]{1,0:T(8,128)(2,1)S(1)} %copy-done, bf16[512,4096]{1,0:T(8,128)(2,1)} %collective-permute-done.5.oth_ref, ...), custom_call_target="tpu_custom_call" | custom-call | flops 200000000 | tf_op jit(solution)/shard_map/pallas_call | solution.py:166
  69.3 0.4 collective-permute-done.14.a_low.refs_3_
  69.8 6.3 %shard_map.92 = (bf16[2,512,512]{2,1,0:T(8,128)(2,1)S(1)}, bf16[2,512,512]{2,1,0:T(8,128)(2,1)S(1)}, bf16[1024,256]{1,0:T(8,128)(2,1)S(1)}, bf16[1024,256]{1,0:T...) custom-call(s32[3]{0:T(128)S(1)} %pad_add_fusion.pos, s32[8]{0:T(128)S(1)} %pad_add_fusion.1.own_numbers, ...), custom_call_target="tpu_custom_call" | custom-call | flops 200000000 | tf_op jit(solution)/shard_map/pallas_call | solution.py:326
  76.1 11.8 %all_to_all.10.st_ref = f32[16,32,128]{2,1,0:T(8,128)S(1)} all-to-all(f32[16,32,128]{2,1,0:T(8,128)S(1)} %get-tuple-element.135), channel_id=1, replica_groups=mesh['z'=4,'x'=4,'core'=2,'dec'=4] {'z','x'}, dimensions={0} | all-to-all | bytes 524288 | tf_op jit(solution)/shard_map/all_to_all | solution.py:671
  87.9 6.0 %shard_map.93 = (bf16[4,1024,256]{2,1,0:T(8,128)(2,1)S(1)}, bf16[2,1024,256]{2,1,0:T(8,128)(2,1)S(1)}, bf16[2,1024,256]{2,1,0:T(8,128)(2,1)S(1)}, bf16[32,16,512]{2,1,0:T(8,128)(2,1)S(1)}) custom-call(s32[3]{0:T(128)S(1)} %pad_add_fusion.pos, s32[8]{0:T(128)S(1)} %pad_add_fusion.1.own_numbers, s32[8]{0:T(128)S(1)} %collective-permute-done.6.other_numbers, ...), custom_call_target="tpu_custom_call" | custom-call | flops 200000000 | tf_op jit(solution)/shard_map/pallas_call | solution.py:498
  94.0 6.6 %collective-permute-start.19 = (bf16[2,1024,256]{2,1,0:T(8,128)(2,1)S(1)}, bf16[2,1024,256]{2,1,0:T(8,128)(2,1)S(1)}, u32[]{:S(2)}, u32[]{:S(2)}) collective-permute-start(bf16[2,1024,256]{2,1,0:T(8,128)(2,1)S(1)} %get-tuple-element.137), channel_id=1, source_target_pairs={{0,4},{4,0},{1,5},{5,1},{2,6},{6,2},{3,7},{7,3},{8,12},{12,8},{9,1... | collective-permute-start | bytes 3145736 | tf_op jit(solution)/shard_map/ppermute | solution.py:30
  100.5 7.4 %shard_map.94 = (bf16[2,2,1024,256]{3,2,1,0:T(8,128)(2,1)S(1)}, bf16[2,2,1024,256]{3,2,1,0:T(8,128)(2,1)S(1)}) custom-call(s32[2]{0:T(128)S(1)} %slice.77.places, bf16[4,1024,256]{2,1,0:T(8,128)(2,1)S(1)} %get-tuple-element.153.kvg_ref, bf16[2,1152,256]{2,1,0:T(8,128)(2,1)S(1)} %shard_map.87.refs_0_, ...), custom_call_target="tpu_custom_call" | custom-call | flops 200000000 | tf_op jit(solution)/shard_map/pallas_call | solution.py:539
  108.3 1.4 collective-permute-start.20
  109.7 1.5 collective-permute-start.21
  111.2 4.9 %shard_map.95 = (f32[1,2,1024,256]{3,2,1,0:T(8,128)S(1)}, bf16[1,2,1024,256]{3,2,1,0:T(8,128)(2,1)}) custom-call(s32[1]{0:T(128)} %get-tuple-element.152.places, bf16[4,1024,256]{2,1,0:T(8,128)(2,1)S(1)} %get-tuple-element.153.kvg_ref, bf16[2,1152,256]{2,1,0:T(8,128)(2,1)S(1)} %shard_map.87.refs_0_, ...), custom_call_target="tpu_custom_call" | custom-call | flops 200000000 | tf_op jit(solution)/shard_map/pallas_call | solution.py:539
  116.1 6.7 %collective-permute-done.20.below_ref = bf16[2,512,256]{2,1,0:T(8,128)(2,1)S(1)} collective-permute-done((bf16[2,512,256]{2,1,0:T(8,128)(2,1)S(1)}, bf16[2,512,256]{2,1,0:T(8,128)(2,1)S(1)}, u32[]{:S(2)}, u32[]{:S(2)}) %collective-permute-start.20) | collective-permute-done | bytes 524320 | tf_op jit(solution)/shard_map/ppermute | solution.py:30
  122.8 1.7 %shard_map.96 = (bf16[2,512,256]{2,1,0:T(8,128)(2,1)}, bf16[2,512,256]{2,1,0:T(8,128)(2,1)}, bf16[2,512,256]{2,1,0:T(8,128)(2,1)}, bf16[2,512,256]{2,1,0:T(8,128)(2,1)}) custom-call(bf16[2,2,1024,256]{3,2,1,0:T(8,128)(2,1)S(1)} %get-tuple-element.143.own_ref, bf16[2,2,1024,256]{3,2,1,0:T(8,128)(2,1)S(1)} %collective-permute-done.22.got_ref, ...), custom_call_target="tpu_custom_call" | custom-call | flops 200000000 | tf_op jit(solution)/shard_map/pallas_call | solution.py:573
  124.5 1.2 collective-permute-start.27
  125.7 1.3 collective-permute-start.23
  127.0 1.4 collective-permute-start.24
  128.5 2.6 %collective-permute-start.26 = (bf16[2,512,256]{2,1,0:T(8,128)(2,1)}, bf16[2,512,256]{2,1,0:T(8,128)(2,1)}, u32[]{:S(2)}, u32[]{:S(2)}) collective-permute-start(bf16[2,512,256]{2,1,0:T(8,128)(2,1)} %get-tuple-element.169), channel_id=1, source_target_pairs={{0,3},{1,0},{2,1},{3,2},{4,7},{5,4},{6,5},{7,6},{8,11},{9,8},{10,9... | collective-permute-start | bytes 1572872 | tf_op jit(solution)/shard_map/ppermute | solution.py:30
  131.1 4.3 %all-to-all-start.1 = ((bf16[16,2,16,512]{3,2,1,0:T(8,128)(2,1)}), bf16[16,2,16,512]{3,2,1,0:T(8,128)(2,1)}, u32[]{:S(2)}, u32[]{:S(2)}) async-start(bf16[16,2,16,512]{3,2,1,0:T(8,128)(2,1)} %bitcast.14), calls=%async_computation.1 | async-start | bytes 1048576 | tf_op jit(solution)/shard_map/all_to_all | solution.py:703
  135.4 10.5 %all-to-all-done.1 = bf16[16,2,16,512]{3,2,1,0:T(8,128)(2,1)} async-done(((bf16[16,2,16,512]{3,2,1,0:T(8,128)(2,1)}), bf16[16,2,16,512]{3,2,1,0:T(8,128)(2,1)}, u32[]{:S(2)}, u32[]{:S(2)}) %all-to-all-start.1) | async-done | bytes 524320 | tf_op jit(solution)/shard_map/all_to_all | solution.py:703
  145.9 6.2 %collective-permute-done.25.up_top = bf16[2,512,256]{2,1,0:T(8,128)(2,1)} collective-permute-done((bf16[2,512,256]{2,1,0:T(8,128)(2,1)}, bf16[2,512,256]{2,1,0:T(8,128)(2,1)}, u32[]{:S(2)}, u32[]{:S(2)}) %collective-permute-start.25) | collective-permute-done | bytes 524320 | tf_op jit(solution)/shard_map/ppermute | solution.py:30
  152.1 1.1 convert_reduce_fusion
  153.3 0.8 collective-permute-start.28
  154.1 5.0 %shard_map.97 = f32[512,1024]{1,0:T(8,128)} custom-call(s32[4]{0:T(128)S(1)} %get-tuple-element.173.place, f32[2,1024,256]{2,1,0:T(8,128)S(1)} %bitcast.13, bf16[2,1024,256]{2,1,0:T(8,128)(2,1)S(1)} %collective-permute-done.27.core_ref, bf16[2,512,256]{2,1,0:T(8,128)(2,1)} %collective-permute-done.25.up_top, ...), custom_call_target="tpu_custom_call" | custom-call | flops 200000000 | tf_op jit(solution)/shard_map/pallas_call | solution.py:599
  159.2 0.6 maximum_select_fusion
  (52 shorter events, 2.5 us)
Async XLA Ops:
  1.8 2.7 %collective-permute-start = (bf16[288,512]{1,0:T(8,128)(2,1)S(1)}, bf16[288,512]{1,0:T(8,128)(2,1)S(1)}, u32[]{:S(2)}, u32[]{:S(2)}) collective-permute-start(bf16[288,512]{1,0:T(8,128)(2,1)S(1)} %constant_dynamic-slice_fusion.1), channel_id=1, source_target_pairs={{0,4},{4,0},{1,5},{5,1},{2,6},{6,2},{3,7},{7,3},{8,12},{12,8},{9,1... | collective-permute-start | bytes 884744 | tf_op jit(solution)/shard_map/ppermute | solution.py:30
  4.5 21.5 %collective-permute-start.5 = (bf16[512,4096]{1,0:T(8,128)(2,1)}, bf16[512,4096]{1,0:T(8,128)(2,1)}, u32[]{:S(2)}, u32[]{:S(2)}) collective-permute-start(bf16[512,4096]{1,0:T(8,128)(2,1)} %own_ref.1), channel_id=1, source_target_pairs={{0,4},{4,0},{1,5},{5,1},{2,6},{6,2},{3,7},{7,3},{8,12},{12,8},{9,1... | collective-permute-start | bytes 12582920 | tf_op jit(solution)/shard_map/ppermute | solution.py:30
  5.1 13.9 %copy-start.2 = (s32[4,1]{0,1:T(1,128)S(1)}, s32[4,1]{0,1:T(1,128)}, u32[]{:S(2)}) copy-start(s32[4,1]{0,1:T(1,128)} %param.13) | copy-start | bytes 52
  5.2 13.9 %copy-start.3 = (s32[1,4]{1,0:T(1,128)S(1)}, s32[1,4]{1,0:T(1,128)}, u32[]{:S(2)}) copy-start(s32[1,4]{1,0:T(1,128)} %param.12) | copy-start | bytes 52
  5.2 8.4 %collective-permute-start.1 = (bf16[288,256]{1,0:T(8,128)(2,1)S(1)}, bf16[288,256]{1,0:T(8,128)(2,1)S(1)}, u32[]{:S(2)}, u32[]{:S(2)}) collective-permute-start(bf16[288,256]{1,0:T(8,128)(2,1)S(1)} %get-tuple-element.92.refs_0_), channel_id=1, source_target_pairs={{0,8},{8,0},{16,24},{24,16},{1,9},{9,1},{17,25},{25,17},{2,10},{10... | collective-permute-start | bytes 442376 | tf_op jit(solution)/shard_map/ppermute | solution.py:43
  6.6 7.0 %collective-permute-start.2 = (bf16[288,256]{1,0:T(8,128)(2,1)S(1)}, bf16[288,256]{1,0:T(8,128)(2,1)S(1)}, u32[]{:S(2)}, u32[]{:S(2)}) collective-permute-start(bf16[288,256]{1,0:T(8,128)(2,1)S(1)} %get-tuple-element.93.refs_2_), channel_id=1, source_target_pairs={{0,24},{8,16},{16,8},{24,0},{1,25},{9,17},{17,9},{25,1},{2,26},{10... | collective-permute-start | bytes 442376 | tf_op jit(solution)/shard_map/ppermute | solution.py:43
  8.4 5.2 %collective-permute-start.3 = (bf16[288,256]{1,0:T(8,128)(2,1)S(1)}, bf16[288,256]{1,0:T(8,128)(2,1)S(1)}, u32[]{:S(2)}, u32[]{:S(2)}) collective-permute-start(bf16[288,256]{1,0:T(8,128)(2,1)S(1)} %get-tuple-element.94.refs_4_), channel_id=1, source_target_pairs={{0,32},{32,0},{64,96},{96,64},{1,33},{33,1},{65,97},{97,65},{2,34}... | collective-permute-start | bytes 442376 | tf_op jit(solution)/shard_map/ppermute | solution.py:43
  10.0 5.6 %collective-permute-start.4 = (bf16[288,256]{1,0:T(8,128)(2,1)S(1)}, bf16[288,256]{1,0:T(8,128)(2,1)S(1)}, u32[]{:S(2)}, u32[]{:S(2)}) collective-permute-start(bf16[288,256]{1,0:T(8,128)(2,1)S(1)} %get-tuple-element.95.refs_6_), channel_id=1, source_target_pairs={{0,96},{32,64},{64,32},{96,0},{1,97},{33,65},{65,33},{97,1},{2,98}... | collective-permute-start | bytes 442376 | tf_op jit(solution)/shard_map/ppermute | solution.py:43
  15.7 6.7 %collective-permute-start.10 = (bf16[576,256]{1,0:T(8,128)(2,1)S(1)}, bf16[576,256]{1,0:T(8,128)(2,1)S(1)}, u32[]{:S(2)}, u32[]{:S(2)}) collective-permute-start(bf16[576,256]{1,0:T(8,128)(2,1)S(1)} %get-tuple-element.106.joined1), channel_id=1, source_target_pairs={{0,32},{32,0},{64,96},{96,64},{1,33},{33,1},{65,97},{97,65},{2,34}... | collective-permute-start | bytes 884744 | tf_op jit(solution)/shard_map/ppermute | solution.py:43
  16.4 8.8 %collective-permute-start.9 = (bf16[576,256]{1,0:T(8,128)(2,1)S(1)}, bf16[576,256]{1,0:T(8,128)(2,1)S(1)}, u32[]{:S(2)}, u32[]{:S(2)}) collective-permute-start(bf16[576,256]{1,0:T(8,128)(2,1)S(1)} %get-tuple-element.105.joined0), channel_id=1, source_target_pairs={{0,96},{32,64},{64,32},{96,0},{1,97},{33,65},{65,33},{97,1},{2,98}... | collective-permute-start | bytes 884744 | tf_op jit(solution)/shard_map/ppermute | solution.py:43
  18.2 7.2 %collective-permute-start.7 = (bf16[576,256]{1,0:T(8,128)(2,1)S(1)}, bf16[576,256]{1,0:T(8,128)(2,1)S(1)}, u32[]{:S(2)}, u32[]{:S(2)}) collective-permute-start(bf16[576,256]{1,0:T(8,128)(2,1)S(1)} %get-tuple-element.103.joined0), channel_id=1, source_target_pairs={{0,24},{8,16},{16,8},{24,0},{1,25},{9,17},{17,9},{25,1},{2,26},{10... | collective-permute-start | bytes 884744 | tf_op jit(solution)/shard_map/ppermute | solution.py:43
  19.0 6.4 %collective-permute-start.8 = (bf16[576,256]{1,0:T(8,128)(2,1)S(1)}, bf16[576,256]{1,0:T(8,128)(2,1)S(1)}, u32[]{:S(2)}, u32[]{:S(2)}) collective-permute-start(bf16[576,256]{1,0:T(8,128)(2,1)S(1)} %get-tuple-element.104.joined1), channel_id=1, source_target_pairs={{0,8},{8,0},{16,24},{24,16},{1,9},{9,1},{17,25},{25,17},{2,10},{10... | collective-permute-start | bytes 884744 | tf_op jit(solution)/shard_map/ppermute | solution.py:43
  22.4 3.6 %collective-permute-start.6 = (s32[8]{0:T(128)S(1)}, s32[8]{0:T(128)S(1)}, u32[]{:S(2)}, u32[]{:S(2)}) collective-permute-start(s32[8]{0:T(128)S(1)} %pad_add_fusion.1.own_numbers), channel_id=1, source_target_pairs={{0,4},{4,0},{1,5},{5,1},{2,6},{6,2},{3,7},{7,3},{8,12},{12,8},{9,1... | collective-permute-start | bytes 104 | tf_op jit(solution)/shard_map/ppermute | solution.py:30
  26.0 24.5 %collective-permute-start.15 = (bf16[2,1152,256]{2,1,0:T(8,128)(2,1)S(1)}, bf16[2,1152,256]{2,1,0:T(8,128)(2,1)S(1)}, u32[]{:S(2)}, u32[]{:S(2)}) collective-permute-start(bf16[2,1152,256]{2,1,0:T(8,128)(2,1)S(1)} %shard_map.88.refs_3_.refs_5_), channel_id=1, source_target_pairs={{0,24},{8,0},{16,8},{24,16},{1,25},{9,1},{17,9},{25,17},{2,26},{10... | collective-permute-start | bytes 3538952 | tf_op jit(solution)/shard_map/ppermute | solution.py:30
  26.9 24.8 %collective-permute-start.16 = (bf16[2,1152,256]{2,1,0:T(8,128)(2,1)S(1)}, bf16[2,1152,256]{2,1,0:T(8,128)(2,1)S(1)}, u32[]{:S(2)}, u32[]{:S(2)}) collective-permute-start(bf16[2,1152,256]{2,1,0:T(8,128)(2,1)S(1)} %shard_map.88.refs_3_.refs_5_), channel_id=1, source_target_pairs={{0,8},{8,16},{16,24},{24,0},{1,9},{9,17},{17,25},{25,1},{2,10},{10... | collective-permute-start | bytes 3538952 | tf_op jit(solution)/shard_map/ppermute | solution.py:30
  27.5 25.3 %collective-permute-start.11 = (bf16[2,1152,256]{2,1,0:T(8,128)(2,1)S(1)}, bf16[2,1152,256]{2,1,0:T(8,128)(2,1)S(1)}, u32[]{:S(2)}, u32[]{:S(2)}) collective-permute-start(bf16[2,1152,256]{2,1,0:T(8,128)(2,1)S(1)} %shard_map.87.refs_0_), channel_id=1, source_target_pairs={{0,96},{32,0},{64,32},{96,64},{1,97},{33,1},{65,33},{97,65},{2,98}... | collective-permute-start | bytes 3538952 | tf_op jit(solution)/shard_map/ppermute | solution.py:30
  29.7 26.2 %collective-permute-start.12 = (bf16[2,1152,256]{2,1,0:T(8,128)(2,1)S(1)}, bf16[2,1152,256]{2,1,0:T(8,128)(2,1)S(1)}, u32[]{:S(2)}, u32[]{:S(2)}) collective-permute-start(bf16[2,1152,256]{2,1,0:T(8,128)(2,1)S(1)} %shard_map.87.refs_0_), channel_id=1, source_target_pairs={{0,32},{32,64},{64,96},{96,0},{1,33},{33,65},{65,97},{97,1},{2,34}... | collective-permute-start | bytes 3538952 | tf_op jit(solution)/shard_map/ppermute | solution.py:30
  55.9 3.3 %copy-start = (bf16[512,4096]{1,0:T(8,128)(2,1)S(1)}, bf16[512,4096]{1,0:T(8,128)(2,1)}, u32[]{:S(2)}) copy-start(bf16[512,4096]{1,0:T(8,128)(2,1)} %own_ref.1) | copy-start | bytes 12582916
  56.0 13.0 %collective-permute-start.17 = (bf16[1152,256]{1,0:T(8,128)(2,1)S(1)}, bf16[1152,256]{1,0:T(8,128)(2,1)S(1)}, u32[]{:S(2)}, u32[]{:S(2)}) collective-permute-start(bf16[1152,256]{1,0:T(8,128)(2,1)S(1)} %get-tuple-element.116), channel_id=1, source_target_pairs={{0,24},{8,0},{16,8},{24,16},{1,25},{9,1},{17,9},{25,17},{2,26},{10... | collective-permute-start | bytes 1769480 | tf_op jit(solution)/shard_map/ppermute | solution.py:30
  57.6 11.8 %collective-permute-start.18 = (bf16[1152,256]{1,0:T(8,128)(2,1)S(1)}, bf16[1152,256]{1,0:T(8,128)(2,1)S(1)}, u32[]{:S(2)}, u32[]{:S(2)}) collective-permute-start(bf16[1152,256]{1,0:T(8,128)(2,1)S(1)} %get-tuple-element.117), channel_id=1, source_target_pairs={{0,8},{8,16},{16,24},{24,0},{1,9},{9,17},{17,25},{25,1},{2,10},{10... | collective-permute-start | bytes 1769480 | tf_op jit(solution)/shard_map/ppermute | solution.py:30
  57.6 11.7 %collective-permute-start.13 = (bf16[1152,256]{1,0:T(8,128)(2,1)S(1)}, bf16[1152,256]{1,0:T(8,128)(2,1)S(1)}, u32[]{:S(2)}, u32[]{:S(2)}) collective-permute-start(bf16[1152,256]{1,0:T(8,128)(2,1)S(1)} %get-tuple-element.111), channel_id=1, source_target_pairs={{0,96},{32,0},{64,32},{96,64},{1,97},{33,1},{65,33},{97,65},{2,98}... | collective-permute-start | bytes 1769480 | tf_op jit(solution)/shard_map/ppermute | solution.py:30
  58.0 11.8 %collective-permute-start.14 = (bf16[1152,256]{1,0:T(8,128)(2,1)S(1)}, bf16[1152,256]{1,0:T(8,128)(2,1)S(1)}, u32[]{:S(2)}, u32[]{:S(2)}) collective-permute-start(bf16[1152,256]{1,0:T(8,128)(2,1)S(1)} %get-tuple-element.112), channel_id=1, source_target_pairs={{0,32},{32,64},{64,96},{96,0},{1,33},{33,65},{65,97},{97,1},{2,34}... | collective-permute-start | bytes 1769480 | tf_op jit(solution)/shard_map/ppermute | solution.py:30
  94.0 14.0 %copy-start.1 = (bf16[32,16,512]{2,1,0:T(8,128)(2,1)}, bf16[32,16,512]{2,1,0:T(8,128)(2,1)S(1)}, u32[]{:S(2)}) copy-start(bf16[32,16,512]{2,1,0:T(8,128)(2,1)S(1)} %get-tuple-element.171) | copy-start | bytes 1572868
  94.0 14.0 %collective-permute-start.19 = (bf16[2,1024,256]{2,1,0:T(8,128)(2,1)S(1)}, bf16[2,1024,256]{2,1,0:T(8,128)(2,1)S(1)}, u32[]{:S(2)}, u32[]{:S(2)}) collective-permute-start(bf16[2,1024,256]{2,1,0:T(8,128)(2,1)S(1)} %get-tuple-element.137), channel_id=1, source_target_pairs={{0,4},{4,0},{1,5},{5,1},{2,6},{6,2},{3,7},{7,3},{8,12},{12,8},{9,1... | collective-permute-start | bytes 3145736 | tf_op jit(solution)/shard_map/ppermute | solution.py:30
  108.2 14.6 %collective-permute-start.22 = (bf16[2,2,1024,256]{3,2,1,0:T(8,128)(2,1)S(1)}, bf16[2,2,1024,256]{3,2,1,0:T(8,128)(2,1)S(1)}, u32[]{:S(2)}, u32[]{:S(2)}) collective-permute-start(bf16[2,2,1024,256]{3,2,1,0:T(8,128)(2,1)S(1)} %get-tuple-element.151), channel_id=1, source_target_pairs={{0,4},{4,0},{1,5},{5,1},{2,6},{6,2},{3,7},{7,3},{8,12},{12,8},{9,1... | collective-permute-start | bytes 6291464 | tf_op jit(solution)/shard_map/ppermute | solution.py:30
  108.3 14.5 %collective-permute-start.20 = (bf16[2,512,256]{2,1,0:T(8,128)(2,1)S(1)}, bf16[2,512,256]{2,1,0:T(8,128)(2,1)S(1)}, u32[]{:S(2)}, u32[]{:S(2)}) collective-permute-start(bf16[2,512,256]{2,1,0:T(8,128)(2,1)S(1)} %get-tuple-element.149), channel_id=1, source_target_pairs={{0,1},{1,2},{2,3},{3,0},{4,5},{5,6},{6,7},{7,4},{8,9},{9,10},{10,1... | collective-permute-start | bytes 1572872 | tf_op jit(solution)/shard_map/ppermute | solution.py:30
  109.7 13.1 %collective-permute-start.21 = (bf16[2,512,256]{2,1,0:T(8,128)(2,1)S(1)}, bf16[2,512,256]{2,1,0:T(8,128)(2,1)S(1)}, u32[]{:S(2)}, u32[]{:S(2)}) collective-permute-start(bf16[2,512,256]{2,1,0:T(8,128)(2,1)S(1)} %get-tuple-element.150), channel_id=1, source_target_pairs={{0,3},{1,0},{2,1},{3,2},{4,7},{5,4},{6,5},{7,6},{8,11},{9,8},{10,9... | collective-permute-start | bytes 1572872 | tf_op jit(solution)/shard_map/ppermute | solution.py:30
  124.5 27.7 %collective-permute-start.27 = (bf16[2,1024,256]{2,1,0:T(8,128)(2,1)}, bf16[2,1024,256]{2,1,0:T(8,128)(2,1)S(1)}, u32[]{:S(2)}, u32[]{:S(2)}) collective-permute-start(bf16[2,1024,256]{2,1,0:T(8,128)(2,1)} %bitcast.7), channel_id=1, source_target_pairs={{0,4},{4,0},{1,5},{5,1},{2,6},{6,2},{3,7},{7,3},{8,12},{12,8},{9,1... | collective-permute-start | bytes 3145736 | tf_op jit(solution)/shard_map/ppermute | solution.py:30
  125.7 20.2 %collective-permute-start.23 = (bf16[2,512,256]{2,1,0:T(8,128)(2,1)}, bf16[2,512,256]{2,1,0:T(8,128)(2,1)}, u32[]{:S(2)}, u32[]{:S(2)}) collective-permute-start(bf16[2,512,256]{2,1,0:T(8,128)(2,1)} %get-tuple-element.166), channel_id=1, source_target_pairs={{0,1},{1,2},{2,3},{3,0},{4,5},{5,6},{6,7},{7,4},{8,9},{9,10},{10,1... | collective-permute-start | bytes 1572872 | tf_op jit(solution)/shard_map/ppermute | solution.py:30
  127.0 18.9 %collective-permute-start.24 = (bf16[2,512,256]{2,1,0:T(8,128)(2,1)}, bf16[2,512,256]{2,1,0:T(8,128)(2,1)}, u32[]{:S(2)}, u32[]{:S(2)}) collective-permute-start(bf16[2,512,256]{2,1,0:T(8,128)(2,1)} %get-tuple-element.167), channel_id=1, source_target_pairs={{0,3},{1,0},{2,1},{3,2},{4,7},{5,4},{6,5},{7,6},{8,11},{9,8},{10,9... | collective-permute-start | bytes 1572872 | tf_op jit(solution)/shard_map/ppermute | solution.py:30
  128.4 23.7 %collective-permute-start.25 = (bf16[2,512,256]{2,1,0:T(8,128)(2,1)}, bf16[2,512,256]{2,1,0:T(8,128)(2,1)}, u32[]{:S(2)}, u32[]{:S(2)}) collective-permute-start(bf16[2,512,256]{2,1,0:T(8,128)(2,1)} %get-tuple-element.168), channel_id=1, source_target_pairs={{0,1},{1,2},{2,3},{3,0},{4,5},{5,6},{6,7},{7,4},{8,9},{9,10},{10,1... | collective-permute-start | bytes 1572872 | tf_op jit(solution)/shard_map/ppermute | solution.py:30
  128.5 23.7 %collective-permute-start.26 = (bf16[2,512,256]{2,1,0:T(8,128)(2,1)}, bf16[2,512,256]{2,1,0:T(8,128)(2,1)}, u32[]{:S(2)}, u32[]{:S(2)}) collective-permute-start(bf16[2,512,256]{2,1,0:T(8,128)(2,1)} %get-tuple-element.169), channel_id=1, source_target_pairs={{0,3},{1,0},{2,1},{3,2},{4,7},{5,4},{6,5},{7,6},{8,11},{9,8},{10,9... | collective-permute-start | bytes 1572872 | tf_op jit(solution)/shard_map/ppermute | solution.py:30
  131.1 14.8 %all-to-all-start.1 = ((bf16[16,2,16,512]{3,2,1,0:T(8,128)(2,1)}), bf16[16,2,16,512]{3,2,1,0:T(8,128)(2,1)}, u32[]{:S(2)}, u32[]{:S(2)}) async-start(bf16[16,2,16,512]{3,2,1,0:T(8,128)(2,1)} %bitcast.14), calls=%async_computation.1 | async-start | bytes 1048576 | tf_op jit(solution)/shard_map/all_to_all | solution.py:703
  153.3 5.9 %collective-permute-start.28 = (f32[16,512]{1,0:T(8,128)S(1)}, f32[16,512]{1,0:T(8,128)S(1)}, u32[]{:S(2)}, u32[]{:S(2)}) collective-permute-start(f32[16,512]{1,0:T(8,128)S(1)} %get-tuple-element.194), channel_id=1, source_target_pairs={{0,4},{4,0},{1,5},{5,1},{2,6},{6,2},{3,7},{7,3},{8,12},{12,8},{9,1... | collective-permute-start | bytes 98312 | tf_op jit(solution)/shard_map/ppermute | solution.py:30

commit v4 on v3

--- a/solution.py
+++ b/solution.py
@@ -1,5 +1,3 @@
-import functools
-
 import jax
 import jax.numpy as jnp
 from jax import lax
@@ -115,6 +113,18 @@
     )(up, down)
 
 
+def key_value(halves):
+    rows = []
+    for half in halves:
+        for at in (0, PIECE):
+            rows.append(
+                jnp.concatenate(
+                    [half[at : at + CHUNK, :], half[at + CHUNK : at + 2 * CHUNK, :]], axis=1
+                )
+            )
+    return jnp.concatenate(rows, axis=0)
+
+
 def near_kernel(pos, own_ref, oth_ref, *refs):
     blocks, (acc_ref, enc_ref, qa_ref, qb_ref) = refs[:6], refs[6:]
     z, x = pos[0], pos[1]
@@ -130,20 +140,16 @@
 
     def run(ref):
         for side in range(2):
-            totals = [None, None]
+            total = None
             for b, outer in enumerate((0, 1, 3)):
-                for h in range(2):
-                    lhs = columns(ref, side, outer, (h * 2, h * 2 + 1))
-                    block = blocks[side * 3 + b].at[h]
-                    for t in range(2):
-                        rhs = jnp.concatenate(
-                            [block[at + t * 256 : at + t * 256 + 256] for at in (0, PIECE)], axis=0
-                        )
-                        term = jnp.dot(lhs, rhs, preferred_element_type=F32)
-                        totals[t] = term if totals[t] is None else totals[t] + term
+                block = blocks[side * 3 + b]
+                rhs = key_value([block.at[h] for h in range(2)])
+                lhs = columns(ref, side, outer, range(4))
+                term = jnp.dot(lhs, rhs, preferred_element_type=F32)
+                total = term if total is None else total + term
             for t in range(2):
                 at = t * HALF + side * CHUNK
-                acc_ref[0, :, at : at + CHUNK] = totals[t]
+                acc_ref[0, :, at : at + CHUNK] = total[:, t * CHUNK : (t + 1) * CHUNK]
             enc_ref[0, :, side * 1024 : (side + 1) * 1024] = columns(ref, side, 2, range(4))
 
     pl.when(step < 2)(lambda: run(own_ref))
@@ -287,31 +293,20 @@
                 at = (8 + inner) * 64
                 out[at : at + 64, :] = far[side][inner // 2][row : row + 64, :]
 
-    row0 = pl.multiple_of((step % 2) * (ROWS // 2), ROWS // 2)
     for side in range(2):
         lhs = enc_ref[0, :, side * 1024 : (side + 1) * 1024]
+        total = jnp.dot(lhs, key_value(far[side]), preferred_element_type=F32)
         for t, out in ((0, k_ref), (1, v_ref)):
-            rhs = jnp.concatenate(
-                [
-                    far[side][inner // 2][(inner % 2) * PIECE + t * 256 : (inner % 2) * PIECE + t * 256 + 256]
-                    for inner in range(4)
-                ],
-                axis=0,
-            )
             at = t * HALF + side * CHUNK
-            total = acc_ref[0, :, at : at + CHUNK] + jnp.dot(
-                lhs, rhs, preferred_element_type=F32
-            )
-            out[step // 2, pl.ds(row0, ROWS // 2), side * CHUNK : (side + 1) * CHUNK] = total.astype(BF)
+            part = total[:, t * CHUNK : (t + 1) * CHUNK] + acc_ref[0, :, at : at + CHUNK]
+            out[step, :, side * CHUNK : (side + 1) * CHUNK] = part.astype(BF)
     for side in range(2):
-        @pl.when(step == side * 2 + 1)
+        @pl.when(step == side)
         def attend():
             forward_side(side, meta, k_ref, v_ref, (qa_ref, qb_ref), st_ref, num_ref)
 
 
 def project_far(meta, enc_far, acc, blocks, qa, qb):
-    tile = ROWS // 2
-
     def whole(shape):
         return pl.BlockSpec(shape, lambda i, *m: (0,) * len(shape))
 
@@ -327,10 +322,10 @@
         far_kernel,
         grid_spec=pltpu.PrefetchScalarGridSpec(
             num_scalar_prefetch=3,
-            grid=(4,),
+            grid=(2,),
             in_specs=[
-                pl.BlockSpec((1, tile, 2048), lambda i, *m: (i // 2, i % 2, 0)),
-                pl.BlockSpec((1, tile, 2 * HALF), lambda i, *m: (i // 2, i % 2, 0)),
+                pl.BlockSpec((1, ROWS, 2048), lambda i, *m: (i, 0, 0)),
+                pl.BlockSpec((1, ROWS, 2 * HALF), lambda i, *m: (i, 0, 0)),
             ]
             + [whole(b.shape) for b in blocks]
             + [whole((1024, CHUNK))] * 2,
@@ -375,42 +370,27 @@
     return tops, inverse, deltas
 
 
-def weight_copy(ref, row, w_ref, sems, side, n):
-    return pltpu.make_async_copy(
-        ref.at[pl.ds(row, 2 * CHUNK)], w_ref.at[side, n], sems.at[side, n]
-    )
-
-
-def wait_copies(sources, w_ref, sems):
-    for side in range(2):
-        for n in range(4):
-            weight_copy(sources[2], 0, w_ref, sems, side, n).wait()
-
-
-def start_copies(place, sources, w_ref, sems):
+def take_weights(place, sources, w_ref):
     a_own, a_up, a_top, a_low, a_down, b_own, b_up, b_top, b_low, b_down = sources
-
-    def copy(ref, row, side, n):
-        return weight_copy(ref, row, w_ref, sems, side, n)
-
+    both = 2 * CHUNK
     for outer in range(4):
         @pl.when(place == outer)
-        def start_a():
+        def take_a():
             for n in range(4):
-                half = {
-                    0: a_own.at[n // 2],
-                    1: a_up.at[n // 2],
-                    2: (a_top, a_low)[n // 2],
-                    3: a_down.at[n // 2],
-                }[outer]
-                copy(half, (n % 2) * PIECE, 0, n).start()
+                rows = pl.ds((n % 2) * PIECE, both)
+                if outer == 2:
+                    w_ref[0, n] = (a_top, a_low)[n // 2][rows, :]
+                else:
+                    w_ref[0, n] = (a_own, a_up, None, a_down)[outer][n // 2, rows, :]
 
     upper = place // 2
-    row = pl.multiple_of((place % 2) * PIECE, 64)
+    rows = pl.ds(pl.multiple_of((place % 2) * PIECE, 64), both)
     for n, ref in ((0, b_own), (1, b_up), (3, b_down)):
-        copy(ref.at[upper], row, 1, n).start()
+        w_ref[1, n] = ref[upper, rows, :]
     for h, ref in ((0, b_top), (1, b_low)):
-        pl.when(upper == h)(copy(ref, row, 1, 2).start)
+        @pl.when(upper == h)
+        def take_b():
+            w_ref[1, 2] = ref[rows, :]
 
 
 def weights_tile(w_ref):
@@ -424,24 +404,22 @@
     return jnp.concatenate(rows, axis=0)
 
 
-WEIGHT_SPECS = [pl.BlockSpec(memory_space=pltpu.HBM)] * 10
-
-
-def weight_scratch(count):
-    return [
-        pltpu.VMEM((count, 2, 4, 2 * CHUNK, CHUNK), BF),
-        pltpu.SemaphoreType.DMA((count, 2, 4)),
-    ]
+def weight_specs():
+    shape = (2, 2 * PIECE, CHUNK)
+    block = pl.BlockSpec(shape, lambda i, *p: (0, 0, 0), pipeline_mode=pl.Buffered(1))
+    half = pl.BlockSpec(shape[1:], lambda i, *p: (0, 0), pipeline_mode=pl.Buffered(1))
+    return [block, block, half, half, block] * 2
+
+
+WEIGHT_SCRATCH = pltpu.VMEM((2, 4, 2 * CHUNK, CHUNK), BF)
 
 
 def backward_kernel(
     pos, own_numbers, other_numbers, k_ref, v_ref, qa_ref, qb_ref, st_ref, num_ref, *refs
 ):
     sources, outs = refs[:10], refs[10:]
-    kvg_ref, own_ref, oth_ref, dense_ref, ctx_ref, w_ref, sems = outs
-    w_ref = w_ref.at[0]
-    sems = sems.at[0]
-    start_copies(pos[2], sources, w_ref, sems)
+    kvg_ref, own_ref, oth_ref, dense_ref, ctx_ref, w_ref = outs
+    take_weights(pos[2], sources, w_ref)
     meta = Passages(pos, own_numbers, other_numbers)
     qg = (qa_ref, qb_ref)
     tops, inverses, deltas = combine(meta, st_ref)
@@ -465,23 +443,17 @@
                 turned = lax.dot_general(
                     lanes, weight, (((0,), (1,)), ((), ())), preferred_element_type=F32
                 ).astype(BF)
-                for n in range(2):
-                    kvg_ref[
-                        side * 2 + n, t * HALF + pair * 128 : t * HALF + (pair + 1) * 128, :
-                    ] = turned[:, n * 256 : (n + 1) * 256]
+                first = t * HALF + pair * 128
+                kvg_ref[first : first + 128, side * ROWS : (side + 1) * ROWS] = turned
             scale = jnp.exp(st_ref[here, at : at + 1, :] - top) * inverse
             context = (num_ref[side, pair] * scale).T
             for p in range(NPASS):
                 ctx_ref[meta.question(side, p), :, cols] += jnp.where(
                     low, context[p * 32 : p * 32 + 16], context[p * 32 + 16 : p * 32 + 32]
                 )
-        if side == 1:
-            wait_copies(sources, w_ref, sems)
-        out = (own_ref, oth_ref)[side]
-        for n in range(2):
-            out[n] = jnp.dot(
-                weights_tile(w_ref), kvg_ref[side * 2 + n], preferred_element_type=F32
-            ).astype(BF)
+    total = jnp.dot(weights_tile(w_ref), kvg_ref[...], preferred_element_type=F32)
+    own_ref[...] = total[:, :ROWS].astype(BF)
+    oth_ref[...] = total[:, ROWS:].astype(BF)
     dense_ref[...] = ctx_ref[...].astype(BF)
 
 
@@ -490,9 +462,9 @@
         return pl.BlockSpec(shape, lambda i, *m: (0,) * len(shape))
 
     shapes = [
-        jax.ShapeDtypeStruct((4, 2 * HALF, ROWS // 2), BF),
-        jax.ShapeDtypeStruct((2, 1024, ROWS // 2), BF),
-        jax.ShapeDtypeStruct((2, 1024, ROWS // 2), BF),
+        jax.ShapeDtypeStruct((2 * HALF, 2 * ROWS), BF),
+        jax.ShapeDtypeStruct((1024, ROWS), BF),
+        jax.ShapeDtypeStruct((1024, ROWS), BF),
         jax.ShapeDtypeStruct((32, DEC, HALF), BF),
     ]
     return pl.pallas_call(
@@ -501,61 +473,41 @@
             num_scalar_prefetch=3,
             grid=(1,),
             in_specs=[whole(a.shape) for a in args]
-            + WEIGHT_SPECS,
+            + weight_specs(),
             out_specs=[whole(s.shape) for s in shapes],
-            scratch_shapes=[pltpu.VMEM((32, DEC, HALF), F32)] + weight_scratch(1),
+            scratch_shapes=[pltpu.VMEM((32, DEC, HALF), F32), WEIGHT_SCRATCH],
         ),
         out_shape=shapes,
-        compiler_params=params(24),
+        compiler_params=params(34),
         cost_estimate=HIDDEN,
     )(*meta, *args, *weights)
 
 
-def grad_kernel(count, places, kvg_ref, *refs):
-    sources, (own_ref, oth_ref, w_ref, sems) = refs[:10], refs[10:]
-    step = pl.program_id(0)
-    for k in range(count):
-        @pl.when(step == 4 * k)
-        def load():
-            first = range(count) if k == 0 else ()
-            for n in first:
-                start_copies(places[n], sources, w_ref.at[n], sems.at[n])
-            wait_copies(sources, w_ref.at[k], sems.at[k])
-
-    total = jnp.dot(weights_tile(w_ref.at[step // 4]), kvg_ref[0], preferred_element_type=F32)
-
-    @pl.when(step % 4 < 2)
-    def other():
-        oth_ref[0, 0] = total.astype(oth_ref.dtype)
-
-    @pl.when(step % 4 >= 2)
-    def own():
-        own_ref[0, 0] = total.astype(own_ref.dtype)
+def grad_kernel(places, kvg_ref, *refs):
+    sources, (own_ref, oth_ref, w_ref) = refs[:10], refs[10:]
+    take_weights(places[pl.program_id(0)], sources, w_ref)
+    total = jnp.dot(weights_tile(w_ref), kvg_ref[...], preferred_element_type=F32)
+    own_ref[0] = total[:, :ROWS].astype(own_ref.dtype)
+    oth_ref[0] = total[:, ROWS:].astype(oth_ref.dtype)
 
 
 def grad_blocks(places, kvg, weights, dtype):
-    tile = ROWS // 2
     count = places.shape[0]
-    return pl.pallas_call(
-        functools.partial(grad_kernel, count),
+    out = pl.BlockSpec((1, 1024, ROWS), lambda i, p: (i, 0, 0))
+    return pl.pallas_call(
+        grad_kernel,
         grid_spec=pltpu.PrefetchScalarGridSpec(
             num_scalar_prefetch=1,
-            grid=(4 * count,),
-            in_specs=[pl.BlockSpec((1, 2 * HALF, tile), lambda i, p: ((i + 2) % 4, 0, 0))]
-            + WEIGHT_SPECS,
-            out_specs=[
-                pl.BlockSpec(
-                    (1, 1, 1024, tile), lambda i, p: (i // 4, jnp.maximum(i % 4 - 2, 0), 0, 0)
-                ),
-                pl.BlockSpec((1, 1, 1024, tile), lambda i, p: (i // 4, jnp.minimum(i % 4, 1), 0, 0)),
-            ],
-            scratch_shapes=weight_scratch(count),
+            grid=(count,),
+            in_specs=[pl.BlockSpec(kvg.shape, lambda i, p: (0, 0))] + weight_specs(),
+            out_specs=[out, out],
+            scratch_shapes=[WEIGHT_SCRATCH],
         ),
         out_shape=[
-            jax.ShapeDtypeStruct((count, 2, 1024, tile), dtype),
-            jax.ShapeDtypeStruct((count, 2, 1024, tile), BF),
+            jax.ShapeDtypeStruct((count, 1024, ROWS), dtype),
+            jax.ShapeDtypeStruct((count, 1024, ROWS), BF),
         ],
-        compiler_params=params(20),
+        compiler_params=params(34),
         cost_estimate=HIDDEN,
     )(places, kvg, *weights)
 
@@ -563,7 +515,7 @@
 def sums_kernel(own_ref, got_ref, below_ref, above_ref, *outs):
     for out, k, h, more in zip(outs, (0, 1, 0, 1), (1, 0, 0, 1), (None, None, below_ref, above_ref)):
         rows = slice(h * 512, (h + 1) * 512)
-        total = own_ref[k, :, rows].astype(F32) + got_ref[k, :, rows].astype(F32)
+        total = own_ref[k, rows].astype(F32) + got_ref[k, rows].astype(F32)
         if more is not None:
             total = total + more[...].astype(F32)
         out[...] = total.astype(BF)
@@ -572,42 +524,59 @@
 def near_sums(own, got, below, above):
     return pl.pallas_call(
         sums_kernel,
-        out_shape=[jax.ShapeDtypeStruct((2, 512, ROWS // 2), BF)] * 4,
+        out_shape=[jax.ShapeDtypeStruct((512, ROWS), BF)] * 4,
         compiler_params=params(16),
         cost_estimate=HIDDEN,
     )(own, got, below, above)
 
 
-def finish_kernel(place, base_ref, core_ref, up_top, up_low, down_top, down_low, out_ref):
+def finish_kernel(
+    place, base_ref, core_ref, up_top, up_low, down_top, down_low, parts_ref, out_ref, ctx_ref
+):
     step = pl.program_id(0)
+
+    @pl.when(step == 0)
+    def context():
+        for core in range(2):
+            total = parts_ref[0, core].astype(F32)
+            for n in range(1, NZ * NX):
+                total = total + parts_ref[n, core].astype(F32)
+            ctx_ref[0, :, core * HALF : (core + 1) * HALF] = total
+
     total = base_ref[...] + core_ref[...].astype(F32)
 
     def write(up, down):
         whole = total + up[...].astype(F32) + down[...].astype(F32)
-        for n in range(2):
-            out_ref[n * 256 : (n + 1) * 256, :] = whole[n].T
+        out_ref[...] = whole.T
 
     pl.when(step < 2)(lambda: write(up_top, down_top))
     pl.when(step >= 2)(lambda: write(up_low, down_low))
 
 
-def finish(place, base, core_part, parts):
-    shape = (2, CHUNK, ROWS // 2)
-    block = pl.BlockSpec(shape, lambda n, p: (0, n, 0))
-    top = pl.BlockSpec(shape, lambda n, p: (0, jnp.minimum(n, 1), 0))
-    low = pl.BlockSpec(shape, lambda n, p: (0, jnp.maximum(n - 2, 0), 0))
+def finish(place, base, core_part, parts, ctx_parts):
+    shape = (CHUNK, ROWS)
+    block = pl.BlockSpec(shape, lambda n, p: (n, 0))
+    top = pl.BlockSpec(shape, lambda n, p: (jnp.minimum(n, 1), 0))
+    low = pl.BlockSpec(shape, lambda n, p: (jnp.maximum(n - 2, 0), 0))
     return pl.pallas_call(
         finish_kernel,
         grid_spec=pltpu.PrefetchScalarGridSpec(
             num_scalar_prefetch=1,
             grid=(4,),
-            in_specs=[block, block, top, low, top, low],
-            out_specs=pl.BlockSpec((ROWS, CHUNK), lambda n, p: (0, p[n])),
+            in_specs=[block, block, top, low, top, low]
+            + [pl.BlockSpec(ctx_parts.shape, lambda n, p: (0, 0, 0, 0))],
+            out_specs=[
+                pl.BlockSpec((ROWS, CHUNK), lambda n, p: (0, p[n])),
+                pl.BlockSpec((1, DEC, 2 * HALF), lambda n, p: (0, 0, 0)),
+            ],
         ),
-        out_shape=jax.ShapeDtypeStruct((ROWS, 4 * CHUNK), F32),
+        out_shape=[
+            jax.ShapeDtypeStruct((ROWS, 4 * CHUNK), F32),
+            jax.ShapeDtypeStruct((1, DEC, 2 * HALF), F32),
+        ],
         compiler_params=params(16),
         cost_estimate=HIDDEN,
-    )(place, base, core_part, *parts)
+    )(place, base, core_part, *parts, ctx_parts)
 
 
 def body(enc_rows, key_weight, value_weight, queries, ctx_grad, passage_len, passage_question):
@@ -681,8 +650,7 @@
     near_own, near_other = grad_blocks(near_places, kvg, weights, BF)
     far_got, near_own, near_other, kvg, dense = phase(far_got, near_own, near_other, kvg, dense)
 
-    far_top = add(far_own[:, :512], far_got[:, :512])
-    far_low = add(far_own[:, 512:], far_got[:, 512:])
+    far_top, far_low = add(far_own[:512], far_got[:512]), add(far_own[512:], far_got[512:])
     far_top, far_low, near_other, kvg, dense = phase(far_top, far_low, near_other, kvg, dense)
     from_below = perm(far_top, "dec", 1)
     from_above = perm(far_low, "dec", -1)
@@ -700,20 +668,13 @@
     top_below = perm(sums[2], "dec", 1)
     low_above = perm(sums[3], "dec", -1)
     base_got = perm(base_other, "core", 1)
-    parts = lax.all_to_all(dense.reshape(NZ * NX, 2, DEC, HALF), ("z", "x"), 0, 0, tiled=True)
+    parts = lax.all_to_all(dense, ENC, 0, 0, tiled=True).reshape(NZ * NX, NC, DEC, HALF)
     low_below, top_above, top_below, low_above, base_got, parts = phase(
         low_below, top_above, top_below, low_above, base_got, parts
     )
-    chip_ctx = jnp.sum(parts.astype(F32), axis=0)
-    keep = lax.dynamic_index_in_dim(chip_ctx, core, 0, keepdims=False)
-    give = lax.dynamic_index_in_dim(chip_ctx, 1 - core, 0, keepdims=False)
-    come = perm(give, "core", 1)
-    ctx = jnp.where(
-        core == 0,
-        jnp.concatenate([keep, come], axis=1),
-        jnp.concatenate([come, keep], axis=1),
-    )[None]
-    enc_grad = finish(xs, base, base_got, (top_below, low_below, top_above, low_above))
+    enc_grad, ctx = finish(
+        xs, base, base_got, (top_below, low_below, top_above, low_above), parts
+    )
     return ctx, enc_grad
 
 

time: 160 us -> 152 us (0.950)
  blocking collectives: 11.8 us -> 27.6 us
  waiting for transfers between devices: 57.5 us -> 47.3 us
  Pallas kernels: 41.6 us -> 34.5 us
  starting transfers between devices: 43.1 us -> 38.1 us
  other arithmetic: 4.04 us -> 2.37 us
    all_to_all x0 -> x1, blocking collectives: none -> 15.6 us  [body(): lax.all_to_all(dense, ENC, 0, 0, tiled=True).reshape(NZ * NX, NC, DEC, HALF)]
    all_to_all x1 -> x0, waiting for transfers between devices: 10.5 us -> none  [body(): lax.all_to_all(dense.reshape(NZ * NX, 2, DEC, HALF), ('z', 'x'), 0, 0, ti...]
    pallas_call x3, Pallas kernels: 14 us -> 9.31 us  [the longest x2 8.7 us: grad_blocks(): pl.pallas_call(grad_kernel, grid_spec=pltpu.PrefetchScalarGridSpec(num_sc...]
    all_to_all x1 -> x0, starting transfers between devices: 4.25 us -> none  [body(): lax.all_to_all(dense.reshape(NZ * NX, 2, DEC, HALF), ('z', 'x'), 0, 0, ti...]
    pallas_call x1, Pallas kernels: 5.03 us -> 3.12 us  [finish(): pl.pallas_call(finish_kernel, grid_spec=pltpu.PrefetchScalarGridSpec(num_...]
    ppermute x21 -> x20, starting transfers between devices: 28.5 us -> 27.7 us  [perm(): return lax.ppermute(v, axis, [(i, (i + shift) % n) for i in range(n)])]
    ppermute x21 -> x20, waiting for transfers between devices: 41.6 us -> 42.1 us  [perm(): return lax.ppermute(v, axis, [(i, (i + shift) % n) for i in range(n)])]
  transfers between devices with their start and end apart: 30 -> 28, of which waited for: 14 -> 13; matrix products, arithmetic and copies ran while one was open for 1% -> 1% of each run, Pallas kernels for 17% -> 12%
where the time goes in v4:
time: 152 us
  waiting for transfers between devices  47.3 us (31%)
  starting transfers between devices  38.1 us (25%)
  Pallas kernels  34.5 us (23%)
  blocking collectives  27.6 us (18%)
  other arithmetic  2.37 us (2%)
    ppermute x20, waiting for transfers between devices, perm(): return lax.ppermute(v, axis, [(i, (i + shift) % n) for i in range(n)])  42.1 us
    ppermute x20, starting transfers between devices, perm(): return lax.ppermute(v, axis, [(i, (i + shift) % n) for i in range(n)])  27.7 us
    all_to_all x1, blocking collectives, body(): lax.all_to_all(dense, ENC, 0, 0, tiled=True).reshape(NZ * NX, NC, DEC, HALF)  15.6 us
    all_to_all x1, blocking collectives, body(): stats_all = lax.all_to_all(stats, ('z', 'x'), 0, 0, tiled=True)  12 us
    ppermute x8, starting transfers between devices, pair_perm(): return lax.ppermute(v, axis, [(i, turn(i) % 4) for i in range(4)])  10.4 us
    pallas_call x1, Pallas kernels, project_near(): pl.pallas_call(near_kernel, grid_spec=pltpu.PrefetchScalarGridSpec(num_sc...  9.86 us
    pallas_call x2, Pallas kernels, grad_blocks(): pl.pallas_call(grad_kernel, grid_spec=pltpu.PrefetchScalarGridSpec(num_sc...  8.7 us
    pallas_call x1, Pallas kernels, project_far(): pl.pallas_call(far_kernel, grid_spec=pltpu.PrefetchScalarGridSpec(num_sca...  5.92 us
  transfers between devices with their start and end apart: 28, of which 13 were waited for; matrix products, arithmetic and copies ran while one was open for 1% of the time, Pallas kernels for 12%

profile of v4, /device:TPU:1, one launch (start us, length us, event | category | flops | bytes accessed | tf_op | source)
XLA Modules:
  0.0 151.6 jit_solution(5156750076577066215)
XLA Ops:
  0.6 1.1 pad_maximum_fusion
  1.8 1.5 collective-permute-start
  3.3 1.2 collective-permute-done
  4.5 0.4 collective-permute-start.5
  5.2 1.4 collective-permute-start.1
  6.6 1.8 %collective-permute-start.2 = (bf16[288,256]{1,0:T(8,128)(2,1)S(1)}, bf16[288,256]{1,0:T(8,128)(2,1)S(1)}, u32[]{:S(2)}, u32[]{:S(2)}) collective-permute-start(bf16[288,256]{1,0:T(8,128)(2,1)S(1)} %get-tuple-element.95.refs_2_), channel_id=1, source_target_pairs={{0,24},{8,16},{16,8},{24,0},{1,25},{9,17},{17,9},{25,1},{2,26},{10... | collective-permute-start | bytes 442376 | tf_op jit(solution)/shard_map/ppermute | solution.py:41
  8.4 1.6 %collective-permute-start.3 = (bf16[288,256]{1,0:T(8,128)(2,1)S(1)}, bf16[288,256]{1,0:T(8,128)(2,1)S(1)}, u32[]{:S(2)}, u32[]{:S(2)}) collective-permute-start(bf16[288,256]{1,0:T(8,128)(2,1)S(1)} %get-tuple-element.96.refs_4_), channel_id=1, source_target_pairs={{0,32},{32,0},{64,96},{96,64},{1,33},{33,1},{65,97},{97,65},{2,34}... | collective-permute-start | bytes 442376 | tf_op jit(solution)/shard_map/ppermute | solution.py:41
  10.1 2.2 %collective-permute-start.4 = (bf16[288,256]{1,0:T(8,128)(2,1)S(1)}, bf16[288,256]{1,0:T(8,128)(2,1)S(1)}, u32[]{:S(2)}, u32[]{:S(2)}) collective-permute-start(bf16[288,256]{1,0:T(8,128)(2,1)S(1)} %get-tuple-element.97.refs_6_), channel_id=1, source_target_pairs={{0,96},{32,64},{64,32},{96,0},{1,97},{33,65},{65,33},{97,1},{2,98}... | collective-permute-start | bytes 442376 | tf_op jit(solution)/shard_map/ppermute | solution.py:41
  12.3 0.6 fusion.3
  13.0 0.7 pad_add_fusion.pos
  13.7 1.9 %collective-permute-done.4.refs_7_ = bf16[288,256]{1,0:T(8,128)(2,1)S(1)} collective-permute-done((bf16[288,256]{1,0:T(8,128)(2,1)S(1)}, bf16[288,256]{1,0:T(8,128)(2,1)S(1)}, u32[]{:S(2)}, u32[]{:S(2)}) %collective-permute-start.4) | collective-permute-done | bytes 147488 | tf_op jit(solution)/shard_map/ppermute | solution.py:41
  15.7 0.7 collective-permute-start.10
  16.4 1.7 %collective-permute-start.9 = (bf16[576,256]{1,0:T(8,128)(2,1)S(1)}, bf16[576,256]{1,0:T(8,128)(2,1)S(1)}, u32[]{:S(2)}, u32[]{:S(2)}) collective-permute-start(bf16[576,256]{1,0:T(8,128)(2,1)S(1)} %get-tuple-element.108.joined0), channel_id=1, source_target_pairs={{0,96},{32,64},{64,32},{96,0},{1,97},{33,65},{65,33},{97,1},{2,98}... | collective-permute-start | bytes 884744 | tf_op jit(solution)/shard_map/ppermute | solution.py:41
  18.2 0.9 collective-permute-start.7
  19.1 3.3 %collective-permute-done.10.second1 = bf16[576,256]{1,0:T(8,128)(2,1)S(1)} collective-permute-done((bf16[576,256]{1,0:T(8,128)(2,1)S(1)}, bf16[576,256]{1,0:T(8,128)(2,1)S(1)}, u32[]{:S(2)}, u32[]{:S(2)}) %collective-permute-start.10) | collective-permute-done | bytes 294944 | tf_op jit(solution)/shard_map/ppermute | solution.py:41
  22.4 2.8 %collective-permute-start.6 = (s32[8]{0:T(128)S(1)}, s32[8]{0:T(128)S(1)}, u32[]{:S(2)}, u32[]{:S(2)}) collective-permute-start(s32[8]{0:T(128)S(1)} %pad_add_fusion.1.own_numbers), channel_id=1, source_target_pairs={{0,4},{4,0},{1,5},{5,1},{2,6},{6,2},{3,7},{7,3},{8,12},{12,8},{9,1... | collective-permute-start | bytes 104 | tf_op jit(solution)/shard_map/ppermute | solution.py:28
  25.5 0.5 collective-permute-done.6.other_numbers
  26.0 0.9 collective-permute-start.15
  26.9 0.6 collective-permute-start.16
  27.5 2.2 %collective-permute-start.11 = (bf16[2,1152,256]{2,1,0:T(8,128)(2,1)S(1)}, bf16[2,1152,256]{2,1,0:T(8,128)(2,1)S(1)}, u32[]{:S(2)}, u32[]{:S(2)}) collective-permute-start(bf16[2,1152,256]{2,1,0:T(8,128)(2,1)S(1)} %shard_map.87.refs_0_), channel_id=1, source_target_pairs={{0,96},{32,0},{64,32},{96,64},{1,97},{33,1},{65,33},{97,65},{2,98}... | collective-permute-start | bytes 3538952 | tf_op jit(solution)/shard_map/ppermute | solution.py:28
  29.7 20.8 %collective-permute-done.15.up_ref.refs_4_.refs_6_ = bf16[2,1152,256]{2,1,0:T(8,128)(2,1)S(1)} collective-permute-done((bf16[2,1152,256]{2,1,0:T(8,128)(2,1)S(1)}, bf16[2,1152,256]{2,1,0:T(8,128)(2,1)S(1)}, u32[]{:S(2)}, u32[]{:S(2)}) %collective-permute-start.15) | collective-permute-done | bytes 1179680 | tf_op jit(solution)/shard_map/ppermute | solution.py:28
  50.5 1.1 collective-permute-done.16.down_ref.refs_5_.refs_9_
  51.7 1.1 collective-permute-done.11.up_ref.refs_1_
  52.8 3.1 %collective-permute-done.12.down_ref.refs_2_.refs_4_ = bf16[2,1152,256]{2,1,0:T(8,128)(2,1)S(1)} collective-permute-done((bf16[2,1152,256]{2,1,0:T(8,128)(2,1)S(1)}, bf16[2,1152,256]{2,1,0:T(8,128)(2,1)S(1)}, u32[]{:S(2)}, u32[]{:S(2)}) %collective-permute-start.12) | collective-permute-done | bytes 1179680 | tf_op jit(solution)/shard_map/ppermute | solution.py:28
  56.0 1.5 %collective-permute-start.17 = (bf16[1152,256]{1,0:T(8,128)(2,1)S(1)}, bf16[1152,256]{1,0:T(8,128)(2,1)S(1)}, u32[]{:S(2)}, u32[]{:S(2)}) collective-permute-start(bf16[1152,256]{1,0:T(8,128)(2,1)S(1)} %get-tuple-element.119), channel_id=1, source_target_pairs={{0,24},{8,0},{16,8},{24,16},{1,25},{9,1},{17,9},{25,17},{2,26},{10... | collective-permute-start | bytes 1769480 | tf_op jit(solution)/shard_map/ppermute | solution.py:28
  57.6 0.4 collective-permute-start.13
  58.0 1.2 collective-permute-start.14
  59.2 9.9 %shard_map.91 = (f32[2,512,1024]{2,1,0:T(8,128)S(1)}, bf16[2,512,2048]{2,1,0:T(8,128)(2,1)S(1)}, bf16[1024,256]{1,0:T(8,128)(2,1)S(1)}, bf16[1024,256]{1,0:T(8,128)(2,1)S(1)}) custom-call(s32[3]{0:T(128)S(1)} %pad_add_fusion.pos, bf16[512,4096]{1,0:T(8,128)(2,1)S(1)} %copy-done, bf16[512,4096]{1,0:T(8,128)(2,1)} %collective-permute-done.5.oth_ref, ...), custom_call_target="tpu_custom_call" | custom-call | flops 200000000 | tf_op jit(solution)/shard_map/pallas_call | solution.py:172
  69.1 0.3 collective-permute-done.18.b_low.refs_8_
  69.3 0.4 collective-permute-done.14.a_low.refs_3_
  69.8 5.9 %shard_map.92 = (bf16[2,512,512]{2,1,0:T(8,128)(2,1)S(1)}, bf16[2,512,512]{2,1,0:T(8,128)(2,1)S(1)}, bf16[1024,256]{1,0:T(8,128)(2,1)S(1)}, bf16[1024,256]{1,0:T...) custom-call(s32[3]{0:T(128)S(1)} %pad_add_fusion.pos, s32[8]{0:T(128)S(1)} %pad_add_fusion.1.own_numbers, ...), custom_call_target="tpu_custom_call" | custom-call | flops 200000000 | tf_op jit(solution)/shard_map/pallas_call | solution.py:321
  75.7 12.0 %all_to_all.10.st_ref = f32[16,32,128]{2,1,0:T(8,128)S(1)} all-to-all(f32[16,32,128]{2,1,0:T(8,128)S(1)} %get-tuple-element.138), channel_id=1, replica_groups=mesh['z'=4,'x'=4,'core'=2,'dec'=4] {'z','x'}, dimensions={0} | all-to-all | bytes 524288 | tf_op jit(solution)/shard_map/all_to_all | solution.py:640
  87.7 5.8 %shard_map.93 = (bf16[1024,1024]{1,0:T(8,128)(2,1)S(1)}, bf16[1024,512]{1,0:T(8,128)(2,1)S(1)}, bf16[1024,512]{1,0:T(8,128)(2,1)S(1)}, bf16[32,16,512]{2,1,0:T(8,128)(2,1)S(1)}) custom-call(s32[3]{0:T(128)S(1)} %pad_add_fusion.pos, s32[8]{0:T(128)S(1)} %pad_add_fusion.1.own_numbers, s32[8]{0:T(128)S(1)} %collective-permute-done.6.other_numbers, ...), custom_call_target="tpu_custom_call" | custom-call | flops 200000000 | tf_op jit(solution)/shard_map/pallas_call | solution.py:470
  93.5 6.6 %collective-permute-start.19 = (bf16[1024,512]{1,0:T(8,128)(2,1)S(1)}, bf16[1024,512]{1,0:T(8,128)(2,1)S(1)}, u32[]{:S(2)}, u32[]{:S(2)}) collective-permute-start(bf16[1024,512]{1,0:T(8,128)(2,1)S(1)} %get-tuple-element.141), channel_id=1, source_target_pairs={{0,4},{4,0},{1,5},{5,1},{2,6},{6,2},{3,7},{7,3},{8,12},{12,8},{9,1... | collective-permute-start | bytes 3145736 | tf_op jit(solution)/shard_map/ppermute | solution.py:28
  100.1 5.6 %shard_map.94 = (bf16[2,1024,512]{2,1,0:T(8,128)(2,1)S(1)}, bf16[2,1024,512]{2,1,0:T(8,128)(2,1)S(1)}) custom-call(s32[2]{0:T(128)S(1)} %slice.77.places, bf16[1024,1024]{1,0:T(8,128)(2,1)S(1)} %get-tuple-element.155.kvg_ref, bf16[2,1152,256]{2,1,0:T(8,128)(2,1)S(1)} %shard_map.87.refs_0_, bf16[2,1152,256]{2,1,0:T(8,128)(2,1)S(1)} %collective-permute-done.11.up_ref.refs_1_, ...), custom_call_target="tpu_custom_call" | custom-call | flops 200000000 | tf_op jit(solution)/shard_map/pallas_call | solution.py:497
  105.7 0.3 add_convert_fusion
  106.0 1.3 collective-permute-start.20
  107.4 1.5 %collective-permute-start.21 = (bf16[512,512]{1,0:T(8,128)(2,1)S(1)}, bf16[512,512]{1,0:T(8,128)(2,1)S(1)}, u32[]{:S(2)}, u32[]{:S(2)}) collective-permute-start(bf16[512,512]{1,0:T(8,128)(2,1)S(1)} %get-tuple-element.152), channel_id=1, source_target_pairs={{0,3},{1,0},{2,1},{3,2},{4,7},{5,4},{6,5},{7,6},{8,11},{9,8},{10,9... | collective-permute-start | bytes 1572872 | tf_op jit(solution)/shard_map/ppermute | solution.py:28
  108.9 3.1 %shard_map.95 = (f32[1,1024,512]{2,1,0:T(8,128)S(1)}, bf16[1,1024,512]{2,1,0:T(8,128)(2,1)S(1)}) custom-call(s32[1]{0:T(128)} %get-tuple-element.154.places, bf16[1024,1024]{1,0:T(8,128)(2,1)S(1)} %get-tuple-element.155.kvg_ref, bf16[2,1152,256]{2,1,0:T(8,128)(2,1)S(1)} %shard_map.87.refs_0_, ...), custom_call_target="tpu_custom_call" | custom-call | flops 200000000 | tf_op jit(solution)/shard_map/pallas_call | solution.py:497
  112.0 8.5 %collective-permute-done.20.below_ref = bf16[512,512]{1,0:T(8,128)(2,1)S(1)} collective-permute-done((bf16[512,512]{1,0:T(8,128)(2,1)S(1)}, bf16[512,512]{1,0:T(8,128)(2,1)S(1)}, u32[]{:S(2)}, u32[]{:S(2)}) %collective-permute-start.20) | collective-permute-done | bytes 524320 | tf_op jit(solution)/shard_map/ppermute | solution.py:28
  120.5 0.6 shard_map.96
  121.1 1.3 collective-permute-start.27
  122.4 1.3 collective-permute-start.23
  123.8 1.4 collective-permute-start.24
  125.2 2.6 %collective-permute-start.26 = (bf16[512,512]{1,0:T(8,128)(2,1)S(1)}, bf16[512,512]{1,0:T(8,128)(2,1)S(1)}, u32[]{:S(2)}, u32[]{:S(2)}) collective-permute-start(bf16[512,512]{1,0:T(8,128)(2,1)S(1)} %get-tuple-element.173), channel_id=1, source_target_pairs={{0,3},{1,0},{2,1},{3,2},{4,7},{5,4},{6,5},{7,6},{8,11},{9,8},{10,9... | collective-permute-start | bytes 1572872 | tf_op jit(solution)/shard_map/ppermute | solution.py:28
  127.9 15.6 %all_to_all.11 = bf16[32,16,512]{2,1,0:T(8,128)(2,1)S(1)} all-to-all(bf16[32,16,512]{2,1,0:T(8,128)(2,1)S(1)} %get-tuple-element.175), channel_id=1, replica_groups=mesh['z'=4,'x'=4,'core'=2,'dec'=4] {'z','x','core'}, dimensions={0} | all-to-all | bytes 1048576 | tf_op jit(solution)/shard_map/all_to_all | solution.py:671
  143.5 5.0 %collective-permute-done.25.up_top = bf16[512,512]{1,0:T(8,128)(2,1)S(1)} collective-permute-done((bf16[512,512]{1,0:T(8,128)(2,1)S(1)}, bf16[512,512]{1,0:T(8,128)(2,1)S(1)}, u32[]{:S(2)}, u32[]{:S(2)}) %collective-permute-start.25) | collective-permute-done | bytes 524320 | tf_op jit(solution)/shard_map/ppermute | solution.py:28
  148.5 3.1 %shard_map.97 = (f32[512,1024]{1,0:T(8,128)}, f32[1,16,1024]{2,1,0:T(8,128)}) custom-call(s32[4]{0:T(128)S(1)} %get-tuple-element.98.place, f32[1024,512]{1,0:T(8,128)S(1)} %bitcast.10, bf16[1024,512]{1,0:T(8,128)(2,1)S(1)} %collective-permute-done.27.core_ref, bf16[512,512]{1,0:T(8,128)(2,1)S(1)} %collective-permute-done.25.up_top, ...), custom_call_target="tpu_custom_call" | custom-call | flops 200000000 | tf_op jit(solution)/shard_map/pallas_call | solution.py:561
  (44 shorter events, 1.2 us)
Async XLA Ops:
  1.8 2.7 %collective-permute-start = (bf16[288,512]{1,0:T(8,128)(2,1)S(1)}, bf16[288,512]{1,0:T(8,128)(2,1)S(1)}, u32[]{:S(2)}, u32[]{:S(2)}) collective-permute-start(bf16[288,512]{1,0:T(8,128)(2,1)S(1)} %constant_dynamic-slice_fusion), channel_id=1, source_target_pairs={{0,4},{4,0},{1,5},{5,1},{2,6},{6,2},{3,7},{7,3},{8,12},{12,8},{9,1... | collective-permute-start | bytes 884744 | tf_op jit(solution)/shard_map/ppermute | solution.py:28
  4.5 21.5 %collective-permute-start.5 = (bf16[512,4096]{1,0:T(8,128)(2,1)}, bf16[512,4096]{1,0:T(8,128)(2,1)}, u32[]{:S(2)}, u32[]{:S(2)}) collective-permute-start(bf16[512,4096]{1,0:T(8,128)(2,1)} %own_ref.1), channel_id=1, source_target_pairs={{0,4},{4,0},{1,5},{5,1},{2,6},{6,2},{3,7},{7,3},{8,12},{12,8},{9,1... | collective-permute-start | bytes 12582920 | tf_op jit(solution)/shard_map/ppermute | solution.py:28
  5.2 13.9 %copy-start.1 = (s32[4,1]{0,1:T(1,128)S(1)}, s32[4,1]{0,1:T(1,128)}, u32[]{:S(2)}) copy-start(s32[4,1]{0,1:T(1,128)} %param.13) | copy-start | bytes 52
  5.2 13.9 %copy-start.2 = (s32[1,4]{1,0:T(1,128)S(1)}, s32[1,4]{1,0:T(1,128)}, u32[]{:S(2)}) copy-start(s32[1,4]{1,0:T(1,128)} %param.12) | copy-start | bytes 52
  5.2 8.5 %collective-permute-start.1 = (bf16[288,256]{1,0:T(8,128)(2,1)S(1)}, bf16[288,256]{1,0:T(8,128)(2,1)S(1)}, u32[]{:S(2)}, u32[]{:S(2)}) collective-permute-start(bf16[288,256]{1,0:T(8,128)(2,1)S(1)} %get-tuple-element.94.refs_0_), channel_id=1, source_target_pairs={{0,8},{8,0},{16,24},{24,16},{1,9},{9,1},{17,25},{25,17},{2,10},{10... | collective-permute-start | bytes 442376 | tf_op jit(solution)/shard_map/ppermute | solution.py:41
  6.6 7.1 %collective-permute-start.2 = (bf16[288,256]{1,0:T(8,128)(2,1)S(1)}, bf16[288,256]{1,0:T(8,128)(2,1)S(1)}, u32[]{:S(2)}, u32[]{:S(2)}) collective-permute-start(bf16[288,256]{1,0:T(8,128)(2,1)S(1)} %get-tuple-element.95.refs_2_), channel_id=1, source_target_pairs={{0,24},{8,16},{16,8},{24,0},{1,25},{9,17},{17,9},{25,1},{2,26},{10... | collective-permute-start | bytes 442376 | tf_op jit(solution)/shard_map/ppermute | solution.py:41
  8.4 5.3 %collective-permute-start.3 = (bf16[288,256]{1,0:T(8,128)(2,1)S(1)}, bf16[288,256]{1,0:T(8,128)(2,1)S(1)}, u32[]{:S(2)}, u32[]{:S(2)}) collective-permute-start(bf16[288,256]{1,0:T(8,128)(2,1)S(1)} %get-tuple-element.96.refs_4_), channel_id=1, source_target_pairs={{0,32},{32,0},{64,96},{96,64},{1,33},{33,1},{65,97},{97,65},{2,34}... | collective-permute-start | bytes 442376 | tf_op jit(solution)/shard_map/ppermute | solution.py:41
  10.1 5.6 %collective-permute-start.4 = (bf16[288,256]{1,0:T(8,128)(2,1)S(1)}, bf16[288,256]{1,0:T(8,128)(2,1)S(1)}, u32[]{:S(2)}, u32[]{:S(2)}) collective-permute-start(bf16[288,256]{1,0:T(8,128)(2,1)S(1)} %get-tuple-element.97.refs_6_), channel_id=1, source_target_pairs={{0,96},{32,64},{64,32},{96,0},{1,97},{33,65},{65,33},{97,1},{2,98}... | collective-permute-start | bytes 442376 | tf_op jit(solution)/shard_map/ppermute | solution.py:41
  15.7 6.7 %collective-permute-start.10 = (bf16[576,256]{1,0:T(8,128)(2,1)S(1)}, bf16[576,256]{1,0:T(8,128)(2,1)S(1)}, u32[]{:S(2)}, u32[]{:S(2)}) collective-permute-start(bf16[576,256]{1,0:T(8,128)(2,1)S(1)} %get-tuple-element.109.joined1), channel_id=1, source_target_pairs={{0,32},{32,0},{64,96},{96,64},{1,33},{33,1},{65,97},{97,65},{2,34}... | collective-permute-start | bytes 884744 | tf_op jit(solution)/shard_map/ppermute | solution.py:41
  16.4 8.8 %collective-permute-start.9 = (bf16[576,256]{1,0:T(8,128)(2,1)S(1)}, bf16[576,256]{1,0:T(8,128)(2,1)S(1)}, u32[]{:S(2)}, u32[]{:S(2)}) collective-permute-start(bf16[576,256]{1,0:T(8,128)(2,1)S(1)} %get-tuple-element.108.joined0), channel_id=1, source_target_pairs={{0,96},{32,64},{64,32},{96,0},{1,97},{33,65},{65,33},{97,1},{2,98}... | collective-permute-start | bytes 884744 | tf_op jit(solution)/shard_map/ppermute | solution.py:41
  18.2 7.2 %collective-permute-start.7 = (bf16[576,256]{1,0:T(8,128)(2,1)S(1)}, bf16[576,256]{1,0:T(8,128)(2,1)S(1)}, u32[]{:S(2)}, u32[]{:S(2)}) collective-permute-start(bf16[576,256]{1,0:T(8,128)(2,1)S(1)} %get-tuple-element.106.joined0), channel_id=1, source_target_pairs={{0,24},{8,16},{16,8},{24,0},{1,25},{9,17},{17,9},{25,1},{2,26},{10... | collective-permute-start | bytes 884744 | tf_op jit(solution)/shard_map/ppermute | solution.py:41
  19.0 6.4 %collective-permute-start.8 = (bf16[576,256]{1,0:T(8,128)(2,1)S(1)}, bf16[576,256]{1,0:T(8,128)(2,1)S(1)}, u32[]{:S(2)}, u32[]{:S(2)}) collective-permute-start(bf16[576,256]{1,0:T(8,128)(2,1)S(1)} %get-tuple-element.107.joined1), channel_id=1, source_target_pairs={{0,8},{8,0},{16,24},{24,16},{1,9},{9,1},{17,25},{25,17},{2,10},{10... | collective-permute-start | bytes 884744 | tf_op jit(solution)/shard_map/ppermute | solution.py:41
  22.4 3.6 %collective-permute-start.6 = (s32[8]{0:T(128)S(1)}, s32[8]{0:T(128)S(1)}, u32[]{:S(2)}, u32[]{:S(2)}) collective-permute-start(s32[8]{0:T(128)S(1)} %pad_add_fusion.1.own_numbers), channel_id=1, source_target_pairs={{0,4},{4,0},{1,5},{5,1},{2,6},{6,2},{3,7},{7,3},{8,12},{12,8},{9,1... | collective-permute-start | bytes 104 | tf_op jit(solution)/shard_map/ppermute | solution.py:28
  26.0 24.5 %collective-permute-start.15 = (bf16[2,1152,256]{2,1,0:T(8,128)(2,1)S(1)}, bf16[2,1152,256]{2,1,0:T(8,128)(2,1)S(1)}, u32[]{:S(2)}, u32[]{:S(2)}) collective-permute-start(bf16[2,1152,256]{2,1,0:T(8,128)(2,1)S(1)} %shard_map.88.refs_3_.refs_5_), channel_id=1, source_target_pairs={{0,24},{8,0},{16,8},{24,16},{1,25},{9,1},{17,9},{25,17},{2,26},{10... | collective-permute-start | bytes 3538952 | tf_op jit(solution)/shard_map/ppermute | solution.py:28
  26.9 24.8 %collective-permute-start.16 = (bf16[2,1152,256]{2,1,0:T(8,128)(2,1)S(1)}, bf16[2,1152,256]{2,1,0:T(8,128)(2,1)S(1)}, u32[]{:S(2)}, u32[]{:S(2)}) collective-permute-start(bf16[2,1152,256]{2,1,0:T(8,128)(2,1)S(1)} %shard_map.88.refs_3_.refs_5_), channel_id=1, source_target_pairs={{0,8},{8,16},{16,24},{24,0},{1,9},{9,17},{17,25},{25,1},{2,10},{10... | collective-permute-start | bytes 3538952 | tf_op jit(solution)/shard_map/ppermute | solution.py:28
  27.5 25.3 %collective-permute-start.11 = (bf16[2,1152,256]{2,1,0:T(8,128)(2,1)S(1)}, bf16[2,1152,256]{2,1,0:T(8,128)(2,1)S(1)}, u32[]{:S(2)}, u32[]{:S(2)}) collective-permute-start(bf16[2,1152,256]{2,1,0:T(8,128)(2,1)S(1)} %shard_map.87.refs_0_), channel_id=1, source_target_pairs={{0,96},{32,0},{64,32},{96,64},{1,97},{33,1},{65,33},{97,65},{2,98}... | collective-permute-start | bytes 3538952 | tf_op jit(solution)/shard_map/ppermute | solution.py:28
  29.7 26.2 %collective-permute-start.12 = (bf16[2,1152,256]{2,1,0:T(8,128)(2,1)S(1)}, bf16[2,1152,256]{2,1,0:T(8,128)(2,1)S(1)}, u32[]{:S(2)}, u32[]{:S(2)}) collective-permute-start(bf16[2,1152,256]{2,1,0:T(8,128)(2,1)S(1)} %shard_map.87.refs_0_), channel_id=1, source_target_pairs={{0,32},{32,64},{64,96},{96,0},{1,33},{33,65},{65,97},{97,1},{2,34}... | collective-permute-start | bytes 3538952 | tf_op jit(solution)/shard_map/ppermute | solution.py:28
  55.9 3.3 %copy-start = (bf16[512,4096]{1,0:T(8,128)(2,1)S(1)}, bf16[512,4096]{1,0:T(8,128)(2,1)}, u32[]{:S(2)}) copy-start(bf16[512,4096]{1,0:T(8,128)(2,1)} %own_ref.1) | copy-start | bytes 12582916
  56.0 13.0 %collective-permute-start.17 = (bf16[1152,256]{1,0:T(8,128)(2,1)S(1)}, bf16[1152,256]{1,0:T(8,128)(2,1)S(1)}, u32[]{:S(2)}, u32[]{:S(2)}) collective-permute-start(bf16[1152,256]{1,0:T(8,128)(2,1)S(1)} %get-tuple-element.119), channel_id=1, source_target_pairs={{0,24},{8,0},{16,8},{24,16},{1,25},{9,1},{17,9},{25,17},{2,26},{10... | collective-permute-start | bytes 1769480 | tf_op jit(solution)/shard_map/ppermute | solution.py:28
  57.6 11.8 %collective-permute-start.18 = (bf16[1152,256]{1,0:T(8,128)(2,1)S(1)}, bf16[1152,256]{1,0:T(8,128)(2,1)S(1)}, u32[]{:S(2)}, u32[]{:S(2)}) collective-permute-start(bf16[1152,256]{1,0:T(8,128)(2,1)S(1)} %get-tuple-element.120), channel_id=1, source_target_pairs={{0,8},{8,16},{16,24},{24,0},{1,9},{9,17},{17,25},{25,1},{2,10},{10... | collective-permute-start | bytes 1769480 | tf_op jit(solution)/shard_map/ppermute | solution.py:28
  57.6 11.7 %collective-permute-start.13 = (bf16[1152,256]{1,0:T(8,128)(2,1)S(1)}, bf16[1152,256]{1,0:T(8,128)(2,1)S(1)}, u32[]{:S(2)}, u32[]{:S(2)}) collective-permute-start(bf16[1152,256]{1,0:T(8,128)(2,1)S(1)} %get-tuple-element.114), channel_id=1, source_target_pairs={{0,96},{32,0},{64,32},{96,64},{1,97},{33,1},{65,33},{97,65},{2,98}... | collective-permute-start | bytes 1769480 | tf_op jit(solution)/shard_map/ppermute | solution.py:28
  58.0 11.8 %collective-permute-start.14 = (bf16[1152,256]{1,0:T(8,128)(2,1)S(1)}, bf16[1152,256]{1,0:T(8,128)(2,1)S(1)}, u32[]{:S(2)}, u32[]{:S(2)}) collective-permute-start(bf16[1152,256]{1,0:T(8,128)(2,1)S(1)} %get-tuple-element.115), channel_id=1, source_target_pairs={{0,32},{32,64},{64,96},{96,0},{1,33},{33,65},{65,97},{97,1},{2,34}... | collective-permute-start | bytes 1769480 | tf_op jit(solution)/shard_map/ppermute | solution.py:28
  93.5 12.2 %collective-permute-start.19 = (bf16[1024,512]{1,0:T(8,128)(2,1)S(1)}, bf16[1024,512]{1,0:T(8,128)(2,1)S(1)}, u32[]{:S(2)}, u32[]{:S(2)}) collective-permute-start(bf16[1024,512]{1,0:T(8,128)(2,1)S(1)} %get-tuple-element.141), channel_id=1, source_target_pairs={{0,4},{4,0},{1,5},{5,1},{2,6},{6,2},{3,7},{7,3},{8,12},{12,8},{9,1... | collective-permute-start | bytes 3145736 | tf_op jit(solution)/shard_map/ppermute | solution.py:28
  105.9 14.6 %collective-permute-start.22 = (bf16[2,1024,512]{2,1,0:T(8,128)(2,1)S(1)}, bf16[2,1024,512]{2,1,0:T(8,128)(2,1)S(1)}, u32[]{:S(2)}, u32[]{:S(2)}) collective-permute-start(bf16[2,1024,512]{2,1,0:T(8,128)(2,1)S(1)} %get-tuple-element.153), channel_id=1, source_target_pairs={{0,4},{4,0},{1,5},{5,1},{2,6},{6,2},{3,7},{7,3},{8,12},{12,8},{9,1... | collective-permute-start | bytes 6291464 | tf_op jit(solution)/shard_map/ppermute | solution.py:28
  106.0 14.5 %collective-permute-start.20 = (bf16[512,512]{1,0:T(8,128)(2,1)S(1)}, bf16[512,512]{1,0:T(8,128)(2,1)S(1)}, u32[]{:S(2)}, u32[]{:S(2)}) collective-permute-start(bf16[512,512]{1,0:T(8,128)(2,1)S(1)} %get-tuple-element.151), channel_id=1, source_target_pairs={{0,1},{1,2},{2,3},{3,0},{4,5},{5,6},{6,7},{7,4},{8,9},{9,10},{10,1... | collective-permute-start | bytes 1572872 | tf_op jit(solution)/shard_map/ppermute | solution.py:28
  107.4 13.1 %collective-permute-start.21 = (bf16[512,512]{1,0:T(8,128)(2,1)S(1)}, bf16[512,512]{1,0:T(8,128)(2,1)S(1)}, u32[]{:S(2)}, u32[]{:S(2)}) collective-permute-start(bf16[512,512]{1,0:T(8,128)(2,1)S(1)} %get-tuple-element.152), channel_id=1, source_target_pairs={{0,3},{1,0},{2,1},{3,2},{4,7},{5,4},{6,5},{7,6},{8,11},{9,8},{10,9... | collective-permute-start | bytes 1572872 | tf_op jit(solution)/shard_map/ppermute | solution.py:28
  121.1 27.4 %collective-permute-start.27 = (bf16[1024,512]{1,0:T(8,128)(2,1)S(1)}, bf16[1024,512]{1,0:T(8,128)(2,1)S(1)}, u32[]{:S(2)}, u32[]{:S(2)}) collective-permute-start(bf16[1024,512]{1,0:T(8,128)(2,1)S(1)} %bitcast.13), channel_id=1, source_target_pairs={{0,4},{4,0},{1,5},{5,1},{2,6},{6,2},{3,7},{7,3},{8,12},{12,8},{9,1... | collective-permute-start | bytes 3145736 | tf_op jit(solution)/shard_map/ppermute | solution.py:28
  122.4 21.0 %collective-permute-start.23 = (bf16[512,512]{1,0:T(8,128)(2,1)S(1)}, bf16[512,512]{1,0:T(8,128)(2,1)S(1)}, u32[]{:S(2)}, u32[]{:S(2)}) collective-permute-start(bf16[512,512]{1,0:T(8,128)(2,1)S(1)} %get-tuple-element.170), channel_id=1, source_target_pairs={{0,1},{1,2},{2,3},{3,0},{4,5},{5,6},{6,7},{7,4},{8,9},{9,10},{10,1... | collective-permute-start | bytes 1572872 | tf_op jit(solution)/shard_map/ppermute | solution.py:28
  123.8 19.7 %collective-permute-start.24 = (bf16[512,512]{1,0:T(8,128)(2,1)S(1)}, bf16[512,512]{1,0:T(8,128)(2,1)S(1)}, u32[]{:S(2)}, u32[]{:S(2)}) collective-permute-start(bf16[512,512]{1,0:T(8,128)(2,1)S(1)} %get-tuple-element.171), channel_id=1, source_target_pairs={{0,3},{1,0},{2,1},{3,2},{4,7},{5,4},{6,5},{7,6},{8,11},{9,8},{10,9... | collective-permute-start | bytes 1572872 | tf_op jit(solution)/shard_map/ppermute | solution.py:28
  125.2 23.3 %collective-permute-start.25 = (bf16[512,512]{1,0:T(8,128)(2,1)S(1)}, bf16[512,512]{1,0:T(8,128)(2,1)S(1)}, u32[]{:S(2)}, u32[]{:S(2)}) collective-permute-start(bf16[512,512]{1,0:T(8,128)(2,1)S(1)} %get-tuple-element.172), channel_id=1, source_target_pairs={{0,1},{1,2},{2,3},{3,0},{4,5},{5,6},{6,7},{7,4},{8,9},{9,10},{10,1... | collective-permute-start | bytes 1572872 | tf_op jit(solution)/shard_map/ppermute | solution.py:28
  125.2 23.3 %collective-permute-start.26 = (bf16[512,512]{1,0:T(8,128)(2,1)S(1)}, bf16[512,512]{1,0:T(8,128)(2,1)S(1)}, u32[]{:S(2)}, u32[]{:S(2)}) collective-permute-start(bf16[512,512]{1,0:T(8,128)(2,1)S(1)} %get-tuple-element.173), channel_id=1, source_target_pairs={{0,3},{1,0},{2,1},{3,2},{4,7},{5,4},{6,5},{7,6},{8,11},{9,8},{10,9... | collective-permute-start | bytes 1572872 | tf_op jit(solution)/shard_map/ppermute | solution.py:28

commit v5 on v4

--- a/solution.py
+++ b/solution.py
@@ -16,7 +16,8 @@
 PIECE = 576
 DEC = 16
 NPASS = 4
-PAIRS = 4
+QUADS = 2
+LANES = 256
 LOW = -1e30
 HIDDEN = pl.CostEstimate(flops=200_000_000, bytes_accessed=0, transcendentals=0)
 NT = (((1,), (1,)), ((), ()))
@@ -221,28 +222,30 @@
         return (outer * 4 + inner) * 64 + core * 16
 
 
-def pair_matrix(meta, qg_refs, side, pair, which):
-    low = lax.broadcasted_iota(jnp.int32, (DEC, 128), 1) < 64
-    half, lane = pair // 2, pair % 2
+def head_of_column(rows):
+    return lax.broadcasted_iota(jnp.int32, (rows, LANES), 1) // 64
+
+
+def head_matrix(meta, qg_refs, side, quad, which):
+    head = head_of_column(DEC)
     parts = []
     for p in range(NPASS):
-        row = pl.multiple_of(meta.row(half, side, p) + which * 32, 16)
-        tile = qg_refs[half][pl.ds(row, DEC), lane * 128 : (lane + 1) * 128]
-        zero = jnp.zeros_like(tile)
-        parts += [jnp.where(low, tile, zero), jnp.where(low, zero, tile)]
+        row = pl.multiple_of(meta.row(quad, side, p) + which * 32, 16)
+        tile = qg_refs[quad][pl.ds(row, DEC), :]
+        parts += [jnp.where(head == a, tile, jnp.zeros_like(tile)) for a in range(4)]
     return jnp.concatenate(parts, axis=0)
 
 
 def lane_value(numbers):
-    lane = lax.broadcasted_iota(jnp.int32, (1, 128), 1) // 32
-    value = jnp.zeros((1, 128), jnp.int32)
+    lane = lax.broadcasted_iota(jnp.int32, (1, LANES), 1) // 64
+    value = jnp.zeros((1, LANES), jnp.int32)
     for p in range(NPASS):
         value = jnp.where(lane == p, numbers[p], value)
     return value
 
 
 def inside_mask(meta, side):
-    row = lax.broadcasted_iota(jnp.int32, (ROWS, 128), 0)
+    row = lax.broadcasted_iota(jnp.int32, (ROWS, LANES), 0)
     starts = [meta.start(side, p) for p in range(NPASS + 1)]
     return (row >= lane_value(starts[:NPASS])) & (row < lane_value(starts[1:]))
 
@@ -255,25 +258,25 @@
     n = st_ref.shape[0]
 
     def put(row, value):
-        st_ref[:, row : row + 1, :] = jnp.broadcast_to(value[None], (n, 1, 128))
+        st_ref[:, row : row + 1, :] = jnp.broadcast_to(value[None], (n, 1, LANES))
 
     inside = inside_mask(meta, side)
     question = lane_value([meta.question(side, p) for p in range(NPASS)]).astype(F32)
-    for pair in range(PAIRS):
-        cols = slice(pair * 128, (pair + 1) * 128)
-        scores = dot_nt(k[side, :, cols], pair_matrix(meta, qg, side, pair, 0))
+    for quad in range(QUADS):
+        cols = slice(quad * CHUNK, (quad + 1) * CHUNK)
+        scores = dot_nt(k[side, :, cols], head_matrix(meta, qg, side, quad, 0))
         scores = jnp.where(inside, scores, LOW)
         top = jnp.max(scores, axis=0, keepdims=True)
         unnorm = jnp.exp(scores - top)
         unnorm_b = unnorm.astype(BF)
         values = v[side, :, cols]
-        dprob = dot_nt(values, pair_matrix(meta, qg, side, pair, 1))
-        at = side * PAIRS + pair
+        dprob = dot_nt(values, head_matrix(meta, qg, side, quad, 1))
+        at = side * QUADS + quad
         put(at, top)
-        put(8 + at, jnp.sum(unnorm, axis=0, keepdims=True))
-        put(16 + at, jnp.sum(unnorm_b.astype(F32) * dprob, axis=0, keepdims=True))
-        put(24 + at, question)
-        num_ref[side, pair] = lax.dot_general(values, unnorm_b, TN, preferred_element_type=F32)
+        put(4 + at, jnp.sum(unnorm, axis=0, keepdims=True))
+        put(8 + at, jnp.sum(unnorm_b.astype(F32) * dprob, axis=0, keepdims=True))
+        put(12 + at, question)
+        num_ref[side, quad] = lax.dot_general(values, unnorm_b, TN, preferred_element_type=F32)
 
 
 def far_kernel(
@@ -315,8 +318,8 @@
         jax.ShapeDtypeStruct((2, ROWS, HALF), BF),
         jax.ShapeDtypeStruct((1024, CHUNK), BF),
         jax.ShapeDtypeStruct((1024, CHUNK), BF),
-        jax.ShapeDtypeStruct((NZ * NX, 32, 128), F32),
-        jax.ShapeDtypeStruct((2, PAIRS, 128, 128), F32),
+        jax.ShapeDtypeStruct((NZ * NX, 16, LANES), F32),
+        jax.ShapeDtypeStruct((2, QUADS, LANES, CHUNK), F32),
     ]
     return pl.pallas_call(
         far_kernel,
@@ -344,29 +347,29 @@
     ]
 
     def turned(value, k):
-        return pltpu.roll(value, 32 * k, 1) if k else value
+        return pltpu.roll(value, 64 * k, 1) if k else value
 
     tops = [None, None]
     for d in range(n):
         for k in range(NPASS):
-            q, m = turned(st_ref[d, 24:32], k), turned(st_ref[d, 0:8], k)
+            q, m = turned(st_ref[d, 12:16], k), turned(st_ref[d, 0:4], k)
             for s in range(2):
                 term = jnp.where(q == own_question[s], m, LOW)
                 tops[s] = term if tops[s] is None else jnp.maximum(tops[s], term)
-    tops = [jnp.maximum(t[0:PAIRS], t[PAIRS:]) for t in tops]
+    tops = [jnp.maximum(t[0:QUADS], t[QUADS:]) for t in tops]
     both = [jnp.concatenate([t, t], axis=0) for t in tops]
     totals, deltas = [0.0, 0.0], [0.0, 0.0]
     for d in range(n):
         for k in range(NPASS):
-            q, m = turned(st_ref[d, 24:32], k), turned(st_ref[d, 0:8], k)
-            l, e = turned(st_ref[d, 8:16], k), turned(st_ref[d, 16:24], k)
+            q, m = turned(st_ref[d, 12:16], k), turned(st_ref[d, 0:4], k)
+            l, e = turned(st_ref[d, 4:8], k), turned(st_ref[d, 8:12], k)
             for s in range(2):
                 hit = q == own_question[s]
                 scale = jnp.where(hit, jnp.exp(jnp.where(hit, m - both[s], 0.0)), 0.0)
                 totals[s] = totals[s] + scale * l
                 deltas[s] = deltas[s] + scale * e
-    inverse = [1.0 / (t[0:PAIRS] + t[PAIRS:]) for t in totals]
-    deltas = [(t[0:PAIRS] + t[PAIRS:]) * i for t, i in zip(deltas, inverse)]
+    inverse = [1.0 / (t[0:QUADS] + t[QUADS:]) for t in totals]
+    deltas = [(t[0:QUADS] + t[QUADS:]) * i for t, i in zip(deltas, inverse)]
     return tops, inverse, deltas
 
 
@@ -418,42 +421,44 @@
     pos, own_numbers, other_numbers, k_ref, v_ref, qa_ref, qb_ref, st_ref, num_ref, *refs
 ):
     sources, outs = refs[:10], refs[10:]
-    kvg_ref, own_ref, oth_ref, dense_ref, ctx_ref, w_ref = outs
+    kvg_ref, oth_ref, dense_ref, ctx_ref, w_ref = outs
     take_weights(pos[2], sources, w_ref)
     meta = Passages(pos, own_numbers, other_numbers)
     qg = (qa_ref, qb_ref)
     tops, inverses, deltas = combine(meta, st_ref)
     here = meta.z * 4 + meta.x
     ctx_ref[...] = jnp.zeros_like(ctx_ref)
-    low = lax.broadcasted_iota(jnp.int32, (DEC, 128), 1) < 64
+    head = head_of_column(DEC)
     for side in (1, 0):
         inside = inside_mask(meta, side)
-        for pair in range(PAIRS):
-            cols = slice(pair * 128, (pair + 1) * 128)
-            at = side * PAIRS + pair
-            top, inverse = tops[side][pair : pair + 1], inverses[side][pair : pair + 1]
-            queries = pair_matrix(meta, qg, side, pair, 0)
-            grads = pair_matrix(meta, qg, side, pair, 1)
+        for quad in range(QUADS):
+            cols = slice(quad * CHUNK, (quad + 1) * CHUNK)
+            at = side * QUADS + quad
+            top, inverse = tops[side][quad : quad + 1], inverses[side][quad : quad + 1]
+            queries = head_matrix(meta, qg, side, quad, 0)
+            grads = head_matrix(meta, qg, side, quad, 1)
             scores = dot_nt(k_ref[side, :, cols], queries)
             unnorm = jnp.where(inside, jnp.exp(jnp.where(inside, scores - top, 0.0)), 0.0)
             probs = unnorm * inverse
             dprob = dot_nt(v_ref[side, :, cols], grads)
-            ds = (probs * (dprob - deltas[side][pair : pair + 1])).astype(BF)
+            ds = (probs * (dprob - deltas[side][quad : quad + 1])).astype(BF)
             for t, lanes, weight in ((0, queries, ds), (1, grads, probs.astype(BF))):
                 turned = lax.dot_general(
                     lanes, weight, (((0,), (1,)), ((), ())), preferred_element_type=F32
                 ).astype(BF)
-                first = t * HALF + pair * 128
-                kvg_ref[first : first + 128, side * ROWS : (side + 1) * ROWS] = turned
+                first = t * HALF + quad * CHUNK
+                kvg_ref[first : first + CHUNK, side * ROWS : (side + 1) * ROWS] = turned
             scale = jnp.exp(st_ref[here, at : at + 1, :] - top) * inverse
-            context = (num_ref[side, pair] * scale).T
+            context = (num_ref[side, quad] * scale).T
             for p in range(NPASS):
-                ctx_ref[meta.question(side, p), :, cols] += jnp.where(
-                    low, context[p * 32 : p * 32 + 16], context[p * 32 + 16 : p * 32 + 32]
-                )
-    total = jnp.dot(weights_tile(w_ref), kvg_ref[...], preferred_element_type=F32)
-    own_ref[...] = total[:, :ROWS].astype(BF)
-    oth_ref[...] = total[:, ROWS:].astype(BF)
+                part = jnp.zeros((DEC, CHUNK), F32)
+                for a in range(4):
+                    first = p * 64 + a * DEC
+                    part = jnp.where(head == a, context[first : first + DEC], part)
+                ctx_ref[meta.question(side, p), :, cols] += part
+    oth_ref[...] = jnp.dot(
+        weights_tile(w_ref), kvg_ref[:, ROWS:], preferred_element_type=F32
+    ).astype(BF)
     dense_ref[...] = ctx_ref[...].astype(BF)
 
 
@@ -463,7 +468,6 @@
 
     shapes = [
         jax.ShapeDtypeStruct((2 * HALF, 2 * ROWS), BF),
-        jax.ShapeDtypeStruct((1024, ROWS), BF),
         jax.ShapeDtypeStruct((1024, ROWS), BF),
         jax.ShapeDtypeStruct((32, DEC, HALF), BF),
     ]
@@ -483,51 +487,91 @@
     )(*meta, *args, *weights)
 
 
-def grad_kernel(places, kvg_ref, *refs):
-    sources, (own_ref, oth_ref, w_ref) = refs[:10], refs[10:]
+def own_kernel(places, kvg_ref, *refs):
+    sources, (far_ref, base_ref, other_ref, w_ref) = refs[:10], refs[10:]
+    take_weights(places[0], sources, w_ref)
+    far_ref[...] = jnp.dot(
+        weights_tile(w_ref), kvg_ref[:, :ROWS], preferred_element_type=F32
+    ).astype(BF)
+    take_weights(places[1], sources, w_ref)
+    total = jnp.dot(weights_tile(w_ref), kvg_ref[...], preferred_element_type=F32)
+    base_ref[...] = total[:, :ROWS]
+    other_ref[...] = total[:, ROWS:].astype(BF)
+
+
+def own_blocks(places, kvg, weights):
+    out = pl.BlockSpec((1024, ROWS), lambda i, p: (0, 0))
+    return pl.pallas_call(
+        own_kernel,
+        grid_spec=pltpu.PrefetchScalarGridSpec(
+            num_scalar_prefetch=1,
+            grid=(1,),
+            in_specs=[pl.BlockSpec(kvg.shape, lambda i, p: (0, 0))] + weight_specs(),
+            out_specs=[out] * 3,
+            scratch_shapes=[WEIGHT_SCRATCH],
+        ),
+        out_shape=[jax.ShapeDtypeStruct((1024, ROWS), t) for t in (BF, F32, BF)],
+        compiler_params=params(34),
+        cost_estimate=HIDDEN,
+    )(places, kvg, *weights)
+
+
+def far_sums_kernel(own_ref, got_ref, top_ref, low_ref):
+    for h, out in enumerate((top_ref, low_ref)):
+        rows = slice(h * 512, (h + 1) * 512)
+        out[...] = (own_ref[rows].astype(F32) + got_ref[rows].astype(F32)).astype(BF)
+
+
+def far_sums(own, got):
+    return pl.pallas_call(
+        far_sums_kernel,
+        out_shape=[jax.ShapeDtypeStruct((512, ROWS), BF)] * 2,
+        compiler_params=params(16),
+        cost_estimate=HIDDEN,
+    )(own, got)
+
+
+def near_grad_kernel(places, kvg_ref, *refs):
+    sources, (out_ref, w_ref) = refs[:10], refs[10:]
     take_weights(places[pl.program_id(0)], sources, w_ref)
     total = jnp.dot(weights_tile(w_ref), kvg_ref[...], preferred_element_type=F32)
-    own_ref[0] = total[:, :ROWS].astype(own_ref.dtype)
-    oth_ref[0] = total[:, ROWS:].astype(oth_ref.dtype)
-
-
-def grad_blocks(places, kvg, weights, dtype):
-    count = places.shape[0]
-    out = pl.BlockSpec((1, 1024, ROWS), lambda i, p: (i, 0, 0))
-    return pl.pallas_call(
-        grad_kernel,
+    core = places[2]
+    out_ref[core, 0] = total[:, :ROWS].astype(BF)
+    out_ref[1 - core, 0] = total[:, ROWS:].astype(BF)
+
+
+def near_blocks(places, kvg, weights):
+    return pl.pallas_call(
+        near_grad_kernel,
         grid_spec=pltpu.PrefetchScalarGridSpec(
             num_scalar_prefetch=1,
-            grid=(count,),
+            grid=(2,),
             in_specs=[pl.BlockSpec(kvg.shape, lambda i, p: (0, 0))] + weight_specs(),
-            out_specs=[out, out],
+            out_specs=pl.BlockSpec((2, 1, 1024, ROWS), lambda i, p: (0, i, 0, 0)),
             scratch_shapes=[WEIGHT_SCRATCH],
         ),
-        out_shape=[
-            jax.ShapeDtypeStruct((count, 1024, ROWS), dtype),
-            jax.ShapeDtypeStruct((count, 1024, ROWS), BF),
-        ],
+        out_shape=jax.ShapeDtypeStruct((2, 2, 1024, ROWS), BF),
         compiler_params=params(34),
         cost_estimate=HIDDEN,
     )(places, kvg, *weights)
 
 
-def sums_kernel(own_ref, got_ref, below_ref, above_ref, *outs):
+def sums_kernel(near_ref, below_ref, above_ref, *outs):
     for out, k, h, more in zip(outs, (0, 1, 0, 1), (1, 0, 0, 1), (None, None, below_ref, above_ref)):
         rows = slice(h * 512, (h + 1) * 512)
-        total = own_ref[k, rows].astype(F32) + got_ref[k, rows].astype(F32)
+        total = near_ref[0, k, rows].astype(F32) + near_ref[1, k, rows].astype(F32)
         if more is not None:
             total = total + more[...].astype(F32)
         out[...] = total.astype(BF)
 
 
-def near_sums(own, got, below, above):
+def near_sums(near, below, above):
     return pl.pallas_call(
         sums_kernel,
         out_shape=[jax.ShapeDtypeStruct((512, ROWS), BF)] * 4,
         compiler_params=params(16),
         cost_estimate=HIDDEN,
-    )(own, got, below, above)
+    )(near, below, above)
 
 
 def finish_kernel(
@@ -584,7 +628,8 @@
     four = jnp.arange(4, dtype=jnp.int32)
     zs, xs = (z + four) % 4, (x + four) % 4
     places = ((y + four - z) % 4).astype(jnp.int32)
-    near_places, base_place = places[1::2], places[0:1]
+    near_places = jnp.stack([places[1], places[3], core.astype(jnp.int32)])
+    own_places = jnp.stack([places[2], places[0]])
     pos = jnp.stack([z, x, places[2]]).astype(jnp.int32)
 
     cat = jnp.concatenate([key_weight, value_weight, queries[0], ctx_grad[0]], axis=0)
@@ -607,11 +652,11 @@
     )
 
     steps = [(v, a, h) for v, (a, h) in zip(halves, (("x", 0), ("x", 1), ("z", 0), ("z", 1)))]
-    met, pos, near_places, base_place, x_place, xs = phase(
+    met, pos, near_places, own_places, x_place, xs = phase(
         [pair_perm(v, a, h) for v, a, h in steps],
         pos,
         near_places,
-        base_place,
+        own_places,
         x.astype(jnp.int32).reshape(1),
         xs.astype(jnp.int32),
     )
@@ -639,29 +684,28 @@
     keys, values, qa, qb, stats, numer = project_far(meta, enc_far, acc, far, qa, qb)
     stats_all = lax.all_to_all(stats, ("z", "x"), 0, 0, tiled=True)
     weights = [a_own, a_up, far[0], far[1], a_down, b_own, b_up, far[2], far[3], b_down]
-    kvg, far_own, far_other, dense = backward(
+    kvg, far_other, dense = backward(
         meta, (keys, values, qa, qb, stats_all, numer), weights
     )
 
-    def add(*values):
-        return sum(v.astype(F32) for v in values).astype(BF)
-
     far_got = perm(far_other, "core", 1)
-    near_own, near_other = grad_blocks(near_places, kvg, weights, BF)
-    far_got, near_own, near_other, kvg, dense = phase(far_got, near_own, near_other, kvg, dense)
-
-    far_top, far_low = add(far_own[:512], far_got[:512]), add(far_own[512:], far_got[512:])
-    far_top, far_low, near_other, kvg, dense = phase(far_top, far_low, near_other, kvg, dense)
+    far_own, base, base_other = own_blocks(own_places, kvg, weights)
+    far_got, far_own, base, base_other, kvg, dense = phase(
+        far_got, far_own, base, base_other, kvg, dense
+    )
+
+    far_top, far_low, base, base_other, kvg, dense = phase(
+        *far_sums(far_own, far_got), base, base_other, kvg, dense
+    )
     from_below = perm(far_top, "dec", 1)
     from_above = perm(far_low, "dec", -1)
-    near_got = perm(near_other, "core", 1)
-    base, base_other = grad_blocks(base_place, kvg, weights, F32)
-    from_below, from_above, near_got, base, base_other, dense = phase(
-        from_below, from_above, near_got, base[0], base_other[0], dense
+    near = lax.all_to_all(near_blocks(near_places, kvg, weights), "core", 0, 0, tiled=True)
+    from_below, from_above, near, base, base_other, dense = phase(
+        from_below, from_above, near, base, base_other, dense
     )
 
     *sums, dense, base_other = phase(
-        *near_sums(near_own, near_got, from_below, from_above), dense, base_other
+        *near_sums(near, from_below, from_above), dense, base_other
     )
     low_below = perm(sums[0], "dec", 1)
     top_above = perm(sums[1], "dec", -1)

time: 152 us -> 150 us (0.987)
  waiting for transfers between devices: 47.3 us -> 36.1 us
  blocking collectives: 27.6 us -> 34.5 us
  other arithmetic: 2.37 us -> 4.59 us
    ppermute x20 -> x19, waiting for transfers between devices: 42.1 us -> 31.4 us  [perm(): return lax.ppermute(v, axis, [(i, (i + shift) % n) for i in range(n)])]
    all_to_all x0 -> x1, blocking collectives: none -> 7.17 us  [body(): lax.all_to_all(near_blocks(near_places, kvg, weights), 'core', 0, 0, tile...]
    pallas_call x2 -> x3, Pallas kernels: 8.7 us -> 10.8 us  [the longest x1 5.87 us: near_blocks(): pl.pallas_call(near_grad_kernel, grid_spec=pltpu.PrefetchScalarGridSpec(n...]
    ppermute x20 -> x19, starting transfers between devices: 27.7 us -> 28.2 us  [perm(): return lax.ppermute(v, axis, [(i, (i + shift) % n) for i in range(n)])]
  transfers between devices with their start and end apart: 28 -> 27, of which waited for: 13 -> 8; matrix products, arithmetic and copies ran while one was open for 1% -> 3% of each run, Pallas kernels for 12% -> 14%
where the time goes in v5:
time: 150 us
  starting transfers between devices  38.4 us (26%)
  waiting for transfers between devices  36.1 us (24%)
  Pallas kernels  34.7 us (23%)
  blocking collectives  34.5 us (23%)
  other arithmetic  4.59 us (3%)
    ppermute x19, waiting for transfers between devices, perm(): return lax.ppermute(v, axis, [(i, (i + shift) % n) for i in range(n)])  31.4 us
    ppermute x19, starting transfers between devices, perm(): return lax.ppermute(v, axis, [(i, (i + shift) % n) for i in range(n)])  28.2 us
    all_to_all x1, blocking collectives, body(): lax.all_to_all(dense, ENC, 0, 0, tiled=True).reshape(NZ * NX, NC, DEC, HALF)  15.8 us
    all_to_all x1, blocking collectives, body(): stats_all = lax.all_to_all(stats, ('z', 'x'), 0, 0, tiled=True)  11.6 us
    ppermute x8, starting transfers between devices, pair_perm(): return lax.ppermute(v, axis, [(i, turn(i) % 4) for i in range(4)])  10.3 us
    pallas_call x1, Pallas kernels, project_near(): pl.pallas_call(near_kernel, grid_spec=pltpu.PrefetchScalarGridSpec(num_sc...  9.86 us
    all_to_all x1, blocking collectives, body(): lax.all_to_all(near_blocks(near_places, kvg, weights), 'core', 0, 0, tile...  7.17 us
    pallas_call x1, Pallas kernels, near_blocks(): pl.pallas_call(near_grad_kernel, grid_spec=pltpu.PrefetchScalarGridSpec(n...  5.87 us
  transfers between devices with their start and end apart: 27, of which 8 were waited for; matrix products, arithmetic and copies ran while one was open for 3% of the time, Pallas kernels for 14%

profile of v5, /device:TPU:1, one launch (start us, length us, event | category | flops | bytes accessed | tf_op | source)
XLA Modules:
  0.0 150.0 jit_solution(2944782239316455202)
XLA Ops:
  0.6 1.1 pad_maximum_fusion
  1.8 1.5 %collective-permute-start = (bf16[288,512]{1,0:T(8,128)(2,1)S(1)}, bf16[288,512]{1,0:T(8,128)(2,1)S(1)}, u32[]{:S(2)}, u32[]{:S(2)}) collective-permute-start(bf16[288,512]{1,0:T(8,128)(2,1)S(1)} %constant_dynamic-slice_fusion), channel_id=1, source_target_pairs={{0,4},{4,0},{1,5},{5,1},{2,6},{6,2},{3,7},{7,3},{8,12},{12,8},{9,1... | collective-permute-start | bytes 884744 | tf_op jit(solution)/shard_map/ppermute | solution.py:29
  3.3 1.2 collective-permute-done
  4.5 0.4 collective-permute-start.5
  4.9 0.7 fusion.3
  5.5 0.1 broadcast_select_fusion
  5.9 1.4 collective-permute-start.1
  7.3 1.8 %collective-permute-start.2 = (bf16[288,256]{1,0:T(8,128)(2,1)S(1)}, bf16[288,256]{1,0:T(8,128)(2,1)S(1)}, u32[]{:S(2)}, u32[]{:S(2)}) collective-permute-start(bf16[288,256]{1,0:T(8,128)(2,1)S(1)} %get-tuple-element.97.refs_2_), channel_id=1, source_target_pairs={{0,24},{8,16},{16,8},{24,0},{1,25},{9,17},{17,9},{25,1},{2,26},{10... | collective-permute-start | bytes 442376 | tf_op jit(solution)/shard_map/ppermute | solution.py:42
  9.1 1.6 %collective-permute-start.3 = (bf16[288,256]{1,0:T(8,128)(2,1)S(1)}, bf16[288,256]{1,0:T(8,128)(2,1)S(1)}, u32[]{:S(2)}, u32[]{:S(2)}) collective-permute-start(bf16[288,256]{1,0:T(8,128)(2,1)S(1)} %get-tuple-element.98.refs_4_), channel_id=1, source_target_pairs={{0,32},{32,0},{64,96},{96,64},{1,33},{33,1},{65,97},{97,65},{2,34}... | collective-permute-start | bytes 442376 | tf_op jit(solution)/shard_map/ppermute | solution.py:42
  10.7 2.2 %collective-permute-start.4 = (bf16[288,256]{1,0:T(8,128)(2,1)S(1)}, bf16[288,256]{1,0:T(8,128)(2,1)S(1)}, u32[]{:S(2)}, u32[]{:S(2)}) collective-permute-start(bf16[288,256]{1,0:T(8,128)(2,1)S(1)} %get-tuple-element.99.refs_6_), channel_id=1, source_target_pairs={{0,96},{32,64},{64,32},{96,0},{1,97},{33,65},{65,33},{97,1},{2,98}... | collective-permute-start | bytes 442376 | tf_op jit(solution)/shard_map/ppermute | solution.py:42
  12.9 1.3 pad_add_fusion.2.places
  14.2 1.9 %pad_add_fusion = (s32[3]{0:T(128)S(1)}, s32[3]{0:T(128)S(1)}) fusion(s32[1]{0:T(128)} %get-tuple-element.202, s32[1]{0:T(128)} %bitcast.3.place, s32[1]{0:T(128)} %bitcast.2, s32[1]{0:T(128)} %bitcast.4, s32[1]{0:T(128)} %get-tuple-element.200, s32[1]{0:T(128)} %get-tuple-element.201), kind=kLoop, calls=%fused_computation.20 | loop fusion | flops 12 | bytes 48 | tf_op jit(solution)/shard_map/stack | solution.py:633
  16.2 0.1 collective-permute-done.4.refs_7_
  16.4 0.9 collective-permute-start.7
  17.3 2.2 %collective-permute-start.9 = (bf16[576,256]{1,0:T(8,128)(2,1)S(1)}, bf16[576,256]{1,0:T(8,128)(2,1)S(1)}, u32[]{:S(2)}, u32[]{:S(2)}) collective-permute-start(bf16[576,256]{1,0:T(8,128)(2,1)S(1)} %get-tuple-element.110.joined0), channel_id=1, source_target_pairs={{0,96},{32,64},{64,32},{96,0},{1,97},{33,65},{65,33},{97,1},{2,98}... | collective-permute-start | bytes 884744 | tf_op jit(solution)/shard_map/ppermute | solution.py:42
  19.6 4.6 %collective-permute-done.7.second0 = bf16[576,256]{1,0:T(8,128)(2,1)S(1)} collective-permute-done((bf16[576,256]{1,0:T(8,128)(2,1)S(1)}, bf16[576,256]{1,0:T(8,128)(2,1)S(1)}, u32[]{:S(2)}, u32[]{:S(2)}) %collective-permute-start.7) | collective-permute-done | bytes 294944 | tf_op jit(solution)/shard_map/ppermute | solution.py:42
  24.2 2.8 %collective-permute-start.6 = (s32[8]{0:T(128)S(1)}, s32[8]{0:T(128)S(1)}, u32[]{:S(2)}, u32[]{:S(2)}) collective-permute-start(s32[8]{0:T(128)S(1)} %pad_add_fusion.3.own_numbers), channel_id=1, source_target_pairs={{0,4},{4,0},{1,5},{5,1},{2,6},{6,2},{3,7},{7,3},{8,12},{12,8},{9,1... | collective-permute-start | bytes 104 | tf_op jit(solution)/shard_map/ppermute | solution.py:29
  27.1 0.1 shard_map.87.refs_0_
  27.2 0.1 shard_map.88.refs_3_.refs_5_
  27.3 0.6 collective-permute-done.6.other_numbers
  27.9 0.7 collective-permute-start.12
  28.5 2.0 %collective-permute-start.11 = (bf16[2,1152,256]{2,1,0:T(8,128)(2,1)S(1)}, bf16[2,1152,256]{2,1,0:T(8,128)(2,1)S(1)}, u32[]{:S(2)}, u32[]{:S(2)}) collective-permute-start(bf16[2,1152,256]{2,1,0:T(8,128)(2,1)S(1)} %shard_map.87.refs_0_), channel_id=1, source_target_pairs={{0,96},{32,0},{64,32},{96,64},{1,97},{33,1},{65,33},{97,65},{2,98}... | collective-permute-start | bytes 3538952 | tf_op jit(solution)/shard_map/ppermute | solution.py:29
  30.6 2.7 %collective-permute-start.15 = (bf16[2,1152,256]{2,1,0:T(8,128)(2,1)S(1)}, bf16[2,1152,256]{2,1,0:T(8,128)(2,1)S(1)}, u32[]{:S(2)}, u32[]{:S(2)}) collective-permute-start(bf16[2,1152,256]{2,1,0:T(8,128)(2,1)S(1)} %shard_map.88.refs_3_.refs_5_), channel_id=1, source_target_pairs={{0,24},{8,0},{16,8},{24,16},{1,25},{9,1},{17,9},{25,17},{2,26},{10... | collective-permute-start | bytes 3538952 | tf_op jit(solution)/shard_map/ppermute | solution.py:29
  33.2 22.0 %collective-permute-done.12.down_ref.refs_2_.refs_4_ = bf16[2,1152,256]{2,1,0:T(8,128)(2,1)S(1)} collective-permute-done((bf16[2,1152,256]{2,1,0:T(8,128)(2,1)S(1)}, bf16[2,1152,256]{2,1,0:T(8,128)(2,1)S(1)}, u32[]{:S(2)}, u32[]{:S(2)}) %collective-permute-start.12) | collective-permute-done | bytes 1179680 | tf_op jit(solution)/shard_map/ppermute | solution.py:29
  55.4 2.5 %collective-permute-start.13 = (bf16[1152,256]{1,0:T(8,128)(2,1)S(1)}, bf16[1152,256]{1,0:T(8,128)(2,1)S(1)}, u32[]{:S(2)}, u32[]{:S(2)}) collective-permute-start(bf16[1152,256]{1,0:T(8,128)(2,1)S(1)} %get-tuple-element.116), channel_id=1, source_target_pairs={{0,96},{32,0},{64,32},{96,64},{1,97},{33,1},{65,33},{97,65},{2,98}... | collective-permute-start | bytes 1769480 | tf_op jit(solution)/shard_map/ppermute | solution.py:29
  57.8 0.1 shard_map.90
  57.9 2.0 %collective-permute-start.17 = (bf16[1152,256]{1,0:T(8,128)(2,1)S(1)}, bf16[1152,256]{1,0:T(8,128)(2,1)S(1)}, u32[]{:S(2)}, u32[]{:S(2)}) collective-permute-start(bf16[1152,256]{1,0:T(8,128)(2,1)S(1)} %get-tuple-element.121), channel_id=1, source_target_pairs={{0,24},{8,0},{16,8},{24,16},{1,25},{9,1},{17,9},{25,17},{2,26},{10... | collective-permute-start | bytes 1769480 | tf_op jit(solution)/shard_map/ppermute | solution.py:29
  59.9 9.9 %shard_map.91 = (f32[2,512,1024]{2,1,0:T(8,128)S(1)}, bf16[2,512,2048]{2,1,0:T(8,128)(2,1)S(1)}, bf16[1024,256]{1,0:T(8,128)(2,1)S(1)}, bf16[1024,256]{1,0:T(8,128)(2,1)S(1)}) custom-call(s32[3]{0:T(128)S(1)} %get-tuple-element.101.pos, bf16[512,4096]{1,0:T(8,128)(2,1)S(1)} %copy-done, bf16[512,4096]{1,0:T(8,128)(2,1)} %collective-permute-done.5.oth_ref, ...), custom_call_target="tpu_custom_call" | custom-call | flops 200000000 | tf_op jit(solution)/shard_map/pallas_call | solution.py:173
  69.8 1.3 collective-permute-done.14.a_low.refs_3_
  71.1 1.6 %collective-permute-done.18.b_low.refs_8_ = bf16[1152,256]{1,0:T(8,128)(2,1)S(1)} collective-permute-done((bf16[1152,256]{1,0:T(8,128)(2,1)S(1)}, bf16[1152,256]{1,0:T(8,128)(2,1)S(1)}, u32[]{:S(2)}, u32[]{:S(2)}) %collective-permute-start.18) | collective-permute-done | bytes 589856 | tf_op jit(solution)/shard_map/ppermute | solution.py:29
  72.6 5.3 %shard_map.92 = (bf16[2,512,512]{2,1,0:T(8,128)(2,1)S(1)}, bf16[2,512,512]{2,1,0:T(8,128)(2,1)S(1)}, bf16[1024,256]{1,0:T(8,128)(2,1)S(1)}, bf16[1024,256]{1,0:T...) custom-call(s32[3]{0:T(128)S(1)} %get-tuple-element.101.pos, ...), custom_call_target="tpu_custom_call" | custom-call | flops 200000000 | tf_op jit(solution)/shard_map/pallas_call | solution.py:324
  78.0 11.6 %all_to_all.15.st_ref = f32[16,16,256]{2,1,0:T(8,128)S(1)} all-to-all(f32[16,16,256]{2,1,0:T(8,128)S(1)} %get-tuple-element.140), channel_id=1, replica_groups=mesh['z'=4,'x'=4,'core'=2,'dec'=4] {'z','x'}, dimensions={0} | all-to-all | bytes 524288 | tf_op jit(solution)/shard_map/all_to_all | solution.py:685
  89.5 4.6 %shard_map.93 = (bf16[1024,1024]{1,0:T(8,128)(2,1)S(1)}, bf16[1024,512]{1,0:T(8,128)(2,1)S(1)}, bf16[32,16,512]{2,1,0:T(8,128)(2,1)S(1)}) custom-call(s32[3]{0:T(128)S(1)} %get-tuple-element.101.pos, s32[8]{0:T(128)S(1)} %pad_add_fusion.3.own_numbers, s32[8]{0:T(128)S(1)} %collective-permute-done.6.other_numbers, ...), custom_call_target="tpu_custom_call" | custom-call | flops 200000000 | tf_op jit(solution)/shard_map/pallas_call | solution.py:474
  94.1 4.9 %collective-permute-start.19 = (bf16[1024,512]{1,0:T(8,128)(2,1)S(1)}, bf16[1024,512]{1,0:T(8,128)(2,1)S(1)}, u32[]{:S(2)}, u32[]{:S(2)}) collective-permute-start(bf16[1024,512]{1,0:T(8,128)(2,1)S(1)} %get-tuple-element.142), channel_id=1, source_target_pairs={{0,4},{4,0},{1,5},{5,1},{2,6},{6,2},{3,7},{7,3},{8,12},{12,8},{9,1... | collective-permute-start | bytes 3145736 | tf_op jit(solution)/shard_map/ppermute | solution.py:29
  99.1 4.7 %shard_map.94 = (bf16[1024,512]{1,0:T(8,128)(2,1)S(1)}, f32[1024,512]{1,0:T(8,128)S(1)}, bf16[1024,512]{1,0:T(8,128)(2,1)S(1)}) custom-call(s32[2]{0:T(128)S(1)} %pad_add_fusion.2.places, bf16[1024,1024]{1,0:T(8,128)(2,1)S(1)} %get-tuple-element.160.kvg_ref, bf16[2,1152,256]{2,1,0:T(8,128)(2,1)S(1)} %shard_map.87.refs_0_, ...), custom_call_target="tpu_custom_call" | custom-call | flops 200000000 | tf_op jit(solution)/shard_map/pallas_call | solution.py:504
  103.7 0.2 shard_map.95
  104.0 1.4 collective-permute-start.20
  105.4 1.5 %collective-permute-start.21 = (bf16[512,512]{1,0:T(8,128)(2,1)S(1)}, bf16[512,512]{1,0:T(8,128)(2,1)S(1)}, u32[]{:S(2)}, u32[]{:S(2)}) collective-permute-start(bf16[512,512]{1,0:T(8,128)(2,1)S(1)} %get-tuple-element.158), channel_id=1, source_target_pairs={{0,3},{1,0},{2,1},{3,2},{4,7},{5,4},{6,5},{7,6},{8,11},{9,8},{10,9... | collective-permute-start | bytes 1572872 | tf_op jit(solution)/shard_map/ppermute | solution.py:29
  106.9 5.9 %shard_map.96 = bf16[2,2,1024,512]{3,2,1,0:T(8,128)(2,1)S(1)} custom-call(s32[3]{0:T(128)S(1)} %get-tuple-element.159.places, bf16[1024,1024]{1,0:T(8,128)(2,1)S(1)} %get-tuple-element.160.kvg_ref, bf16[2,1152,256]{2,1,0:T(8,128)(2,1)S(1)} %shard_map.87.refs_0_, bf16[2,1152,256]{2,1,0:T(8,128)(2,1)S(1)} %collective-permute-done.11.up_ref.refs_1_, ...), custom_call_target="tpu_custom_call" | custom-call | flops 200000000 | tf_op jit(solution)/shard_map/pallas_call | solution.py:544
  112.8 7.2 %all_to_all.16.near_ref = bf16[2,2,1024,512]{3,2,1,0:T(8,128)(2,1)S(1)} all-to-all(bf16[2,2,1024,512]{3,2,1,0:T(8,128)(2,1)S(1)} %shard_map.96), channel_id=1, replica_groups=mesh['z'=4,'x'=4,'core'=2,'dec'=4] {'core'}, dimensions={0} | all-to-all | bytes 8388608 | tf_op jit(solution)/shard_map/all_to_all | solution.py:702
  119.9 0.6 shard_map.97
  120.6 0.5 collective-permute-start.26
  121.0 0.7 collective-permute-start.22
  121.7 2.0 %collective-permute-start.23 = (bf16[512,512]{1,0:T(8,128)(2,1)S(1)}, bf16[512,512]{1,0:T(8,128)(2,1)S(1)}, u32[]{:S(2)}, u32[]{:S(2)}) collective-permute-start(bf16[512,512]{1,0:T(8,128)(2,1)S(1)} %get-tuple-element.175), channel_id=1, source_target_pairs={{0,3},{1,0},{2,1},{3,2},{4,7},{5,4},{6,5},{7,6},{8,11},{9,8},{10,9... | collective-permute-start | bytes 1572872 | tf_op jit(solution)/shard_map/ppermute | solution.py:29
  123.7 2.7 %collective-permute-start.25 = (bf16[512,512]{1,0:T(8,128)(2,1)S(1)}, bf16[512,512]{1,0:T(8,128)(2,1)S(1)}, u32[]{:S(2)}, u32[]{:S(2)}) collective-permute-start(bf16[512,512]{1,0:T(8,128)(2,1)S(1)} %get-tuple-element.177), channel_id=1, source_target_pairs={{0,3},{1,0},{2,1},{3,2},{4,7},{5,4},{6,5},{7,6},{8,11},{9,8},{10,9... | collective-permute-start | bytes 1572872 | tf_op jit(solution)/shard_map/ppermute | solution.py:29
  126.4 15.8 %all_to_all.17 = bf16[32,16,512]{2,1,0:T(8,128)(2,1)S(1)} all-to-all(bf16[32,16,512]{2,1,0:T(8,128)(2,1)S(1)} %get-tuple-element.179), channel_id=1, replica_groups=mesh['z'=4,'x'=4,'core'=2,'dec'=4] {'z','x','core'}, dimensions={0} | all-to-all | bytes 1048576 | tf_op jit(solution)/shard_map/all_to_all | solution.py:715
  142.2 4.7 %collective-permute-done.24.up_top = bf16[512,512]{1,0:T(8,128)(2,1)S(1)} collective-permute-done((bf16[512,512]{1,0:T(8,128)(2,1)S(1)}, bf16[512,512]{1,0:T(8,128)(2,1)S(1)}, u32[]{:S(2)}, u32[]{:S(2)}) %collective-permute-start.24) | collective-permute-done | bytes 524320 | tf_op jit(solution)/shard_map/ppermute | solution.py:29
  146.9 3.1 %shard_map.98 = (f32[512,1024]{1,0:T(8,128)}, f32[1,16,1024]{2,1,0:T(8,128)}) custom-call(s32[4]{0:T(128)S(1)} %and_select_fusion.place, f32[1024,512]{1,0:T(8,128)S(1)} %get-tuple-element.164.base_ref, bf16[1024,512]{1,0:T(8,128)(2,1)S(1)} %collective-permute-done.26.core_ref, bf16[512,512]{1,0:T(8,128)(2,1)S(1)} %collective-permute-done.24.up_top, ...), custom_call_target="tpu_custom_call" | custom-call | flops 200000000 | tf_op jit(solution)/shard_map/pallas_call | solution.py:605
  (44 shorter events, 0.5 us)
Async XLA Ops:
  1.8 2.7 %collective-permute-start = (bf16[288,512]{1,0:T(8,128)(2,1)S(1)}, bf16[288,512]{1,0:T(8,128)(2,1)S(1)}, u32[]{:S(2)}, u32[]{:S(2)}) collective-permute-start(bf16[288,512]{1,0:T(8,128)(2,1)S(1)} %constant_dynamic-slice_fusion), channel_id=1, source_target_pairs={{0,4},{4,0},{1,5},{5,1},{2,6},{6,2},{3,7},{7,3},{8,12},{12,8},{9,1... | collective-permute-start | bytes 884744 | tf_op jit(solution)/shard_map/ppermute | solution.py:29
  4.5 23.4 %collective-permute-start.5 = (bf16[512,4096]{1,0:T(8,128)(2,1)}, bf16[512,4096]{1,0:T(8,128)(2,1)}, u32[]{:S(2)}, u32[]{:S(2)}) collective-permute-start(bf16[512,4096]{1,0:T(8,128)(2,1)} %own_ref.1), channel_id=1, source_target_pairs={{0,4},{4,0},{1,5},{5,1},{2,6},{6,2},{3,7},{7,3},{8,12},{12,8},{9,1... | collective-permute-start | bytes 12582920 | tf_op jit(solution)/shard_map/ppermute | solution.py:29
  5.8 13.7 %copy-start.1 = (s32[4,1]{0,1:T(1,128)S(1)}, s32[4,1]{0,1:T(1,128)}, u32[]{:S(2)}) copy-start(s32[4,1]{0,1:T(1,128)} %param.13) | copy-start | bytes 52
  5.8 13.7 %copy-start.2 = (s32[1,4]{1,0:T(1,128)S(1)}, s32[1,4]{1,0:T(1,128)}, u32[]{:S(2)}) copy-start(s32[1,4]{1,0:T(1,128)} %param.12) | copy-start | bytes 52
  5.9 10.3 %collective-permute-start.1 = (bf16[288,256]{1,0:T(8,128)(2,1)S(1)}, bf16[288,256]{1,0:T(8,128)(2,1)S(1)}, u32[]{:S(2)}, u32[]{:S(2)}) collective-permute-start(bf16[288,256]{1,0:T(8,128)(2,1)S(1)} %get-tuple-element.96.refs_0_), channel_id=1, source_target_pairs={{0,8},{8,0},{16,24},{24,16},{1,9},{9,1},{17,25},{25,17},{2,10},{10... | collective-permute-start | bytes 442376 | tf_op jit(solution)/shard_map/ppermute | solution.py:42
  7.3 8.9 %collective-permute-start.2 = (bf16[288,256]{1,0:T(8,128)(2,1)S(1)}, bf16[288,256]{1,0:T(8,128)(2,1)S(1)}, u32[]{:S(2)}, u32[]{:S(2)}) collective-permute-start(bf16[288,256]{1,0:T(8,128)(2,1)S(1)} %get-tuple-element.97.refs_2_), channel_id=1, source_target_pairs={{0,24},{8,16},{16,8},{24,0},{1,25},{9,17},{17,9},{25,1},{2,26},{10... | collective-permute-start | bytes 442376 | tf_op jit(solution)/shard_map/ppermute | solution.py:42
  9.1 7.1 %collective-permute-start.3 = (bf16[288,256]{1,0:T(8,128)(2,1)S(1)}, bf16[288,256]{1,0:T(8,128)(2,1)S(1)}, u32[]{:S(2)}, u32[]{:S(2)}) collective-permute-start(bf16[288,256]{1,0:T(8,128)(2,1)S(1)} %get-tuple-element.98.refs_4_), channel_id=1, source_target_pairs={{0,32},{32,0},{64,96},{96,64},{1,33},{33,1},{65,97},{97,65},{2,34}... | collective-permute-start | bytes 442376 | tf_op jit(solution)/shard_map/ppermute | solution.py:42
  10.7 5.6 %collective-permute-start.4 = (bf16[288,256]{1,0:T(8,128)(2,1)S(1)}, bf16[288,256]{1,0:T(8,128)(2,1)S(1)}, u32[]{:S(2)}, u32[]{:S(2)}) collective-permute-start(bf16[288,256]{1,0:T(8,128)(2,1)S(1)} %get-tuple-element.99.refs_6_), channel_id=1, source_target_pairs={{0,96},{32,64},{64,32},{96,0},{1,97},{33,65},{65,33},{97,1},{2,98}... | collective-permute-start | bytes 442376 | tf_op jit(solution)/shard_map/ppermute | solution.py:42
  16.4 7.9 %collective-permute-start.7 = (bf16[576,256]{1,0:T(8,128)(2,1)S(1)}, bf16[576,256]{1,0:T(8,128)(2,1)S(1)}, u32[]{:S(2)}, u32[]{:S(2)}) collective-permute-start(bf16[576,256]{1,0:T(8,128)(2,1)S(1)} %get-tuple-element.108.joined0), channel_id=1, source_target_pairs={{0,24},{8,16},{16,8},{24,0},{1,25},{9,17},{17,9},{25,1},{2,26},{10... | collective-permute-start | bytes 884744 | tf_op jit(solution)/shard_map/ppermute | solution.py:42
  17.3 9.8 %collective-permute-start.8 = (bf16[576,256]{1,0:T(8,128)(2,1)S(1)}, bf16[576,256]{1,0:T(8,128)(2,1)S(1)}, u32[]{:S(2)}, u32[]{:S(2)}) collective-permute-start(bf16[576,256]{1,0:T(8,128)(2,1)S(1)} %get-tuple-element.109.joined1), channel_id=1, source_target_pairs={{0,8},{8,0},{16,24},{24,16},{1,9},{9,1},{17,25},{25,17},{2,10},{10... | collective-permute-start | bytes 884744 | tf_op jit(solution)/shard_map/ppermute | solution.py:42
  17.3 9.9 %collective-permute-start.9 = (bf16[576,256]{1,0:T(8,128)(2,1)S(1)}, bf16[576,256]{1,0:T(8,128)(2,1)S(1)}, u32[]{:S(2)}, u32[]{:S(2)}) collective-permute-start(bf16[576,256]{1,0:T(8,128)(2,1)S(1)} %get-tuple-element.110.joined0), channel_id=1, source_target_pairs={{0,96},{32,64},{64,32},{96,0},{1,97},{33,65},{65,33},{97,1},{2,98}... | collective-permute-start | bytes 884744 | tf_op jit(solution)/shard_map/ppermute | solution.py:42
  19.5 7.6 %collective-permute-start.10 = (bf16[576,256]{1,0:T(8,128)(2,1)S(1)}, bf16[576,256]{1,0:T(8,128)(2,1)S(1)}, u32[]{:S(2)}, u32[]{:S(2)}) collective-permute-start(bf16[576,256]{1,0:T(8,128)(2,1)S(1)} %get-tuple-element.111.joined1), channel_id=1, source_target_pairs={{0,32},{32,0},{64,96},{96,64},{1,33},{33,1},{65,97},{97,65},{2,34}... | collective-permute-start | bytes 884744 | tf_op jit(solution)/shard_map/ppermute | solution.py:42
  24.2 3.6 %collective-permute-start.6 = (s32[8]{0:T(128)S(1)}, s32[8]{0:T(128)S(1)}, u32[]{:S(2)}, u32[]{:S(2)}) collective-permute-start(s32[8]{0:T(128)S(1)} %pad_add_fusion.3.own_numbers), channel_id=1, source_target_pairs={{0,4},{4,0},{1,5},{5,1},{2,6},{6,2},{3,7},{7,3},{8,12},{12,8},{9,1... | collective-permute-start | bytes 104 | tf_op jit(solution)/shard_map/ppermute | solution.py:29
  27.9 27.4 %collective-permute-start.12 = (bf16[2,1152,256]{2,1,0:T(8,128)(2,1)S(1)}, bf16[2,1152,256]{2,1,0:T(8,128)(2,1)S(1)}, u32[]{:S(2)}, u32[]{:S(2)}) collective-permute-start(bf16[2,1152,256]{2,1,0:T(8,128)(2,1)S(1)} %shard_map.87.refs_0_), channel_id=1, source_target_pairs={{0,32},{32,64},{64,96},{96,0},{1,33},{33,65},{65,97},{97,1},{2,34}... | collective-permute-start | bytes 3538952 | tf_op jit(solution)/shard_map/ppermute | solution.py:29
  28.5 26.7 %collective-permute-start.11 = (bf16[2,1152,256]{2,1,0:T(8,128)(2,1)S(1)}, bf16[2,1152,256]{2,1,0:T(8,128)(2,1)S(1)}, u32[]{:S(2)}, u32[]{:S(2)}) collective-permute-start(bf16[2,1152,256]{2,1,0:T(8,128)(2,1)S(1)} %shard_map.87.refs_0_), channel_id=1, source_target_pairs={{0,96},{32,0},{64,32},{96,64},{1,97},{33,1},{65,33},{97,65},{2,98}... | collective-permute-start | bytes 3538952 | tf_op jit(solution)/shard_map/ppermute | solution.py:29
  30.6 27.3 %collective-permute-start.16 = (bf16[2,1152,256]{2,1,0:T(8,128)(2,1)S(1)}, bf16[2,1152,256]{2,1,0:T(8,128)(2,1)S(1)}, u32[]{:S(2)}, u32[]{:S(2)}) collective-permute-start(bf16[2,1152,256]{2,1,0:T(8,128)(2,1)S(1)} %shard_map.88.refs_3_.refs_5_), channel_id=1, source_target_pairs={{0,8},{8,16},{16,24},{24,0},{1,9},{9,17},{17,25},{25,1},{2,10},{10... | collective-permute-start | bytes 3538952 | tf_op jit(solution)/shard_map/ppermute | solution.py:29
  30.6 27.3 %collective-permute-start.15 = (bf16[2,1152,256]{2,1,0:T(8,128)(2,1)S(1)}, bf16[2,1152,256]{2,1,0:T(8,128)(2,1)S(1)}, u32[]{:S(2)}, u32[]{:S(2)}) collective-permute-start(bf16[2,1152,256]{2,1,0:T(8,128)(2,1)S(1)} %shard_map.88.refs_3_.refs_5_), channel_id=1, source_target_pairs={{0,24},{8,0},{16,8},{24,16},{1,25},{9,1},{17,9},{25,17},{2,26},{10... | collective-permute-start | bytes 3538952 | tf_op jit(solution)/shard_map/ppermute | solution.py:29
  55.3 4.7 %copy-start = (bf16[512,4096]{1,0:T(8,128)(2,1)S(1)}, bf16[512,4096]{1,0:T(8,128)(2,1)}, u32[]{:S(2)}) copy-start(bf16[512,4096]{1,0:T(8,128)(2,1)} %own_ref.1) | copy-start | bytes 12582916
  55.4 14.5 %collective-permute-start.13 = (bf16[1152,256]{1,0:T(8,128)(2,1)S(1)}, bf16[1152,256]{1,0:T(8,128)(2,1)S(1)}, u32[]{:S(2)}, u32[]{:S(2)}) collective-permute-start(bf16[1152,256]{1,0:T(8,128)(2,1)S(1)} %get-tuple-element.116), channel_id=1, source_target_pairs={{0,96},{32,0},{64,32},{96,64},{1,97},{33,1},{65,33},{97,65},{2,98}... | collective-permute-start | bytes 1769480 | tf_op jit(solution)/shard_map/ppermute | solution.py:29
  57.8 13.3 %collective-permute-start.14 = (bf16[1152,256]{1,0:T(8,128)(2,1)S(1)}, bf16[1152,256]{1,0:T(8,128)(2,1)S(1)}, u32[]{:S(2)}, u32[]{:S(2)}) collective-permute-start(bf16[1152,256]{1,0:T(8,128)(2,1)S(1)} %get-tuple-element.117), channel_id=1, source_target_pairs={{0,32},{32,64},{64,96},{96,0},{1,33},{33,65},{65,97},{97,1},{2,34}... | collective-permute-start | bytes 1769480 | tf_op jit(solution)/shard_map/ppermute | solution.py:29
  57.9 13.2 %collective-permute-start.17 = (bf16[1152,256]{1,0:T(8,128)(2,1)S(1)}, bf16[1152,256]{1,0:T(8,128)(2,1)S(1)}, u32[]{:S(2)}, u32[]{:S(2)}) collective-permute-start(bf16[1152,256]{1,0:T(8,128)(2,1)S(1)} %get-tuple-element.121), channel_id=1, source_target_pairs={{0,24},{8,0},{16,8},{24,16},{1,25},{9,1},{17,9},{25,17},{2,26},{10... | collective-permute-start | bytes 1769480 | tf_op jit(solution)/shard_map/ppermute | solution.py:29
  59.9 12.7 %collective-permute-start.18 = (bf16[1152,256]{1,0:T(8,128)(2,1)S(1)}, bf16[1152,256]{1,0:T(8,128)(2,1)S(1)}, u32[]{:S(2)}, u32[]{:S(2)}) collective-permute-start(bf16[1152,256]{1,0:T(8,128)(2,1)S(1)} %get-tuple-element.122), channel_id=1, source_target_pairs={{0,8},{8,16},{16,24},{24,0},{1,9},{9,17},{17,25},{25,1},{2,10},{10... | collective-permute-start | bytes 1769480 | tf_op jit(solution)/shard_map/ppermute | solution.py:29
  94.1 9.6 %collective-permute-start.19 = (bf16[1024,512]{1,0:T(8,128)(2,1)S(1)}, bf16[1024,512]{1,0:T(8,128)(2,1)S(1)}, u32[]{:S(2)}, u32[]{:S(2)}) collective-permute-start(bf16[1024,512]{1,0:T(8,128)(2,1)S(1)} %get-tuple-element.142), channel_id=1, source_target_pairs={{0,4},{4,0},{1,5},{5,1},{2,6},{6,2},{3,7},{7,3},{8,12},{12,8},{9,1... | collective-permute-start | bytes 3145736 | tf_op jit(solution)/shard_map/ppermute | solution.py:29
  104.0 15.9 %collective-permute-start.20 = (bf16[512,512]{1,0:T(8,128)(2,1)S(1)}, bf16[512,512]{1,0:T(8,128)(2,1)S(1)}, u32[]{:S(2)}, u32[]{:S(2)}) collective-permute-start(bf16[512,512]{1,0:T(8,128)(2,1)S(1)} %get-tuple-element.157), channel_id=1, source_target_pairs={{0,1},{1,2},{2,3},{3,0},{4,5},{5,6},{6,7},{7,4},{8,9},{9,10},{10,1... | collective-permute-start | bytes 1572872 | tf_op jit(solution)/shard_map/ppermute | solution.py:29
  105.4 14.6 %collective-permute-start.21 = (bf16[512,512]{1,0:T(8,128)(2,1)S(1)}, bf16[512,512]{1,0:T(8,128)(2,1)S(1)}, u32[]{:S(2)}, u32[]{:S(2)}) collective-permute-start(bf16[512,512]{1,0:T(8,128)(2,1)S(1)} %get-tuple-element.158), channel_id=1, source_target_pairs={{0,3},{1,0},{2,1},{3,2},{4,7},{5,4},{6,5},{7,6},{8,11},{9,8},{10,9... | collective-permute-start | bytes 1572872 | tf_op jit(solution)/shard_map/ppermute | solution.py:29
  120.6 26.3 %collective-permute-start.26 = (bf16[1024,512]{1,0:T(8,128)(2,1)S(1)}, bf16[1024,512]{1,0:T(8,128)(2,1)S(1)}, u32[]{:S(2)}, u32[]{:S(2)}) collective-permute-start(bf16[1024,512]{1,0:T(8,128)(2,1)S(1)} %get-tuple-element.178), channel_id=1, source_target_pairs={{0,4},{4,0},{1,5},{5,1},{2,6},{6,2},{3,7},{7,3},{8,12},{12,8},{9,1... | collective-permute-start | bytes 3145736 | tf_op jit(solution)/shard_map/ppermute | solution.py:29
  121.0 21.1 %collective-permute-start.22 = (bf16[512,512]{1,0:T(8,128)(2,1)S(1)}, bf16[512,512]{1,0:T(8,128)(2,1)S(1)}, u32[]{:S(2)}, u32[]{:S(2)}) collective-permute-start(bf16[512,512]{1,0:T(8,128)(2,1)S(1)} %get-tuple-element.174), channel_id=1, source_target_pairs={{0,1},{1,2},{2,3},{3,0},{4,5},{5,6},{6,7},{7,4},{8,9},{9,10},{10,1... | collective-permute-start | bytes 1572872 | tf_op jit(solution)/shard_map/ppermute | solution.py:29
  121.7 20.4 %collective-permute-start.23 = (bf16[512,512]{1,0:T(8,128)(2,1)S(1)}, bf16[512,512]{1,0:T(8,128)(2,1)S(1)}, u32[]{:S(2)}, u32[]{:S(2)}) collective-permute-start(bf16[512,512]{1,0:T(8,128)(2,1)S(1)} %get-tuple-element.175), channel_id=1, source_target_pairs={{0,3},{1,0},{2,1},{3,2},{4,7},{5,4},{6,5},{7,6},{8,11},{9,8},{10,9... | collective-permute-start | bytes 1572872 | tf_op jit(solution)/shard_map/ppermute | solution.py:29
  123.7 23.2 %collective-permute-start.24 = (bf16[512,512]{1,0:T(8,128)(2,1)S(1)}, bf16[512,512]{1,0:T(8,128)(2,1)S(1)}, u32[]{:S(2)}, u32[]{:S(2)}) collective-permute-start(bf16[512,512]{1,0:T(8,128)(2,1)S(1)} %get-tuple-element.176), channel_id=1, source_target_pairs={{0,1},{1,2},{2,3},{3,0},{4,5},{5,6},{6,7},{7,4},{8,9},{9,10},{10,1... | collective-permute-start | bytes 1572872 | tf_op jit(solution)/shard_map/ppermute | solution.py:29
  123.7 23.2 %collective-permute-start.25 = (bf16[512,512]{1,0:T(8,128)(2,1)S(1)}, bf16[512,512]{1,0:T(8,128)(2,1)S(1)}, u32[]{:S(2)}, u32[]{:S(2)}) collective-permute-start(bf16[512,512]{1,0:T(8,128)(2,1)S(1)} %get-tuple-element.177), channel_id=1, source_target_pairs={{0,3},{1,0},{2,1},{3,2},{4,7},{5,4},{6,5},{7,6},{8,11},{9,8},{10,9... | collective-permute-start | bytes 1572872 | tf_op jit(solution)/shard_map/ppermute | solution.py:29

commit v6 on v5

--- a/solution.py
+++ b/solution.py
@@ -1,3 +1,5 @@
+import functools
+
 import jax
 import jax.numpy as jnp
 from jax import lax
@@ -127,7 +129,7 @@
 
 
 def near_kernel(pos, own_ref, oth_ref, *refs):
-    blocks, (acc_ref, enc_ref, qa_ref, qb_ref) = refs[:6], refs[6:]
+    blocks, (acc_refs, enc_refs, (qa_ref, qb_ref)) = refs[:6], (refs[6:8], refs[8:10], refs[10:])
     z, x = pos[0], pos[1]
     step = pl.program_id(0)
 
@@ -148,10 +150,8 @@
                 lhs = columns(ref, side, outer, range(4))
                 term = jnp.dot(lhs, rhs, preferred_element_type=F32)
                 total = term if total is None else total + term
-            for t in range(2):
-                at = t * HALF + side * CHUNK
-                acc_ref[0, :, at : at + CHUNK] = total[:, t * CHUNK : (t + 1) * CHUNK]
-            enc_ref[0, :, side * 1024 : (side + 1) * 1024] = columns(ref, side, 2, range(4))
+            acc_refs[side][0] = total
+            enc_refs[side][0] = columns(ref, side, 2, range(4))
 
     pl.when(step < 2)(lambda: run(own_ref))
     pl.when(step >= 2)(lambda: run(oth_ref))
@@ -181,15 +181,19 @@
             ]
             + [pl.BlockSpec(b.shape, lambda i, o: (0, 0, 0)) for b in blocks],
             out_specs=[
-                pl.BlockSpec((1, tile, 2 * HALF), lambda i, o: (i // 2, i % 2, 0)),
-                pl.BlockSpec((1, tile, 2048), lambda i, o: (i // 2, i % 2, 0)),
+                pl.BlockSpec((1, tile, HALF), lambda i, o: (i // 2, i % 2, 0)),
+                pl.BlockSpec((1, tile, HALF), lambda i, o: (i // 2, i % 2, 0)),
+                pl.BlockSpec((1, tile, 1024), lambda i, o: (i // 2, i % 2, 0)),
+                pl.BlockSpec((1, tile, 1024), lambda i, o: (i // 2, i % 2, 0)),
                 fixed,
                 fixed,
             ],
         ),
         out_shape=[
-            jax.ShapeDtypeStruct((2, ROWS, 2 * HALF), F32),
-            jax.ShapeDtypeStruct((2, ROWS, 2048), BF),
+            jax.ShapeDtypeStruct((2, ROWS, HALF), F32),
+            jax.ShapeDtypeStruct((2, ROWS, HALF), F32),
+            jax.ShapeDtypeStruct((2, ROWS, 1024), BF),
+            jax.ShapeDtypeStruct((2, ROWS, 1024), BF),
             jax.ShapeDtypeStruct((1024, CHUNK), BF),
             jax.ShapeDtypeStruct((1024, CHUNK), BF),
         ],
@@ -226,12 +230,12 @@
     return lax.broadcasted_iota(jnp.int32, (rows, LANES), 1) // 64
 
 
-def head_matrix(meta, qg_refs, side, quad, which):
+def head_matrix(meta, q_ref, side, quad, which):
     head = head_of_column(DEC)
     parts = []
     for p in range(NPASS):
         row = pl.multiple_of(meta.row(quad, side, p) + which * 32, 16)
-        tile = qg_refs[quad][pl.ds(row, DEC), :]
+        tile = q_ref[pl.ds(row, DEC), :]
         parts += [jnp.where(head == a, tile, jnp.zeros_like(tile)) for a in range(4)]
     return jnp.concatenate(parts, axis=0)
 
@@ -254,90 +258,92 @@
     return lax.dot_general(a, b, NT, preferred_element_type=F32)
 
 
-def forward_side(side, meta, k, v, qg, st_ref, num_ref):
-    n = st_ref.shape[0]
-
-    def put(row, value):
-        st_ref[:, row : row + 1, :] = jnp.broadcast_to(value[None], (n, 1, LANES))
-
+def forward_side(side, quad, meta, k, v, q_ref, put, num_ref):
     inside = inside_mask(meta, side)
-    question = lane_value([meta.question(side, p) for p in range(NPASS)]).astype(F32)
-    for quad in range(QUADS):
-        cols = slice(quad * CHUNK, (quad + 1) * CHUNK)
-        scores = dot_nt(k[side, :, cols], head_matrix(meta, qg, side, quad, 0))
-        scores = jnp.where(inside, scores, LOW)
-        top = jnp.max(scores, axis=0, keepdims=True)
-        unnorm = jnp.exp(scores - top)
-        unnorm_b = unnorm.astype(BF)
-        values = v[side, :, cols]
-        dprob = dot_nt(values, head_matrix(meta, qg, side, quad, 1))
-        at = side * QUADS + quad
-        put(at, top)
-        put(4 + at, jnp.sum(unnorm, axis=0, keepdims=True))
-        put(8 + at, jnp.sum(unnorm_b.astype(F32) * dprob, axis=0, keepdims=True))
-        put(12 + at, question)
-        num_ref[side, quad] = lax.dot_general(values, unnorm_b, TN, preferred_element_type=F32)
-
-
-def far_kernel(
-    pos, own_numbers, other_numbers, enc_ref, acc_ref, a_top, a_low, b_top, b_low, qa_in, qb_in,
-    k_ref, v_ref, qa_ref, qb_ref, st_ref, num_ref,
-):
+    scores = dot_nt(k, head_matrix(meta, q_ref, side, quad, 0))
+    scores = jnp.where(inside, scores, LOW)
+    top = jnp.max(scores, axis=0, keepdims=True)
+    unnorm = jnp.exp(scores - top)
+    unnorm_b = unnorm.astype(BF)
+    dprob = dot_nt(v, head_matrix(meta, q_ref, side, quad, 1))
+    put(0, top)
+    put(1, jnp.sum(unnorm, axis=0, keepdims=True))
+    put(2, jnp.sum(unnorm_b.astype(F32) * dprob, axis=0, keepdims=True))
+    num_ref[side] = lax.dot_general(v, unnorm_b, TN, preferred_element_type=F32)
+
+
+def far_kernel(quad, pos, own_numbers, other_numbers, *refs):
     meta = Passages(pos, own_numbers, other_numbers)
+    enc_ref, acc_ref, top, low, q_in = refs[:5]
+    before_ref = refs[5] if quad else None
+    k_ref, v_ref, q_ref, st_ref, num_ref = refs[-5:]
     step = pl.program_id(0)
-    far = ((a_top, a_low), (b_top, b_low))
 
     @pl.when(step == 0)
     def questions():
-        for side, source, out in ((0, qa_in, qa_ref), (1, qb_in, qb_ref)):
-            out[...] = source[...]
-            for inner in range(4):
-                row = (inner % 2) * PIECE + 512
-                at = (8 + inner) * 64
-                out[at : at + 64, :] = far[side][inner // 2][row : row + 64, :]
+        q_ref[...] = q_in[...]
+        for inner in range(4):
+            row = (inner % 2) * PIECE + 512
+            at = (8 + inner) * 64
+            q_ref[at : at + 64, :] = (top, low)[inner // 2][row : row + 64, :]
+
+    total = acc_ref[0] + jnp.dot(
+        enc_ref[0], key_value((top, low)), preferred_element_type=F32
+    )
+    keys, values = total[:, :CHUNK].astype(BF), total[:, CHUNK:].astype(BF)
+    k_ref[step] = keys
+    v_ref[step] = values
+
+    def put_all(row, value):
+        st_ref[:, row : row + 1, :] = jnp.broadcast_to(value[None], (NZ * NX, 1, LANES))
 
     for side in range(2):
-        lhs = enc_ref[0, :, side * 1024 : (side + 1) * 1024]
-        total = jnp.dot(lhs, key_value(far[side]), preferred_element_type=F32)
-        for t, out in ((0, k_ref), (1, v_ref)):
-            at = t * HALF + side * CHUNK
-            part = total[:, t * CHUNK : (t + 1) * CHUNK] + acc_ref[0, :, at : at + CHUNK]
-            out[step, :, side * CHUNK : (side + 1) * CHUNK] = part.astype(BF)
-    for side in range(2):
+        def put(r, value):
+            if quad:
+                put_all(4 * r + side * 2 + 1, value)
+            else:
+                st_ref[r * 2 + side : r * 2 + side + 1, :] = value
+
         @pl.when(step == side)
         def attend():
-            forward_side(side, meta, k_ref, v_ref, (qa_ref, qb_ref), st_ref, num_ref)
-
-
-def project_far(meta, enc_far, acc, blocks, qa, qb):
+            forward_side(side, quad, meta, k_ref[side], v_ref[side], q_ref, put, num_ref)
+            if quad:
+                question = lane_value([meta.question(side, p) for p in range(NPASS)]).astype(F32)
+                for r in range(3):
+                    put_all(4 * r + side * 2, before_ref[r * 2 + side : r * 2 + side + 1, :])
+                for q in range(QUADS):
+                    put_all(12 + side * 2 + q, question)
+
+
+def project_far(quad, meta, enc_far, acc, blocks, q, before):
     def whole(shape):
         return pl.BlockSpec(shape, lambda i, *m: (0,) * len(shape))
 
+    stats = (NZ * NX, 16, LANES) if quad else (8, LANES)
     shapes = [
-        jax.ShapeDtypeStruct((2, ROWS, HALF), BF),
-        jax.ShapeDtypeStruct((2, ROWS, HALF), BF),
+        jax.ShapeDtypeStruct((2, ROWS, CHUNK), BF),
+        jax.ShapeDtypeStruct((2, ROWS, CHUNK), BF),
         jax.ShapeDtypeStruct((1024, CHUNK), BF),
-        jax.ShapeDtypeStruct((1024, CHUNK), BF),
-        jax.ShapeDtypeStruct((NZ * NX, 16, LANES), F32),
-        jax.ShapeDtypeStruct((2, QUADS, LANES, CHUNK), F32),
+        jax.ShapeDtypeStruct(stats, F32),
+        jax.ShapeDtypeStruct((2, LANES, CHUNK), F32),
     ]
-    return pl.pallas_call(
-        far_kernel,
+    extra = [before] if quad else []
+    return pl.pallas_call(
+        functools.partial(far_kernel, quad),
         grid_spec=pltpu.PrefetchScalarGridSpec(
             num_scalar_prefetch=3,
             grid=(2,),
             in_specs=[
-                pl.BlockSpec((1, ROWS, 2048), lambda i, *m: (i, 0, 0)),
-                pl.BlockSpec((1, ROWS, 2 * HALF), lambda i, *m: (i, 0, 0)),
+                pl.BlockSpec((1, ROWS, 1024), lambda i, *m: (i, 0, 0)),
+                pl.BlockSpec((1, ROWS, HALF), lambda i, *m: (i, 0, 0)),
             ]
-            + [whole(b.shape) for b in blocks]
-            + [whole((1024, CHUNK))] * 2,
+            + [whole(b.shape) for b in blocks + [q] + extra],
             out_specs=[whole(s.shape) for s in shapes],
         ),
         out_shape=shapes,
-        compiler_params=params(24),
-        cost_estimate=HIDDEN,
-    )(*meta, enc_far, acc, *blocks, qa, qb)
+        compiler_params=params(20),
+        cost_estimate=HIDDEN,
+    )(*meta, enc_far, acc, *blocks, q, *extra)
 
 
 def combine(meta, st_ref):
@@ -418,13 +424,14 @@
 
 
 def backward_kernel(
-    pos, own_numbers, other_numbers, k_ref, v_ref, qa_ref, qb_ref, st_ref, num_ref, *refs
+    pos, own_numbers, other_numbers, ka_ref, va_ref, qa_ref, na_ref, kb_ref, vb_ref, qb_ref, nb_ref,
+    st_ref, *refs
 ):
     sources, outs = refs[:10], refs[10:]
-    kvg_ref, oth_ref, dense_ref, ctx_ref, w_ref = outs
+    kvg_ref, own_ref, oth_ref, dense_ref, ctx_ref, w_ref = outs
     take_weights(pos[2], sources, w_ref)
     meta = Passages(pos, own_numbers, other_numbers)
-    qg = (qa_ref, qb_ref)
+    halves = ((ka_ref, va_ref, qa_ref, na_ref), (kb_ref, vb_ref, qb_ref, nb_ref))
     tops, inverses, deltas = combine(meta, st_ref)
     here = meta.z * 4 + meta.x
     ctx_ref[...] = jnp.zeros_like(ctx_ref)
@@ -435,12 +442,13 @@
             cols = slice(quad * CHUNK, (quad + 1) * CHUNK)
             at = side * QUADS + quad
             top, inverse = tops[side][quad : quad + 1], inverses[side][quad : quad + 1]
-            queries = head_matrix(meta, qg, side, quad, 0)
-            grads = head_matrix(meta, qg, side, quad, 1)
-            scores = dot_nt(k_ref[side, :, cols], queries)
+            k_ref, v_ref, q_ref, num_ref = halves[quad]
+            queries = head_matrix(meta, q_ref, side, quad, 0)
+            grads = head_matrix(meta, q_ref, side, quad, 1)
+            scores = dot_nt(k_ref[side], queries)
             unnorm = jnp.where(inside, jnp.exp(jnp.where(inside, scores - top, 0.0)), 0.0)
             probs = unnorm * inverse
-            dprob = dot_nt(v_ref[side, :, cols], grads)
+            dprob = dot_nt(v_ref[side], grads)
             ds = (probs * (dprob - deltas[side][quad : quad + 1])).astype(BF)
             for t, lanes, weight in ((0, queries, ds), (1, grads, probs.astype(BF))):
                 turned = lax.dot_general(
@@ -449,16 +457,16 @@
                 first = t * HALF + quad * CHUNK
                 kvg_ref[first : first + CHUNK, side * ROWS : (side + 1) * ROWS] = turned
             scale = jnp.exp(st_ref[here, at : at + 1, :] - top) * inverse
-            context = (num_ref[side, quad] * scale).T
+            context = (num_ref[side] * scale).T
             for p in range(NPASS):
                 part = jnp.zeros((DEC, CHUNK), F32)
                 for a in range(4):
                     first = p * 64 + a * DEC
                     part = jnp.where(head == a, context[first : first + DEC], part)
                 ctx_ref[meta.question(side, p), :, cols] += part
-    oth_ref[...] = jnp.dot(
-        weights_tile(w_ref), kvg_ref[:, ROWS:], preferred_element_type=F32
-    ).astype(BF)
+    total = jnp.dot(weights_tile(w_ref), kvg_ref[...], preferred_element_type=F32)
+    own_ref[...] = total[:, :ROWS].astype(BF)
+    oth_ref[...] = total[:, ROWS:].astype(BF)
     dense_ref[...] = ctx_ref[...].astype(BF)
 
 
@@ -468,6 +476,7 @@
 
     shapes = [
         jax.ShapeDtypeStruct((2 * HALF, 2 * ROWS), BF),
+        jax.ShapeDtypeStruct((1024, ROWS), BF),
         jax.ShapeDtypeStruct((1024, ROWS), BF),
         jax.ShapeDtypeStruct((32, DEC, HALF), BF),
     ]
@@ -487,30 +496,26 @@
     )(*meta, *args, *weights)
 
 
-def own_kernel(places, kvg_ref, *refs):
-    sources, (far_ref, base_ref, other_ref, w_ref) = refs[:10], refs[10:]
+def base_kernel(places, kvg_ref, *refs):
+    sources, (base_ref, other_ref, w_ref) = refs[:10], refs[10:]
     take_weights(places[0], sources, w_ref)
-    far_ref[...] = jnp.dot(
-        weights_tile(w_ref), kvg_ref[:, :ROWS], preferred_element_type=F32
-    ).astype(BF)
-    take_weights(places[1], sources, w_ref)
     total = jnp.dot(weights_tile(w_ref), kvg_ref[...], preferred_element_type=F32)
     base_ref[...] = total[:, :ROWS]
     other_ref[...] = total[:, ROWS:].astype(BF)
 
 
-def own_blocks(places, kvg, weights):
+def base_blocks(places, kvg, weights):
     out = pl.BlockSpec((1024, ROWS), lambda i, p: (0, 0))
     return pl.pallas_call(
-        own_kernel,
+        base_kernel,
         grid_spec=pltpu.PrefetchScalarGridSpec(
             num_scalar_prefetch=1,
             grid=(1,),
             in_specs=[pl.BlockSpec(kvg.shape, lambda i, p: (0, 0))] + weight_specs(),
-            out_specs=[out] * 3,
+            out_specs=[out] * 2,
             scratch_shapes=[WEIGHT_SCRATCH],
         ),
-        out_shape=[jax.ShapeDtypeStruct((1024, ROWS), t) for t in (BF, F32, BF)],
+        out_shape=[jax.ShapeDtypeStruct((1024, ROWS), t) for t in (F32, BF)],
         compiler_params=params(34),
         cost_estimate=HIDDEN,
     )(places, kvg, *weights)
@@ -629,7 +634,7 @@
     zs, xs = (z + four) % 4, (x + four) % 4
     places = ((y + four - z) % 4).astype(jnp.int32)
     near_places = jnp.stack([places[1], places[3], core.astype(jnp.int32)])
-    own_places = jnp.stack([places[2], places[0]])
+    base_place = places[0:1]
     pos = jnp.stack([z, x, places[2]]).astype(jnp.int32)
 
     cat = jnp.concatenate([key_weight, value_weight, queries[0], ctx_grad[0]], axis=0)
@@ -652,11 +657,11 @@
     )
 
     steps = [(v, a, h) for v, (a, h) in zip(halves, (("x", 0), ("x", 1), ("z", 0), ("z", 1)))]
-    met, pos, near_places, own_places, x_place, xs = phase(
+    met, pos, near_places, base_place, x_place, xs = phase(
         [pair_perm(v, a, h) for v, a, h in steps],
         pos,
         near_places,
-        own_places,
+        base_place,
         x.astype(jnp.int32).reshape(1),
         xs.astype(jnp.int32),
     )
@@ -676,20 +681,24 @@
         perm(b_first, "x", -1),
         perm(b_second, "x", 1),
     ]
-    acc, enc_far, qa, qb = project_near(
+    acc_a, acc_b, enc_a, enc_b, qa, qb = project_near(
         pos, enc_rows, enc_other, [a_own, a_up, a_down, b_own, b_up, b_down]
     )
-    far, acc, enc_far, qa, qb = phase(far, acc, enc_far, qa, qb)
     meta = (pos, numbers, other_numbers)
-    keys, values, qa, qb, stats, numer = project_far(meta, enc_far, acc, far, qa, qb)
+    acc_a, acc_b, enc_a, enc_b, qa, qb, far[0], far[1] = phase(
+        acc_a, acc_b, enc_a, enc_b, qa, qb, *far[:2]
+    )
+    ka, va, qa, stats_a, numer_a = project_far(0, meta, enc_a, acc_a, far[:2], qa, None)
+    stats_a, far[2], far[3] = phase(stats_a, far[2], far[3])
+    kb, vb, qb, stats, numer_b = project_far(1, meta, enc_b, acc_b, far[2:], qb, stats_a)
     stats_all = lax.all_to_all(stats, ("z", "x"), 0, 0, tiled=True)
     weights = [a_own, a_up, far[0], far[1], a_down, b_own, b_up, far[2], far[3], b_down]
-    kvg, far_other, dense = backward(
-        meta, (keys, values, qa, qb, stats_all, numer), weights
+    kvg, far_own, far_other, dense = backward(
+        meta, (ka, va, qa, numer_a, kb, vb, qb, numer_b, stats_all), weights
     )
 
     far_got = perm(far_other, "core", 1)
-    far_own, base, base_other = own_blocks(own_places, kvg, weights)
+    base, base_other = base_blocks(base_place, kvg, weights)
     far_got, far_own, base, base_other, kvg, dense = phase(
         far_got, far_own, base, base_other, kvg, dense
     )

time: 150 us -> 150 us (level)
  waiting for transfers between devices: 36.1 us -> 41.2 us
  starting transfers between devices: 38.4 us -> 34.1 us
  Pallas kernels: 34.7 us -> 36.2 us
    ppermute x19, starting transfers between devices: 28.2 us -> 23.9 us  [perm(): return lax.ppermute(v, axis, [(i, (i + shift) % n) for i in range(n)])]
    ppermute x19, waiting for transfers between devices: 31.4 us -> 35.1 us  [perm(): return lax.ppermute(v, axis, [(i, (i + shift) % n) for i in range(n)])]
    pallas_call x2 -> x3, Pallas kernels: 9.98 us -> 10.3 us  [the longest x2 6.98 us: project_far(): pl.pallas_call(functools.partial(far_kernel, quad), grid_spec=pltpu.Prefe...]
  transfers between devices with their start and end apart: 27 -> 27, of which waited for: 8 -> 9; matrix products, arithmetic and copies ran while one was open for 3% -> 2% of each run, Pallas kernels for 14% -> 15%
where the time goes in v6:
time: 150 us; the launch traced here: 149 us
  waiting for transfers between devices  41.2 us (27%)
  Pallas kernels  36.2 us (24%)
  starting transfers between devices  34.1 us (23%)
  blocking collectives  33.1 us (22%)
  other arithmetic  3.21 us (2%)
    ppermute x19, waiting for transfers between devices, perm(): return lax.ppermute(v, axis, [(i, (i + shift) % n) for i in range(n)])  35.1 us
    ppermute x19, starting transfers between devices, perm(): return lax.ppermute(v, axis, [(i, (i + shift) % n) for i in range(n)])  23.9 us
    all_to_all x1, blocking collectives, body(): lax.all_to_all(dense, ENC, 0, 0, tiled=True).reshape(NZ * NX, NC, DEC, HALF)  15.8 us
    ppermute x8, starting transfers between devices, pair_perm(): return lax.ppermute(v, axis, [(i, turn(i) % 4) for i in range(4)])  10.3 us
    all_to_all x1, blocking collectives, body(): stats_all = lax.all_to_all(stats, ('z', 'x'), 0, 0, tiled=True)  10.1 us
    pallas_call x1, Pallas kernels, project_near(): pl.pallas_call(near_kernel, grid_spec=pltpu.PrefetchScalarGridSpec(num_sc...  9.9 us
    all_to_all x1, blocking collectives, body(): lax.all_to_all(near_blocks(near_places, kvg, weights), 'core', 0, 0, tile...  7.17 us
    pallas_call x2, Pallas kernels, project_far(): pl.pallas_call(functools.partial(far_kernel, quad), grid_spec=pltpu.Prefe...  6.98 us
  transfers between devices with their start and end apart: 27, of which 9 were waited for; matrix products, arithmetic and copies ran while one was open for 2% of the time, Pallas kernels for 15%

profile of v6, /device:TPU:1, one launch (start us, length us, event | category | flops | bytes accessed | tf_op | source)
XLA Modules:
  0.0 149.5 jit_solution(9359327355644365134)
XLA Ops:
  0.6 1.1 pad_maximum_fusion
  1.8 1.5 %collective-permute-start = (bf16[288,512]{1,0:T(8,128)(2,1)S(1)}, bf16[288,512]{1,0:T(8,128)(2,1)S(1)}, u32[]{:S(2)}, u32[]{:S(2)}) collective-permute-start(bf16[288,512]{1,0:T(8,128)(2,1)S(1)} %constant_dynamic-slice_fusion), channel_id=1, source_target_pairs={{0,4},{4,0},{1,5},{5,1},{2,6},{6,2},{3,7},{7,3},{8,12},{12,8},{9,1... | collective-permute-start | bytes 884744 | tf_op jit(solution)/shard_map/ppermute | solution.py:31
  3.3 1.2 collective-permute-done
  4.5 0.4 collective-permute-start.5
  4.9 0.6 fusion.3
  5.5 0.1 broadcast_select_fusion
  5.9 1.4 collective-permute-start.1
  7.2 1.8 %collective-permute-start.2 = (bf16[288,256]{1,0:T(8,128)(2,1)S(1)}, bf16[288,256]{1,0:T(8,128)(2,1)S(1)}, u32[]{:S(2)}, u32[]{:S(2)}) collective-permute-start(bf16[288,256]{1,0:T(8,128)(2,1)S(1)} %get-tuple-element.106.refs_2_), channel_id=1, source_target_pairs={{0,24},{8,16},{16,8},{24,0},{1,25},{9,17},{17,9},{25,1},{2,26},{10... | collective-permute-start | bytes 442376 | tf_op jit(solution)/shard_map/ppermute | solution.py:44
  9.0 1.6 %collective-permute-start.3 = (bf16[288,256]{1,0:T(8,128)(2,1)S(1)}, bf16[288,256]{1,0:T(8,128)(2,1)S(1)}, u32[]{:S(2)}, u32[]{:S(2)}) collective-permute-start(bf16[288,256]{1,0:T(8,128)(2,1)S(1)} %get-tuple-element.107.refs_4_), channel_id=1, source_target_pairs={{0,32},{32,0},{64,96},{96,64},{1,33},{33,1},{65,97},{97,65},{2,34}... | collective-permute-start | bytes 442376 | tf_op jit(solution)/shard_map/ppermute | solution.py:44
  10.7 2.2 %collective-permute-start.4 = (bf16[288,256]{1,0:T(8,128)(2,1)S(1)}, bf16[288,256]{1,0:T(8,128)(2,1)S(1)}, u32[]{:S(2)}, u32[]{:S(2)}) collective-permute-start(bf16[288,256]{1,0:T(8,128)(2,1)S(1)} %get-tuple-element.108.refs_6_), channel_id=1, source_target_pairs={{0,96},{32,64},{64,32},{96,0},{1,97},{33,65},{65,33},{97,1},{2,98}... | collective-permute-start | bytes 442376 | tf_op jit(solution)/shard_map/ppermute | solution.py:44
  12.9 1.8 %pad_add_fusion = (s32[3]{0:T(128)S(1)}, s32[3]{0:T(128)S(1)}) fusion(s32[1]{0:T(128)} %get-tuple-element.220, s32[1]{0:T(128)} %bitcast.3.place, s32[1]{0:T(128)} %bitcast.2, s32[1]{0:T(128)} %bitcast.4, s32[1]{0:T(128)} %get-tuple-element.218, s32[1]{0:T(128)} %get-tuple-element.219), kind=kLoop, calls=%fused_computation.20 | loop fusion | flops 12 | bytes 48 | tf_op jit(solution)/shard_map/stack | solution.py:638
  14.8 1.5 collective-permute-done.4.refs_7_
  16.3 0.9 collective-permute-start.7
  17.3 2.2 %collective-permute-start.9 = (bf16[576,256]{1,0:T(8,128)(2,1)S(1)}, bf16[576,256]{1,0:T(8,128)(2,1)S(1)}, u32[]{:S(2)}, u32[]{:S(2)}) collective-permute-start(bf16[576,256]{1,0:T(8,128)(2,1)S(1)} %get-tuple-element.119.joined0), channel_id=1, source_target_pairs={{0,96},{32,64},{64,32},{96,0},{1,97},{33,65},{65,33},{97,1},{2,98}... | collective-permute-start | bytes 884744 | tf_op jit(solution)/shard_map/ppermute | solution.py:44
  19.6 4.6 %collective-permute-done.7.second0 = bf16[576,256]{1,0:T(8,128)(2,1)S(1)} collective-permute-done((bf16[576,256]{1,0:T(8,128)(2,1)S(1)}, bf16[576,256]{1,0:T(8,128)(2,1)S(1)}, u32[]{:S(2)}, u32[]{:S(2)}) %collective-permute-start.7) | collective-permute-done | bytes 294944 | tf_op jit(solution)/shard_map/ppermute | solution.py:44
  24.2 2.8 %collective-permute-start.6 = (s32[8]{0:T(128)S(1)}, s32[8]{0:T(128)S(1)}, u32[]{:S(2)}, u32[]{:S(2)}) collective-permute-start(s32[8]{0:T(128)S(1)} %pad_add_fusion.2.own_numbers), channel_id=1, source_target_pairs={{0,4},{4,0},{1,5},{5,1},{2,6},{6,2},{3,7},{7,3},{8,12},{12,8},{9,1... | collective-permute-start | bytes 104 | tf_op jit(solution)/shard_map/ppermute | solution.py:31
  27.2 0.1 shard_map.88.refs_3_.refs_5_
  27.3 0.6 collective-permute-done.6.other_numbers
  27.9 2.2 %collective-permute-start.11 = (bf16[2,1152,256]{2,1,0:T(8,128)(2,1)S(1)}, bf16[2,1152,256]{2,1,0:T(8,128)(2,1)S(1)}, u32[]{:S(2)}, u32[]{:S(2)}) collective-permute-start(bf16[2,1152,256]{2,1,0:T(8,128)(2,1)S(1)} %shard_map.87.refs_0_), channel_id=1, source_target_pairs={{0,96},{32,0},{64,32},{96,64},{1,97},{33,1},{65,33},{97,65},{2,98}... | collective-permute-start | bytes 3538952 | tf_op jit(solution)/shard_map/ppermute | solution.py:31
  30.1 0.9 collective-permute-start.13
  31.0 0.6 collective-permute-start.14
  31.6 23.6 %collective-permute-done.11.refs_1_.up_ref = bf16[2,1152,256]{2,1,0:T(8,128)(2,1)S(1)} collective-permute-done((bf16[2,1152,256]{2,1,0:T(8,128)(2,1)S(1)}, bf16[2,1152,256]{2,1,0:T(8,128)(2,1)S(1)}, u32[]{:S(2)}, u32[]{:S(2)}) %collective-permute-start.11) | collective-permute-done | bytes 1179680 | tf_op jit(solution)/shard_map/ppermute | solution.py:31
  55.2 3.1 %collective-permute-done.12.refs_2_.down_ref.refs_4_ = bf16[2,1152,256]{2,1,0:T(8,128)(2,1)S(1)} collective-permute-done((bf16[2,1152,256]{2,1,0:T(8,128)(2,1)S(1)}, bf16[2,1152,256]{2,1,0:T(8,128)(2,1)S(1)}, u32[]{:S(2)}, u32[]{:S(2)}) %collective-permute-start.12) | collective-permute-done | bytes 1179680 | tf_op jit(solution)/shard_map/ppermute | solution.py:31
  58.3 0.4 collective-permute-start.15
  58.7 1.1 collective-permute-start.16
  60.0 1.5 collective-permute-start.18
  61.5 9.9 %shard_map.89 = (f32[2,512,512]{2,1,0:T(8,128)S(1)}, f32[2,512,512]{2,1,0:T(8,128)S(1)}, bf16[2,512,1024]{2,1,0:T(8,128)(2,1)S(1)}, bf16[2,512,1024]{2,1,0:T(8,1...) custom-call(s32[3]{0:T(128)S(1)} %get-tuple-element.110.pos, bf16[512,4096]{1,0:T(8,128)(2,1)S(1)} %copy-done, ...), custom_call_target="tpu_custom_call" | custom-call | flops 200000000 | tf_op jit(solution)/shard_map/pallas_call | solution.py:173
  71.4 0.4 collective-permute-done.15.refs_2_
  71.8 1.6 %collective-permute-done.16.refs_3_ = bf16[1152,256]{1,0:T(8,128)(2,1)S(1)} collective-permute-done((bf16[1152,256]{1,0:T(8,128)(2,1)S(1)}, bf16[1152,256]{1,0:T(8,128)(2,1)S(1)}, u32[]{:S(2)}, u32[]{:S(2)}) %collective-permute-start.16) | collective-permute-done | bytes 589856 | tf_op jit(solution)/shard_map/ppermute | solution.py:31
  73.4 3.5 %shard_map.91 = (bf16[2,512,256]{2,1,0:T(8,128)(2,1)S(1)}, bf16[2,512,256]{2,1,0:T(8,128)(2,1)S(1)}, bf16[1024,256]{1,0:T(8,128)(2,1)S(1)}, f32[8,256]{1,0:T(8,128)S(1)}, f32[2,256,256]{2,1,0:T(8,128)S(1)}) custom-call(s32[3]{0:T(128)S(1)} %get-tuple-element.110.pos, s32[8]{0:T(128)S(1)} %pad_add_fusion.2.own_numbers, ...), custom_call_target="tpu_custom_call" | custom-call | flops 200000000 | tf_op jit(solution)/shard_map/pallas_call | solution.py:331
  76.8 3.5 %shard_map.93 = (bf16[2,512,256]{2,1,0:T(8,128)(2,1)S(1)}, bf16[2,512,256]{2,1,0:T(8,128)(2,1)S(1)}, bf16[1024,256]{1,0:T(8,128)(2,1)S(1)}, f32[16,16,256]{2,1,0:T(8,128)S(1)}, f32[2,256,256]{2,1,0:T(8,128)S(1)}) custom-call(s32[3]{0:T(128)S(1)} %get-tuple-element.110.pos, s32[8]{0:T(128)S(1)} %pad_add_fusion.2.own_numbers, ...), custom_call_target="tpu_custom_call" | custom-call | flops 200000000 | tf_op jit(solution)/shard_map/pallas_call | solution.py:331
  80.4 10.1 %all_to_all.15.st_ref = f32[16,16,256]{2,1,0:T(8,128)S(1)} all-to-all(f32[16,16,256]{2,1,0:T(8,128)S(1)} %get-tuple-element.159), channel_id=1, replica_groups=mesh['z'=4,'x'=4,'core'=2,'dec'=4] {'z','x'}, dimensions={0} | all-to-all | bytes 524288 | tf_op jit(solution)/shard_map/all_to_all | solution.py:694
  90.5 5.7 %shard_map.94 = (bf16[1024,1024]{1,0:T(8,128)(2,1)S(1)}, bf16[1024,512]{1,0:T(8,128)(2,1)S(1)}, bf16[1024,512]{1,0:T(8,128)(2,1)S(1)}, bf16[32,16,512]{2,1,0:T(8,128)(2,1)S(1)}) custom-call(s32[3]{0:T(128)S(1)} %get-tuple-element.110.pos, s32[8]{0:T(128)S(1)} %pad_add_fusion.2.own_numbers, s32[8]{0:T(128)S(1)} %collective-permute-done.6.other_numbers, ...), custom_call_target="tpu_custom_call" | custom-call | flops 200000000 | tf_op jit(solution)/shard_map/pallas_call | solution.py:483
  96.2 3.7 %collective-permute-start.19 = (bf16[1024,512]{1,0:T(8,128)(2,1)S(1)}, bf16[1024,512]{1,0:T(8,128)(2,1)S(1)}, u32[]{:S(2)}, u32[]{:S(2)}) collective-permute-start(bf16[1024,512]{1,0:T(8,128)(2,1)S(1)} %get-tuple-element.160), channel_id=1, source_target_pairs={{0,4},{4,0},{1,5},{5,1},{2,6},{6,2},{3,7},{7,3},{8,12},{12,8},{9,1... | collective-permute-start | bytes 3145736 | tf_op jit(solution)/shard_map/ppermute | solution.py:31
  99.9 3.4 %shard_map.95 = (f32[1024,512]{1,0:T(8,128)S(1)}, bf16[1024,512]{1,0:T(8,128)(2,1)S(1)}) custom-call(s32[1]{0:T(128)} %get-tuple-element.162.places, bf16[1024,1024]{1,0:T(8,128)(2,1)S(1)} %get-tuple-element.178.kvg_ref, bf16[2,1152,256]{2,1,0:T(8,128)(2,1)S(1)} %shard_map.87.refs_0_, bf16[2,1152,256]{2,1,0:T(8,128)(2,1)S(1)} %collective-permute-done.11.refs_1_.up_ref, ...), custom_call_target="tpu_custom_call" | custom-call | flops 200000000 | tf_op jit(solution)/shard_map/pallas_call | solution.py:509
  103.3 0.2 shard_map.96
  103.5 1.4 collective-permute-start.20
  104.9 1.5 %collective-permute-start.21 = (bf16[512,512]{1,0:T(8,128)(2,1)S(1)}, bf16[512,512]{1,0:T(8,128)(2,1)S(1)}, u32[]{:S(2)}, u32[]{:S(2)}) collective-permute-start(bf16[512,512]{1,0:T(8,128)(2,1)S(1)} %get-tuple-element.176), channel_id=1, source_target_pairs={{0,3},{1,0},{2,1},{3,2},{4,7},{5,4},{6,5},{7,6},{8,11},{9,8},{10,9... | collective-permute-start | bytes 1572872 | tf_op jit(solution)/shard_map/ppermute | solution.py:31
  106.4 5.9 %shard_map.97 = bf16[2,2,1024,512]{3,2,1,0:T(8,128)(2,1)S(1)} custom-call(s32[3]{0:T(128)S(1)} %get-tuple-element.177.places, bf16[1024,1024]{1,0:T(8,128)(2,1)S(1)} %get-tuple-element.178.kvg_ref, bf16[2,1152,256]{2,1,0:T(8,128)(2,1)S(1)} %shard_map.87.refs_0_, bf16[2,1152,256]{2,1,0:T(8,128)(2,1)S(1)} %collective-permute-done.11.refs_1_.up_ref, ...), custom_call_target="tpu_custom_call" | custom-call | flops 200000000 | tf_op jit(solution)/shard_map/pallas_call | solution.py:549
  112.3 7.2 %all_to_all.16.near_ref = bf16[2,2,1024,512]{3,2,1,0:T(8,128)(2,1)S(1)} all-to-all(bf16[2,2,1024,512]{3,2,1,0:T(8,128)(2,1)S(1)} %shard_map.97), channel_id=1, replica_groups=mesh['z'=4,'x'=4,'core'=2,'dec'=4] {'core'}, dimensions={0} | all-to-all | bytes 8388608 | tf_op jit(solution)/shard_map/all_to_all | solution.py:711
  119.4 0.6 shard_map.98
  120.1 0.5 collective-permute-start.26
  120.5 0.7 collective-permute-start.22
  121.2 2.0 %collective-permute-start.23 = (bf16[512,512]{1,0:T(8,128)(2,1)S(1)}, bf16[512,512]{1,0:T(8,128)(2,1)S(1)}, u32[]{:S(2)}, u32[]{:S(2)}) collective-permute-start(bf16[512,512]{1,0:T(8,128)(2,1)S(1)} %get-tuple-element.193), channel_id=1, source_target_pairs={{0,3},{1,0},{2,1},{3,2},{4,7},{5,4},{6,5},{7,6},{8,11},{9,8},{10,9... | collective-permute-start | bytes 1572872 | tf_op jit(solution)/shard_map/ppermute | solution.py:31
  123.2 2.7 %collective-permute-start.25 = (bf16[512,512]{1,0:T(8,128)(2,1)S(1)}, bf16[512,512]{1,0:T(8,128)(2,1)S(1)}, u32[]{:S(2)}, u32[]{:S(2)}) collective-permute-start(bf16[512,512]{1,0:T(8,128)(2,1)S(1)} %get-tuple-element.195), channel_id=1, source_target_pairs={{0,3},{1,0},{2,1},{3,2},{4,7},{5,4},{6,5},{7,6},{8,11},{9,8},{10,9... | collective-permute-start | bytes 1572872 | tf_op jit(solution)/shard_map/ppermute | solution.py:31
  125.9 15.8 %all_to_all.17 = bf16[32,16,512]{2,1,0:T(8,128)(2,1)S(1)} all-to-all(bf16[32,16,512]{2,1,0:T(8,128)(2,1)S(1)} %get-tuple-element.197), channel_id=1, replica_groups=mesh['z'=4,'x'=4,'core'=2,'dec'=4] {'z','x','core'}, dimensions={0} | all-to-all | bytes 1048576 | tf_op jit(solution)/shard_map/all_to_all | solution.py:724
  141.7 4.7 %collective-permute-done.24.up_top = bf16[512,512]{1,0:T(8,128)(2,1)S(1)} collective-permute-done((bf16[512,512]{1,0:T(8,128)(2,1)S(1)}, bf16[512,512]{1,0:T(8,128)(2,1)S(1)}, u32[]{:S(2)}, u32[]{:S(2)}) %collective-permute-start.24) | collective-permute-done | bytes 524320 | tf_op jit(solution)/shard_map/ppermute | solution.py:31
  146.4 3.1 %shard_map.99 = (f32[512,1024]{1,0:T(8,128)}, f32[1,16,1024]{2,1,0:T(8,128)}) custom-call(s32[4]{0:T(128)S(1)} %and_select_fusion.place, f32[1024,512]{1,0:T(8,128)S(1)} %get-tuple-element.182.base_ref, bf16[1024,512]{1,0:T(8,128)(2,1)S(1)} %collective-permute-done.26.core_ref, bf16[512,512]{1,0:T(8,128)(2,1)S(1)} %collective-permute-done.24.up_top, ...), custom_call_target="tpu_custom_call" | custom-call | flops 200000000 | tf_op jit(solution)/shard_map/pallas_call | solution.py:610
  (44 shorter events, 0.7 us)
Async XLA Ops:
  1.8 2.7 %collective-permute-start = (bf16[288,512]{1,0:T(8,128)(2,1)S(1)}, bf16[288,512]{1,0:T(8,128)(2,1)S(1)}, u32[]{:S(2)}, u32[]{:S(2)}) collective-permute-start(bf16[288,512]{1,0:T(8,128)(2,1)S(1)} %constant_dynamic-slice_fusion), channel_id=1, source_target_pairs={{0,4},{4,0},{1,5},{5,1},{2,6},{6,2},{3,7},{7,3},{8,12},{12,8},{9,1... | collective-permute-start | bytes 884744 | tf_op jit(solution)/shard_map/ppermute | solution.py:31
  4.5 23.4 %collective-permute-start.5 = (bf16[512,4096]{1,0:T(8,128)(2,1)}, bf16[512,4096]{1,0:T(8,128)(2,1)}, u32[]{:S(2)}, u32[]{:S(2)}) collective-permute-start(bf16[512,4096]{1,0:T(8,128)(2,1)} %own_ref.1), channel_id=1, source_target_pairs={{0,4},{4,0},{1,5},{5,1},{2,6},{6,2},{3,7},{7,3},{8,12},{12,8},{9,1... | collective-permute-start | bytes 12582920 | tf_op jit(solution)/shard_map/ppermute | solution.py:31
  5.8 13.7 %copy-start.1 = (s32[4,1]{0,1:T(1,128)S(1)}, s32[4,1]{0,1:T(1,128)}, u32[]{:S(2)}) copy-start(s32[4,1]{0,1:T(1,128)} %param.13) | copy-start | bytes 52
  5.8 13.7 %copy-start.2 = (s32[1,4]{1,0:T(1,128)S(1)}, s32[1,4]{1,0:T(1,128)}, u32[]{:S(2)}) copy-start(s32[1,4]{1,0:T(1,128)} %param.12) | copy-start | bytes 52
  5.9 8.9 %collective-permute-start.1 = (bf16[288,256]{1,0:T(8,128)(2,1)S(1)}, bf16[288,256]{1,0:T(8,128)(2,1)S(1)}, u32[]{:S(2)}, u32[]{:S(2)}) collective-permute-start(bf16[288,256]{1,0:T(8,128)(2,1)S(1)} %get-tuple-element.105.refs_0_), channel_id=1, source_target_pairs={{0,8},{8,0},{16,24},{24,16},{1,9},{9,1},{17,25},{25,17},{2,10},{10... | collective-permute-start | bytes 442376 | tf_op jit(solution)/shard_map/ppermute | solution.py:44
  7.2 7.5 %collective-permute-start.2 = (bf16[288,256]{1,0:T(8,128)(2,1)S(1)}, bf16[288,256]{1,0:T(8,128)(2,1)S(1)}, u32[]{:S(2)}, u32[]{:S(2)}) collective-permute-start(bf16[288,256]{1,0:T(8,128)(2,1)S(1)} %get-tuple-element.106.refs_2_), channel_id=1, source_target_pairs={{0,24},{8,16},{16,8},{24,0},{1,25},{9,17},{17,9},{25,1},{2,26},{10... | collective-permute-start | bytes 442376 | tf_op jit(solution)/shard_map/ppermute | solution.py:44
  9.0 5.7 %collective-permute-start.3 = (bf16[288,256]{1,0:T(8,128)(2,1)S(1)}, bf16[288,256]{1,0:T(8,128)(2,1)S(1)}, u32[]{:S(2)}, u32[]{:S(2)}) collective-permute-start(bf16[288,256]{1,0:T(8,128)(2,1)S(1)} %get-tuple-element.107.refs_4_), channel_id=1, source_target_pairs={{0,32},{32,0},{64,96},{96,64},{1,33},{33,1},{65,97},{97,65},{2,34}... | collective-permute-start | bytes 442376 | tf_op jit(solution)/shard_map/ppermute | solution.py:44
  10.7 5.6 %collective-permute-start.4 = (bf16[288,256]{1,0:T(8,128)(2,1)S(1)}, bf16[288,256]{1,0:T(8,128)(2,1)S(1)}, u32[]{:S(2)}, u32[]{:S(2)}) collective-permute-start(bf16[288,256]{1,0:T(8,128)(2,1)S(1)} %get-tuple-element.108.refs_6_), channel_id=1, source_target_pairs={{0,96},{32,64},{64,32},{96,0},{1,97},{33,65},{65,33},{97,1},{2,98}... | collective-permute-start | bytes 442376 | tf_op jit(solution)/shard_map/ppermute | solution.py:44
  16.3 7.9 %collective-permute-start.7 = (bf16[576,256]{1,0:T(8,128)(2,1)S(1)}, bf16[576,256]{1,0:T(8,128)(2,1)S(1)}, u32[]{:S(2)}, u32[]{:S(2)}) collective-permute-start(bf16[576,256]{1,0:T(8,128)(2,1)S(1)} %get-tuple-element.117.joined0), channel_id=1, source_target_pairs={{0,24},{8,16},{16,8},{24,0},{1,25},{9,17},{17,9},{25,1},{2,26},{10... | collective-permute-start | bytes 884744 | tf_op jit(solution)/shard_map/ppermute | solution.py:44
  17.3 9.8 %collective-permute-start.8 = (bf16[576,256]{1,0:T(8,128)(2,1)S(1)}, bf16[576,256]{1,0:T(8,128)(2,1)S(1)}, u32[]{:S(2)}, u32[]{:S(2)}) collective-permute-start(bf16[576,256]{1,0:T(8,128)(2,1)S(1)} %get-tuple-element.118.joined1), channel_id=1, source_target_pairs={{0,8},{8,0},{16,24},{24,16},{1,9},{9,1},{17,25},{25,17},{2,10},{10... | collective-permute-start | bytes 884744 | tf_op jit(solution)/shard_map/ppermute | solution.py:44
  17.3 9.9 %collective-permute-start.9 = (bf16[576,256]{1,0:T(8,128)(2,1)S(1)}, bf16[576,256]{1,0:T(8,128)(2,1)S(1)}, u32[]{:S(2)}, u32[]{:S(2)}) collective-permute-start(bf16[576,256]{1,0:T(8,128)(2,1)S(1)} %get-tuple-element.119.joined0), channel_id=1, source_target_pairs={{0,96},{32,64},{64,32},{96,0},{1,97},{33,65},{65,33},{97,1},{2,98}... | collective-permute-start | bytes 884744 | tf_op jit(solution)/shard_map/ppermute | solution.py:44
  19.5 7.6 %collective-permute-start.10 = (bf16[576,256]{1,0:T(8,128)(2,1)S(1)}, bf16[576,256]{1,0:T(8,128)(2,1)S(1)}, u32[]{:S(2)}, u32[]{:S(2)}) collective-permute-start(bf16[576,256]{1,0:T(8,128)(2,1)S(1)} %get-tuple-element.120.joined1), channel_id=1, source_target_pairs={{0,32},{32,0},{64,96},{96,64},{1,33},{33,1},{65,97},{97,65},{2,34}... | collective-permute-start | bytes 884744 | tf_op jit(solution)/shard_map/ppermute | solution.py:44
  24.2 3.6 %collective-permute-start.6 = (s32[8]{0:T(128)S(1)}, s32[8]{0:T(128)S(1)}, u32[]{:S(2)}, u32[]{:S(2)}) collective-permute-start(s32[8]{0:T(128)S(1)} %pad_add_fusion.2.own_numbers), channel_id=1, source_target_pairs={{0,4},{4,0},{1,5},{5,1},{2,6},{6,2},{3,7},{7,3},{8,12},{12,8},{9,1... | collective-permute-start | bytes 104 | tf_op jit(solution)/shard_map/ppermute | solution.py:31
  27.9 27.3 %collective-permute-start.11 = (bf16[2,1152,256]{2,1,0:T(8,128)(2,1)S(1)}, bf16[2,1152,256]{2,1,0:T(8,128)(2,1)S(1)}, u32[]{:S(2)}, u32[]{:S(2)}) collective-permute-start(bf16[2,1152,256]{2,1,0:T(8,128)(2,1)S(1)} %shard_map.87.refs_0_), channel_id=1, source_target_pairs={{0,96},{32,0},{64,32},{96,64},{1,97},{33,1},{65,33},{97,65},{2,98}... | collective-permute-start | bytes 3538952 | tf_op jit(solution)/shard_map/ppermute | solution.py:31
  30.1 28.1 %collective-permute-start.12 = (bf16[2,1152,256]{2,1,0:T(8,128)(2,1)S(1)}, bf16[2,1152,256]{2,1,0:T(8,128)(2,1)S(1)}, u32[]{:S(2)}, u32[]{:S(2)}) collective-permute-start(bf16[2,1152,256]{2,1,0:T(8,128)(2,1)S(1)} %shard_map.87.refs_0_), channel_id=1, source_target_pairs={{0,32},{32,64},{64,96},{96,0},{1,33},{33,65},{65,97},{97,1},{2,34}... | collective-permute-start | bytes 3538952 | tf_op jit(solution)/shard_map/ppermute | solution.py:31
  30.1 29.8 %collective-permute-start.13 = (bf16[2,1152,256]{2,1,0:T(8,128)(2,1)S(1)}, bf16[2,1152,256]{2,1,0:T(8,128)(2,1)S(1)}, u32[]{:S(2)}, u32[]{:S(2)}) collective-permute-start(bf16[2,1152,256]{2,1,0:T(8,128)(2,1)S(1)} %shard_map.88.refs_3_.refs_5_), channel_id=1, source_target_pairs={{0,24},{8,0},{16,8},{24,16},{1,25},{9,1},{17,9},{25,17},{2,26},{10... | collective-permute-start | bytes 3538952 | tf_op jit(solution)/shard_map/ppermute | solution.py:31
  31.0 28.9 %collective-permute-start.14 = (bf16[2,1152,256]{2,1,0:T(8,128)(2,1)S(1)}, bf16[2,1152,256]{2,1,0:T(8,128)(2,1)S(1)}, u32[]{:S(2)}, u32[]{:S(2)}) collective-permute-start(bf16[2,1152,256]{2,1,0:T(8,128)(2,1)S(1)} %shard_map.88.refs_3_.refs_5_), channel_id=1, source_target_pairs={{0,8},{8,16},{16,24},{24,0},{1,9},{9,17},{17,25},{25,1},{2,10},{10... | collective-permute-start | bytes 3538952 | tf_op jit(solution)/shard_map/ppermute | solution.py:31
  58.3 3.2 %copy-start = (bf16[512,4096]{1,0:T(8,128)(2,1)S(1)}, bf16[512,4096]{1,0:T(8,128)(2,1)}, u32[]{:S(2)}) copy-start(bf16[512,4096]{1,0:T(8,128)(2,1)} %own_ref.1) | copy-start | bytes 12582916
  58.3 13.4 %collective-permute-start.15 = (bf16[1152,256]{1,0:T(8,128)(2,1)S(1)}, bf16[1152,256]{1,0:T(8,128)(2,1)S(1)}, u32[]{:S(2)}, u32[]{:S(2)}) collective-permute-start(bf16[1152,256]{1,0:T(8,128)(2,1)S(1)} %get-tuple-element.135), channel_id=1, source_target_pairs={{0,96},{32,0},{64,32},{96,64},{1,97},{33,1},{65,33},{97,65},{2,98}... | collective-permute-start | bytes 1769480 | tf_op jit(solution)/shard_map/ppermute | solution.py:31
  58.7 14.6 %collective-permute-start.16 = (bf16[1152,256]{1,0:T(8,128)(2,1)S(1)}, bf16[1152,256]{1,0:T(8,128)(2,1)S(1)}, u32[]{:S(2)}, u32[]{:S(2)}) collective-permute-start(bf16[1152,256]{1,0:T(8,128)(2,1)S(1)} %get-tuple-element.136), channel_id=1, source_target_pairs={{0,32},{32,64},{64,96},{96,0},{1,33},{33,65},{65,97},{97,1},{2,34}... | collective-permute-start | bytes 1769480 | tf_op jit(solution)/shard_map/ppermute | solution.py:31
  60.0 16.9 %collective-permute-start.17 = (bf16[1152,256]{1,0:T(8,128)(2,1)S(1)}, bf16[1152,256]{1,0:T(8,128)(2,1)S(1)}, u32[]{:S(2)}, u32[]{:S(2)}) collective-permute-start(bf16[1152,256]{1,0:T(8,128)(2,1)S(1)} %get-tuple-element.149), channel_id=1, source_target_pairs={{0,24},{8,0},{16,8},{24,16},{1,25},{9,1},{17,9},{25,17},{2,26},{10... | collective-permute-start | bytes 1769480 | tf_op jit(solution)/shard_map/ppermute | solution.py:31
  60.0 16.8 %collective-permute-start.18 = (bf16[1152,256]{1,0:T(8,128)(2,1)S(1)}, bf16[1152,256]{1,0:T(8,128)(2,1)S(1)}, u32[]{:S(2)}, u32[]{:S(2)}) collective-permute-start(bf16[1152,256]{1,0:T(8,128)(2,1)S(1)} %get-tuple-element.150), channel_id=1, source_target_pairs={{0,8},{8,16},{16,24},{24,0},{1,9},{9,17},{17,25},{25,1},{2,10},{10... | collective-permute-start | bytes 1769480 | tf_op jit(solution)/shard_map/ppermute | solution.py:31
  96.2 7.1 %collective-permute-start.19 = (bf16[1024,512]{1,0:T(8,128)(2,1)S(1)}, bf16[1024,512]{1,0:T(8,128)(2,1)S(1)}, u32[]{:S(2)}, u32[]{:S(2)}) collective-permute-start(bf16[1024,512]{1,0:T(8,128)(2,1)S(1)} %get-tuple-element.160), channel_id=1, source_target_pairs={{0,4},{4,0},{1,5},{5,1},{2,6},{6,2},{3,7},{7,3},{8,12},{12,8},{9,1... | collective-permute-start | bytes 3145736 | tf_op jit(solution)/shard_map/ppermute | solution.py:31
  103.5 15.9 %collective-permute-start.20 = (bf16[512,512]{1,0:T(8,128)(2,1)S(1)}, bf16[512,512]{1,0:T(8,128)(2,1)S(1)}, u32[]{:S(2)}, u32[]{:S(2)}) collective-permute-start(bf16[512,512]{1,0:T(8,128)(2,1)S(1)} %get-tuple-element.175), channel_id=1, source_target_pairs={{0,1},{1,2},{2,3},{3,0},{4,5},{5,6},{6,7},{7,4},{8,9},{9,10},{10,1... | collective-permute-start | bytes 1572872 | tf_op jit(solution)/shard_map/ppermute | solution.py:31
  104.9 14.6 %collective-permute-start.21 = (bf16[512,512]{1,0:T(8,128)(2,1)S(1)}, bf16[512,512]{1,0:T(8,128)(2,1)S(1)}, u32[]{:S(2)}, u32[]{:S(2)}) collective-permute-start(bf16[512,512]{1,0:T(8,128)(2,1)S(1)} %get-tuple-element.176), channel_id=1, source_target_pairs={{0,3},{1,0},{2,1},{3,2},{4,7},{5,4},{6,5},{7,6},{8,11},{9,8},{10,9... | collective-permute-start | bytes 1572872 | tf_op jit(solution)/shard_map/ppermute | solution.py:31
  120.1 26.3 %collective-permute-start.26 = (bf16[1024,512]{1,0:T(8,128)(2,1)S(1)}, bf16[1024,512]{1,0:T(8,128)(2,1)S(1)}, u32[]{:S(2)}, u32[]{:S(2)}) collective-permute-start(bf16[1024,512]{1,0:T(8,128)(2,1)S(1)} %get-tuple-element.196), channel_id=1, source_target_pairs={{0,4},{4,0},{1,5},{5,1},{2,6},{6,2},{3,7},{7,3},{8,12},{12,8},{9,1... | collective-permute-start | bytes 3145736 | tf_op jit(solution)/shard_map/ppermute | solution.py:31
  120.5 21.1 %collective-permute-start.22 = (bf16[512,512]{1,0:T(8,128)(2,1)S(1)}, bf16[512,512]{1,0:T(8,128)(2,1)S(1)}, u32[]{:S(2)}, u32[]{:S(2)}) collective-permute-start(bf16[512,512]{1,0:T(8,128)(2,1)S(1)} %get-tuple-element.192), channel_id=1, source_target_pairs={{0,1},{1,2},{2,3},{3,0},{4,5},{5,6},{6,7},{7,4},{8,9},{9,10},{10,1... | collective-permute-start | bytes 1572872 | tf_op jit(solution)/shard_map/ppermute | solution.py:31
  121.2 20.4 %collective-permute-start.23 = (bf16[512,512]{1,0:T(8,128)(2,1)S(1)}, bf16[512,512]{1,0:T(8,128)(2,1)S(1)}, u32[]{:S(2)}, u32[]{:S(2)}) collective-permute-start(bf16[512,512]{1,0:T(8,128)(2,1)S(1)} %get-tuple-element.193), channel_id=1, source_target_pairs={{0,3},{1,0},{2,1},{3,2},{4,7},{5,4},{6,5},{7,6},{8,11},{9,8},{10,9... | collective-permute-start | bytes 1572872 | tf_op jit(solution)/shard_map/ppermute | solution.py:31
  123.2 23.2 %collective-permute-start.24 = (bf16[512,512]{1,0:T(8,128)(2,1)S(1)}, bf16[512,512]{1,0:T(8,128)(2,1)S(1)}, u32[]{:S(2)}, u32[]{:S(2)}) collective-permute-start(bf16[512,512]{1,0:T(8,128)(2,1)S(1)} %get-tuple-element.194), channel_id=1, source_target_pairs={{0,1},{1,2},{2,3},{3,0},{4,5},{5,6},{6,7},{7,4},{8,9},{9,10},{10,1... | collective-permute-start | bytes 1572872 | tf_op jit(solution)/shard_map/ppermute | solution.py:31
  123.2 23.2 %collective-permute-start.25 = (bf16[512,512]{1,0:T(8,128)(2,1)S(1)}, bf16[512,512]{1,0:T(8,128)(2,1)S(1)}, u32[]{:S(2)}, u32[]{:S(2)}) collective-permute-start(bf16[512,512]{1,0:T(8,128)(2,1)S(1)} %get-tuple-element.195), channel_id=1, source_target_pairs={{0,3},{1,0},{2,1},{3,2},{4,7},{5,4},{6,5},{7,6},{8,11},{9,8},{10,9... | collective-permute-start | bytes 1572872 | tf_op jit(solution)/shard_map/ppermute | solution.py:31

commit v7 on v6

--- a/solution.py
+++ b/solution.py
@@ -394,20 +394,23 @@
 
     upper = place // 2
     rows = pl.ds(pl.multiple_of((place % 2) * PIECE, 64), both)
-    for n, ref in ((0, b_own), (1, b_up), (3, b_down)):
-        w_ref[1, n] = ref[upper, rows, :]
     for h, ref in ((0, b_top), (1, b_low)):
         @pl.when(upper == h)
         def take_b():
             w_ref[1, 2] = ref[rows, :]
 
 
-def weights_tile(w_ref):
+def weights_tile(place, sources, w_ref):
+    b_own, b_up, b_down = sources[5], sources[6], sources[9]
+
+    def piece(side, n, t):
+        if side == 0 or n == 2:
+            return w_ref[side, n, t * CHUNK : (t + 1) * CHUNK]
+        row = pl.multiple_of((place % 2) * PIECE + t * CHUNK, 64)
+        return {0: b_own, 1: b_up, 3: b_down}[n][place // 2, pl.ds(row, CHUNK), :]
+
     rows = [
-        jnp.concatenate(
-            [w_ref[side, n, t * CHUNK : (t + 1) * CHUNK] for t in range(2) for side in range(2)],
-            axis=1,
-        )
+        jnp.concatenate([piece(side, n, t) for t in range(2) for side in range(2)], axis=1)
         for n in range(4)
     ]
     return jnp.concatenate(rows, axis=0)
@@ -464,7 +467,7 @@
                     first = p * 64 + a * DEC
                     part = jnp.where(head == a, context[first : first + DEC], part)
                 ctx_ref[meta.question(side, p), :, cols] += part
-    total = jnp.dot(weights_tile(w_ref), kvg_ref[...], preferred_element_type=F32)
+    total = jnp.dot(weights_tile(pos[2], sources, w_ref), kvg_ref[...], preferred_element_type=F32)
     own_ref[...] = total[:, :ROWS].astype(BF)
     oth_ref[...] = total[:, ROWS:].astype(BF)
     dense_ref[...] = ctx_ref[...].astype(BF)
@@ -499,7 +502,7 @@
 def base_kernel(places, kvg_ref, *refs):
     sources, (base_ref, other_ref, w_ref) = refs[:10], refs[10:]
     take_weights(places[0], sources, w_ref)
-    total = jnp.dot(weights_tile(w_ref), kvg_ref[...], preferred_element_type=F32)
+    total = jnp.dot(weights_tile(places[0], sources, w_ref), kvg_ref[...], preferred_element_type=F32)
     base_ref[...] = total[:, :ROWS]
     other_ref[...] = total[:, ROWS:].astype(BF)
 
@@ -539,7 +542,7 @@
 def near_grad_kernel(places, kvg_ref, *refs):
     sources, (out_ref, w_ref) = refs[:10], refs[10:]
     take_weights(places[pl.program_id(0)], sources, w_ref)
-    total = jnp.dot(weights_tile(w_ref), kvg_ref[...], preferred_element_type=F32)
+    total = jnp.dot(weights_tile(places[pl.program_id(0)], sources, w_ref), kvg_ref[...], preferred_element_type=F32)
     core = places[2]
     out_ref[core, 0] = total[:, :ROWS].astype(BF)
     out_ref[1 - core, 0] = total[:, ROWS:].astype(BF)

time: 150 us -> 150 us (level)
  no operation moved by 1% of the time
where the time goes in v7:
time: 150 us; the launch traced here: 149 us
  waiting for transfers between devices  41.2 us (27%)
  Pallas kernels  36 us (24%)
  starting transfers between devices  34.1 us (23%)
  blocking collectives  33.1 us (22%)
  other arithmetic  3.21 us (2%)
    ppermute x19, waiting for transfers between devices, perm(): return lax.ppermute(v, axis, [(i, (i + shift) % n) for i in range(n)])  35.1 us
    ppermute x19, starting transfers between devices, perm(): return lax.ppermute(v, axis, [(i, (i + shift) % n) for i in range(n)])  23.9 us
    all_to_all x1, blocking collectives, body(): lax.all_to_all(dense, ENC, 0, 0, tiled=True).reshape(NZ * NX, NC, DEC, HALF)  15.8 us
    ppermute x8, starting transfers between devices, pair_perm(): return lax.ppermute(v, axis, [(i, turn(i) % 4) for i in range(4)])  10.3 us
    all_to_all x1, blocking collectives, body(): stats_all = lax.all_to_all(stats, ('z', 'x'), 0, 0, tiled=True)  10.1 us
    pallas_call x1, Pallas kernels, project_near(): pl.pallas_call(near_kernel, grid_spec=pltpu.PrefetchScalarGridSpec(num_sc...  9.9 us
    all_to_all x1, blocking collectives, body(): lax.all_to_all(near_blocks(near_places, kvg, weights), 'core', 0, 0, tile...  7.17 us
    pallas_call x2, Pallas kernels, project_far(): pl.pallas_call(functools.partial(far_kernel, quad), grid_spec=pltpu.Prefe...  6.98 us
  transfers between devices with their start and end apart: 27, of which 9 were waited for; matrix products, arithmetic and copies ran while one was open for 2% of the time, Pallas kernels for 15%

profile of v7, /device:TPU:1, one launch (start us, length us, event | category | flops | bytes accessed | tf_op | source)
XLA Modules:
  0.0 149.3 jit_solution(3424967019721395241)
XLA Ops:
  0.6 1.1 pad_maximum_fusion
  1.8 1.5 %collective-permute-start = (bf16[288,512]{1,0:T(8,128)(2,1)S(1)}, bf16[288,512]{1,0:T(8,128)(2,1)S(1)}, u32[]{:S(2)}, u32[]{:S(2)}) collective-permute-start(bf16[288,512]{1,0:T(8,128)(2,1)S(1)} %constant_dynamic-slice_fusion), channel_id=1, source_target_pairs={{0,4},{4,0},{1,5},{5,1},{2,6},{6,2},{3,7},{7,3},{8,12},{12,8},{9,1... | collective-permute-start | bytes 884744 | tf_op jit(solution)/shard_map/ppermute | solution.py:31
  3.3 1.2 collective-permute-done
  4.5 0.4 collective-permute-start.5
  4.9 0.6 fusion.3
  5.5 0.1 broadcast_select_fusion
  5.9 1.4 collective-permute-start.1
  7.2 1.8 %collective-permute-start.2 = (bf16[288,256]{1,0:T(8,128)(2,1)S(1)}, bf16[288,256]{1,0:T(8,128)(2,1)S(1)}, u32[]{:S(2)}, u32[]{:S(2)}) collective-permute-start(bf16[288,256]{1,0:T(8,128)(2,1)S(1)} %get-tuple-element.106.refs_2_), channel_id=1, source_target_pairs={{0,24},{8,16},{16,8},{24,0},{1,25},{9,17},{17,9},{25,1},{2,26},{10... | collective-permute-start | bytes 442376 | tf_op jit(solution)/shard_map/ppermute | solution.py:44
  9.0 1.6 %collective-permute-start.3 = (bf16[288,256]{1,0:T(8,128)(2,1)S(1)}, bf16[288,256]{1,0:T(8,128)(2,1)S(1)}, u32[]{:S(2)}, u32[]{:S(2)}) collective-permute-start(bf16[288,256]{1,0:T(8,128)(2,1)S(1)} %get-tuple-element.107.refs_4_), channel_id=1, source_target_pairs={{0,32},{32,0},{64,96},{96,64},{1,33},{33,1},{65,97},{97,65},{2,34}... | collective-permute-start | bytes 442376 | tf_op jit(solution)/shard_map/ppermute | solution.py:44
  10.7 2.2 %collective-permute-start.4 = (bf16[288,256]{1,0:T(8,128)(2,1)S(1)}, bf16[288,256]{1,0:T(8,128)(2,1)S(1)}, u32[]{:S(2)}, u32[]{:S(2)}) collective-permute-start(bf16[288,256]{1,0:T(8,128)(2,1)S(1)} %get-tuple-element.108.refs_6_), channel_id=1, source_target_pairs={{0,96},{32,64},{64,32},{96,0},{1,97},{33,65},{65,33},{97,1},{2,98}... | collective-permute-start | bytes 442376 | tf_op jit(solution)/shard_map/ppermute | solution.py:44
  12.9 1.8 %pad_add_fusion = (s32[3]{0:T(128)S(1)}, s32[3]{0:T(128)S(1)}) fusion(s32[1]{0:T(128)} %get-tuple-element.220, s32[1]{0:T(128)} %bitcast.3.place, s32[1]{0:T(128)} %bitcast.2, s32[1]{0:T(128)} %bitcast.4, s32[1]{0:T(128)} %get-tuple-element.218, s32[1]{0:T(128)} %get-tuple-element.219), kind=kLoop, calls=%fused_computation.20 | loop fusion | flops 12 | bytes 48 | tf_op jit(solution)/shard_map/stack | solution.py:641
  14.8 1.5 collective-permute-done.4.refs_7_
  16.3 0.9 collective-permute-start.7
  17.3 2.2 %collective-permute-start.9 = (bf16[576,256]{1,0:T(8,128)(2,1)S(1)}, bf16[576,256]{1,0:T(8,128)(2,1)S(1)}, u32[]{:S(2)}, u32[]{:S(2)}) collective-permute-start(bf16[576,256]{1,0:T(8,128)(2,1)S(1)} %get-tuple-element.119.joined0), channel_id=1, source_target_pairs={{0,96},{32,64},{64,32},{96,0},{1,97},{33,65},{65,33},{97,1},{2,98}... | collective-permute-start | bytes 884744 | tf_op jit(solution)/shard_map/ppermute | solution.py:44
  19.6 4.6 %collective-permute-done.7.second0 = bf16[576,256]{1,0:T(8,128)(2,1)S(1)} collective-permute-done((bf16[576,256]{1,0:T(8,128)(2,1)S(1)}, bf16[576,256]{1,0:T(8,128)(2,1)S(1)}, u32[]{:S(2)}, u32[]{:S(2)}) %collective-permute-start.7) | collective-permute-done | bytes 294944 | tf_op jit(solution)/shard_map/ppermute | solution.py:44
  24.2 2.8 %collective-permute-start.6 = (s32[8]{0:T(128)S(1)}, s32[8]{0:T(128)S(1)}, u32[]{:S(2)}, u32[]{:S(2)}) collective-permute-start(s32[8]{0:T(128)S(1)} %pad_add_fusion.2.own_numbers), channel_id=1, source_target_pairs={{0,4},{4,0},{1,5},{5,1},{2,6},{6,2},{3,7},{7,3},{8,12},{12,8},{9,1... | collective-permute-start | bytes 104 | tf_op jit(solution)/shard_map/ppermute | solution.py:31
  27.2 0.1 shard_map.88.refs_3_.refs_5_
  27.3 0.6 collective-permute-done.6.other_numbers
  27.9 2.2 %collective-permute-start.11 = (bf16[2,1152,256]{2,1,0:T(8,128)(2,1)S(1)}, bf16[2,1152,256]{2,1,0:T(8,128)(2,1)S(1)}, u32[]{:S(2)}, u32[]{:S(2)}) collective-permute-start(bf16[2,1152,256]{2,1,0:T(8,128)(2,1)S(1)} %shard_map.87.refs_0_), channel_id=1, source_target_pairs={{0,96},{32,0},{64,32},{96,64},{1,97},{33,1},{65,33},{97,65},{2,98}... | collective-permute-start | bytes 3538952 | tf_op jit(solution)/shard_map/ppermute | solution.py:31
  30.1 0.9 collective-permute-start.13
  31.0 0.6 collective-permute-start.14
  31.6 23.6 %collective-permute-done.11.refs_1_.up_ref = bf16[2,1152,256]{2,1,0:T(8,128)(2,1)S(1)} collective-permute-done((bf16[2,1152,256]{2,1,0:T(8,128)(2,1)S(1)}, bf16[2,1152,256]{2,1,0:T(8,128)(2,1)S(1)}, u32[]{:S(2)}, u32[]{:S(2)}) %collective-permute-start.11) | collective-permute-done | bytes 1179680 | tf_op jit(solution)/shard_map/ppermute | solution.py:31
  55.2 3.1 %collective-permute-done.12.refs_2_.down_ref.refs_4_ = bf16[2,1152,256]{2,1,0:T(8,128)(2,1)S(1)} collective-permute-done((bf16[2,1152,256]{2,1,0:T(8,128)(2,1)S(1)}, bf16[2,1152,256]{2,1,0:T(8,128)(2,1)S(1)}, u32[]{:S(2)}, u32[]{:S(2)}) %collective-permute-start.12) | collective-permute-done | bytes 1179680 | tf_op jit(solution)/shard_map/ppermute | solution.py:31
  58.3 0.4 collective-permute-start.15
  58.7 1.1 collective-permute-start.16
  60.0 1.5 collective-permute-start.18
  61.5 9.9 %shard_map.89 = (f32[2,512,512]{2,1,0:T(8,128)S(1)}, f32[2,512,512]{2,1,0:T(8,128)S(1)}, bf16[2,512,1024]{2,1,0:T(8,128)(2,1)S(1)}, bf16[2,512,1024]{2,1,0:T(8,1...) custom-call(s32[3]{0:T(128)S(1)} %get-tuple-element.110.pos, bf16[512,4096]{1,0:T(8,128)(2,1)S(1)} %copy-done, ...), custom_call_target="tpu_custom_call" | custom-call | flops 200000000 | tf_op jit(solution)/shard_map/pallas_call | solution.py:173
  71.4 0.4 collective-permute-done.15.refs_2_
  71.8 1.6 %collective-permute-done.16.refs_3_ = bf16[1152,256]{1,0:T(8,128)(2,1)S(1)} collective-permute-done((bf16[1152,256]{1,0:T(8,128)(2,1)S(1)}, bf16[1152,256]{1,0:T(8,128)(2,1)S(1)}, u32[]{:S(2)}, u32[]{:S(2)}) %collective-permute-start.16) | collective-permute-done | bytes 589856 | tf_op jit(solution)/shard_map/ppermute | solution.py:31
  73.4 3.5 %shard_map.91 = (bf16[2,512,256]{2,1,0:T(8,128)(2,1)S(1)}, bf16[2,512,256]{2,1,0:T(8,128)(2,1)S(1)}, bf16[1024,256]{1,0:T(8,128)(2,1)S(1)}, f32[8,256]{1,0:T(8,128)S(1)}, f32[2,256,256]{2,1,0:T(8,128)S(1)}) custom-call(s32[3]{0:T(128)S(1)} %get-tuple-element.110.pos, s32[8]{0:T(128)S(1)} %pad_add_fusion.2.own_numbers, ...), custom_call_target="tpu_custom_call" | custom-call | flops 200000000 | tf_op jit(solution)/shard_map/pallas_call | solution.py:331
  76.8 3.5 %shard_map.93 = (bf16[2,512,256]{2,1,0:T(8,128)(2,1)S(1)}, bf16[2,512,256]{2,1,0:T(8,128)(2,1)S(1)}, bf16[1024,256]{1,0:T(8,128)(2,1)S(1)}, f32[16,16,256]{2,1,0:T(8,128)S(1)}, f32[2,256,256]{2,1,0:T(8,128)S(1)}) custom-call(s32[3]{0:T(128)S(1)} %get-tuple-element.110.pos, s32[8]{0:T(128)S(1)} %pad_add_fusion.2.own_numbers, ...), custom_call_target="tpu_custom_call" | custom-call | flops 200000000 | tf_op jit(solution)/shard_map/pallas_call | solution.py:331
  80.4 10.1 %all_to_all.15.st_ref = f32[16,16,256]{2,1,0:T(8,128)S(1)} all-to-all(f32[16,16,256]{2,1,0:T(8,128)S(1)} %get-tuple-element.159), channel_id=1, replica_groups=mesh['z'=4,'x'=4,'core'=2,'dec'=4] {'z','x'}, dimensions={0} | all-to-all | bytes 524288 | tf_op jit(solution)/shard_map/all_to_all | solution.py:697
  90.5 5.6 %shard_map.94 = (bf16[1024,1024]{1,0:T(8,128)(2,1)S(1)}, bf16[1024,512]{1,0:T(8,128)(2,1)S(1)}, bf16[1024,512]{1,0:T(8,128)(2,1)S(1)}, bf16[32,16,512]{2,1,0:T(8,128)(2,1)S(1)}) custom-call(s32[3]{0:T(128)S(1)} %get-tuple-element.110.pos, s32[8]{0:T(128)S(1)} %pad_add_fusion.2.own_numbers, s32[8]{0:T(128)S(1)} %collective-permute-done.6.other_numbers, ...), custom_call_target="tpu_custom_call" | custom-call | flops 200000000 | tf_op jit(solution)/shard_map/pallas_call | solution.py:486
  96.1 3.7 %collective-permute-start.19 = (bf16[1024,512]{1,0:T(8,128)(2,1)S(1)}, bf16[1024,512]{1,0:T(8,128)(2,1)S(1)}, u32[]{:S(2)}, u32[]{:S(2)}) collective-permute-start(bf16[1024,512]{1,0:T(8,128)(2,1)S(1)} %get-tuple-element.160), channel_id=1, source_target_pairs={{0,4},{4,0},{1,5},{5,1},{2,6},{6,2},{3,7},{7,3},{8,12},{12,8},{9,1... | collective-permute-start | bytes 3145736 | tf_op jit(solution)/shard_map/ppermute | solution.py:31
  99.8 3.3 %shard_map.95 = (f32[1024,512]{1,0:T(8,128)S(1)}, bf16[1024,512]{1,0:T(8,128)(2,1)S(1)}) custom-call(s32[1]{0:T(128)} %get-tuple-element.162.places, bf16[1024,1024]{1,0:T(8,128)(2,1)S(1)} %get-tuple-element.178.kvg_ref, bf16[2,1152,256]{2,1,0:T(8,128)(2,1)S(1)} %shard_map.87.refs_0_, bf16[2,1152,256]{2,1,0:T(8,128)(2,1)S(1)} %collective-permute-done.11.refs_1_.up_ref, ...), custom_call_target="tpu_custom_call" | custom-call | flops 200000000 | tf_op jit(solution)/shard_map/pallas_call | solution.py:512
  103.2 0.2 shard_map.96
  103.4 1.4 collective-permute-start.20
  104.8 1.5 %collective-permute-start.21 = (bf16[512,512]{1,0:T(8,128)(2,1)S(1)}, bf16[512,512]{1,0:T(8,128)(2,1)S(1)}, u32[]{:S(2)}, u32[]{:S(2)}) collective-permute-start(bf16[512,512]{1,0:T(8,128)(2,1)S(1)} %get-tuple-element.176), channel_id=1, source_target_pairs={{0,3},{1,0},{2,1},{3,2},{4,7},{5,4},{6,5},{7,6},{8,11},{9,8},{10,9... | collective-permute-start | bytes 1572872 | tf_op jit(solution)/shard_map/ppermute | solution.py:31
  106.3 5.8 %shard_map.97 = bf16[2,2,1024,512]{3,2,1,0:T(8,128)(2,1)S(1)} custom-call(s32[3]{0:T(128)S(1)} %get-tuple-element.177.places, bf16[1024,1024]{1,0:T(8,128)(2,1)S(1)} %get-tuple-element.178.kvg_ref, bf16[2,1152,256]{2,1,0:T(8,128)(2,1)S(1)} %shard_map.87.refs_0_, bf16[2,1152,256]{2,1,0:T(8,128)(2,1)S(1)} %collective-permute-done.11.refs_1_.up_ref, ...), custom_call_target="tpu_custom_call" | custom-call | flops 200000000 | tf_op jit(solution)/shard_map/pallas_call | solution.py:552
  112.1 7.2 %all_to_all.16.near_ref = bf16[2,2,1024,512]{3,2,1,0:T(8,128)(2,1)S(1)} all-to-all(bf16[2,2,1024,512]{3,2,1,0:T(8,128)(2,1)S(1)} %shard_map.97), channel_id=1, replica_groups=mesh['z'=4,'x'=4,'core'=2,'dec'=4] {'core'}, dimensions={0} | all-to-all | bytes 8388608 | tf_op jit(solution)/shard_map/all_to_all | solution.py:714
  119.2 0.6 shard_map.98
  119.9 0.5 collective-permute-start.26
  120.4 0.8 collective-permute-start.22
  121.1 1.9 %collective-permute-start.23 = (bf16[512,512]{1,0:T(8,128)(2,1)S(1)}, bf16[512,512]{1,0:T(8,128)(2,1)S(1)}, u32[]{:S(2)}, u32[]{:S(2)}) collective-permute-start(bf16[512,512]{1,0:T(8,128)(2,1)S(1)} %get-tuple-element.193), channel_id=1, source_target_pairs={{0,3},{1,0},{2,1},{3,2},{4,7},{5,4},{6,5},{7,6},{8,11},{9,8},{10,9... | collective-permute-start | bytes 1572872 | tf_op jit(solution)/shard_map/ppermute | solution.py:31
  123.0 2.7 %collective-permute-start.25 = (bf16[512,512]{1,0:T(8,128)(2,1)S(1)}, bf16[512,512]{1,0:T(8,128)(2,1)S(1)}, u32[]{:S(2)}, u32[]{:S(2)}) collective-permute-start(bf16[512,512]{1,0:T(8,128)(2,1)S(1)} %get-tuple-element.195), channel_id=1, source_target_pairs={{0,3},{1,0},{2,1},{3,2},{4,7},{5,4},{6,5},{7,6},{8,11},{9,8},{10,9... | collective-permute-start | bytes 1572872 | tf_op jit(solution)/shard_map/ppermute | solution.py:31
  125.7 15.8 %all_to_all.17 = bf16[32,16,512]{2,1,0:T(8,128)(2,1)S(1)} all-to-all(bf16[32,16,512]{2,1,0:T(8,128)(2,1)S(1)} %get-tuple-element.197), channel_id=1, replica_groups=mesh['z'=4,'x'=4,'core'=2,'dec'=4] {'z','x','core'}, dimensions={0} | all-to-all | bytes 1048576 | tf_op jit(solution)/shard_map/all_to_all | solution.py:727
  141.5 4.7 %collective-permute-done.24.up_top = bf16[512,512]{1,0:T(8,128)(2,1)S(1)} collective-permute-done((bf16[512,512]{1,0:T(8,128)(2,1)S(1)}, bf16[512,512]{1,0:T(8,128)(2,1)S(1)}, u32[]{:S(2)}, u32[]{:S(2)}) %collective-permute-start.24) | collective-permute-done | bytes 524320 | tf_op jit(solution)/shard_map/ppermute | solution.py:31
  146.2 3.1 %shard_map.99 = (f32[512,1024]{1,0:T(8,128)}, f32[1,16,1024]{2,1,0:T(8,128)}) custom-call(s32[4]{0:T(128)S(1)} %and_select_fusion.place, f32[1024,512]{1,0:T(8,128)S(1)} %get-tuple-element.182.base_ref, bf16[1024,512]{1,0:T(8,128)(2,1)S(1)} %collective-permute-done.26.core_ref, bf16[512,512]{1,0:T(8,128)(2,1)S(1)} %collective-permute-done.24.up_top, ...), custom_call_target="tpu_custom_call" | custom-call | flops 200000000 | tf_op jit(solution)/shard_map/pallas_call | solution.py:613
  (44 shorter events, 0.7 us)
Async XLA Ops:
  1.8 2.7 %collective-permute-start = (bf16[288,512]{1,0:T(8,128)(2,1)S(1)}, bf16[288,512]{1,0:T(8,128)(2,1)S(1)}, u32[]{:S(2)}, u32[]{:S(2)}) collective-permute-start(bf16[288,512]{1,0:T(8,128)(2,1)S(1)} %constant_dynamic-slice_fusion), channel_id=1, source_target_pairs={{0,4},{4,0},{1,5},{5,1},{2,6},{6,2},{3,7},{7,3},{8,12},{12,8},{9,1... | collective-permute-start | bytes 884744 | tf_op jit(solution)/shard_map/ppermute | solution.py:31
  4.5 23.4 %collective-permute-start.5 = (bf16[512,4096]{1,0:T(8,128)(2,1)}, bf16[512,4096]{1,0:T(8,128)(2,1)}, u32[]{:S(2)}, u32[]{:S(2)}) collective-permute-start(bf16[512,4096]{1,0:T(8,128)(2,1)} %own_ref.1), channel_id=1, source_target_pairs={{0,4},{4,0},{1,5},{5,1},{2,6},{6,2},{3,7},{7,3},{8,12},{12,8},{9,1... | collective-permute-start | bytes 12582920 | tf_op jit(solution)/shard_map/ppermute | solution.py:31
  5.8 13.7 %copy-start.1 = (s32[4,1]{0,1:T(1,128)S(1)}, s32[4,1]{0,1:T(1,128)}, u32[]{:S(2)}) copy-start(s32[4,1]{0,1:T(1,128)} %param.13) | copy-start | bytes 52
  5.8 13.7 %copy-start.2 = (s32[1,4]{1,0:T(1,128)S(1)}, s32[1,4]{1,0:T(1,128)}, u32[]{:S(2)}) copy-start(s32[1,4]{1,0:T(1,128)} %param.12) | copy-start | bytes 52
  5.9 8.9 %collective-permute-start.1 = (bf16[288,256]{1,0:T(8,128)(2,1)S(1)}, bf16[288,256]{1,0:T(8,128)(2,1)S(1)}, u32[]{:S(2)}, u32[]{:S(2)}) collective-permute-start(bf16[288,256]{1,0:T(8,128)(2,1)S(1)} %get-tuple-element.105.refs_0_), channel_id=1, source_target_pairs={{0,8},{8,0},{16,24},{24,16},{1,9},{9,1},{17,25},{25,17},{2,10},{10... | collective-permute-start | bytes 442376 | tf_op jit(solution)/shard_map/ppermute | solution.py:44
  7.2 7.5 %collective-permute-start.2 = (bf16[288,256]{1,0:T(8,128)(2,1)S(1)}, bf16[288,256]{1,0:T(8,128)(2,1)S(1)}, u32[]{:S(2)}, u32[]{:S(2)}) collective-permute-start(bf16[288,256]{1,0:T(8,128)(2,1)S(1)} %get-tuple-element.106.refs_2_), channel_id=1, source_target_pairs={{0,24},{8,16},{16,8},{24,0},{1,25},{9,17},{17,9},{25,1},{2,26},{10... | collective-permute-start | bytes 442376 | tf_op jit(solution)/shard_map/ppermute | solution.py:44
  9.0 5.7 %collective-permute-start.3 = (bf16[288,256]{1,0:T(8,128)(2,1)S(1)}, bf16[288,256]{1,0:T(8,128)(2,1)S(1)}, u32[]{:S(2)}, u32[]{:S(2)}) collective-permute-start(bf16[288,256]{1,0:T(8,128)(2,1)S(1)} %get-tuple-element.107.refs_4_), channel_id=1, source_target_pairs={{0,32},{32,0},{64,96},{96,64},{1,33},{33,1},{65,97},{97,65},{2,34}... | collective-permute-start | bytes 442376 | tf_op jit(solution)/shard_map/ppermute | solution.py:44
  10.7 5.6 %collective-permute-start.4 = (bf16[288,256]{1,0:T(8,128)(2,1)S(1)}, bf16[288,256]{1,0:T(8,128)(2,1)S(1)}, u32[]{:S(2)}, u32[]{:S(2)}) collective-permute-start(bf16[288,256]{1,0:T(8,128)(2,1)S(1)} %get-tuple-element.108.refs_6_), channel_id=1, source_target_pairs={{0,96},{32,64},{64,32},{96,0},{1,97},{33,65},{65,33},{97,1},{2,98}... | collective-permute-start | bytes 442376 | tf_op jit(solution)/shard_map/ppermute | solution.py:44
  16.3 7.9 %collective-permute-start.7 = (bf16[576,256]{1,0:T(8,128)(2,1)S(1)}, bf16[576,256]{1,0:T(8,128)(2,1)S(1)}, u32[]{:S(2)}, u32[]{:S(2)}) collective-permute-start(bf16[576,256]{1,0:T(8,128)(2,1)S(1)} %get-tuple-element.117.joined0), channel_id=1, source_target_pairs={{0,24},{8,16},{16,8},{24,0},{1,25},{9,17},{17,9},{25,1},{2,26},{10... | collective-permute-start | bytes 884744 | tf_op jit(solution)/shard_map/ppermute | solution.py:44
  17.3 9.8 %collective-permute-start.8 = (bf16[576,256]{1,0:T(8,128)(2,1)S(1)}, bf16[576,256]{1,0:T(8,128)(2,1)S(1)}, u32[]{:S(2)}, u32[]{:S(2)}) collective-permute-start(bf16[576,256]{1,0:T(8,128)(2,1)S(1)} %get-tuple-element.118.joined1), channel_id=1, source_target_pairs={{0,8},{8,0},{16,24},{24,16},{1,9},{9,1},{17,25},{25,17},{2,10},{10... | collective-permute-start | bytes 884744 | tf_op jit(solution)/shard_map/ppermute | solution.py:44
  17.3 9.9 %collective-permute-start.9 = (bf16[576,256]{1,0:T(8,128)(2,1)S(1)}, bf16[576,256]{1,0:T(8,128)(2,1)S(1)}, u32[]{:S(2)}, u32[]{:S(2)}) collective-permute-start(bf16[576,256]{1,0:T(8,128)(2,1)S(1)} %get-tuple-element.119.joined0), channel_id=1, source_target_pairs={{0,96},{32,64},{64,32},{96,0},{1,97},{33,65},{65,33},{97,1},{2,98}... | collective-permute-start | bytes 884744 | tf_op jit(solution)/shard_map/ppermute | solution.py:44
  19.5 7.6 %collective-permute-start.10 = (bf16[576,256]{1,0:T(8,128)(2,1)S(1)}, bf16[576,256]{1,0:T(8,128)(2,1)S(1)}, u32[]{:S(2)}, u32[]{:S(2)}) collective-permute-start(bf16[576,256]{1,0:T(8,128)(2,1)S(1)} %get-tuple-element.120.joined1), channel_id=1, source_target_pairs={{0,32},{32,0},{64,96},{96,64},{1,33},{33,1},{65,97},{97,65},{2,34}... | collective-permute-start | bytes 884744 | tf_op jit(solution)/shard_map/ppermute | solution.py:44
  24.2 3.6 %collective-permute-start.6 = (s32[8]{0:T(128)S(1)}, s32[8]{0:T(128)S(1)}, u32[]{:S(2)}, u32[]{:S(2)}) collective-permute-start(s32[8]{0:T(128)S(1)} %pad_add_fusion.2.own_numbers), channel_id=1, source_target_pairs={{0,4},{4,0},{1,5},{5,1},{2,6},{6,2},{3,7},{7,3},{8,12},{12,8},{9,1... | collective-permute-start | bytes 104 | tf_op jit(solution)/shard_map/ppermute | solution.py:31
  27.9 27.3 %collective-permute-start.11 = (bf16[2,1152,256]{2,1,0:T(8,128)(2,1)S(1)}, bf16[2,1152,256]{2,1,0:T(8,128)(2,1)S(1)}, u32[]{:S(2)}, u32[]{:S(2)}) collective-permute-start(bf16[2,1152,256]{2,1,0:T(8,128)(2,1)S(1)} %shard_map.87.refs_0_), channel_id=1, source_target_pairs={{0,96},{32,0},{64,32},{96,64},{1,97},{33,1},{65,33},{97,65},{2,98}... | collective-permute-start | bytes 3538952 | tf_op jit(solution)/shard_map/ppermute | solution.py:31
  30.1 28.1 %collective-permute-start.12 = (bf16[2,1152,256]{2,1,0:T(8,128)(2,1)S(1)}, bf16[2,1152,256]{2,1,0:T(8,128)(2,1)S(1)}, u32[]{:S(2)}, u32[]{:S(2)}) collective-permute-start(bf16[2,1152,256]{2,1,0:T(8,128)(2,1)S(1)} %shard_map.87.refs_0_), channel_id=1, source_target_pairs={{0,32},{32,64},{64,96},{96,0},{1,33},{33,65},{65,97},{97,1},{2,34}... | collective-permute-start | bytes 3538952 | tf_op jit(solution)/shard_map/ppermute | solution.py:31
  30.1 29.8 %collective-permute-start.13 = (bf16[2,1152,256]{2,1,0:T(8,128)(2,1)S(1)}, bf16[2,1152,256]{2,1,0:T(8,128)(2,1)S(1)}, u32[]{:S(2)}, u32[]{:S(2)}) collective-permute-start(bf16[2,1152,256]{2,1,0:T(8,128)(2,1)S(1)} %shard_map.88.refs_3_.refs_5_), channel_id=1, source_target_pairs={{0,24},{8,0},{16,8},{24,16},{1,25},{9,1},{17,9},{25,17},{2,26},{10... | collective-permute-start | bytes 3538952 | tf_op jit(solution)/shard_map/ppermute | solution.py:31
  31.0 28.9 %collective-permute-start.14 = (bf16[2,1152,256]{2,1,0:T(8,128)(2,1)S(1)}, bf16[2,1152,256]{2,1,0:T(8,128)(2,1)S(1)}, u32[]{:S(2)}, u32[]{:S(2)}) collective-permute-start(bf16[2,1152,256]{2,1,0:T(8,128)(2,1)S(1)} %shard_map.88.refs_3_.refs_5_), channel_id=1, source_target_pairs={{0,8},{8,16},{16,24},{24,0},{1,9},{9,17},{17,25},{25,1},{2,10},{10... | collective-permute-start | bytes 3538952 | tf_op jit(solution)/shard_map/ppermute | solution.py:31
  58.3 3.2 %copy-start = (bf16[512,4096]{1,0:T(8,128)(2,1)S(1)}, bf16[512,4096]{1,0:T(8,128)(2,1)}, u32[]{:S(2)}) copy-start(bf16[512,4096]{1,0:T(8,128)(2,1)} %own_ref.1) | copy-start | bytes 12582916
  58.3 13.4 %collective-permute-start.15 = (bf16[1152,256]{1,0:T(8,128)(2,1)S(1)}, bf16[1152,256]{1,0:T(8,128)(2,1)S(1)}, u32[]{:S(2)}, u32[]{:S(2)}) collective-permute-start(bf16[1152,256]{1,0:T(8,128)(2,1)S(1)} %get-tuple-element.135), channel_id=1, source_target_pairs={{0,96},{32,0},{64,32},{96,64},{1,97},{33,1},{65,33},{97,65},{2,98}... | collective-permute-start | bytes 1769480 | tf_op jit(solution)/shard_map/ppermute | solution.py:31
  58.7 14.6 %collective-permute-start.16 = (bf16[1152,256]{1,0:T(8,128)(2,1)S(1)}, bf16[1152,256]{1,0:T(8,128)(2,1)S(1)}, u32[]{:S(2)}, u32[]{:S(2)}) collective-permute-start(bf16[1152,256]{1,0:T(8,128)(2,1)S(1)} %get-tuple-element.136), channel_id=1, source_target_pairs={{0,32},{32,64},{64,96},{96,0},{1,33},{33,65},{65,97},{97,1},{2,34}... | collective-permute-start | bytes 1769480 | tf_op jit(solution)/shard_map/ppermute | solution.py:31
  60.0 16.9 %collective-permute-start.17 = (bf16[1152,256]{1,0:T(8,128)(2,1)S(1)}, bf16[1152,256]{1,0:T(8,128)(2,1)S(1)}, u32[]{:S(2)}, u32[]{:S(2)}) collective-permute-start(bf16[1152,256]{1,0:T(8,128)(2,1)S(1)} %get-tuple-element.149), channel_id=1, source_target_pairs={{0,24},{8,0},{16,8},{24,16},{1,25},{9,1},{17,9},{25,17},{2,26},{10... | collective-permute-start | bytes 1769480 | tf_op jit(solution)/shard_map/ppermute | solution.py:31
  60.0 16.8 %collective-permute-start.18 = (bf16[1152,256]{1,0:T(8,128)(2,1)S(1)}, bf16[1152,256]{1,0:T(8,128)(2,1)S(1)}, u32[]{:S(2)}, u32[]{:S(2)}) collective-permute-start(bf16[1152,256]{1,0:T(8,128)(2,1)S(1)} %get-tuple-element.150), channel_id=1, source_target_pairs={{0,8},{8,16},{16,24},{24,0},{1,9},{9,17},{17,25},{25,1},{2,10},{10... | collective-permute-start | bytes 1769480 | tf_op jit(solution)/shard_map/ppermute | solution.py:31
  96.1 7.0 %collective-permute-start.19 = (bf16[1024,512]{1,0:T(8,128)(2,1)S(1)}, bf16[1024,512]{1,0:T(8,128)(2,1)S(1)}, u32[]{:S(2)}, u32[]{:S(2)}) collective-permute-start(bf16[1024,512]{1,0:T(8,128)(2,1)S(1)} %get-tuple-element.160), channel_id=1, source_target_pairs={{0,4},{4,0},{1,5},{5,1},{2,6},{6,2},{3,7},{7,3},{8,12},{12,8},{9,1... | collective-permute-start | bytes 3145736 | tf_op jit(solution)/shard_map/ppermute | solution.py:31
  103.4 15.8 %collective-permute-start.20 = (bf16[512,512]{1,0:T(8,128)(2,1)S(1)}, bf16[512,512]{1,0:T(8,128)(2,1)S(1)}, u32[]{:S(2)}, u32[]{:S(2)}) collective-permute-start(bf16[512,512]{1,0:T(8,128)(2,1)S(1)} %get-tuple-element.175), channel_id=1, source_target_pairs={{0,1},{1,2},{2,3},{3,0},{4,5},{5,6},{6,7},{7,4},{8,9},{9,10},{10,1... | collective-permute-start | bytes 1572872 | tf_op jit(solution)/shard_map/ppermute | solution.py:31
  104.8 14.5 %collective-permute-start.21 = (bf16[512,512]{1,0:T(8,128)(2,1)S(1)}, bf16[512,512]{1,0:T(8,128)(2,1)S(1)}, u32[]{:S(2)}, u32[]{:S(2)}) collective-permute-start(bf16[512,512]{1,0:T(8,128)(2,1)S(1)} %get-tuple-element.176), channel_id=1, source_target_pairs={{0,3},{1,0},{2,1},{3,2},{4,7},{5,4},{6,5},{7,6},{8,11},{9,8},{10,9... | collective-permute-start | bytes 1572872 | tf_op jit(solution)/shard_map/ppermute | solution.py:31
  119.9 26.3 %collective-permute-start.26 = (bf16[1024,512]{1,0:T(8,128)(2,1)S(1)}, bf16[1024,512]{1,0:T(8,128)(2,1)S(1)}, u32[]{:S(2)}, u32[]{:S(2)}) collective-permute-start(bf16[1024,512]{1,0:T(8,128)(2,1)S(1)} %get-tuple-element.196), channel_id=1, source_target_pairs={{0,4},{4,0},{1,5},{5,1},{2,6},{6,2},{3,7},{7,3},{8,12},{12,8},{9,1... | collective-permute-start | bytes 3145736 | tf_op jit(solution)/shard_map/ppermute | solution.py:31
  120.4 21.1 %collective-permute-start.22 = (bf16[512,512]{1,0:T(8,128)(2,1)S(1)}, bf16[512,512]{1,0:T(8,128)(2,1)S(1)}, u32[]{:S(2)}, u32[]{:S(2)}) collective-permute-start(bf16[512,512]{1,0:T(8,128)(2,1)S(1)} %get-tuple-element.192), channel_id=1, source_target_pairs={{0,1},{1,2},{2,3},{3,0},{4,5},{5,6},{6,7},{7,4},{8,9},{9,10},{10,1... | collective-permute-start | bytes 1572872 | tf_op jit(solution)/shard_map/ppermute | solution.py:31
  121.1 20.3 %collective-permute-start.23 = (bf16[512,512]{1,0:T(8,128)(2,1)S(1)}, bf16[512,512]{1,0:T(8,128)(2,1)S(1)}, u32[]{:S(2)}, u32[]{:S(2)}) collective-permute-start(bf16[512,512]{1,0:T(8,128)(2,1)S(1)} %get-tuple-element.193), channel_id=1, source_target_pairs={{0,3},{1,0},{2,1},{3,2},{4,7},{5,4},{6,5},{7,6},{8,11},{9,8},{10,9... | collective-permute-start | bytes 1572872 | tf_op jit(solution)/shard_map/ppermute | solution.py:31
  123.0 23.2 %collective-permute-start.24 = (bf16[512,512]{1,0:T(8,128)(2,1)S(1)}, bf16[512,512]{1,0:T(8,128)(2,1)S(1)}, u32[]{:S(2)}, u32[]{:S(2)}) collective-permute-start(bf16[512,512]{1,0:T(8,128)(2,1)S(1)} %get-tuple-element.194), channel_id=1, source_target_pairs={{0,1},{1,2},{2,3},{3,0},{4,5},{5,6},{6,7},{7,4},{8,9},{9,10},{10,1... | collective-permute-start | bytes 1572872 | tf_op jit(solution)/shard_map/ppermute | solution.py:31
  123.0 23.2 %collective-permute-start.25 = (bf16[512,512]{1,0:T(8,128)(2,1)S(1)}, bf16[512,512]{1,0:T(8,128)(2,1)S(1)}, u32[]{:S(2)}, u32[]{:S(2)}) collective-permute-start(bf16[512,512]{1,0:T(8,128)(2,1)S(1)} %get-tuple-element.195), channel_id=1, source_target_pairs={{0,3},{1,0},{2,1},{3,2},{4,7},{5,4},{6,5},{7,6},{8,11},{9,8},{10,9... | collective-permute-start | bytes 1572872 | tf_op jit(solution)/shard_map/ppermute | solution.py:31
